TPU v7x, 32 devices: a whole 2x2x4 slice. The times are simulated.
32 devices in a mesh: group: 2 (over x), kvp: 16 (over z, y, core).
Axes of the slice: x: 2, y: 2, z: 4, core: 2. Of those that a mesh axis runs over, the one named last changes fastest.
Arguments:
- queries: bfloat16 [8, 8192], P('group'), parts along dimension 0, may hold values from -240 to 240
- key_cache: bfloat16 [1536, 64, 512], P(('group', 'kvp')), parts along dimension 0, may hold values from -6 to 6
- value_cache: bfloat16 [1536, 64, 512], P(('group', 'kvp')), parts along dimension 0, may hold values from -6 to 6
- key_scale: float32 [1536, 4], P(('group', 'kvp')), parts along dimension 0, may hold values from 0.5 to 2
- value_scale: float32 [1536, 4], P(('group', 'kvp')), parts along dimension 0, may hold values from 0.5 to 2
- page_table: int32 [8, 192], P('group', 'kvp'), parts along dimension 0, may hold values from 0 to 47, as said below
- lengths: int32 [8], P('group'), parts along dimension 0, may hold values from 9217 to 12288, as said below
- out_weight: bfloat16 [8192, 16384], P('kvp'), may hold values from -2 to 2
Outputs:
- projected: bfloat16 [8, 16384], P('group'), parts along dimension 0
There are 2 independent parts, one for each index of `group`. A program takes and returns all parts, laid end to end along the dimension named above; an argument that names none is the same for every part. Nothing has to cross between parts.
Inputs may be any that keep to these rules, and one draw needn't show every extreme that they name: `page_table`: every kvp index's 48 slots are each used by exactly one page of one request. `lengths`: some request uses its whole cache of 12288 positions.
All inputs are finite; a program needn't handle non-finite values.
Results may differ from a plain program's by a relative error of at most 0.0064.
Values may be sent and summed in bfloat16 or wider, within the bound.
No kernel may reach another device: no remote copies, remote signals or barrier semaphores. Data moves between devices by JAX's collectives and lax.ppermute only.
A program may use at most 128 MiB of HBM per device.

v0:
```python
import math

import jax
import jax.numpy as jnp
from jax import lax
from jax.sharding import PartitionSpec as P

QH = 64
KVH = 4
HD = 128
PAGE = 64


def combine_blocks(partials, maxima, totals, axis):
    highest = jnp.max(maxima, axis=axis, keepdims=True)
    rescale = jnp.exp(maxima - highest)
    numerator = jnp.sum(partials * rescale[..., None], axis=axis)
    denominator = jnp.sum(totals * rescale, axis=axis)
    return numerator / denominator[..., None]


def body(queries, key_cache, value_cache, key_scale, value_scale, page_table, lengths, out_weight):
    device_index = lax.axis_index("kvp")
    row_count = queries.shape[0]
    pages_dev = page_table.shape[1]
    group_size = QH // KVH
    page_keys = key_cache[page_table].reshape(row_count, pages_dev * PAGE, KVH, HD)
    page_values = value_cache[page_table].reshape(row_count, pages_dev * PAGE, KVH, HD)
    key_factor = jnp.transpose(key_scale[page_table], (0, 2, 1)) * (1.0 / math.sqrt(HD))
    value_factor = jnp.transpose(value_scale[page_table], (0, 2, 1))
    query = queries.reshape(row_count, KVH, group_size, HD)
    raw_scores = jnp.einsum("rkgd,rtkd->rkgt", query, page_keys, preferred_element_type=jnp.float32)
    raw_scores = raw_scores.reshape(row_count, KVH, group_size, pages_dev, PAGE)
    scores = raw_scores * key_factor[:, :, None, :, None]
    page_start = (device_index * pages_dev + jnp.arange(pages_dev, dtype=jnp.int32)) * PAGE
    positions = page_start[:, None] + jnp.arange(PAGE, dtype=jnp.int32)[None, :]
    visible = (positions[None, :, :] < lengths[:, None, None])[:, None, None, :, :]
    maxima = jnp.max(jnp.where(visible, scores, -1e30), axis=(3, 4))
    probs = jnp.where(visible, jnp.exp(scores - maxima[..., None, None]), 0.0)
    totals = jnp.sum(probs, axis=(3, 4))
    weights = (probs * value_factor[:, :, None, :, None]).astype(jnp.bfloat16)
    weights = weights.reshape(row_count, KVH, group_size, pages_dev * PAGE)
    partials = jnp.einsum(
        "rkgt,rtkd->rkgd", weights, page_values, preferred_element_type=jnp.float32
    )
    rounded = lax.optimization_barrier(partials.astype(jnp.bfloat16)).astype(jnp.float32)
    rounded = rounded.reshape(row_count, QH, HD)
    maxima = maxima.reshape(row_count, QH)
    totals = totals.reshape(row_count, QH)
    heads_dev = out_weight.shape[0] // HD
    attended = combine_blocks(
        lax.all_to_all(rounded[None], "kvp", split_axis=2, concat_axis=0, tiled=True),
        lax.all_to_all(maxima[None], "kvp", split_axis=2, concat_axis=0, tiled=True),
        lax.all_to_all(totals[None], "kvp", split_axis=2, concat_axis=0, tiled=True),
        0,
    )
    attended_rounded = attended.astype(jnp.bfloat16).reshape(attended.shape[0], heads_dev * HD)
    partial_terms = jnp.dot(attended_rounded, out_weight, preferred_element_type=jnp.float32)
    projected = lax.psum(partial_terms, "kvp").astype(jnp.bfloat16)
    return projected


def solution(mesh):
    placed = (
        P("group", None),
        P(("group", "kvp"), None, None),
        P(("group", "kvp"), None, None),
        P(("group", "kvp"), None),
        P(("group", "kvp"), None),
        P("group", "kvp"),
        P("group"),
        P("kvp", None),
    )
    return jax.shard_map(
        body, mesh=mesh, in_specs=placed, out_specs=P("group", None), check_vma=False
    )
```

profile of v0, /device:TPU:0, one launch (start us, length us, event | category | flops | bytes accessed | tf_op | source)
XLA Modules:
  0.0 129.7 jit_solution(10616795839329662468)
XLA Ops:
  0.0 0.8 compare_select_fusion
  0.9 1.0 copy-done
  1.9 2.6 %gather_fusion = bf16[48,64,512]{2,1,0:T(8,128)(2,1)} fusion(bf16[48,64,512]{2,1,0:T(8,128)(2,1)S(1)} %copy-done, s32[1024]{0:T(1024)S(1)} %pad_clamp_fusion), kind=kCustom, calls=%fused_computation | custom fusion | bytes 6291648 | tf_op jit(solution)/shard_map/gather | solution.py:27
  4.5 5.6 %reshape.67 = bf16[4,768,4,128]{3,2,1,0:T(4,128)(2,1)} reshape(bf16[48,64,512]{2,1,0:T(8,128)(2,1)} %gather_fusion) | data formatting | bytes 6291456 | tf_op jit(solution)/shard_map/reshape | solution.py:27
  10.0 0.1 copy.66
  10.1 0.6 gather_fusion.1
  10.9 0.1 mul.64
  11.0 0.1 mul.65
  11.4 3.7 %select_reduce_fusion = (f32[4,4,16]{2,1,0:T(4,128)S(1)}, f32[4,4,768,16]{2,3,1,0:T(8,128)}) fusion(pred[4,768]{1,0:T(4,128)(4,1)S(1)} %broadcast_compare_fusion, f32[4,4,768]{2,1,0:T(4,128)S(1)} %mul.65, bf16[4,4,16,128]{3,2,1,0:T(8,128)(2,1)S(1)} %bitcast.50, bf16[4,768,4,128]{3,2,1,0:T(4,128)(2,1)} %reshape.67), kind=kOutput, calls=%fused_computation.14 | convolution fusion | flops 50921216 | bytes 4050944 | tf_op jit(solution)/shard_map/rkgd,rtkd->rkgt/dot_general | solution.py:32
  15.1 0.7 copy.74
  15.8 7.4 %all-to-all-start.1 = ((f32[1,4,64]{1,0,2:T(1,128)}), f32[1,4,64]{1,0,2:T(1,128)S(1)}, u32[]{:S(2)}, u32[]{:S(2)}) async-start(f32[1,4,64]{1,0,2:T(1,128)} %bitcast.7), calls=%async_computation.1 | async-start | bytes 65536 | tf_op jit(solution)/shard_map/all_to_all | solution.py:53
  23.2 1.4 %bitcast_reduce_fusion = f32[4,4,16]{2,1,0:T(4,128)S(1)} fusion(f32[4,4,768,16]{2,3,1,0:T(8,128)} %get-tuple-element.8, f32[4,4,16]{2,1,0:T(4,128)S(1)} %get-tuple-element.7, pred[4,768]{1,0:T(4,128)(4,1)S(1)} %broadcast_compare_fusion), kind=kLoop, calls=%fused_computation.10 | loop fusion | flops 589568 | bytes 791552 | tf_op jit(solution)/shard_map/reduce_sum | solution.py:40
  24.6 0.7 copy.81
  25.3 4.4 %gather_fusion.3 = bf16[48,64,512]{2,1,0:T(8,128)(2,1)} fusion(bf16[48,64,512]{2,1,0:T(8,128)(2,1)} %param.10, s32[1024]{0:T(1024)S(1)} %pad_clamp_fusion), kind=kCustom, calls=%fused_computation.3 | custom fusion | bytes 6291648 | tf_op jit(solution)/shard_map/gather | solution.py:28
  29.8 5.5 %reshape.69 = bf16[4,768,4,128]{3,2,1,0:T(4,128)(2,1)} reshape(bf16[48,64,512]{2,1,0:T(8,128)(2,1)} %gather_fusion.3) | data formatting | bytes 6291456 | tf_op jit(solution)/shard_map/reshape | solution.py:28
  35.3 0.1 copy.69
  35.4 0.6 gather_fusion.2
  36.2 0.1 mul.68
  36.3 0.1 mul.69
  36.4 6.0 %all-to-all-start.2 = ((f32[1,4,64]{1,0,2:T(1,128)}), f32[1,4,64]{1,0,2:T(1,128)S(1)}, u32[]{:S(2)}, u32[]{:S(2)}) async-start(f32[1,4,64]{1,0,2:T(1,128)} %bitcast.11), calls=%async_computation.2 | async-start | bytes 65536 | tf_op jit(solution)/shard_map/all_to_all | solution.py:54
  42.4 2.8 %fusion.7 = bf16[4,4,16,128]{3,2,1,0:T(8,128)(2,1)S(1)} fusion(bf16[4,768,4,128]{3,2,1,0:T(4,128)(2,1)} %reshape.69, f32[4,4,768,16]{2,3,1,0:T(8,128)} %get-tuple-element.8, f32[4,4,768]{2,1,0:T(4,128)S(1)} %mul.69, f32[4,4,16]{2,1,0:T(4,128)S(1)} %get-tuple-element.7, pred[4,768]{1,0:T(4,128)(4,1)S(1)} %broadcast_compare_fusion), kind=kOutput, calls=%fused_computation.9 | convolution fusion | flops 51150848 | bytes 4050944 | tf_op jit(solution)/shard_map/rkgt,rtkd->rkgd/dot_general | solution.py:43
  45.2 0.7 copy.73
  45.9 0.2 copy.80
  46.1 2.9 %all-to-all-done.2 = f32[1,4,64]{1,0,2:T(1,128)S(1)} async-done(((f32[1,4,64]{1,0,2:T(1,128)}), f32[1,4,64]{1,0,2:T(1,128)S(1)}, u32[]{:S(2)}, u32[]{:S(2)}) %all-to-all-start.2) | async-done | bytes 1056 | tf_op jit(solution)/shard_map/all_to_all | solution.py:54
  49.0 3.5 %all-to-all-start = ((f32[1,4,64,128]{3,1,0,2:T(4,128)}), f32[1,4,64,128]{3,1,0,2:T(4,128)S(1)}, u32[]{:S(2)}, u32[]{:S(2)}) async-start(f32[1,4,64,128]{3,1,0,2:T(4,128)} %copy.73), calls=%async_computation | async-start | bytes 262144 | tf_op jit(solution)/shard_map/all_to_all | solution.py:52
  52.6 0.2 copy.82
  52.8 0.2 copy.76
  53.0 0.1 copy.79
  53.1 7.3 %all-to-all-done = f32[1,4,64,128]{3,1,0,2:T(4,128)S(1)} async-done(((f32[1,4,64,128]{3,1,0,2:T(4,128)}), f32[1,4,64,128]{3,1,0,2:T(4,128)S(1)}, u32[]{:S(2)}, u32[]{:S(2)}) %all-to-all-start) | async-done | bytes 131104 | tf_op jit(solution)/shard_map/all_to_all | solution.py:52
  60.5 0.1 multiply_reduce_fusion
  60.6 8.1 %fusion.18 = f32[4,16384]{1,0:T(4,128)S(1)} fusion(bf16[512,16384]{1,0:T(8,128)(2,1)} %param.15, f32[4,4,128]{2,0,1:T(4,128)S(1)} %multiply_reduce_fusion, f32[4,4]{0,1:T(4,128)S(1)} %copy.79), kind=kOutput, calls=%fused_computation.31 | convolution fusion | flops 67112960 | bytes 17047616 | tf_op jit(solution)/shard_map/dot_general | solution.py:58
  68.7 61.1 %all-reduce.1 = bf16[4,16384]{1,0:T(4,128)(2,1)} all-reduce(f32[4,16384]{1,0:T(4,128)S(1)} %fusion.18), channel_id=1, replica_groups=mesh['group'=2,'kvp'=16] {'kvp'}, use_global_device_ids=true, to_apply=%region_5.6 | all-reduce | flops 65536 | bytes 393216 | tf_op jit(solution)/shard_map/psum | solution.py:59
  (26 shorter events, 0.7 us)
Async XLA Ops:
  0.0 1.9 %copy-start = (bf16[48,64,512]{2,1,0:T(8,128)(2,1)S(1)}, bf16[48,64,512]{2,1,0:T(8,128)(2,1)}, u32[]{:S(2)}) copy-start(bf16[48,64,512]{2,1,0:T(8,128)(2,1)} %param.9) | copy-start | bytes 9437188
  4.5 5.6 %copy-start.2 = (f32[48,4]{0,1:T(4,128)S(1)}, f32[48,4]{0,1:T(4,128)}, u32[]{:S(2)}) copy-start(f32[48,4]{0,1:T(4,128)} %param.11) | copy-start | bytes 2308
  4.5 6.8 %copy-start.1 = (bf16[4,8192]{1,0:T(4,128)(2,1)S(1)}, bf16[4,8192]{1,0:T(4,128)(2,1)}, u32[]{:S(2)}) copy-start(bf16[4,8192]{1,0:T(4,128)(2,1)} %param.8) | copy-start | bytes 196612
  4.5 6.8 %copy-start.4 = (s32[4]{0:T(128)S(1)}, s32[4]{0:T(128)}, u32[]{:S(2)}) copy-start(s32[4]{0:T(128)} %param.14) | copy-start | bytes 52
  15.8 20.6 %all-to-all-start.1 = ((f32[1,4,64]{1,0,2:T(1,128)}), f32[1,4,64]{1,0,2:T(1,128)S(1)}, u32[]{:S(2)}, u32[]{:S(2)}) async-start(f32[1,4,64]{1,0,2:T(1,128)} %bitcast.7), calls=%async_computation.1 | async-start | bytes 65536 | tf_op jit(solution)/shard_map/all_to_all | solution.py:53
  29.8 5.5 %copy-start.3 = (f32[48,4]{0,1:T(4,128)S(1)}, f32[48,4]{0,1:T(4,128)}, u32[]{:S(2)}) copy-start(f32[48,4]{0,1:T(4,128)} %param.12) | copy-start | bytes 2308
  36.4 12.7 %all-to-all-start.2 = ((f32[1,4,64]{1,0,2:T(1,128)}), f32[1,4,64]{1,0,2:T(1,128)S(1)}, u32[]{:S(2)}, u32[]{:S(2)}) async-start(f32[1,4,64]{1,0,2:T(1,128)} %bitcast.11), calls=%async_computation.2 | async-start | bytes 65536 | tf_op jit(solution)/shard_map/all_to_all | solution.py:54
  49.0 11.4 %all-to-all-start = ((f32[1,4,64,128]{3,1,0,2:T(4,128)}), f32[1,4,64,128]{3,1,0,2:T(4,128)S(1)}, u32[]{:S(2)}, u32[]{:S(2)}) async-start(f32[1,4,64,128]{3,1,0,2:T(4,128)} %copy.73), calls=%async_computation | async-start | bytes 262144 | tf_op jit(solution)/shard_map/all_to_all | solution.py:52
where the time goes:
time: 130 us
  blocking collectives  61.1 us (47%)
  local copies, waits for them, and re-layouts  24.2 us (19%)
  starting transfers between devices  16.9 us (13%)
  matrix products  14.6 us (11%)
  waiting for transfers between devices  10.3 us (8%)
  other arithmetic  2.61 us (2%)
    psum x1, blocking collectives, body(): projected = lax.psum(partial_terms, 'kvp').astype(jnp.bfloat16)  61.1 us
    dot_general x1, matrix products, body(): jnp.dot(attended_rounded, out_weight, preferred_element_type=jnp.float32)  8.09 us
    all_to_all x1, starting transfers between devices, body(): lax.all_to_all(maxima[None], 'kvp', split_axis=2, concat_axis=0, tiled=True)  7.39 us
    all_to_all x1, waiting for transfers between devices, body(): lax.all_to_all(rounded[None], 'kvp', split_axis=2, concat_axis=0, tiled=T...  7.34 us
    all_to_all x1, starting transfers between devices, body(): lax.all_to_all(totals[None], 'kvp', split_axis=2, concat_axis=0, tiled=True)  6.02 us
    reshape x1, local copies, waits for them, and re-layouts, body(): key_cache[page_table].reshape(row_count, pages_dev * PAGE, KVH, HD)  5.56 us
    reshape x1, local copies, waits for them, and re-layouts, body(): value_cache[page_table].reshape(row_count, pages_dev * PAGE, KVH, HD)  5.54 us
    gather x1, local copies, waits for them, and re-layouts, body(): value_cache[page_table].reshape(row_count, pages_dev * PAGE, KVH, HD)  4.44 us
  transfers between devices with their start and end apart: 3, of which 2 were waited for; matrix products, arithmetic and copies ran while one was open for 13% of the time, Pallas kernels for 0%

commit v1 on v0

v1 whole, which is shorter than its diff:
```python
import functools
import math

import jax
import jax.numpy as jnp
from jax import lax
from jax.experimental import pallas as pl
from jax.experimental.pallas import tpu as pltpu
from jax.sharding import PartitionSpec as P

HD = 128
PAGE = 64
ATTEND_VMEM = 24 * 1024 * 1024
PROJECT_VMEM = 40 * 1024 * 1024


def split_two(value):
    high = value.astype(jnp.bfloat16).astype(jnp.float32)
    low = (value - high).astype(jnp.bfloat16).astype(jnp.float32)
    return high, low


def attend_kernel(
    heads_dev, table, lengths, key_scale, value_scale, queries, keys, values, packed,
    key_buf, value_buf, query_rows, staged, sems,
):
    rows, pages = table.shape
    kv_heads = key_scale.shape[0]
    heads = queries.shape[1] // HD
    group = heads // kv_heads
    devices, stacked, _ = packed.shape
    part_rows = stacked // 2
    context = pages * PAGE

    for r in range(rows):
        for which, source, target in ((0, keys, key_buf), (1, values, value_buf)):
            for p in range(pages):
                pltpu.make_async_copy(
                    source.at[table[r, p]], target.at[r, pl.ds(p * PAGE, PAGE), :], sems.at[which, r]
                ).start()

    for h in range(heads):
        query_rows[h * rows : (h + 1) * rows, :] = queries[:, h * HD : (h + 1) * HD].astype(jnp.float32)
    if part_rows > rows * heads_dev:
        staged[...] = jnp.zeros_like(staged)

    first = lax.axis_index("kvp") * context
    place = first + lax.broadcasted_iota(jnp.int32, (group, context), 1)
    lane = lax.broadcasted_iota(jnp.int32, (group, HD), 1)

    def factors(scales, r, k, times):
        columns = []
        for p in range(0, pages, 2):
            left = scales[k, table[r, p]] * times
            right = scales[k, table[r, p + 1]] * times
            columns.append(jnp.where(lane < PAGE, left, right))
        return jnp.concatenate(columns, axis=1)

    for r in range(rows):
        pltpu.make_async_copy(key_buf.at[r], key_buf.at[r], sems.at[0, r]).wait()
        visible = place < lengths[r]
        query = query_rows[pl.ds(r, heads, stride=rows), :].astype(jnp.bfloat16)
        probs = []
        stats = []
        for k in range(kv_heads):
            scores = lax.dot_general(
                query[k * group : (k + 1) * group],
                key_buf[r, :, k * HD : (k + 1) * HD],
                (((1,), (1,)), ((), ())),
                preferred_element_type=jnp.float32,
            )
            scores = scores * factors(key_scale, r, k, 1.0 / math.sqrt(HD))
            highest = jnp.max(jnp.where(visible, scores, -1e30), axis=1, keepdims=True)
            high, low = split_two(highest)
            prob = jnp.where(visible, jnp.exp(scores - (high + low)), 0.0)
            total_high, total_low = split_two(jnp.sum(prob, axis=1, keepdims=True))
            stats.append(
                jnp.where(lane == 0, high, jnp.where(lane == 1, low, jnp.where(lane == 2, total_high, total_low)))
            )
            probs.append((prob * factors(value_scale, r, k, 1.0)).astype(jnp.bfloat16))
        pltpu.make_async_copy(value_buf.at[r], value_buf.at[r], sems.at[1, r]).wait()
        for k in range(kv_heads):
            partial = jnp.dot(
                probs[k], value_buf[r, :, k * HD : (k + 1) * HD], preferred_element_type=jnp.float32
            )
            for start in range(0, group, heads_dev):
                d = (k * group + start) // heads_dev
                here = slice(r * heads_dev, (r + 1) * heads_dev)
                staged[0, d, here, :] = partial[start : start + heads_dev]
                staged[1, d, here, :] = stats[k][start : start + heads_dev]
    packed[:, :part_rows, :] = staged[0].astype(jnp.bfloat16)
    packed[:, part_rows:, :] = staged[1].astype(jnp.bfloat16)


def project_kernel(heads_dev, packed, weight, terms, weight_buf, attended, sems):
    devices, rows, width = terms.shape
    copies = []
    for d in range(devices):
        copy = pltpu.make_async_copy(weight.at[:, pl.ds(d * width, width)], weight_buf.at[d], sems.at[d])
        copy.start()
        copies.append(copy)
    part_rows = packed.shape[1] // 2
    partial = packed[:, :part_rows, :].astype(jnp.float32)
    stats = packed[:, part_rows:, :].astype(jnp.float32)
    maxima = stats[:, :, 0:1] + stats[:, :, 1:2]
    totals = stats[:, :, 2:3] + stats[:, :, 3:4]
    rescale = jnp.exp(maxima - jnp.max(maxima, axis=0, keepdims=True))
    attended[...] = jnp.sum(partial * rescale, axis=0) / jnp.sum(totals * rescale, axis=0)
    left = jnp.concatenate(
        [attended[pl.ds(j, rows, stride=heads_dev), :].astype(jnp.bfloat16) for j in range(heads_dev)], axis=1
    )
    for d in range(devices):
        copies[d].wait()
        terms[d] = jnp.dot(left, weight_buf[d], preferred_element_type=jnp.float32).astype(terms.dtype)


def body(queries, key_cache, value_cache, key_scale, value_scale, page_table, lengths, out_weight, *, devices):
    rows, pages = page_table.shape
    heads_dev = out_weight.shape[0] // HD
    heads = queries.shape[1] // HD
    features = out_weight.shape[1]
    columns = key_cache.shape[2]
    part_rows = -(-rows * heads_dev // 16) * 16
    smem = pl.BlockSpec(memory_space=pltpu.SMEM)
    vmem = pl.BlockSpec(memory_space=pltpu.VMEM)
    hbm = pl.BlockSpec(memory_space=pltpu.HBM)
    packed = pl.pallas_call(
        functools.partial(attend_kernel, heads_dev),
        out_shape=jax.ShapeDtypeStruct((devices, 2 * part_rows, HD), jnp.bfloat16),
        in_specs=[smem, smem, smem, smem, vmem, hbm, hbm],
        out_specs=vmem,
        scratch_shapes=[
            pltpu.VMEM((rows, pages * PAGE, columns), jnp.bfloat16),
            pltpu.VMEM((rows, pages * PAGE, columns), jnp.bfloat16),
            pltpu.VMEM((heads * rows, HD), jnp.float32),
            pltpu.VMEM((2, devices, part_rows, HD), jnp.float32),
            pltpu.SemaphoreType.DMA((2, rows)),
        ],
        compiler_params=pltpu.CompilerParams(vmem_limit_bytes=ATTEND_VMEM),
        cost_estimate=pl.CostEstimate(
            flops=4 * heads * rows * pages * PAGE * HD,
            bytes_accessed=4 * rows * pages * PAGE * columns,
            transcendentals=heads * rows * pages * PAGE,
        ),
        name="attend",
    )(page_table, lengths, key_scale.T, value_scale.T, queries, key_cache, value_cache)

    received = lax.all_to_all(packed, "kvp", split_axis=0, concat_axis=0, tiled=True)

    width = features // devices
    terms = pl.pallas_call(
        functools.partial(project_kernel, heads_dev),
        out_shape=jax.ShapeDtypeStruct((devices, rows, width), jnp.bfloat16),
        in_specs=[vmem, hbm],
        out_specs=vmem,
        scratch_shapes=[
            pltpu.VMEM((devices, heads_dev * HD, width), jnp.bfloat16),
            pltpu.VMEM((part_rows, HD), jnp.float32),
            pltpu.SemaphoreType.DMA((devices,)),
        ],
        compiler_params=pltpu.CompilerParams(vmem_limit_bytes=PROJECT_VMEM),
        cost_estimate=pl.CostEstimate(
            flops=2 * rows * out_weight.size, bytes_accessed=2 * out_weight.size, transcendentals=0
        ),
        name="project",
    )(received, out_weight)

    spread = lax.all_to_all(terms, "kvp", split_axis=0, concat_axis=0, tiled=True)
    mine = jnp.sum(spread.astype(jnp.float32), axis=0).astype(jnp.bfloat16)
    return lax.all_gather(mine, "kvp", axis=1, tiled=True)


def solution(mesh):
    placed = (
        P("group", None),
        P(("group", "kvp"), None, None),
        P(("group", "kvp"), None, None),
        P(("group", "kvp"), None),
        P(("group", "kvp"), None),
        P("group", "kvp"),
        P("group"),
        P("kvp", None),
    )
    return jax.shard_map(
        functools.partial(body, devices=mesh.shape["kvp"]),
        mesh=mesh,
        in_specs=placed,
        out_specs=P("group", None),
        check_vma=False,
    )
```

time: 130 us -> 70.9 us (0.55)
  Pallas kernels: 0 us -> 18.4 us
  blocking collectives: 61.1 us -> 44.1 us
  starting transfers between devices: 16.9 us -> 0 us
  local copies, waits for them, and re-layouts: 24.2 us -> 7.97 us
  matrix products: 14.6 us -> 0 us
  waiting for transfers between devices: 10.3 us -> 0 us
  other arithmetic: 2.61 us -> 0.07 us
    psum x1 -> x0, blocking collectives: 61.1 us -> none  [body(): projected = lax.psum(partial_terms, 'kvp').astype(jnp.bfloat16)]
    all_to_all x0 -> x2, blocking collectives: none -> 25.6 us  [the longest x1 15.1 us: body(): lax.all_to_all(packed, 'kvp', split_axis=0, concat_axis=0, tiled=True)]
    all_gather x0 -> x1, blocking collectives: none -> 18.4 us  [body(): return lax.all_gather(mine, 'kvp', axis=1, tiled=True)]
    pallas_call x0 -> x2, Pallas kernels: none -> 18.4 us  [the longest x1 12.1 us: body(): pl.pallas_call(functools.partial(attend_kernel, heads_dev), out_shape=jax...]
    all_to_all x3 -> x0, starting transfers between devices: 16.9 us -> none  [the longest x1 7.39 us: body(): lax.all_to_all(maxima[None], 'kvp', split_axis=2, concat_axis=0, tiled=True)]
    dot_general x3 -> x0, matrix products: 14.6 us -> none  [the longest x1 8.09 us: body(): jnp.dot(attended_rounded, out_weight, preferred_element_type=jnp.float32)]
    reshape x2 -> x0, local copies, waits for them, and re-layouts: 11.1 us -> none  [the longest x1 5.56 us: body(): key_cache[page_table].reshape(row_count, pages_dev * PAGE, KVH, HD)]
    all_to_all x3 -> x0, waiting for transfers between devices: 10.3 us -> none  [the longest x1 7.34 us: body(): lax.all_to_all(rounded[None], 'kvp', split_axis=2, concat_axis=0, tiled=T...]
  transfers between devices with their start and end apart: 3 -> 0, of which waited for: 2 -> 0; matrix products, arithmetic and copies ran while one was open for 13% -> 0% of each run, Pallas kernels for 0% -> 0%
where the time goes in v1:
time: 70.9 us; the launch traced here: 70.5 us
  blocking collectives  44.1 us (62%)
  Pallas kernels  18.4 us (26%)
  local copies, waits for them, and re-layouts  7.97 us (11%)
    all_gather x1, blocking collectives, body(): return lax.all_gather(mine, 'kvp', axis=1, tiled=True)  18.4 us
    all_to_all x1, blocking collectives, body(): lax.all_to_all(packed, 'kvp', split_axis=0, concat_axis=0, tiled=True)  15.1 us
    pallas_call x1, Pallas kernels, body(): pl.pallas_call(functools.partial(attend_kernel, heads_dev), out_shape=jax...  12.1 us
    all_to_all x1, blocking collectives, body(): lax.all_to_all(terms, 'kvp', split_axis=0, concat_axis=0, tiled=True)  10.5 us
    unnamed x15, local copies, waits for them, and re-layouts  7.97 us
    pallas_call x1, Pallas kernels, body(): pl.pallas_call(functools.partial(project_kernel, heads_dev), out_shape=ja...  6.26 us

profile of v1, /device:TPU:0, one launch (start us, length us, event | category | flops | bytes accessed | tf_op | source)
XLA Modules:
  0.0 70.5 jit_solution(13393096673180055799)
XLA Ops:
  0.0 0.0 copy-start
  0.0 1.9 %copy-done = bf16[48,64,512]{2,1,0:T(8,128)(2,1)S(1)} copy-done((bf16[48,64,512]{2,1,0:T(8,128)(2,1)S(1)}, bf16[48,64,512]{2,1,0:T(8,128)(2,1)}, u32[]{:S(2)}) %copy-start) | copy-done | bytes 3145752
  1.9 0.0 copy-start.1
  1.9 1.9 %copy-done.1 = bf16[48,64,512]{2,1,0:T(8,128)(2,1)S(1)} copy-done((bf16[48,64,512]{2,1,0:T(8,128)(2,1)S(1)}, bf16[48,64,512]{2,1,0:T(8,128)(2,1)}, u32[]{:S(2)}) %copy-start.1) | copy-done | bytes 3145752
  3.8 0.0 copy-start.2
  3.8 0.8 %copy-done.2 = bf16[4,8192]{1,0:T(4,128)(2,1)S(1)} copy-done((bf16[4,8192]{1,0:T(4,128)(2,1)S(1)}, bf16[4,8192]{1,0:T(4,128)(2,1)}, u32[]{:S(2)}) %copy-start.2) | copy-done | bytes 65560
  4.6 0.0 copy-start.3
  4.6 0.7 copy-done.3
  5.3 0.0 copy-start.4
  5.3 0.7 copy-done.4
  6.0 0.0 copy-start.5
  6.0 0.7 copy-done.5
  6.7 0.0 copy-start.6
  6.7 0.7 copy-done.6
  7.3 12.1 %attend.1 = bf16[16,32,128]{2,1,0:T(8,128)(2,1)S(1)} custom-call(s32[4,12]{1,0:T(4,128)S(1)} %copy-done.3, s32[4]{0:T(128)S(1)} %copy-done.6, f32[4,48]{1,0:T(4,128)S(1)} %bitcast.2, f32[4,48]{1,0:T(4,128)S(1)} %bitcast.3, bf16[4,8192]{1,0:T(4,128)(2,1)S(1)} %copy-done.2, bf16[48,64,512]{2,1,0:T(8,128)(2,1)S(1)} %copy-done, bf16[48,64,512]{2,1,0:T(8,128)(2,1)S(1)} %copy-done.1), custom_call_target="tpu_custom_call" | custom-call | flops 100663296 | bytes 6291456 | tf_op jit(solution)/shard_map/attend/pallas_call | solution.py:127
  19.4 15.1 %all_to_all.10.packed = bf16[16,32,128]{2,1,0:T(8,128)(2,1)S(1)} all-to-all(bf16[16,32,128]{2,1,0:T(8,128)(2,1)S(1)} %attend.1), channel_id=1, replica_groups=mesh['group'=2,'kvp'=16] {'kvp'}, dimensions={0} | all-to-all | bytes 262144 | tf_op jit(solution)/shard_map/all_to_all | solution.py:148
  34.6 6.3 %project.1 = bf16[16,4,1024]{2,1,0:T(4,128)(2,1)S(1)} custom-call(bf16[16,32,128]{2,1,0:T(8,128)(2,1)S(1)} %all_to_all.10.packed, bf16[512,16384]{1,0:T(8,128)(2,1)} %weight.1), custom_call_target="tpu_custom_call" | custom-call | flops 67108864 | bytes 16777216 | tf_op jit(solution)/shard_map/project/pallas_call | solution.py:151
  40.8 10.5 %all_to_all.11 = bf16[16,4,1024]{2,1,0:T(4,128)(2,1)S(1)} all-to-all(bf16[16,4,1024]{2,1,0:T(4,128)(2,1)S(1)} %project.1), channel_id=1, replica_groups=mesh['group'=2,'kvp'=16] {'kvp'}, dimensions={0} | all-to-all | bytes 262144 | tf_op jit(solution)/shard_map/all_to_all | solution.py:168
  51.4 0.1 reduce_sum.12
  51.4 18.4 %all_gather.3 = bf16[4,16384]{1,0:T(4,128)(2,1)S(1)} all-gather(bf16[4,1024]{1,0:T(4,128)(2,1)S(1)} %reduce_sum.12), channel_id=1, replica_groups=mesh['group'=2,'kvp'=16] {'kvp'}, dimensions={1}, use_global_device_ids=true | all-gather | bytes 139264 | tf_op jit(solution)/shard_map/all_gather | solution.py:170
  69.8 0.7 copy.10
Async XLA Ops:
  0.0 1.9 %copy-start = (bf16[48,64,512]{2,1,0:T(8,128)(2,1)S(1)}, bf16[48,64,512]{2,1,0:T(8,128)(2,1)}, u32[]{:S(2)}) copy-start(bf16[48,64,512]{2,1,0:T(8,128)(2,1)} %keys.1) | copy-start | bytes 9437188
  1.9 1.9 %copy-start.1 = (bf16[48,64,512]{2,1,0:T(8,128)(2,1)S(1)}, bf16[48,64,512]{2,1,0:T(8,128)(2,1)}, u32[]{:S(2)}) copy-start(bf16[48,64,512]{2,1,0:T(8,128)(2,1)} %values.1) | copy-start | bytes 9437188
  3.8 0.8 %copy-start.2 = (bf16[4,8192]{1,0:T(4,128)(2,1)S(1)}, bf16[4,8192]{1,0:T(4,128)(2,1)}, u32[]{:S(2)}) copy-start(bf16[4,8192]{1,0:T(4,128)(2,1)} %queries.1) | copy-start | bytes 196612
  4.6 0.7 copy-start.3
  5.3 0.7 copy-start.4
  6.0 0.7 copy-start.5
  6.7 0.7 copy-start.6

commit v2 on v1

v2 whole, which is shorter than its diff:
```python
import functools
import math

import jax
import jax.numpy as jnp
from jax import lax
from jax.experimental import pallas as pl
from jax.experimental.pallas import tpu as pltpu
from jax.sharding import PartitionSpec as P

HD = 128
PAGE = 64
ATTEND_VMEM = 24 * 1024 * 1024
PROJECT_VMEM = 40 * 1024 * 1024
SMALL_VMEM = 8 * 1024 * 1024
VMEM = pl.BlockSpec(memory_space=pltpu.VMEM)
HBM = pl.BlockSpec(memory_space=pltpu.HBM)


def split_two(value):
    high = value.astype(jnp.bfloat16).astype(jnp.float32)
    low = (value - high).astype(jnp.bfloat16).astype(jnp.float32)
    return high, low


def attend_kernel(heads_dev, devices, *refs):
    table_hbm, lengths_hbm, key_scale_hbm, value_scale_hbm, queries_hbm, keys, values = refs[:7]
    packed = refs[7 : 7 + devices]
    (table, lengths, key_scale, value_scale, queries, key_buf, value_buf, query_rows, staged, small_sems, sems) = refs[
        7 + devices :
    ]
    rows, pages = table.shape
    kv_heads = key_scale.shape[0]
    heads = queries.shape[1] // HD
    group = heads // kv_heads
    part_rows = packed[0].shape[0] // 2
    context = pages * PAGE
    pieces = sems.shape[1]
    piece = keys.shape[0] // pieces

    small = []
    for i, (source, target) in enumerate(
        (
            (table_hbm, table),
            (lengths_hbm, lengths),
            (key_scale_hbm, key_scale),
            (value_scale_hbm, value_scale),
            (queries_hbm, queries),
        )
    ):
        small.append(pltpu.make_async_copy(source, target, small_sems.at[i]))
        small[-1].start()
    large = []
    for which, source, target in ((0, keys, key_buf), (1, values, value_buf)):
        large.append([])
        for i in range(pieces):
            here = pl.ds(i * piece, piece)
            large[-1].append(pltpu.make_async_copy(source.at[here], target.at[here], sems.at[which, i]))
            large[-1][-1].start()

    if part_rows > rows * heads_dev:
        staged[...] = jnp.zeros_like(staged)
    me = lax.axis_index("kvp")
    place = me * context + lax.broadcasted_iota(jnp.int32, (group, context), 1)
    lane = lax.broadcasted_iota(jnp.int32, (group, HD), 1)
    zeros = jnp.zeros((group, HD), jnp.bfloat16)
    for copy in small:
        copy.wait()
    for h in range(heads):
        query_rows[h * rows : (h + 1) * rows, :] = queries[:, h * HD : (h + 1) * HD].astype(jnp.float32)
    for copy in large[0]:
        copy.wait()

    def factors(scales, r, k, times):
        columns = []
        for p in range(0, pages, 2):
            left = scales[k, table[r, p]] * times
            right = scales[k, table[r, p + 1]] * times
            columns.append(jnp.where(lane < PAGE, left, right))
        return jnp.concatenate(columns, axis=1)

    def pages_of(buf, r, k):
        return jnp.concatenate(
            [buf[table[r, p], :, k * HD : (k + 2) * HD] for p in range(pages)], axis=0
        )

    probs = {}
    for r in range(rows):
        visible = place < lengths[r]
        query = query_rows[pl.ds(r, heads, stride=rows), :].astype(jnp.bfloat16)
        for k in range(0, kv_heads, 2):
            left = jnp.concatenate(
                [
                    jnp.concatenate([query[k * group : (k + 1) * group], zeros], axis=1),
                    jnp.concatenate([zeros, query[(k + 1) * group : (k + 2) * group]], axis=1),
                ],
                axis=0,
            )
            both = lax.dot_general(
                left, pages_of(key_buf, r, k), (((1,), (1,)), ((), ())), preferred_element_type=jnp.float32
            )
            weights = []
            for i in (0, 1):
                scores = both[i * group : (i + 1) * group] * factors(key_scale, r, k + i, 1.0 / math.sqrt(HD))
                highest = jnp.max(jnp.where(visible, scores, -1e30), axis=1, keepdims=True)
                high, low = split_two(highest)
                prob = jnp.where(visible, jnp.exp(scores - (high + low)), 0.0)
                total_high, total_low = split_two(jnp.sum(prob, axis=1, keepdims=True))
                stats = jnp.where(lane == 0, high, jnp.where(lane == 1, low, jnp.where(lane == 2, total_high, total_low)))
                for start in range(0, group, heads_dev):
                    d = ((k + i) * group + start) // heads_dev
                    staged[1, d, r * heads_dev : (r + 1) * heads_dev, :] = stats[start : start + heads_dev]
                weights.append((prob * factors(value_scale, r, k + i, 1.0)).astype(jnp.bfloat16))
            probs[r, k] = jnp.concatenate(weights, axis=0)
    for copy in large[1]:
        copy.wait()
    for r in range(rows):
        for k in range(0, kv_heads, 2):
            both = jnp.dot(probs[r, k], pages_of(value_buf, r, k), preferred_element_type=jnp.float32)
            for i in (0, 1):
                partial = both[i * group : (i + 1) * group, i * HD : (i + 1) * HD]
                for start in range(0, group, heads_dev):
                    d = ((k + i) * group + start) // heads_dev
                    staged[0, d, r * heads_dev : (r + 1) * heads_dev, :] = partial[start : start + heads_dev]
    for x in range(devices):
        other = jnp.bitwise_xor(me, x)
        packed[x][:part_rows, :] = staged[0, other].astype(jnp.bfloat16)
        packed[x][part_rows:, :] = staged[1, other].astype(jnp.bfloat16)


def project_kernel(heads_dev, devices, *refs):
    packed = refs[:devices]
    weight = refs[devices]
    outs = refs[devices + 1 : -3]
    weight_buf, attended, sems = refs[-3:]
    _, rows, width = outs[0].shape
    per_out = outs[0].shape[0]
    me = lax.axis_index("kvp")
    copies = []
    for x in range(devices):
        other = jnp.bitwise_xor(me, x)
        start = pl.multiple_of(other * width, width)
        copy = pltpu.make_async_copy(weight.at[:, pl.ds(start, width)], weight_buf.at[x], sems.at[x])
        copy.start()
        copies.append(copy)
    part_rows = packed[0].shape[0] // 2
    partials = [ref[:part_rows, :].astype(jnp.float32) for ref in packed]
    stats = [ref[part_rows:, :].astype(jnp.float32) for ref in packed]
    maxima = [s[:, 0:1] + s[:, 1:2] for s in stats]
    totals = [s[:, 2:3] + s[:, 3:4] for s in stats]
    highest = functools.reduce(jnp.maximum, maxima)
    rescale = [jnp.exp(m - highest) for m in maxima]
    numerator = sum(p * e for p, e in zip(partials, rescale))
    denominator = sum(t * e for t, e in zip(totals, rescale))
    attended[...] = numerator / denominator
    left = jnp.concatenate(
        [attended[pl.ds(j, rows, stride=heads_dev), :].astype(jnp.bfloat16) for j in range(heads_dev)], axis=1
    )
    for x in reversed(range(devices)):
        copies[x].wait()
        terms = jnp.dot(left, weight_buf[x], preferred_element_type=jnp.float32)
        outs[x // per_out][x % per_out] = terms.astype(jnp.bfloat16)


def add_kernel(outs_of, *refs):
    terms, outs = refs[:-outs_of], refs[-outs_of:]
    per_out = outs[0].shape[0]
    for i, out in enumerate(outs):
        here = slice(i * per_out, (i + 1) * per_out)
        out[...] = sum(term[here].astype(jnp.float32) for term in terms).astype(out.dtype)


def lay_kernel(devices, *refs):
    parts, out = refs[:-1], refs[-1]
    me = lax.axis_index("kvp")
    per_part = parts[0].shape[0]
    width = parts[0].shape[2]
    for x in range(devices):
        start = pl.multiple_of(jnp.bitwise_xor(me, x) * width, width)
        out[:, pl.ds(start, width)] = parts[x // per_part][x % per_part]


def exchange(array, partner, devices):
    return lax.ppermute(array, "kvp", [(i, i ^ partner) for i in range(devices)])


def in_hbm(array):
    return pltpu.with_memory_space_constraint(array, pltpu.HBM)


def body(queries, key_cache, value_cache, key_scale, value_scale, page_table, lengths, out_weight, *, devices):
    rows, pages = page_table.shape
    slots, _, columns = key_cache.shape
    kv_heads = key_scale.shape[1]
    heads_dev = out_weight.shape[0] // HD
    heads = queries.shape[1] // HD
    features = out_weight.shape[1]
    part_rows = -(-rows * heads_dev // 16) * 16
    width = features // devices
    inner = 4
    outer = devices // inner
    packed = pl.pallas_call(
        functools.partial(attend_kernel, heads_dev, devices),
        out_shape=[jax.ShapeDtypeStruct((2 * part_rows, HD), jnp.bfloat16)] * devices,
        in_specs=[HBM] * 7,
        out_specs=[VMEM] * devices,
        scratch_shapes=[
            pltpu.SMEM((rows, pages), jnp.int32),
            pltpu.SMEM((rows,), jnp.int32),
            pltpu.SMEM((kv_heads, slots), jnp.float32),
            pltpu.SMEM((kv_heads, slots), jnp.float32),
            pltpu.VMEM((rows, heads * HD), jnp.bfloat16),
            pltpu.VMEM((slots, PAGE, columns), jnp.bfloat16),
            pltpu.VMEM((slots, PAGE, columns), jnp.bfloat16),
            pltpu.VMEM((heads * rows, HD), jnp.float32),
            pltpu.VMEM((2, devices, part_rows, HD), jnp.float32),
            pltpu.SemaphoreType.DMA((5,)),
            pltpu.SemaphoreType.DMA((2, 4)),
        ],
        compiler_params=pltpu.CompilerParams(vmem_limit_bytes=ATTEND_VMEM),
        cost_estimate=pl.CostEstimate(
            flops=4 * heads * rows * pages * PAGE * HD,
            bytes_accessed=4 * rows * pages * PAGE * columns,
            transcendentals=heads * rows * pages * PAGE,
        ),
        name="attend",
    )(*[in_hbm(a) for a in (page_table, lengths, key_scale.T, value_scale.T, queries, key_cache, value_cache)])

    received = [packed[0]] + [exchange(packed[x], x, devices) for x in range(1, devices)]

    terms = pl.pallas_call(
        functools.partial(project_kernel, heads_dev, devices),
        out_shape=[jax.ShapeDtypeStruct((inner, rows, width), jnp.bfloat16)] * outer,
        in_specs=[VMEM] * devices + [HBM],
        out_specs=[VMEM] * outer,
        scratch_shapes=[
            pltpu.VMEM((devices, heads_dev * HD, width), jnp.bfloat16),
            pltpu.VMEM((part_rows, HD), jnp.float32),
            pltpu.SemaphoreType.DMA((devices,)),
        ],
        compiler_params=pltpu.CompilerParams(vmem_limit_bytes=PROJECT_VMEM),
        cost_estimate=pl.CostEstimate(
            flops=2 * rows * out_weight.size, bytes_accessed=2 * out_weight.size, transcendentals=0
        ),
        name="project",
    )(*received, in_hbm(out_weight))

    small = pltpu.CompilerParams(vmem_limit_bytes=SMALL_VMEM)
    arrived = [terms[0]] + [exchange(terms[i], i * inner, devices) for i in range(1, outer)]
    quarters = pl.pallas_call(
        functools.partial(add_kernel, inner),
        out_shape=[jax.ShapeDtypeStruct((1, rows, width), jnp.bfloat16)] * inner,
        in_specs=[VMEM] * outer,
        out_specs=[VMEM] * inner,
        compiler_params=small,
        name="add_outer",
    )(*arrived)
    arrived = [quarters[0]] + [exchange(quarters[i], i, devices) for i in range(1, inner)]
    mine = pl.pallas_call(
        functools.partial(add_kernel, 1),
        out_shape=[jax.ShapeDtypeStruct((1, rows, width), jnp.bfloat16)],
        in_specs=[VMEM] * inner,
        out_specs=[VMEM],
        compiler_params=small,
        name="add_inner",
    )(*arrived)[0]
    near = jnp.concatenate([mine] + [exchange(mine, i, devices) for i in range(1, inner)], axis=0)
    parts = [near] + [exchange(near, i * inner, devices) for i in range(1, outer)]
    return pl.pallas_call(
        functools.partial(lay_kernel, devices),
        out_shape=jax.ShapeDtypeStruct((rows, features), jnp.bfloat16),
        in_specs=[VMEM] * outer,
        out_specs=VMEM,
        compiler_params=small,
        name="lay",
    )(*parts)


def solution(mesh):
    placed = (
        P("group", None),
        P(("group", "kvp"), None, None),
        P(("group", "kvp"), None, None),
        P(("group", "kvp"), None),
        P(("group", "kvp"), None),
        P("group", "kvp"),
        P("group"),
        P("kvp", None),
    )
    return jax.shard_map(
        functools.partial(body, devices=mesh.shape["kvp"]),
        mesh=mesh,
        in_specs=placed,
        out_specs=P("group", None),
        check_vma=False,
    )
```

time: 70.9 us -> 67.5 us (0.952)
  blocking collectives: 44.1 us -> 0 us
  starting transfers between devices: 0 us -> 34.9 us
  waiting for transfers between devices: 0 us -> 16.7 us
  local copies, waits for them, and re-layouts: 7.97 us -> 0 us
  Pallas kernels: 18.4 us -> 15.6 us
    ppermute x0 -> x27, starting transfers between devices: none -> 34.9 us  [exchange(): lax.ppermute(array, 'kvp', [(i, i ^ partner) for i in range(devices)])]
    all_to_all x2 -> x0, blocking collectives: 25.6 us -> none  [the longest x1 15.1 us: body(): lax.all_to_all(packed, 'kvp', split_axis=0, concat_axis=0, tiled=True)]
    all_gather x1 -> x0, blocking collectives: 18.4 us -> none  [body(): return lax.all_gather(mine, 'kvp', axis=1, tiled=True)]
    ppermute x0 -> x27, waiting for transfers between devices: none -> 16.7 us  [exchange(): lax.ppermute(array, 'kvp', [(i, i ^ partner) for i in range(devices)])]
    unnamed x15 -> x0, local copies, waits for them, and re-layouts: 7.97 us -> none
    pallas_call x2 -> x5, Pallas kernels: 18.4 us -> 15.6 us  [the longest x1 10.2 us: body(): pl.pallas_call(functools.partial(project_kernel, heads_dev, devices), out...]
  transfers between devices with their start and end apart: 0 -> 27, of which waited for: 0 -> 11; matrix products, arithmetic and copies ran while one was open for 0% -> 0% of each run, Pallas kernels for 0% -> 0%
where the time goes in v2:
time: 67.5 us; the launch traced here: 67.3 us
  starting transfers between devices  34.9 us (52%)
  waiting for transfers between devices  16.7 us (25%)
  Pallas kernels  15.6 us (23%)
    ppermute x27, starting transfers between devices, exchange(): lax.ppermute(array, 'kvp', [(i, i ^ partner) for i in range(devices)])  34.9 us
    ppermute x27, waiting for transfers between devices, exchange(): lax.ppermute(array, 'kvp', [(i, i ^ partner) for i in range(devices)])  16.7 us
    pallas_call x1, Pallas kernels, body(): pl.pallas_call(functools.partial(project_kernel, heads_dev, devices), out...  10.2 us
    pallas_call x1, Pallas kernels, body(): pl.pallas_call(functools.partial(attend_kernel, heads_dev, devices), out_...  4.67 us
  transfers between devices with their start and end apart: 27, of which 11 were waited for; matrix products, arithmetic and copies ran while one was open for 0% of the time, Pallas kernels for 0%

profile of v2, /device:TPU:0, one launch (start us, length us, event | category | flops | bytes accessed | tf_op | source)
XLA Modules:
  0.0 67.3 jit_solution(4955612618425457341)
XLA Ops:
  0.0 4.7 %attend.1 = (bf16[32,128]{1,0:T(8,128)(2,1)S(1)}, bf16[32,128]{1,0:T(8,128)(2,1)S(1)}, bf16[32,128]{1,0:T(8,128)(2,1)S(1)}, bf16[32,128]{1,0:T(8,128)(2,1)S(1)},...) custom-call(s32[4,12]{1,0:T(4,128)} %refs_0_.1, ...), custom_call_target="tpu_custom_call" | custom-call | flops 100663296 | bytes 6291456 | tf_op jit(solution)/shard_map/attend/pallas_call | solution.py:202
  4.7 0.5 collective-permute-start
  5.2 2.6 %collective-permute-start.1 = (bf16[32,128]{1,0:T(8,128)(2,1)S(1)}, bf16[32,128]{1,0:T(8,128)(2,1)S(1)}, u32[]{:S(2)}, u32[]{:S(2)}) collective-permute-start(bf16[32,128]{1,0:T(8,128)(2,1)S(1)} %get-tuple-element.31), channel_id=1, source_target_pairs={{0,2},{1,3},{2,0},{3,1},{4,6},{5,7},{6,4},{7,5},{8,10},{9,11},{10,... | collective-permute-start | bytes 24584 | tf_op jit(solution)/shard_map/ppermute | solution.py:184
  7.9 1.8 %collective-permute-start.3 = (bf16[32,128]{1,0:T(8,128)(2,1)S(1)}, bf16[32,128]{1,0:T(8,128)(2,1)S(1)}, u32[]{:S(2)}, u32[]{:S(2)}) collective-permute-start(bf16[32,128]{1,0:T(8,128)(2,1)S(1)} %get-tuple-element.33), channel_id=1, source_target_pairs={{0,4},{1,5},{2,6},{3,7},{4,0},{5,1},{6,2},{7,3},{8,12},{9,13},{10,... | collective-permute-start | bytes 24584 | tf_op jit(solution)/shard_map/ppermute | solution.py:184
  9.7 2.6 %collective-permute-start.5 = (bf16[32,128]{1,0:T(8,128)(2,1)S(1)}, bf16[32,128]{1,0:T(8,128)(2,1)S(1)}, u32[]{:S(2)}, u32[]{:S(2)}) collective-permute-start(bf16[32,128]{1,0:T(8,128)(2,1)S(1)} %get-tuple-element.35), channel_id=1, source_target_pairs={{0,6},{1,7},{2,4},{3,5},{4,2},{5,3},{6,0},{7,1},{8,14},{9,15},{10,... | collective-permute-start | bytes 24584 | tf_op jit(solution)/shard_map/ppermute | solution.py:184
  12.3 0.1 collective-permute-start.6
  12.4 2.6 %collective-permute-start.7 = (bf16[32,128]{1,0:T(8,128)(2,1)S(1)}, bf16[32,128]{1,0:T(8,128)(2,1)S(1)}, u32[]{:S(2)}, u32[]{:S(2)}) collective-permute-start(bf16[32,128]{1,0:T(8,128)(2,1)S(1)} %get-tuple-element.37), channel_id=1, source_target_pairs={{0,8},{1,9},{2,10},{3,11},{4,12},{5,13},{6,14},{7,15},{8,0},{9,1},... | collective-permute-start | bytes 24584 | tf_op jit(solution)/shard_map/ppermute | solution.py:184
  15.1 3.5 %collective-permute-start.9 = (bf16[32,128]{1,0:T(8,128)(2,1)S(1)}, bf16[32,128]{1,0:T(8,128)(2,1)S(1)}, u32[]{:S(2)}, u32[]{:S(2)}) collective-permute-start(bf16[32,128]{1,0:T(8,128)(2,1)S(1)} %get-tuple-element.39), channel_id=1, source_target_pairs={{0,10},{1,11},{2,8},{3,9},{4,14},{5,15},{6,12},{7,13},{8,2},{9,3},... | collective-permute-start | bytes 24584 | tf_op jit(solution)/shard_map/ppermute | solution.py:184
  18.6 0.1 collective-permute-start.10
  18.8 3.5 %collective-permute-start.11 = (bf16[32,128]{1,0:T(8,128)(2,1)S(1)}, bf16[32,128]{1,0:T(8,128)(2,1)S(1)}, u32[]{:S(2)}, u32[]{:S(2)}) collective-permute-start(bf16[32,128]{1,0:T(8,128)(2,1)S(1)} %get-tuple-element.41), channel_id=1, source_target_pairs={{0,12},{1,13},{2,14},{3,15},{4,8},{5,9},{6,10},{7,11},{8,4},{9,5},... | collective-permute-start | bytes 24584 | tf_op jit(solution)/shard_map/ppermute | solution.py:184
  22.3 4.4 %collective-permute-start.13 = (bf16[32,128]{1,0:T(8,128)(2,1)S(1)}, bf16[32,128]{1,0:T(8,128)(2,1)S(1)}, u32[]{:S(2)}, u32[]{:S(2)}) collective-permute-start(bf16[32,128]{1,0:T(8,128)(2,1)S(1)} %get-tuple-element.43), channel_id=1, source_target_pairs={{0,14},{1,15},{2,12},{3,13},{4,10},{5,11},{6,8},{7,9},{8,6},{9,7},... | collective-permute-start | bytes 24584 | tf_op jit(solution)/shard_map/ppermute | solution.py:184
  26.9 0.3 collective-permute-done.12.refs_13_
  27.2 1.5 %collective-permute-done.13.refs_14_ = bf16[32,128]{1,0:T(8,128)(2,1)S(1)} collective-permute-done((bf16[32,128]{1,0:T(8,128)(2,1)S(1)}, bf16[32,128]{1,0:T(8,128)(2,1)S(1)}, u32[]{:S(2)}, u32[]{:S(2)}) %collective-permute-start.13) | collective-permute-done | bytes 8224 | tf_op jit(solution)/shard_map/ppermute | solution.py:184
  28.7 3.8 %collective-permute-done.14.refs_15_ = bf16[32,128]{1,0:T(8,128)(2,1)S(1)} collective-permute-done((bf16[32,128]{1,0:T(8,128)(2,1)S(1)}, bf16[32,128]{1,0:T(8,128)(2,1)S(1)}, u32[]{:S(2)}, u32[]{:S(2)}) %collective-permute-start.14) | collective-permute-done | bytes 8224 | tf_op jit(solution)/shard_map/ppermute | solution.py:184
  32.5 10.2 %project.1 = (bf16[4,4,1024]{2,1,0:T(4,128)(2,1)S(1)}, bf16[4,4,1024]{2,1,0:T(4,128)(2,1)S(1)}, bf16[4,4,1024]{2,1,0:T(4,128)(2,1)S(1)}, bf16[4,4,1024]{2,1,0:T(4,128)(2,1)S(1)}) custom-call(bf16[32,128]{1,0:T(8,128)(2,1)S(1)} %get-tuple-element.29.refs_0_, bf16[32,128]{1,0:T(8,128)(2,1)S(1)} %collective-permute-done.refs_1_, ...), custom_call_target="tpu_custom_call" | custom-call | flops 67108864 | bytes 16777216 | tf_op jit(solution)/shard_map/project/pallas_call | solution.py:231
  42.8 0.9 %collective-permute-start.16 = (bf16[4,4,1024]{2,1,0:T(4,128)(2,1)S(1)}, bf16[4,4,1024]{2,1,0:T(4,128)(2,1)S(1)}, u32[]{:S(2)}, u32[]{:S(2)}) collective-permute-start(bf16[4,4,1024]{2,1,0:T(4,128)(2,1)S(1)} %get-tuple-element.47), channel_id=1, source_target_pairs={{0,8},{1,9},{2,10},{3,11},{4,12},{5,13},{6,14},{7,15},{8,0},{9,1},... | collective-permute-start | bytes 98312 | tf_op jit(solution)/shard_map/ppermute | solution.py:184
  43.8 3.4 %collective-permute-start.17 = (bf16[4,4,1024]{2,1,0:T(4,128)(2,1)S(1)}, bf16[4,4,1024]{2,1,0:T(4,128)(2,1)S(1)}, u32[]{:S(2)}, u32[]{:S(2)}) collective-permute-start(bf16[4,4,1024]{2,1,0:T(4,128)(2,1)S(1)} %get-tuple-element.48), channel_id=1, source_target_pairs={{0,12},{1,13},{2,14},{3,15},{4,8},{5,9},{6,10},{7,11},{8,4},{9,5},... | collective-permute-start | bytes 98312 | tf_op jit(solution)/shard_map/ppermute | solution.py:184
  47.2 0.5 collective-permute-done.16.refs_2_
  47.7 1.8 %collective-permute-done.17.refs_3_ = bf16[4,4,1024]{2,1,0:T(4,128)(2,1)S(1)} collective-permute-done((bf16[4,4,1024]{2,1,0:T(4,128)(2,1)S(1)}, bf16[4,4,1024]{2,1,0:T(4,128)(2,1)S(1)}, u32[]{:S(2)}, u32[]{:S(2)}) %collective-permute-start.17) | collective-permute-done | bytes 32800 | tf_op jit(solution)/shard_map/ppermute | solution.py:184
  49.6 0.8 %collective-permute-start.19 = (bf16[1,4,1024]{2,1,0:T(4,128)(2,1)S(1)}, bf16[1,4,1024]{2,1,0:T(4,128)(2,1)S(1)}, u32[]{:S(2)}, u32[]{:S(2)}) collective-permute-start(bf16[1,4,1024]{2,1,0:T(4,128)(2,1)S(1)} %get-tuple-element.51), channel_id=1, source_target_pairs={{0,2},{1,3},{2,0},{3,1},{4,6},{5,7},{6,4},{7,5},{8,10},{9,11},{10,... | collective-permute-start | bytes 24584 | tf_op jit(solution)/shard_map/ppermute | solution.py:184
  50.4 1.1 %collective-permute-start.20 = (bf16[1,4,1024]{2,1,0:T(4,128)(2,1)S(1)}, bf16[1,4,1024]{2,1,0:T(4,128)(2,1)S(1)}, u32[]{:S(2)}, u32[]{:S(2)}) collective-permute-start(bf16[1,4,1024]{2,1,0:T(4,128)(2,1)S(1)} %get-tuple-element.52), channel_id=1, source_target_pairs={{0,3},{1,2},{2,1},{3,0},{4,7},{5,6},{6,5},{7,4},{8,11},{9,10},{10,... | collective-permute-start | bytes 24584 | tf_op jit(solution)/shard_map/ppermute | solution.py:184
  51.5 1.9 %collective-permute-done.19.refs_2_ = bf16[1,4,1024]{2,1,0:T(4,128)(2,1)S(1)} collective-permute-done((bf16[1,4,1024]{2,1,0:T(4,128)(2,1)S(1)}, bf16[1,4,1024]{2,1,0:T(4,128)(2,1)S(1)}, u32[]{:S(2)}, u32[]{:S(2)}) %collective-permute-start.19) | collective-permute-done | bytes 8224 | tf_op jit(solution)/shard_map/ppermute | solution.py:184
  53.3 0.2 collective-permute-done.20.refs_3_
  53.5 1.1 %collective-permute-start.23 = (bf16[1,4,1024]{2,1,0:T(4,128)(2,1)S(1)}, bf16[1,4,1024]{2,1,0:T(4,128)(2,1)S(1)}, u32[]{:S(2)}, u32[]{:S(2)}) collective-permute-start(bf16[1,4,1024]{2,1,0:T(4,128)(2,1)S(1)} %add_inner.1), channel_id=1, source_target_pairs={{0,3},{1,2},{2,1},{3,0},{4,7},{5,6},{6,5},{7,4},{8,11},{9,10},{10,... | collective-permute-start | bytes 24584 | tf_op jit(solution)/shard_map/ppermute | solution.py:184
  54.6 0.7 %collective-permute-start.22 = (bf16[1,4,1024]{2,1,0:T(4,128)(2,1)S(1)}, bf16[1,4,1024]{2,1,0:T(4,128)(2,1)S(1)}, u32[]{:S(2)}, u32[]{:S(2)}) collective-permute-start(bf16[1,4,1024]{2,1,0:T(4,128)(2,1)S(1)} %add_inner.1), channel_id=1, source_target_pairs={{0,2},{1,3},{2,0},{3,1},{4,6},{5,7},{6,4},{7,5},{8,10},{9,11},{10,... | collective-permute-start | bytes 24584 | tf_op jit(solution)/shard_map/ppermute | solution.py:184
  55.4 1.2 %collective-permute-done.23 = bf16[1,4,1024]{2,1,0:T(4,128)(2,1)S(1)} collective-permute-done((bf16[1,4,1024]{2,1,0:T(4,128)(2,1)S(1)}, bf16[1,4,1024]{2,1,0:T(4,128)(2,1)S(1)}, u32[]{:S(2)}, u32[]{:S(2)}) %collective-permute-start.23) | collective-permute-done | bytes 8224 | tf_op jit(solution)/shard_map/ppermute | solution.py:184
  56.7 1.6 %collective-permute-done.22 = bf16[1,4,1024]{2,1,0:T(4,128)(2,1)S(1)} collective-permute-done((bf16[1,4,1024]{2,1,0:T(4,128)(2,1)S(1)}, bf16[1,4,1024]{2,1,0:T(4,128)(2,1)S(1)}, u32[]{:S(2)}, u32[]{:S(2)}) %collective-permute-start.22) | collective-permute-done | bytes 8224 | tf_op jit(solution)/shard_map/ppermute | solution.py:184
  58.3 3.5 %collective-permute-start.26 = (bf16[4,4,1024]{2,1,0:T(4,128)(2,1)S(1)}, bf16[4,4,1024]{2,1,0:T(4,128)(2,1)S(1)}, u32[]{:S(2)}, u32[]{:S(2)}) collective-permute-start(bf16[4,4,1024]{2,1,0:T(4,128)(2,1)S(1)} %pad_maximum_fusion.refs_0_), channel_id=1, source_target_pairs={{0,12},{1,13},{2,14},{3,15},{4,8},{5,9},{6,10},{7,11},{8,4},{9,5},... | collective-permute-start | bytes 98312 | tf_op jit(solution)/shard_map/ppermute | solution.py:184
  61.8 1.0 %collective-permute-start.24 = (bf16[4,4,1024]{2,1,0:T(4,128)(2,1)S(1)}, bf16[4,4,1024]{2,1,0:T(4,128)(2,1)S(1)}, u32[]{:S(2)}, u32[]{:S(2)}) collective-permute-start(bf16[4,4,1024]{2,1,0:T(4,128)(2,1)S(1)} %pad_maximum_fusion.refs_0_), channel_id=1, source_target_pairs={{0,4},{1,5},{2,6},{3,7},{4,0},{5,1},{6,2},{7,3},{8,12},{9,13},{10,... | collective-permute-start | bytes 98312 | tf_op jit(solution)/shard_map/ppermute | solution.py:184
  62.8 1.3 %collective-permute-done.26.refs_3_ = bf16[4,4,1024]{2,1,0:T(4,128)(2,1)S(1)} collective-permute-done((bf16[4,4,1024]{2,1,0:T(4,128)(2,1)S(1)}, bf16[4,4,1024]{2,1,0:T(4,128)(2,1)S(1)}, u32[]{:S(2)}, u32[]{:S(2)}) %collective-permute-start.26) | collective-permute-done | bytes 32800 | tf_op jit(solution)/shard_map/ppermute | solution.py:184
  64.1 2.5 %collective-permute-done.25.refs_2_ = bf16[4,4,1024]{2,1,0:T(4,128)(2,1)S(1)} collective-permute-done((bf16[4,4,1024]{2,1,0:T(4,128)(2,1)S(1)}, bf16[4,4,1024]{2,1,0:T(4,128)(2,1)S(1)}, u32[]{:S(2)}, u32[]{:S(2)}) %collective-permute-start.25) | collective-permute-done | bytes 32800 | tf_op jit(solution)/shard_map/ppermute | solution.py:184
  66.6 0.7 %lay.1 = bf16[4,16384]{1,0:T(4,128)(2,1)} custom-call(bf16[4,4,1024]{2,1,0:T(4,128)(2,1)S(1)} %pad_maximum_fusion.refs_0_, bf16[4,4,1024]{2,1,0:T(4,128)(2,1)S(1)} %collective-permute-done.24.refs_1_, bf16[4,4,1024]{2,1,0:T(4,128)(2,1)S(1)} %collective-permute-done.25.refs_2_, bf16[4,4,1024]{2,1,0:T(4,128)(2,1)S(1)} %collective-permute-done.26.refs_3_), custom_call_target="tpu_custom_call" | custom-call | tf_op jit(solution)/shard_map/lay/pallas_call | solution.py:269
  (28 shorter events, 0.6 us)
Async XLA Ops:
  4.7 5.0 %collective-permute-start = (bf16[32,128]{1,0:T(8,128)(2,1)S(1)}, bf16[32,128]{1,0:T(8,128)(2,1)S(1)}, u32[]{:S(2)}, u32[]{:S(2)}) collective-permute-start(bf16[32,128]{1,0:T(8,128)(2,1)S(1)} %get-tuple-element.30), channel_id=1, source_target_pairs={{0,1},{1,0},{2,3},{3,2},{4,5},{5,4},{6,7},{7,6},{8,9},{9,8},{10,11... | collective-permute-start | bytes 24584 | tf_op jit(solution)/shard_map/ppermute | solution.py:184
  5.2 7.1 %collective-permute-start.1 = (bf16[32,128]{1,0:T(8,128)(2,1)S(1)}, bf16[32,128]{1,0:T(8,128)(2,1)S(1)}, u32[]{:S(2)}, u32[]{:S(2)}) collective-permute-start(bf16[32,128]{1,0:T(8,128)(2,1)S(1)} %get-tuple-element.31), channel_id=1, source_target_pairs={{0,2},{1,3},{2,0},{3,1},{4,6},{5,7},{6,4},{7,5},{8,10},{9,11},{10,... | collective-permute-start | bytes 24584 | tf_op jit(solution)/shard_map/ppermute | solution.py:184
  7.8 4.6 %collective-permute-start.2 = (bf16[32,128]{1,0:T(8,128)(2,1)S(1)}, bf16[32,128]{1,0:T(8,128)(2,1)S(1)}, u32[]{:S(2)}, u32[]{:S(2)}) collective-permute-start(bf16[32,128]{1,0:T(8,128)(2,1)S(1)} %get-tuple-element.32), channel_id=1, source_target_pairs={{0,3},{1,2},{2,1},{3,0},{4,7},{5,6},{6,5},{7,4},{8,11},{9,10},{10,... | collective-permute-start | bytes 24584 | tf_op jit(solution)/shard_map/ppermute | solution.py:184
  7.9 7.2 %collective-permute-start.3 = (bf16[32,128]{1,0:T(8,128)(2,1)S(1)}, bf16[32,128]{1,0:T(8,128)(2,1)S(1)}, u32[]{:S(2)}, u32[]{:S(2)}) collective-permute-start(bf16[32,128]{1,0:T(8,128)(2,1)S(1)} %get-tuple-element.33), channel_id=1, source_target_pairs={{0,4},{1,5},{2,6},{3,7},{4,0},{5,1},{6,2},{7,3},{8,12},{9,13},{10,... | collective-permute-start | bytes 24584 | tf_op jit(solution)/shard_map/ppermute | solution.py:184
  9.7 5.4 %collective-permute-start.4 = (bf16[32,128]{1,0:T(8,128)(2,1)S(1)}, bf16[32,128]{1,0:T(8,128)(2,1)S(1)}, u32[]{:S(2)}, u32[]{:S(2)}) collective-permute-start(bf16[32,128]{1,0:T(8,128)(2,1)S(1)} %get-tuple-element.34), channel_id=1, source_target_pairs={{0,5},{1,4},{2,7},{3,6},{4,1},{5,0},{6,3},{7,2},{8,13},{9,12},{10,... | collective-permute-start | bytes 24584 | tf_op jit(solution)/shard_map/ppermute | solution.py:184
  9.7 9.0 %collective-permute-start.5 = (bf16[32,128]{1,0:T(8,128)(2,1)S(1)}, bf16[32,128]{1,0:T(8,128)(2,1)S(1)}, u32[]{:S(2)}, u32[]{:S(2)}) collective-permute-start(bf16[32,128]{1,0:T(8,128)(2,1)S(1)} %get-tuple-element.35), channel_id=1, source_target_pairs={{0,6},{1,7},{2,4},{3,5},{4,2},{5,3},{6,0},{7,1},{8,14},{9,15},{10,... | collective-permute-start | bytes 24584 | tf_op jit(solution)/shard_map/ppermute | solution.py:184
  12.3 6.4 %collective-permute-start.6 = (bf16[32,128]{1,0:T(8,128)(2,1)S(1)}, bf16[32,128]{1,0:T(8,128)(2,1)S(1)}, u32[]{:S(2)}, u32[]{:S(2)}) collective-permute-start(bf16[32,128]{1,0:T(8,128)(2,1)S(1)} %get-tuple-element.36), channel_id=1, source_target_pairs={{0,7},{1,6},{2,5},{3,4},{4,3},{5,2},{6,1},{7,0},{8,15},{9,14},{10,... | collective-permute-start | bytes 24584 | tf_op jit(solution)/shard_map/ppermute | solution.py:184
  12.4 9.9 %collective-permute-start.7 = (bf16[32,128]{1,0:T(8,128)(2,1)S(1)}, bf16[32,128]{1,0:T(8,128)(2,1)S(1)}, u32[]{:S(2)}, u32[]{:S(2)}) collective-permute-start(bf16[32,128]{1,0:T(8,128)(2,1)S(1)} %get-tuple-element.37), channel_id=1, source_target_pairs={{0,8},{1,9},{2,10},{3,11},{4,12},{5,13},{6,14},{7,15},{8,0},{9,1},... | collective-permute-start | bytes 24584 | tf_op jit(solution)/shard_map/ppermute | solution.py:184
  15.1 7.3 %collective-permute-start.8 = (bf16[32,128]{1,0:T(8,128)(2,1)S(1)}, bf16[32,128]{1,0:T(8,128)(2,1)S(1)}, u32[]{:S(2)}, u32[]{:S(2)}) collective-permute-start(bf16[32,128]{1,0:T(8,128)(2,1)S(1)} %get-tuple-element.38), channel_id=1, source_target_pairs={{0,9},{1,8},{2,11},{3,10},{4,13},{5,12},{6,15},{7,14},{8,1},{9,0},... | collective-permute-start | bytes 24584 | tf_op jit(solution)/shard_map/ppermute | solution.py:184
  15.1 11.6 %collective-permute-start.9 = (bf16[32,128]{1,0:T(8,128)(2,1)S(1)}, bf16[32,128]{1,0:T(8,128)(2,1)S(1)}, u32[]{:S(2)}, u32[]{:S(2)}) collective-permute-start(bf16[32,128]{1,0:T(8,128)(2,1)S(1)} %get-tuple-element.39), channel_id=1, source_target_pairs={{0,10},{1,11},{2,8},{3,9},{4,14},{5,15},{6,12},{7,13},{8,2},{9,3},... | collective-permute-start | bytes 24584 | tf_op jit(solution)/shard_map/ppermute | solution.py:184
  18.6 8.2 %collective-permute-start.10 = (bf16[32,128]{1,0:T(8,128)(2,1)S(1)}, bf16[32,128]{1,0:T(8,128)(2,1)S(1)}, u32[]{:S(2)}, u32[]{:S(2)}) collective-permute-start(bf16[32,128]{1,0:T(8,128)(2,1)S(1)} %get-tuple-element.40), channel_id=1, source_target_pairs={{0,11},{1,10},{2,9},{3,8},{4,15},{5,14},{6,13},{7,12},{8,3},{9,2},... | collective-permute-start | bytes 24584 | tf_op jit(solution)/shard_map/ppermute | solution.py:184
  18.8 8.1 %collective-permute-start.11 = (bf16[32,128]{1,0:T(8,128)(2,1)S(1)}, bf16[32,128]{1,0:T(8,128)(2,1)S(1)}, u32[]{:S(2)}, u32[]{:S(2)}) collective-permute-start(bf16[32,128]{1,0:T(8,128)(2,1)S(1)} %get-tuple-element.41), channel_id=1, source_target_pairs={{0,12},{1,13},{2,14},{3,15},{4,8},{5,9},{6,10},{7,11},{8,4},{9,5},... | collective-permute-start | bytes 24584 | tf_op jit(solution)/shard_map/ppermute | solution.py:184
  22.3 4.9 %collective-permute-start.12 = (bf16[32,128]{1,0:T(8,128)(2,1)S(1)}, bf16[32,128]{1,0:T(8,128)(2,1)S(1)}, u32[]{:S(2)}, u32[]{:S(2)}) collective-permute-start(bf16[32,128]{1,0:T(8,128)(2,1)S(1)} %get-tuple-element.42), channel_id=1, source_target_pairs={{0,13},{1,12},{2,15},{3,14},{4,9},{5,8},{6,11},{7,10},{8,5},{9,4},... | collective-permute-start | bytes 24584 | tf_op jit(solution)/shard_map/ppermute | solution.py:184
  22.3 6.4 %collective-permute-start.13 = (bf16[32,128]{1,0:T(8,128)(2,1)S(1)}, bf16[32,128]{1,0:T(8,128)(2,1)S(1)}, u32[]{:S(2)}, u32[]{:S(2)}) collective-permute-start(bf16[32,128]{1,0:T(8,128)(2,1)S(1)} %get-tuple-element.43), channel_id=1, source_target_pairs={{0,14},{1,15},{2,12},{3,13},{4,10},{5,11},{6,8},{7,9},{8,6},{9,7},... | collective-permute-start | bytes 24584 | tf_op jit(solution)/shard_map/ppermute | solution.py:184
  26.7 5.8 %collective-permute-start.14 = (bf16[32,128]{1,0:T(8,128)(2,1)S(1)}, bf16[32,128]{1,0:T(8,128)(2,1)S(1)}, u32[]{:S(2)}, u32[]{:S(2)}) collective-permute-start(bf16[32,128]{1,0:T(8,128)(2,1)S(1)} %get-tuple-element.44), channel_id=1, source_target_pairs={{0,15},{1,14},{2,13},{3,12},{4,11},{5,10},{6,9},{7,8},{8,7},{9,6},... | collective-permute-start | bytes 24584 | tf_op jit(solution)/shard_map/ppermute | solution.py:184
  42.8 4.5 %collective-permute-start.15 = (bf16[4,4,1024]{2,1,0:T(4,128)(2,1)S(1)}, bf16[4,4,1024]{2,1,0:T(4,128)(2,1)S(1)}, u32[]{:S(2)}, u32[]{:S(2)}) collective-permute-start(bf16[4,4,1024]{2,1,0:T(4,128)(2,1)S(1)} %get-tuple-element.46), channel_id=1, source_target_pairs={{0,4},{1,5},{2,6},{3,7},{4,0},{5,1},{6,2},{7,3},{8,12},{9,13},{10,... | collective-permute-start | bytes 98312 | tf_op jit(solution)/shard_map/ppermute | solution.py:184
  42.8 4.9 %collective-permute-start.16 = (bf16[4,4,1024]{2,1,0:T(4,128)(2,1)S(1)}, bf16[4,4,1024]{2,1,0:T(4,128)(2,1)S(1)}, u32[]{:S(2)}, u32[]{:S(2)}) collective-permute-start(bf16[4,4,1024]{2,1,0:T(4,128)(2,1)S(1)} %get-tuple-element.47), channel_id=1, source_target_pairs={{0,8},{1,9},{2,10},{3,11},{4,12},{5,13},{6,14},{7,15},{8,0},{9,1},... | collective-permute-start | bytes 98312 | tf_op jit(solution)/shard_map/ppermute | solution.py:184
  43.8 5.7 %collective-permute-start.17 = (bf16[4,4,1024]{2,1,0:T(4,128)(2,1)S(1)}, bf16[4,4,1024]{2,1,0:T(4,128)(2,1)S(1)}, u32[]{:S(2)}, u32[]{:S(2)}) collective-permute-start(bf16[4,4,1024]{2,1,0:T(4,128)(2,1)S(1)} %get-tuple-element.48), channel_id=1, source_target_pairs={{0,12},{1,13},{2,14},{3,15},{4,8},{5,9},{6,10},{7,11},{8,4},{9,5},... | collective-permute-start | bytes 98312 | tf_op jit(solution)/shard_map/ppermute | solution.py:184
  49.5 1.9 %collective-permute-start.18 = (bf16[1,4,1024]{2,1,0:T(4,128)(2,1)S(1)}, bf16[1,4,1024]{2,1,0:T(4,128)(2,1)S(1)}, u32[]{:S(2)}, u32[]{:S(2)}) collective-permute-start(bf16[1,4,1024]{2,1,0:T(4,128)(2,1)S(1)} %get-tuple-element.50), channel_id=1, source_target_pairs={{0,1},{1,0},{2,3},{3,2},{4,5},{5,4},{6,7},{7,6},{8,9},{9,8},{10,11... | collective-permute-start | bytes 24584 | tf_op jit(solution)/shard_map/ppermute | solution.py:184
  49.6 3.7 %collective-permute-start.19 = (bf16[1,4,1024]{2,1,0:T(4,128)(2,1)S(1)}, bf16[1,4,1024]{2,1,0:T(4,128)(2,1)S(1)}, u32[]{:S(2)}, u32[]{:S(2)}) collective-permute-start(bf16[1,4,1024]{2,1,0:T(4,128)(2,1)S(1)} %get-tuple-element.51), channel_id=1, source_target_pairs={{0,2},{1,3},{2,0},{3,1},{4,6},{5,7},{6,4},{7,5},{8,10},{9,11},{10,... | collective-permute-start | bytes 24584 | tf_op jit(solution)/shard_map/ppermute | solution.py:184
  50.4 3.1 %collective-permute-start.20 = (bf16[1,4,1024]{2,1,0:T(4,128)(2,1)S(1)}, bf16[1,4,1024]{2,1,0:T(4,128)(2,1)S(1)}, u32[]{:S(2)}, u32[]{:S(2)}) collective-permute-start(bf16[1,4,1024]{2,1,0:T(4,128)(2,1)S(1)} %get-tuple-element.52), channel_id=1, source_target_pairs={{0,3},{1,2},{2,1},{3,0},{4,7},{5,6},{6,5},{7,4},{8,11},{9,10},{10,... | collective-permute-start | bytes 24584 | tf_op jit(solution)/shard_map/ppermute | solution.py:184
  53.5 3.1 %collective-permute-start.23 = (bf16[1,4,1024]{2,1,0:T(4,128)(2,1)S(1)}, bf16[1,4,1024]{2,1,0:T(4,128)(2,1)S(1)}, u32[]{:S(2)}, u32[]{:S(2)}) collective-permute-start(bf16[1,4,1024]{2,1,0:T(4,128)(2,1)S(1)} %add_inner.1), channel_id=1, source_target_pairs={{0,3},{1,2},{2,1},{3,0},{4,7},{5,6},{6,5},{7,4},{8,11},{9,10},{10,... | collective-permute-start | bytes 24584 | tf_op jit(solution)/shard_map/ppermute | solution.py:184
  54.6 3.7 %collective-permute-start.22 = (bf16[1,4,1024]{2,1,0:T(4,128)(2,1)S(1)}, bf16[1,4,1024]{2,1,0:T(4,128)(2,1)S(1)}, u32[]{:S(2)}, u32[]{:S(2)}) collective-permute-start(bf16[1,4,1024]{2,1,0:T(4,128)(2,1)S(1)} %add_inner.1), channel_id=1, source_target_pairs={{0,2},{1,3},{2,0},{3,1},{4,6},{5,7},{6,4},{7,5},{8,10},{9,11},{10,... | collective-permute-start | bytes 24584 | tf_op jit(solution)/shard_map/ppermute | solution.py:184
  55.4 2.9 %collective-permute-start.21 = (bf16[1,4,1024]{2,1,0:T(4,128)(2,1)S(1)}, bf16[1,4,1024]{2,1,0:T(4,128)(2,1)S(1)}, u32[]{:S(2)}, u32[]{:S(2)}) collective-permute-start(bf16[1,4,1024]{2,1,0:T(4,128)(2,1)S(1)} %add_inner.1), channel_id=1, source_target_pairs={{0,1},{1,0},{2,3},{3,2},{4,5},{5,4},{6,7},{7,6},{8,9},{9,8},{10,11... | collective-permute-start | bytes 24584 | tf_op jit(solution)/shard_map/ppermute | solution.py:184
  58.3 5.8 %collective-permute-start.26 = (bf16[4,4,1024]{2,1,0:T(4,128)(2,1)S(1)}, bf16[4,4,1024]{2,1,0:T(4,128)(2,1)S(1)}, u32[]{:S(2)}, u32[]{:S(2)}) collective-permute-start(bf16[4,4,1024]{2,1,0:T(4,128)(2,1)S(1)} %pad_maximum_fusion.refs_0_), channel_id=1, source_target_pairs={{0,12},{1,13},{2,14},{3,15},{4,8},{5,9},{6,10},{7,11},{8,4},{9,5},... | collective-permute-start | bytes 98312 | tf_op jit(solution)/shard_map/ppermute | solution.py:184
  61.8 4.8 %collective-permute-start.25 = (bf16[4,4,1024]{2,1,0:T(4,128)(2,1)S(1)}, bf16[4,4,1024]{2,1,0:T(4,128)(2,1)S(1)}, u32[]{:S(2)}, u32[]{:S(2)}) collective-permute-start(bf16[4,4,1024]{2,1,0:T(4,128)(2,1)S(1)} %pad_maximum_fusion.refs_0_), channel_id=1, source_target_pairs={{0,8},{1,9},{2,10},{3,11},{4,12},{5,13},{6,14},{7,15},{8,0},{9,1},... | collective-permute-start | bytes 98312 | tf_op jit(solution)/shard_map/ppermute | solution.py:184
  61.8 4.8 %collective-permute-start.24 = (bf16[4,4,1024]{2,1,0:T(4,128)(2,1)S(1)}, bf16[4,4,1024]{2,1,0:T(4,128)(2,1)S(1)}, u32[]{:S(2)}, u32[]{:S(2)}) collective-permute-start(bf16[4,4,1024]{2,1,0:T(4,128)(2,1)S(1)} %pad_maximum_fusion.refs_0_), channel_id=1, source_target_pairs={{0,4},{1,5},{2,6},{3,7},{4,0},{5,1},{6,2},{7,3},{8,12},{9,13},{10,... | collective-permute-start | bytes 98312 | tf_op jit(solution)/shard_map/ppermute | solution.py:184

commit v3 on v2

v3 whole, which is shorter than its diff:
```python
import functools
import math

import jax
import jax.numpy as jnp
from jax import lax
from jax.experimental import pallas as pl
from jax.experimental.pallas import tpu as pltpu
from jax.sharding import PartitionSpec as P

HD = 128
PAGE = 64
ATTEND_VMEM = 24 * 1024 * 1024
PROJECT_VMEM = 40 * 1024 * 1024
WEIGHT_PIECES = 16
SMALL_VMEM = 8 * 1024 * 1024
VMEM = pl.BlockSpec(memory_space=pltpu.VMEM)
HBM = pl.BlockSpec(memory_space=pltpu.HBM)


def split_two(value):
    high = value.astype(jnp.bfloat16).astype(jnp.float32)
    low = (value - high).astype(jnp.bfloat16).astype(jnp.float32)
    return high, low


def attend_kernel(heads_dev, devices, *refs):
    table_hbm, lengths_hbm, key_scale_hbm, value_scale_hbm, queries_hbm, keys, values = refs[:7]
    (packed, table, lengths, key_scale, value_scale, queries, key_buf, value_buf, query_rows, staged, small_sems, sems) = refs[7:]
    rows, pages = table.shape
    kv_heads = key_scale.shape[0]
    heads = queries.shape[1] // HD
    group = heads // kv_heads
    part_rows = rows * heads_dev
    context = pages * PAGE
    pieces = sems.shape[1]
    piece = keys.shape[0] // pieces

    small = []
    for i, (source, target) in enumerate(
        (
            (table_hbm, table),
            (lengths_hbm, lengths),
            (key_scale_hbm, key_scale),
            (value_scale_hbm, value_scale),
            (queries_hbm, queries),
        )
    ):
        small.append(pltpu.make_async_copy(source, target, small_sems.at[i]))
        small[-1].start()
    large = []
    for which, source, target in ((0, keys, key_buf), (1, values, value_buf)):
        large.append([])
        for i in range(pieces):
            here = pl.ds(i * piece, piece)
            large[-1].append(pltpu.make_async_copy(source.at[here], target.at[here], sems.at[which, i]))
            large[-1][-1].start()

    staged[:, part_rows:, :] = jnp.zeros((devices, staged.shape[1] - part_rows, HD), jnp.float32)
    me = lax.axis_index("kvp")
    place = me * context + lax.broadcasted_iota(jnp.int32, (group, context), 1)
    lane = lax.broadcasted_iota(jnp.int32, (group, HD), 1)
    zeros = jnp.zeros((group, HD), jnp.bfloat16)
    for copy in small:
        copy.wait()
    for h in range(heads):
        query_rows[h * rows : (h + 1) * rows, :] = queries[:, h * HD : (h + 1) * HD].astype(jnp.float32)
    for copy in large[0]:
        copy.wait()

    def factors(scales, r, k, times):
        columns = []
        for p in range(0, pages, 2):
            left = scales[k, table[r, p]] * times
            right = scales[k, table[r, p + 1]] * times
            columns.append(jnp.where(lane < PAGE, left, right))
        return jnp.concatenate(columns, axis=1)

    def pages_of(buf, r, k):
        return jnp.concatenate(
            [buf[table[r, p], :, k * HD : (k + 2) * HD] for p in range(pages)], axis=0
        )

    probs = {}
    stats = [jnp.zeros((group, HD), jnp.float32)] * kv_heads
    for r in range(rows):
        visible = place < lengths[r]
        query = query_rows[pl.ds(r, heads, stride=rows), :].astype(jnp.bfloat16)
        for k in range(0, kv_heads, 2):
            left = jnp.concatenate(
                [
                    jnp.concatenate([query[k * group : (k + 1) * group], zeros], axis=1),
                    jnp.concatenate([zeros, query[(k + 1) * group : (k + 2) * group]], axis=1),
                ],
                axis=0,
            )
            both = lax.dot_general(
                left, pages_of(key_buf, r, k), (((1,), (1,)), ((), ())), preferred_element_type=jnp.float32
            )
            weights = []
            for i in (0, 1):
                scores = both[i * group : (i + 1) * group] * factors(key_scale, r, k + i, 1.0 / math.sqrt(HD))
                highest = jnp.max(jnp.where(visible, scores, -1e30), axis=1, keepdims=True)
                high, low = split_two(highest)
                prob = jnp.where(visible, jnp.exp(scores - (high + low)), 0.0)
                total_high, total_low = split_two(jnp.sum(prob, axis=1, keepdims=True))
                for at, value in enumerate((high, low, total_high, total_low)):
                    stats[k + i] = jnp.where(lane == 4 * r + at, value, stats[k + i])
                weights.append((prob * factors(value_scale, r, k + i, 1.0)).astype(jnp.bfloat16))
            probs[r, k] = jnp.concatenate(weights, axis=0)
    for copy in large[1]:
        copy.wait()
    for r in range(rows):
        for k in range(0, kv_heads, 2):
            both = jnp.dot(probs[r, k], pages_of(value_buf, r, k), preferred_element_type=jnp.float32)
            for i in (0, 1):
                partial = both[i * group : (i + 1) * group, i * HD : (i + 1) * HD]
                for start in range(0, group, heads_dev):
                    d = ((k + i) * group + start) // heads_dev
                    staged[d, r * heads_dev : (r + 1) * heads_dev, :] = partial[start : start + heads_dev]
    for k in range(kv_heads):
        for start in range(0, group, heads_dev):
            d = (k * group + start) // heads_dev
            staged[d, part_rows : part_rows + heads_dev, :] = stats[k][start : start + heads_dev]
    packed[...] = staged[...].astype(jnp.bfloat16)


def project_kernel(heads_dev, packed, weight, *refs):
    outs, (weight_buf, attended, sems) = refs[:-3], refs[-3:]
    rows, part = outs[0].shape
    pieces, _, width = weight_buf.shape
    per_out = pieces // len(outs)
    quarter = lax.rem(lax.axis_index("kvp"), len(outs))
    copies = []
    for piece in range(pieces):
        start = jnp.bitwise_xor(quarter, piece // per_out) * part + piece % per_out * width
        source = weight.at[:, pl.ds(pl.multiple_of(start, width), width)]
        copies.append(pltpu.make_async_copy(source, weight_buf.at[piece], sems.at[piece]))
        copies[-1].start()
    blocks = packed[...].astype(jnp.float32)
    stats = blocks[:, rows * heads_dev : (rows + 1) * heads_dev, :]
    for r in range(rows):
        partial = blocks[:, r * heads_dev : (r + 1) * heads_dev, :]
        maxima = stats[:, :, 4 * r : 4 * r + 1] + stats[:, :, 4 * r + 1 : 4 * r + 2]
        totals = stats[:, :, 4 * r + 2 : 4 * r + 3] + stats[:, :, 4 * r + 3 : 4 * r + 4]
        rescale = jnp.exp(maxima - jnp.max(maxima, axis=0, keepdims=True))
        attended[r * heads_dev : (r + 1) * heads_dev, :] = jnp.sum(partial * rescale, axis=0) / jnp.sum(
            totals * rescale, axis=0
        )
    left = jnp.concatenate(
        [attended[pl.ds(j, rows, stride=heads_dev), :].astype(jnp.bfloat16) for j in range(heads_dev)], axis=1
    )
    for piece in range(pieces):
        copies[piece].wait()
        terms = jnp.dot(left, weight_buf[piece], preferred_element_type=jnp.float32)
        at = piece % per_out * width
        outs[piece // per_out][:, at : at + width] = terms.astype(jnp.bfloat16)


def add_kernel(*refs):
    terms = [ref[...].astype(jnp.float32) for ref in refs[:-1]]
    while len(terms) > 1:
        terms = [terms[i] + terms[i + 1] for i in range(0, len(terms), 2)]
    refs[-1][...] = terms[0].astype(refs[-1].dtype)


def lay_kernel(*refs):
    parts, out = refs[:-1], refs[-1]
    quarter = lax.rem(lax.axis_index("kvp"), len(parts))
    width = parts[0].shape[1]
    for x, part in enumerate(parts):
        start = pl.multiple_of(jnp.bitwise_xor(quarter, x) * width, width)
        out[:, pl.ds(start, width)] = part[...]


def exchange(array, partner, devices):
    return lax.ppermute(array, "kvp", [(i, i ^ partner) for i in range(devices)])


def in_hbm(array):
    return pltpu.with_memory_space_constraint(array, pltpu.HBM)


def body(queries, key_cache, value_cache, key_scale, value_scale, page_table, lengths, out_weight, *, devices):
    rows, pages = page_table.shape
    slots, _, columns = key_cache.shape
    kv_heads = key_scale.shape[1]
    heads_dev = out_weight.shape[0] // HD
    heads = queries.shape[1] // HD
    features = out_weight.shape[1]
    chunk = -(-(rows + 1) * heads_dev // 8) * 8
    inner = 4
    outer = devices // inner
    part = features // inner
    packed = pl.pallas_call(
        functools.partial(attend_kernel, heads_dev, devices),
        out_shape=jax.ShapeDtypeStruct((devices, chunk, HD), jnp.bfloat16),
        in_specs=[HBM] * 7,
        out_specs=VMEM,
        scratch_shapes=[
            pltpu.SMEM((rows, pages), jnp.int32),
            pltpu.SMEM((rows,), jnp.int32),
            pltpu.SMEM((kv_heads, slots), jnp.float32),
            pltpu.SMEM((kv_heads, slots), jnp.float32),
            pltpu.VMEM((rows, heads * HD), jnp.bfloat16),
            pltpu.VMEM((slots, PAGE, columns), jnp.bfloat16),
            pltpu.VMEM((slots, PAGE, columns), jnp.bfloat16),
            pltpu.VMEM((heads * rows, HD), jnp.float32),
            pltpu.VMEM((devices, chunk, HD), jnp.float32),
            pltpu.SemaphoreType.DMA((5,)),
            pltpu.SemaphoreType.DMA((2, 4)),
        ],
        compiler_params=pltpu.CompilerParams(vmem_limit_bytes=ATTEND_VMEM),
        cost_estimate=pl.CostEstimate(
            flops=4 * heads * rows * pages * PAGE * HD,
            bytes_accessed=4 * rows * pages * PAGE * columns,
            transcendentals=heads * rows * pages * PAGE,
        ),
        name="attend",
    )(*[in_hbm(a) for a in (page_table, lengths, key_scale.T, value_scale.T, queries, key_cache, value_cache)])

    received = lax.all_to_all(packed, "kvp", split_axis=0, concat_axis=0, tiled=True)

    terms = pl.pallas_call(
        functools.partial(project_kernel, heads_dev),
        out_shape=[jax.ShapeDtypeStruct((rows, part), jnp.bfloat16)] * inner,
        in_specs=[VMEM, HBM],
        out_specs=[VMEM] * inner,
        scratch_shapes=[
            pltpu.VMEM((WEIGHT_PIECES, heads_dev * HD, features // WEIGHT_PIECES), jnp.bfloat16),
            pltpu.VMEM((rows * heads_dev, HD), jnp.float32),
            pltpu.SemaphoreType.DMA((WEIGHT_PIECES,)),
        ],
        compiler_params=pltpu.CompilerParams(vmem_limit_bytes=PROJECT_VMEM),
        cost_estimate=pl.CostEstimate(
            flops=2 * rows * out_weight.size, bytes_accessed=2 * out_weight.size, transcendentals=0
        ),
        name="project",
    )(received, in_hbm(out_weight))

    def add(terms, name):
        return pl.pallas_call(
            add_kernel,
            out_shape=jax.ShapeDtypeStruct((rows, part), jnp.bfloat16),
            in_specs=[VMEM] * len(terms),
            out_specs=VMEM,
            compiler_params=pltpu.CompilerParams(vmem_limit_bytes=SMALL_VMEM),
            name=name,
        )(*terms)

    mine = add([terms[0]] + [exchange(terms[x], x, devices) for x in range(1, inner)], "add_near")
    mine = add([mine] + [exchange(mine, x * inner, devices) for x in range(1, outer)], "add_far")
    parts = [mine] + [exchange(mine, x, devices) for x in range(1, inner)]
    return pl.pallas_call(
        lay_kernel,
        out_shape=jax.ShapeDtypeStruct((rows, features), jnp.bfloat16),
        in_specs=[VMEM] * inner,
        out_specs=VMEM,
        compiler_params=pltpu.CompilerParams(vmem_limit_bytes=SMALL_VMEM),
        name="lay",
    )(*parts)


def solution(mesh):
    placed = (
        P("group", None),
        P(("group", "kvp"), None, None),
        P(("group", "kvp"), None, None),
        P(("group", "kvp"), None),
        P(("group", "kvp"), None),
        P("group", "kvp"),
        P("group"),
        P("kvp", None),
    )
    return jax.shard_map(
        functools.partial(body, devices=mesh.shape["kvp"]),
        mesh=mesh,
        in_specs=placed,
        out_specs=P("group", None),
        check_vma=False,
    )
```

time: 67.5 us -> 41.4 us (0.61)
  starting transfers between devices: 34.9 us -> 8.3 us
  blocking collectives: 0 us -> 14.6 us
  waiting for transfers between devices: 16.7 us -> 6.65 us
  Pallas kernels: 15.6 us -> 11.6 us
    ppermute x27 -> x9, starting transfers between devices: 34.9 us -> 8.3 us  [exchange(): lax.ppermute(array, 'kvp', [(i, i ^ partner) for i in range(devices)])]
    all_to_all x0 -> x1, blocking collectives: none -> 14.6 us  [body(): lax.all_to_all(packed, 'kvp', split_axis=0, concat_axis=0, tiled=True)]
    ppermute x27 -> x9, waiting for transfers between devices: 16.7 us -> 6.65 us  [exchange(): lax.ppermute(array, 'kvp', [(i, i ^ partner) for i in range(devices)])]
    pallas_call x4, Pallas kernels: 11 us -> 7.04 us  [the longest x1 6.31 us: body(): pl.pallas_call(functools.partial(project_kernel, heads_dev), out_shape=[j...]
  transfers between devices with their start and end apart: 27 -> 9, of which waited for: 11 -> 5; matrix products, arithmetic and copies ran while one was open for 0% -> 0% of each run, Pallas kernels for 0% -> 0%
where the time goes in v3:
time: 41.4 us; the launch traced here: 41.2 us
  blocking collectives  14.6 us (35%)
  Pallas kernels  11.6 us (28%)
  starting transfers between devices  8.3 us (20%)
  waiting for transfers between devices  6.65 us (16%)
    all_to_all x1, blocking collectives, body(): lax.all_to_all(packed, 'kvp', split_axis=0, concat_axis=0, tiled=True)  14.6 us
    ppermute x9, starting transfers between devices, exchange(): lax.ppermute(array, 'kvp', [(i, i ^ partner) for i in range(devices)])  8.3 us
    ppermute x9, waiting for transfers between devices, exchange(): lax.ppermute(array, 'kvp', [(i, i ^ partner) for i in range(devices)])  6.65 us
    pallas_call x1, Pallas kernels, body(): pl.pallas_call(functools.partial(project_kernel, heads_dev), out_shape=[j...  6.31 us
    pallas_call x1, Pallas kernels, body(): pl.pallas_call(functools.partial(attend_kernel, heads_dev, devices), out_...  4.56 us
  transfers between devices with their start and end apart: 9, of which 5 were waited for; matrix products, arithmetic and copies ran while one was open for 0% of the time, Pallas kernels for 0%

profile of v3, /device:TPU:0, one launch (start us, length us, event | category | flops | bytes accessed | tf_op | source)
XLA Modules:
  0.0 41.2 jit_solution(7816955065885446560)
XLA Ops:
  0.0 4.6 %attend.1 = bf16[16,24,128]{2,1,0:T(8,128)(2,1)S(1)} custom-call(s32[4,12]{1,0:T(4,128)} %refs_0_.1, s32[4]{0:T(128)} %refs_1_.1, f32[4,48]{1,0:T(4,128)} %bitcast.2, f32[4,48]{1,0:T(4,128)} %bitcast.3, bf16[4,8192]{1,0:T(4,128)(2,1)} %refs_4_.1, bf16[48,64,512]{2,1,0:T(8,128)(2,1)} %refs_5_.1, bf16[48,64,512]{2,1,0:T(8,128)(2,1)} %refs_6_.1), custom_call_target="tpu_custom_call" | custom-call | flops 100663296 | bytes 6291456 | tf_op jit(solution)/shard_map/attend/pallas_call | solution.py:195
  4.6 14.6 %all_to_all.5.packed = bf16[16,24,128]{2,1,0:T(8,128)(2,1)S(1)} all-to-all(bf16[16,24,128]{2,1,0:T(8,128)(2,1)S(1)} %attend.1), channel_id=1, replica_groups=mesh['group'=2,'kvp'=16] {'kvp'}, dimensions={0} | all-to-all | bytes 196608 | tf_op jit(solution)/shard_map/all_to_all | solution.py:222
  19.2 6.3 %project.1 = (bf16[4,4096]{1,0:T(4,128)(2,1)S(1)}, bf16[4,4096]{1,0:T(4,128)(2,1)S(1)}, bf16[4,4096]{1,0:T(4,128)(2,1)S(1)}, bf16[4,4096]{1,0:T(4,128)(2,1)S(1)}) custom-call(bf16[16,24,128]{2,1,0:T(8,128)(2,1)S(1)} %all_to_all.5.packed, bf16[512,16384]{1,0:T(8,128)(2,1)} %weight.1), custom_call_target="tpu_custom_call" | custom-call | flops 67108864 | bytes 16777216 | tf_op jit(solution)/shard_map/project/pallas_call | solution.py:224
  25.5 0.1 collective-permute-start
  25.6 0.1 collective-permute-start.1
  25.7 1.8 %collective-permute-start.2 = (bf16[4,4096]{1,0:T(4,128)(2,1)S(1)}, bf16[4,4096]{1,0:T(4,128)(2,1)S(1)}, u32[]{:S(2)}, u32[]{:S(2)}) collective-permute-start(bf16[4,4096]{1,0:T(4,128)(2,1)S(1)} %get-tuple-element.12), channel_id=1, source_target_pairs={{0,3},{1,2},{2,1},{3,0},{4,7},{5,6},{6,5},{7,4},{8,11},{9,10},{10,... | collective-permute-start | bytes 98312 | tf_op jit(solution)/shard_map/ppermute | solution.py:177
  27.4 0.0 collective-permute-done.refs_1_
  27.4 2.3 %collective-permute-done.1.refs_2_ = bf16[4,4096]{1,0:T(4,128)(2,1)S(1)} collective-permute-done((bf16[4,4096]{1,0:T(4,128)(2,1)S(1)}, bf16[4,4096]{1,0:T(4,128)(2,1)S(1)}, u32[]{:S(2)}, u32[]{:S(2)}) %collective-permute-start.1) | collective-permute-done | bytes 32800 | tf_op jit(solution)/shard_map/ppermute | solution.py:177
  29.7 0.0 collective-permute-done.2.refs_3_
  29.8 1.1 %collective-permute-start.5 = (bf16[4,4096]{1,0:T(4,128)(2,1)S(1)}, bf16[4,4096]{1,0:T(4,128)(2,1)S(1)}, u32[]{:S(2)}, u32[]{:S(2)}) collective-permute-start(bf16[4,4096]{1,0:T(4,128)(2,1)S(1)} %add_near.1.refs_0_), channel_id=1, source_target_pairs={{0,12},{1,13},{2,14},{3,15},{4,8},{5,9},{6,10},{7,11},{8,4},{9,5},... | collective-permute-start | bytes 98312 | tf_op jit(solution)/shard_map/ppermute | solution.py:177
  30.8 0.8 %collective-permute-start.4 = (bf16[4,4096]{1,0:T(4,128)(2,1)S(1)}, bf16[4,4096]{1,0:T(4,128)(2,1)S(1)}, u32[]{:S(2)}, u32[]{:S(2)}) collective-permute-start(bf16[4,4096]{1,0:T(4,128)(2,1)S(1)} %add_near.1.refs_0_), channel_id=1, source_target_pairs={{0,8},{1,9},{2,10},{3,11},{4,12},{5,13},{6,14},{7,15},{8,0},{9,1},... | collective-permute-start | bytes 98312 | tf_op jit(solution)/shard_map/ppermute | solution.py:177
  31.6 2.6 %collective-permute-start.3 = (bf16[4,4096]{1,0:T(4,128)(2,1)S(1)}, bf16[4,4096]{1,0:T(4,128)(2,1)S(1)}, u32[]{:S(2)}, u32[]{:S(2)}) collective-permute-start(bf16[4,4096]{1,0:T(4,128)(2,1)S(1)} %add_near.1.refs_0_), channel_id=1, source_target_pairs={{0,4},{1,5},{2,6},{3,7},{4,0},{5,1},{6,2},{7,3},{8,12},{9,13},{10,... | collective-permute-start | bytes 98312 | tf_op jit(solution)/shard_map/ppermute | solution.py:177
  34.2 1.5 %collective-permute-done.5.refs_3_ = bf16[4,4096]{1,0:T(4,128)(2,1)S(1)} collective-permute-done((bf16[4,4096]{1,0:T(4,128)(2,1)S(1)}, bf16[4,4096]{1,0:T(4,128)(2,1)S(1)}, u32[]{:S(2)}, u32[]{:S(2)}) %collective-permute-start.5) | collective-permute-done | bytes 32800 | tf_op jit(solution)/shard_map/ppermute | solution.py:177
  35.7 0.6 %collective-permute-done.4.refs_2_ = bf16[4,4096]{1,0:T(4,128)(2,1)S(1)} collective-permute-done((bf16[4,4096]{1,0:T(4,128)(2,1)S(1)}, bf16[4,4096]{1,0:T(4,128)(2,1)S(1)}, u32[]{:S(2)}, u32[]{:S(2)}) %collective-permute-start.4) | collective-permute-done | bytes 32800 | tf_op jit(solution)/shard_map/ppermute | solution.py:177
  36.3 0.0 collective-permute-done.3.refs_1_
  36.3 0.1 collective-permute-start.8
  36.4 1.2 %collective-permute-start.7 = (bf16[4,4096]{1,0:T(4,128)(2,1)S(1)}, bf16[4,4096]{1,0:T(4,128)(2,1)S(1)}, u32[]{:S(2)}, u32[]{:S(2)}) collective-permute-start(bf16[4,4096]{1,0:T(4,128)(2,1)S(1)} %add_far.1.refs_0_), channel_id=1, source_target_pairs={{0,2},{1,3},{2,0},{3,1},{4,6},{5,7},{6,4},{7,5},{8,10},{9,11},{10,... | collective-permute-start | bytes 98312 | tf_op jit(solution)/shard_map/ppermute | solution.py:177
  37.6 0.6 %collective-permute-start.6 = (bf16[4,4096]{1,0:T(4,128)(2,1)S(1)}, bf16[4,4096]{1,0:T(4,128)(2,1)S(1)}, u32[]{:S(2)}, u32[]{:S(2)}) collective-permute-start(bf16[4,4096]{1,0:T(4,128)(2,1)S(1)} %add_far.1.refs_0_), channel_id=1, source_target_pairs={{0,1},{1,0},{2,3},{3,2},{4,5},{5,4},{6,7},{7,6},{8,9},{9,8},{10,11... | collective-permute-start | bytes 98312 | tf_op jit(solution)/shard_map/ppermute | solution.py:177
  38.2 1.5 %collective-permute-done.8.refs_3_ = bf16[4,4096]{1,0:T(4,128)(2,1)S(1)} collective-permute-done((bf16[4,4096]{1,0:T(4,128)(2,1)S(1)}, bf16[4,4096]{1,0:T(4,128)(2,1)S(1)}, u32[]{:S(2)}, u32[]{:S(2)}) %collective-permute-start.8) | collective-permute-done | bytes 32800 | tf_op jit(solution)/shard_map/ppermute | solution.py:177
  39.8 0.7 %collective-permute-done.7.refs_2_ = bf16[4,4096]{1,0:T(4,128)(2,1)S(1)} collective-permute-done((bf16[4,4096]{1,0:T(4,128)(2,1)S(1)}, bf16[4,4096]{1,0:T(4,128)(2,1)S(1)}, u32[]{:S(2)}, u32[]{:S(2)}) %collective-permute-start.7) | collective-permute-done | bytes 32800 | tf_op jit(solution)/shard_map/ppermute | solution.py:177
  40.5 0.0 collective-permute-done.6.refs_1_
  40.5 0.7 %lay.1 = bf16[4,16384]{1,0:T(4,128)(2,1)} custom-call(bf16[4,4096]{1,0:T(4,128)(2,1)S(1)} %add_far.1.refs_0_, bf16[4,4096]{1,0:T(4,128)(2,1)S(1)} %collective-permute-done.6.refs_1_, bf16[4,4096]{1,0:T(4,128)(2,1)S(1)} %collective-permute-done.7.refs_2_, bf16[4,4096]{1,0:T(4,128)(2,1)S(1)} %collective-permute-done.8.refs_3_), custom_call_target="tpu_custom_call" | custom-call | tf_op jit(solution)/shard_map/lay/pallas_call | solution.py:254
  (2 shorter events, 0.1 us)
Async XLA Ops:
  25.5 1.9 %collective-permute-start = (bf16[4,4096]{1,0:T(4,128)(2,1)S(1)}, bf16[4,4096]{1,0:T(4,128)(2,1)S(1)}, u32[]{:S(2)}, u32[]{:S(2)}) collective-permute-start(bf16[4,4096]{1,0:T(4,128)(2,1)S(1)} %get-tuple-element.10), channel_id=1, source_target_pairs={{0,1},{1,0},{2,3},{3,2},{4,5},{5,4},{6,7},{7,6},{8,9},{9,8},{10,11... | collective-permute-start | bytes 98312 | tf_op jit(solution)/shard_map/ppermute | solution.py:177
  25.6 4.2 %collective-permute-start.1 = (bf16[4,4096]{1,0:T(4,128)(2,1)S(1)}, bf16[4,4096]{1,0:T(4,128)(2,1)S(1)}, u32[]{:S(2)}, u32[]{:S(2)}) collective-permute-start(bf16[4,4096]{1,0:T(4,128)(2,1)S(1)} %get-tuple-element.11), channel_id=1, source_target_pairs={{0,2},{1,3},{2,0},{3,1},{4,6},{5,7},{6,4},{7,5},{8,10},{9,11},{10,... | collective-permute-start | bytes 98312 | tf_op jit(solution)/shard_map/ppermute | solution.py:177
  25.7 4.1 %collective-permute-start.2 = (bf16[4,4096]{1,0:T(4,128)(2,1)S(1)}, bf16[4,4096]{1,0:T(4,128)(2,1)S(1)}, u32[]{:S(2)}, u32[]{:S(2)}) collective-permute-start(bf16[4,4096]{1,0:T(4,128)(2,1)S(1)} %get-tuple-element.12), channel_id=1, source_target_pairs={{0,3},{1,2},{2,1},{3,0},{4,7},{5,6},{6,5},{7,4},{8,11},{9,10},{10,... | collective-permute-start | bytes 98312 | tf_op jit(solution)/shard_map/ppermute | solution.py:177
  29.8 6.0 %collective-permute-start.5 = (bf16[4,4096]{1,0:T(4,128)(2,1)S(1)}, bf16[4,4096]{1,0:T(4,128)(2,1)S(1)}, u32[]{:S(2)}, u32[]{:S(2)}) collective-permute-start(bf16[4,4096]{1,0:T(4,128)(2,1)S(1)} %add_near.1.refs_0_), channel_id=1, source_target_pairs={{0,12},{1,13},{2,14},{3,15},{4,8},{5,9},{6,10},{7,11},{8,4},{9,5},... | collective-permute-start | bytes 98312 | tf_op jit(solution)/shard_map/ppermute | solution.py:177
  30.8 5.4 %collective-permute-start.4 = (bf16[4,4096]{1,0:T(4,128)(2,1)S(1)}, bf16[4,4096]{1,0:T(4,128)(2,1)S(1)}, u32[]{:S(2)}, u32[]{:S(2)}) collective-permute-start(bf16[4,4096]{1,0:T(4,128)(2,1)S(1)} %add_near.1.refs_0_), channel_id=1, source_target_pairs={{0,8},{1,9},{2,10},{3,11},{4,12},{5,13},{6,14},{7,15},{8,0},{9,1},... | collective-permute-start | bytes 98312 | tf_op jit(solution)/shard_map/ppermute | solution.py:177
  31.6 4.7 %collective-permute-start.3 = (bf16[4,4096]{1,0:T(4,128)(2,1)S(1)}, bf16[4,4096]{1,0:T(4,128)(2,1)S(1)}, u32[]{:S(2)}, u32[]{:S(2)}) collective-permute-start(bf16[4,4096]{1,0:T(4,128)(2,1)S(1)} %add_near.1.refs_0_), channel_id=1, source_target_pairs={{0,4},{1,5},{2,6},{3,7},{4,0},{5,1},{6,2},{7,3},{8,12},{9,13},{10,... | collective-permute-start | bytes 98312 | tf_op jit(solution)/shard_map/ppermute | solution.py:177
  36.3 3.5 %collective-permute-start.8 = (bf16[4,4096]{1,0:T(4,128)(2,1)S(1)}, bf16[4,4096]{1,0:T(4,128)(2,1)S(1)}, u32[]{:S(2)}, u32[]{:S(2)}) collective-permute-start(bf16[4,4096]{1,0:T(4,128)(2,1)S(1)} %add_far.1.refs_0_), channel_id=1, source_target_pairs={{0,3},{1,2},{2,1},{3,0},{4,7},{5,6},{6,5},{7,4},{8,11},{9,10},{10,... | collective-permute-start | bytes 98312 | tf_op jit(solution)/shard_map/ppermute | solution.py:177
  36.4 4.1 %collective-permute-start.7 = (bf16[4,4096]{1,0:T(4,128)(2,1)S(1)}, bf16[4,4096]{1,0:T(4,128)(2,1)S(1)}, u32[]{:S(2)}, u32[]{:S(2)}) collective-permute-start(bf16[4,4096]{1,0:T(4,128)(2,1)S(1)} %add_far.1.refs_0_), channel_id=1, source_target_pairs={{0,2},{1,3},{2,0},{3,1},{4,6},{5,7},{6,4},{7,5},{8,10},{9,11},{10,... | collective-permute-start | bytes 98312 | tf_op jit(solution)/shard_map/ppermute | solution.py:177
  37.6 2.9 %collective-permute-start.6 = (bf16[4,4096]{1,0:T(4,128)(2,1)S(1)}, bf16[4,4096]{1,0:T(4,128)(2,1)S(1)}, u32[]{:S(2)}, u32[]{:S(2)}) collective-permute-start(bf16[4,4096]{1,0:T(4,128)(2,1)S(1)} %add_far.1.refs_0_), channel_id=1, source_target_pairs={{0,1},{1,0},{2,3},{3,2},{4,5},{5,4},{6,7},{7,6},{8,9},{9,8},{10,11... | collective-permute-start | bytes 98312 | tf_op jit(solution)/shard_map/ppermute | solution.py:177

commit v4 on v3

--- a/solution.py
+++ b/solution.py
@@ -11,11 +11,11 @@
 HD = 128
 PAGE = 64
 ATTEND_VMEM = 24 * 1024 * 1024
-PROJECT_VMEM = 40 * 1024 * 1024
-WEIGHT_PIECES = 16
+WEIGHT_PIECES = 8
 SMALL_VMEM = 8 * 1024 * 1024
 VMEM = pl.BlockSpec(memory_space=pltpu.VMEM)
 HBM = pl.BlockSpec(memory_space=pltpu.HBM)
+ANY = pl.BlockSpec(memory_space=pl.ANY)
 
 
 def split_two(value):
@@ -125,18 +125,25 @@
     packed[...] = staged[...].astype(jnp.bfloat16)
 
 
-def project_kernel(heads_dev, packed, weight, *refs):
-    outs, (weight_buf, attended, sems) = refs[:-3], refs[-3:]
-    rows, part = outs[0].shape
-    pieces, _, width = weight_buf.shape
-    per_out = pieces // len(outs)
-    quarter = lax.rem(lax.axis_index("kvp"), len(outs))
+def fetch_kernel(parts, _, weight, buf, sems):
+    pieces, _, width = buf.shape
+    per_part = pieces // parts
+    quarter = lax.rem(lax.axis_index("kvp"), parts)
     copies = []
     for piece in range(pieces):
-        start = jnp.bitwise_xor(quarter, piece // per_out) * part + piece % per_out * width
+        start = (jnp.bitwise_xor(quarter, piece // per_part) * per_part + piece % per_part) * width
         source = weight.at[:, pl.ds(pl.multiple_of(start, width), width)]
-        copies.append(pltpu.make_async_copy(source, weight_buf.at[piece], sems.at[piece]))
+        copies.append(pltpu.make_async_copy(source, buf.at[piece], sems.at[piece]))
         copies[-1].start()
+    for copy in copies:
+        copy.wait()
+
+
+def project_kernel(heads_dev, packed, weight, left, *refs):
+    outs, attended = refs[:-1], refs[-1]
+    rows = left.shape[0]
+    width = weight.shape[2]
+    per_out = weight.shape[0] // (len(outs) + 1)
     blocks = packed[...].astype(jnp.float32)
     stats = blocks[:, rows * heads_dev : (rows + 1) * heads_dev, :]
     for r in range(rows):
@@ -147,14 +154,21 @@
         attended[r * heads_dev : (r + 1) * heads_dev, :] = jnp.sum(partial * rescale, axis=0) / jnp.sum(
             totals * rescale, axis=0
         )
-    left = jnp.concatenate(
+    rounded = jnp.concatenate(
         [attended[pl.ds(j, rows, stride=heads_dev), :].astype(jnp.bfloat16) for j in range(heads_dev)], axis=1
     )
-    for piece in range(pieces):
-        copies[piece].wait()
-        terms = jnp.dot(left, weight_buf[piece], preferred_element_type=jnp.float32)
-        at = piece % per_out * width
-        outs[piece // per_out][:, at : at + width] = terms.astype(jnp.bfloat16)
+    left[...] = rounded
+    for x, out in enumerate(outs):
+        for i in range(per_out):
+            terms = jnp.dot(rounded, weight[(x + 1) * per_out + i], preferred_element_type=jnp.float32)
+            out[:, i * width : (i + 1) * width] = terms.astype(jnp.bfloat16)
+
+
+def project_own_kernel(left, weight, out):
+    width = weight.shape[2]
+    for i in range(out.shape[1] // width):
+        terms = jnp.dot(left[...], weight[i], preferred_element_type=jnp.float32)
+        out[:, i * width : (i + 1) * width] = terms.astype(jnp.bfloat16)
 
 
 def add_kernel(*refs):
@@ -221,22 +235,46 @@
 
     received = lax.all_to_all(packed, "kvp", split_axis=0, concat_axis=0, tiled=True)
 
-    terms = pl.pallas_call(
+    depth = heads_dev * HD
+    width = features // WEIGHT_PIECES
+    fetched = pl.pallas_call(
+        functools.partial(fetch_kernel, inner),
+        out_shape=pltpu.VMEM((WEIGHT_PIECES, depth, width), jnp.bfloat16),
+        in_specs=[ANY, HBM],
+        out_specs=VMEM,
+        scratch_shapes=[pltpu.SemaphoreType.DMA((WEIGHT_PIECES,))],
+        compiler_params=pltpu.CompilerParams(vmem_limit_bytes=SMALL_VMEM),
+        cost_estimate=pl.CostEstimate(flops=0, bytes_accessed=2 * out_weight.size, transcendentals=0),
+        name="fetch",
+    )(packed, in_hbm(out_weight))
+
+    left, *others = pl.pallas_call(
         functools.partial(project_kernel, heads_dev),
-        out_shape=[jax.ShapeDtypeStruct((rows, part), jnp.bfloat16)] * inner,
-        in_specs=[VMEM, HBM],
+        out_shape=[jax.ShapeDtypeStruct((rows, depth), jnp.bfloat16)]
+        + [jax.ShapeDtypeStruct((rows, part), jnp.bfloat16)] * (inner - 1),
+        in_specs=[VMEM, VMEM],
         out_specs=[VMEM] * inner,
-        scratch_shapes=[
-            pltpu.VMEM((WEIGHT_PIECES, heads_dev * HD, features // WEIGHT_PIECES), jnp.bfloat16),
-            pltpu.VMEM((rows * heads_dev, HD), jnp.float32),
-            pltpu.SemaphoreType.DMA((WEIGHT_PIECES,)),
-        ],
-        compiler_params=pltpu.CompilerParams(vmem_limit_bytes=PROJECT_VMEM),
+        scratch_shapes=[pltpu.VMEM((rows * heads_dev, HD), jnp.float32)],
+        compiler_params=pltpu.CompilerParams(vmem_limit_bytes=SMALL_VMEM),
         cost_estimate=pl.CostEstimate(
-            flops=2 * rows * out_weight.size, bytes_accessed=2 * out_weight.size, transcendentals=0
+            flops=2 * rows * depth * part * (inner - 1),
+            bytes_accessed=2 * depth * part * (inner - 1),
+            transcendentals=0,
         ),
-        name="project",
-    )(received, in_hbm(out_weight))
+        name="project_others",
+    )(received, fetched)
+    sent = [exchange(others[x - 1], x, devices) for x in range(1, inner)]
+    own = pl.pallas_call(
+        project_own_kernel,
+        out_shape=jax.ShapeDtypeStruct((rows, part), jnp.bfloat16),
+        in_specs=[VMEM, VMEM],
+        out_specs=VMEM,
+        compiler_params=pltpu.CompilerParams(vmem_limit_bytes=SMALL_VMEM),
+        cost_estimate=pl.CostEstimate(
+            flops=2 * rows * depth * part, bytes_accessed=2 * depth * part, transcendentals=0
+        ),
+        name="project_own",
+    )(left, fetched)
 
     def add(terms, name):
         return pl.pallas_call(
@@ -248,7 +286,7 @@
             name=name,
         )(*terms)
 
-    mine = add([terms[0]] + [exchange(terms[x], x, devices) for x in range(1, inner)], "add_near")
+    mine = add([own] + sent, "add_near")
     mine = add([mine] + [exchange(mine, x * inner, devices) for x in range(1, outer)], "add_far")
     parts = [mine] + [exchange(mine, x, devices) for x in range(1, inner)]
     return pl.pallas_call(

time: 41.4 us -> 51.1 us (1.23)
  blocking collectives: 14.6 us -> 0 us
  local copies, waits for them, and re-layouts: 0 us -> 11.5 us
  starting transfers between devices: 8.3 us -> 15.9 us
  Pallas kernels: 11.6 us -> 14.6 us
  waiting for transfers between devices: 6.65 us -> 8.85 us
    all_to_all x1 -> x0, blocking collectives: 14.6 us -> none  [body(): lax.all_to_all(packed, 'kvp', split_axis=0, concat_axis=0, tiled=True)]
    unnamed x0 -> x4, local copies, waits for them, and re-layouts: none -> 11.5 us
    all_to_all x0 -> x1, starting transfers between devices: none -> 7.4 us  [body(): lax.all_to_all(packed, 'kvp', split_axis=0, concat_axis=0, tiled=True)]
    pallas_call x0 -> x2, Pallas kernels: none -> 6.61 us  [the longest x1 5.96 us: body(): pl.pallas_call(functools.partial(fetch_kernel, inner), out_shape=pltpu.VM...]
    pallas_call x1, Pallas kernels: 6.31 us -> 2.07 us  [body(): pl.pallas_call(functools.partial(project_kernel, heads_dev), out_shape=[j...]
    ppermute x9, waiting for transfers between devices: 6.65 us -> 8.85 us  [exchange(): lax.ppermute(array, 'kvp', [(i, i ^ partner) for i in range(devices)])]
    pallas_call x1, Pallas kernels: 4.56 us -> 5.19 us  [body(): pl.pallas_call(functools.partial(attend_kernel, heads_dev, devices), out_...]
  transfers between devices with their start and end apart: 9 -> 10, of which waited for: 5 -> 6; matrix products, arithmetic and copies ran while one was open for 0% -> 0% of each run, Pallas kernels for 0% -> 13%
where the time goes in v4:
time: 51.1 us; the launch traced here: 50.9 us
  starting transfers between devices  15.9 us (31%)
  Pallas kernels  14.6 us (29%)
  local copies, waits for them, and re-layouts  11.5 us (23%)
  waiting for transfers between devices  8.85 us (17%)
    unnamed x4, local copies, waits for them, and re-layouts  11.5 us
    ppermute x9, waiting for transfers between devices, exchange(): lax.ppermute(array, 'kvp', [(i, i ^ partner) for i in range(devices)])  8.85 us
    ppermute x9, starting transfers between devices, exchange(): lax.ppermute(array, 'kvp', [(i, i ^ partner) for i in range(devices)])  8.46 us
    all_to_all x1, starting transfers between devices, body(): lax.all_to_all(packed, 'kvp', split_axis=0, concat_axis=0, tiled=True)  7.4 us
    pallas_call x1, Pallas kernels, body(): pl.pallas_call(functools.partial(fetch_kernel, inner), out_shape=pltpu.VM...  5.96 us
    pallas_call x1, Pallas kernels, body(): pl.pallas_call(functools.partial(attend_kernel, heads_dev, devices), out_...  5.19 us
    pallas_call x1, Pallas kernels, body(): pl.pallas_call(functools.partial(project_kernel, heads_dev), out_shape=[j...  2.07 us
  transfers between devices with their start and end apart: 10, of which 6 were waited for; matrix products, arithmetic and copies ran while one was open for 0% of the time, Pallas kernels for 13%

profile of v4, /device:TPU:0, one launch (start us, length us, event | category | flops | bytes accessed | tf_op | source)
XLA Modules:
  0.0 50.9 jit_solution(6669282050012376759)
XLA Ops:
  0.0 5.2 %attend.1._ = bf16[16,24,128]{2,1,0:T(8,128)(2,1)} custom-call(s32[4,12]{1,0:T(4,128)} %refs_0_.1, s32[4]{0:T(128)} %refs_1_.1, f32[4,48]{1,0:T(4,128)} %bitcast.2, f32[4,48]{1,0:T(4,128)} %bitcast.3, bf16[4,8192]{1,0:T(4,128)(2,1)} %refs_4_.1, bf16[48,64,512]{2,1,0:T(8,128)(2,1)} %refs_5_.1, bf16[48,64,512]{2,1,0:T(8,128)(2,1)} %refs_6_.1), custom_call_target="tpu_custom_call" | custom-call | flops 100663296 | bytes 6291456 | tf_op jit(solution)/shard_map/attend/pallas_call | solution.py:209
  5.2 7.4 %all-to-all-start = ((bf16[16,24,128]{2,1,0:T(8,128)(2,1)}), bf16[16,24,128]{2,1,0:T(8,128)(2,1)S(1)}, u32[]{:S(2)}, u32[]{:S(2)}) async-start(bf16[16,24,128]{2,1,0:T(8,128)(2,1)} %attend.1._), calls=%async_computation | async-start | bytes 196608 | tf_op jit(solution)/shard_map/all_to_all | solution.py:236
  12.6 6.0 %fetch.1.weight = bf16[8,512,2048]{2,1,0:T(8,128)(2,1)S(1)} custom-call(bf16[16,24,128]{2,1,0:T(8,128)(2,1)} %attend.1._, bf16[512,16384]{1,0:T(8,128)(2,1)} %weight.1), custom_call_target="tpu_custom_call" | custom-call | bytes 16777216 | tf_op jit(solution)/shard_map/fetch/pallas_call | solution.py:240
  18.6 0.0 copy-start
  18.6 5.7 %copy-done = bf16[8,512,2048]{2,1,0:T(8,128)(2,1)} copy-done((bf16[8,512,2048]{2,1,0:T(8,128)(2,1)}, bf16[8,512,2048]{2,1,0:T(8,128)(2,1)S(1)}, u32[]{:S(2)}) %copy-start) | copy-done | bytes 16777240
  24.3 0.0 all-to-all-done.packed
  24.3 0.0 copy-start.1
  24.3 5.8 %copy-done.1 = bf16[8,512,2048]{2,1,0:T(8,128)(2,1)S(1)} copy-done((bf16[8,512,2048]{2,1,0:T(8,128)(2,1)S(1)}, bf16[8,512,2048]{2,1,0:T(8,128)(2,1)}, u32[]{:S(2)}) %copy-start.1) | copy-done | bytes 16777240
  30.1 2.1 %project_others.1 = (bf16[4,512]{1,0:T(4,128)(2,1)S(1)}, bf16[4,4096]{1,0:T(4,128)(2,1)S(1)}, bf16[4,4096]{1,0:T(4,128)(2,1)S(1)}, bf16[4,4096]{1,0:T(4,128)(2,1)S(1)}) custom-call(bf16[16,24,128]{2,1,0:T(8,128)(2,1)S(1)} %all-to-all-done.packed, bf16[8,512,2048]{2,1,0:T(8,128)(2,1)S(1)} %copy-done.1), custom_call_target="tpu_custom_call" | custom-call | flops 50331648 | bytes 12582912 | tf_op jit(solution)/shard_map/project_others/pallas_call | solution.py:251
  32.2 0.4 collective-permute-start
  32.6 1.7 %collective-permute-start.1 = (bf16[4,4096]{1,0:T(4,128)(2,1)S(1)}, bf16[4,4096]{1,0:T(4,128)(2,1)S(1)}, u32[]{:S(2)}, u32[]{:S(2)}) collective-permute-start(bf16[4,4096]{1,0:T(4,128)(2,1)S(1)} %get-tuple-element.11), channel_id=1, source_target_pairs={{0,2},{1,3},{2,0},{3,1},{4,6},{5,7},{6,4},{7,5},{8,10},{9,11},{10,... | collective-permute-start | bytes 98312 | tf_op jit(solution)/shard_map/ppermute | solution.py:191
  34.2 0.0 collective-permute-start.2
  34.2 0.6 %project_own.1.refs_0_ = bf16[4,4096]{1,0:T(4,128)(2,1)S(1)} custom-call(bf16[4,512]{1,0:T(4,128)(2,1)S(1)} %get-tuple-element.9.left, bf16[8,512,2048]{2,1,0:T(8,128)(2,1)S(1)} %copy-done.1), custom_call_target="tpu_custom_call" | custom-call | flops 16777216 | bytes 4194304 | tf_op jit(solution)/shard_map/project_own/pallas_call | solution.py:267
  34.9 0.0 collective-permute-done.refs_1_
  34.9 1.6 %collective-permute-done.1.refs_2_ = bf16[4,4096]{1,0:T(4,128)(2,1)S(1)} collective-permute-done((bf16[4,4096]{1,0:T(4,128)(2,1)S(1)}, bf16[4,4096]{1,0:T(4,128)(2,1)S(1)}, u32[]{:S(2)}, u32[]{:S(2)}) %collective-permute-start.1) | collective-permute-done | bytes 32800 | tf_op jit(solution)/shard_map/ppermute | solution.py:191
  36.5 1.2 %collective-permute-done.2.refs_3_ = bf16[4,4096]{1,0:T(4,128)(2,1)S(1)} collective-permute-done((bf16[4,4096]{1,0:T(4,128)(2,1)S(1)}, bf16[4,4096]{1,0:T(4,128)(2,1)S(1)}, u32[]{:S(2)}, u32[]{:S(2)}) %collective-permute-start.2) | collective-permute-done | bytes 32800 | tf_op jit(solution)/shard_map/ppermute | solution.py:191
  37.7 3.3 %collective-permute-start.5 = (bf16[4,4096]{1,0:T(4,128)(2,1)S(1)}, bf16[4,4096]{1,0:T(4,128)(2,1)S(1)}, u32[]{:S(2)}, u32[]{:S(2)}) collective-permute-start(bf16[4,4096]{1,0:T(4,128)(2,1)S(1)} %add_near.1.refs_0_), channel_id=1, source_target_pairs={{0,12},{1,13},{2,14},{3,15},{4,8},{5,9},{6,10},{7,11},{8,4},{9,5},... | collective-permute-start | bytes 98312 | tf_op jit(solution)/shard_map/ppermute | solution.py:191
  41.1 0.0 collective-permute-start.4
  41.1 1.1 %collective-permute-start.3 = (bf16[4,4096]{1,0:T(4,128)(2,1)S(1)}, bf16[4,4096]{1,0:T(4,128)(2,1)S(1)}, u32[]{:S(2)}, u32[]{:S(2)}) collective-permute-start(bf16[4,4096]{1,0:T(4,128)(2,1)S(1)} %add_near.1.refs_0_), channel_id=1, source_target_pairs={{0,4},{1,5},{2,6},{3,7},{4,0},{5,1},{6,2},{7,3},{8,12},{9,13},{10,... | collective-permute-start | bytes 98312 | tf_op jit(solution)/shard_map/ppermute | solution.py:191
  42.2 1.4 %collective-permute-done.5.refs_3_ = bf16[4,4096]{1,0:T(4,128)(2,1)S(1)} collective-permute-done((bf16[4,4096]{1,0:T(4,128)(2,1)S(1)}, bf16[4,4096]{1,0:T(4,128)(2,1)S(1)}, u32[]{:S(2)}, u32[]{:S(2)}) %collective-permute-start.5) | collective-permute-done | bytes 32800 | tf_op jit(solution)/shard_map/ppermute | solution.py:191
  43.5 2.3 %collective-permute-done.4.refs_2_ = bf16[4,4096]{1,0:T(4,128)(2,1)S(1)} collective-permute-done((bf16[4,4096]{1,0:T(4,128)(2,1)S(1)}, bf16[4,4096]{1,0:T(4,128)(2,1)S(1)}, u32[]{:S(2)}, u32[]{:S(2)}) %collective-permute-start.4) | collective-permute-done | bytes 32800 | tf_op jit(solution)/shard_map/ppermute | solution.py:191
  45.9 0.0 collective-permute-done.3.refs_1_
  45.9 0.1 collective-permute-start.8
  46.0 0.9 %collective-permute-start.7 = (bf16[4,4096]{1,0:T(4,128)(2,1)S(1)}, bf16[4,4096]{1,0:T(4,128)(2,1)S(1)}, u32[]{:S(2)}, u32[]{:S(2)}) collective-permute-start(bf16[4,4096]{1,0:T(4,128)(2,1)S(1)} %add_far.1.refs_0_), channel_id=1, source_target_pairs={{0,2},{1,3},{2,0},{3,1},{4,6},{5,7},{6,4},{7,5},{8,10},{9,11},{10,... | collective-permute-start | bytes 98312 | tf_op jit(solution)/shard_map/ppermute | solution.py:191
  46.9 1.0 %collective-permute-start.6 = (bf16[4,4096]{1,0:T(4,128)(2,1)S(1)}, bf16[4,4096]{1,0:T(4,128)(2,1)S(1)}, u32[]{:S(2)}, u32[]{:S(2)}) collective-permute-start(bf16[4,4096]{1,0:T(4,128)(2,1)S(1)} %add_far.1.refs_0_), channel_id=1, source_target_pairs={{0,1},{1,0},{2,3},{3,2},{4,5},{5,4},{6,7},{7,6},{8,9},{9,8},{10,11... | collective-permute-start | bytes 98312 | tf_op jit(solution)/shard_map/ppermute | solution.py:191
  47.8 1.5 %collective-permute-done.8.refs_3_ = bf16[4,4096]{1,0:T(4,128)(2,1)S(1)} collective-permute-done((bf16[4,4096]{1,0:T(4,128)(2,1)S(1)}, bf16[4,4096]{1,0:T(4,128)(2,1)S(1)}, u32[]{:S(2)}, u32[]{:S(2)}) %collective-permute-start.8) | collective-permute-done | bytes 32800 | tf_op jit(solution)/shard_map/ppermute | solution.py:191
  49.3 0.9 %collective-permute-done.7.refs_2_ = bf16[4,4096]{1,0:T(4,128)(2,1)S(1)} collective-permute-done((bf16[4,4096]{1,0:T(4,128)(2,1)S(1)}, bf16[4,4096]{1,0:T(4,128)(2,1)S(1)}, u32[]{:S(2)}, u32[]{:S(2)}) %collective-permute-start.7) | collective-permute-done | bytes 32800 | tf_op jit(solution)/shard_map/ppermute | solution.py:191
  50.2 0.0 collective-permute-done.6.refs_1_
  50.2 0.7 %lay.1 = bf16[4,16384]{1,0:T(4,128)(2,1)} custom-call(bf16[4,4096]{1,0:T(4,128)(2,1)S(1)} %add_far.1.refs_0_, bf16[4,4096]{1,0:T(4,128)(2,1)S(1)} %collective-permute-done.6.refs_1_, bf16[4,4096]{1,0:T(4,128)(2,1)S(1)} %collective-permute-done.7.refs_2_, bf16[4,4096]{1,0:T(4,128)(2,1)S(1)} %collective-permute-done.8.refs_3_), custom_call_target="tpu_custom_call" | custom-call | tf_op jit(solution)/shard_map/lay/pallas_call | solution.py:292
  (2 shorter events, 0.1 us)
Async XLA Ops:
  5.2 19.1 %all-to-all-start = ((bf16[16,24,128]{2,1,0:T(8,128)(2,1)}), bf16[16,24,128]{2,1,0:T(8,128)(2,1)S(1)}, u32[]{:S(2)}, u32[]{:S(2)}) async-start(bf16[16,24,128]{2,1,0:T(8,128)(2,1)} %attend.1._), calls=%async_computation | async-start | bytes 196608 | tf_op jit(solution)/shard_map/all_to_all | solution.py:236
  18.6 5.7 %copy-start = (bf16[8,512,2048]{2,1,0:T(8,128)(2,1)}, bf16[8,512,2048]{2,1,0:T(8,128)(2,1)S(1)}, u32[]{:S(2)}) copy-start(bf16[8,512,2048]{2,1,0:T(8,128)(2,1)S(1)} %fetch.1.weight) | copy-start | bytes 50331652
  24.3 5.8 %copy-start.1 = (bf16[8,512,2048]{2,1,0:T(8,128)(2,1)S(1)}, bf16[8,512,2048]{2,1,0:T(8,128)(2,1)}, u32[]{:S(2)}) copy-start(bf16[8,512,2048]{2,1,0:T(8,128)(2,1)} %copy-done) | copy-start | bytes 50331652
  32.2 2.7 %collective-permute-start = (bf16[4,4096]{1,0:T(4,128)(2,1)S(1)}, bf16[4,4096]{1,0:T(4,128)(2,1)S(1)}, u32[]{:S(2)}, u32[]{:S(2)}) collective-permute-start(bf16[4,4096]{1,0:T(4,128)(2,1)S(1)} %get-tuple-element.10), channel_id=1, source_target_pairs={{0,1},{1,0},{2,3},{3,2},{4,5},{5,4},{6,7},{7,6},{8,9},{9,8},{10,11... | collective-permute-start | bytes 98312 | tf_op jit(solution)/shard_map/ppermute | solution.py:191
  32.6 3.9 %collective-permute-start.1 = (bf16[4,4096]{1,0:T(4,128)(2,1)S(1)}, bf16[4,4096]{1,0:T(4,128)(2,1)S(1)}, u32[]{:S(2)}, u32[]{:S(2)}) collective-permute-start(bf16[4,4096]{1,0:T(4,128)(2,1)S(1)} %get-tuple-element.11), channel_id=1, source_target_pairs={{0,2},{1,3},{2,0},{3,1},{4,6},{5,7},{6,4},{7,5},{8,10},{9,11},{10,... | collective-permute-start | bytes 98312 | tf_op jit(solution)/shard_map/ppermute | solution.py:191
  34.2 3.4 %collective-permute-start.2 = (bf16[4,4096]{1,0:T(4,128)(2,1)S(1)}, bf16[4,4096]{1,0:T(4,128)(2,1)S(1)}, u32[]{:S(2)}, u32[]{:S(2)}) collective-permute-start(bf16[4,4096]{1,0:T(4,128)(2,1)S(1)} %get-tuple-element.12), channel_id=1, source_target_pairs={{0,3},{1,2},{2,1},{3,0},{4,7},{5,6},{6,5},{7,4},{8,11},{9,10},{10,... | collective-permute-start | bytes 98312 | tf_op jit(solution)/shard_map/ppermute | solution.py:191
  37.7 5.8 %collective-permute-start.5 = (bf16[4,4096]{1,0:T(4,128)(2,1)S(1)}, bf16[4,4096]{1,0:T(4,128)(2,1)S(1)}, u32[]{:S(2)}, u32[]{:S(2)}) collective-permute-start(bf16[4,4096]{1,0:T(4,128)(2,1)S(1)} %add_near.1.refs_0_), channel_id=1, source_target_pairs={{0,12},{1,13},{2,14},{3,15},{4,8},{5,9},{6,10},{7,11},{8,4},{9,5},... | collective-permute-start | bytes 98312 | tf_op jit(solution)/shard_map/ppermute | solution.py:191
  41.1 4.8 %collective-permute-start.4 = (bf16[4,4096]{1,0:T(4,128)(2,1)S(1)}, bf16[4,4096]{1,0:T(4,128)(2,1)S(1)}, u32[]{:S(2)}, u32[]{:S(2)}) collective-permute-start(bf16[4,4096]{1,0:T(4,128)(2,1)S(1)} %add_near.1.refs_0_), channel_id=1, source_target_pairs={{0,8},{1,9},{2,10},{3,11},{4,12},{5,13},{6,14},{7,15},{8,0},{9,1},... | collective-permute-start | bytes 98312 | tf_op jit(solution)/shard_map/ppermute | solution.py:191
  41.1 4.8 %collective-permute-start.3 = (bf16[4,4096]{1,0:T(4,128)(2,1)S(1)}, bf16[4,4096]{1,0:T(4,128)(2,1)S(1)}, u32[]{:S(2)}, u32[]{:S(2)}) collective-permute-start(bf16[4,4096]{1,0:T(4,128)(2,1)S(1)} %add_near.1.refs_0_), channel_id=1, source_target_pairs={{0,4},{1,5},{2,6},{3,7},{4,0},{5,1},{6,2},{7,3},{8,12},{9,13},{10,... | collective-permute-start | bytes 98312 | tf_op jit(solution)/shard_map/ppermute | solution.py:191
  45.9 3.4 %collective-permute-start.8 = (bf16[4,4096]{1,0:T(4,128)(2,1)S(1)}, bf16[4,4096]{1,0:T(4,128)(2,1)S(1)}, u32[]{:S(2)}, u32[]{:S(2)}) collective-permute-start(bf16[4,4096]{1,0:T(4,128)(2,1)S(1)} %add_far.1.refs_0_), channel_id=1, source_target_pairs={{0,3},{1,2},{2,1},{3,0},{4,7},{5,6},{6,5},{7,4},{8,11},{9,10},{10,... | collective-permute-start | bytes 98312 | tf_op jit(solution)/shard_map/ppermute | solution.py:191
  46.0 4.2 %collective-permute-start.7 = (bf16[4,4096]{1,0:T(4,128)(2,1)S(1)}, bf16[4,4096]{1,0:T(4,128)(2,1)S(1)}, u32[]{:S(2)}, u32[]{:S(2)}) collective-permute-start(bf16[4,4096]{1,0:T(4,128)(2,1)S(1)} %add_far.1.refs_0_), channel_id=1, source_target_pairs={{0,2},{1,3},{2,0},{3,1},{4,6},{5,7},{6,4},{7,5},{8,10},{9,11},{10,... | collective-permute-start | bytes 98312 | tf_op jit(solution)/shard_map/ppermute | solution.py:191
  46.9 3.3 %collective-permute-start.6 = (bf16[4,4096]{1,0:T(4,128)(2,1)S(1)}, bf16[4,4096]{1,0:T(4,128)(2,1)S(1)}, u32[]{:S(2)}, u32[]{:S(2)}) collective-permute-start(bf16[4,4096]{1,0:T(4,128)(2,1)S(1)} %add_far.1.refs_0_), channel_id=1, source_target_pairs={{0,1},{1,0},{2,3},{3,2},{4,5},{5,4},{6,7},{7,6},{8,9},{9,8},{10,11... | collective-permute-start | bytes 98312 | tf_op jit(solution)/shard_map/ppermute | solution.py:191

commit v5 on v4

--- a/solution.py
+++ b/solution.py
@@ -11,11 +11,12 @@
 HD = 128
 PAGE = 64
 ATTEND_VMEM = 24 * 1024 * 1024
-WEIGHT_PIECES = 8
+PROJECT_VMEM = 12 * 1024 * 1024
+WEIGHT_PIECES = 16
+FETCHED_PIECES = 6
 SMALL_VMEM = 8 * 1024 * 1024
 VMEM = pl.BlockSpec(memory_space=pltpu.VMEM)
 HBM = pl.BlockSpec(memory_space=pltpu.HBM)
-ANY = pl.BlockSpec(memory_space=pl.ANY)
 
 
 def split_two(value):
@@ -24,9 +25,23 @@
     return high, low
 
 
-def attend_kernel(heads_dev, devices, *refs):
-    table_hbm, lengths_hbm, key_scale_hbm, value_scale_hbm, queries_hbm, keys, values = refs[:7]
-    (packed, table, lengths, key_scale, value_scale, queries, key_buf, value_buf, query_rows, staged, small_sems, sems) = refs[7:]
+def piece_copies(weight, buf, sems, parts, pieces, first):
+    count, _, width = buf.shape
+    per_part = pieces // parts
+    quarter = lax.rem(lax.axis_index("kvp"), parts)
+    copies = []
+    for i in range(count):
+        x, j = divmod(first + i, per_part)
+        start = pl.multiple_of((jnp.bitwise_xor(quarter, x) * per_part + j) * width, width)
+        copies.append(pltpu.make_async_copy(weight.at[:, pl.ds(start, width)], buf.at[i], sems.at[i]))
+    return copies
+
+
+def attend_kernel(heads_dev, devices, parts, *refs):
+    table_hbm, lengths_hbm, key_scale_hbm, value_scale_hbm, queries_hbm, keys, values, weight = refs[:8]
+    packed, fetched = refs[8:10]
+    table, lengths, key_scale, value_scale, queries, key_buf, value_buf, query_rows, staged = refs[10:19]
+    small_sems, sems, weight_sems = refs[19:]
     rows, pages = table.shape
     kv_heads = key_scale.shape[0]
     heads = queries.shape[1] // HD
@@ -55,6 +70,9 @@
             here = pl.ds(i * piece, piece)
             large[-1].append(pltpu.make_async_copy(source.at[here], target.at[here], sems.at[which, i]))
             large[-1][-1].start()
+    ahead = piece_copies(weight, fetched, weight_sems, parts, WEIGHT_PIECES, WEIGHT_PIECES // parts)
+    for copy in ahead:
+        copy.start()
 
     staged[:, part_rows:, :] = jnp.zeros((devices, staged.shape[1] - part_rows, HD), jnp.float32)
     me = lax.axis_index("kvp")
@@ -123,27 +141,18 @@
             d = (k * group + start) // heads_dev
             staged[d, part_rows : part_rows + heads_dev, :] = stats[k][start : start + heads_dev]
     packed[...] = staged[...].astype(jnp.bfloat16)
-
-
-def fetch_kernel(parts, _, weight, buf, sems):
-    pieces, _, width = buf.shape
-    per_part = pieces // parts
-    quarter = lax.rem(lax.axis_index("kvp"), parts)
-    copies = []
-    for piece in range(pieces):
-        start = (jnp.bitwise_xor(quarter, piece // per_part) * per_part + piece % per_part) * width
-        source = weight.at[:, pl.ds(pl.multiple_of(start, width), width)]
-        copies.append(pltpu.make_async_copy(source, buf.at[piece], sems.at[piece]))
-        copies[-1].start()
+    for copy in ahead:
+        copy.wait()
+
+
+def project_kernel(heads_dev, packed, fetched, weight, left, *refs):
+    outs, (attended, buf, sems) = refs[:-3], refs[-3:]
+    rows = left.shape[0]
+    ready, _, width = fetched.shape
+    per_out = WEIGHT_PIECES // (len(outs) + 1)
+    copies = piece_copies(weight, buf, sems, len(outs) + 1, WEIGHT_PIECES, per_out + ready)
     for copy in copies:
-        copy.wait()
-
-
-def project_kernel(heads_dev, packed, weight, left, *refs):
-    outs, attended = refs[:-1], refs[-1]
-    rows = left.shape[0]
-    width = weight.shape[2]
-    per_out = weight.shape[0] // (len(outs) + 1)
+        copy.start()
     blocks = packed[...].astype(jnp.float32)
     stats = blocks[:, rows * heads_dev : (rows + 1) * heads_dev, :]
     for r in range(rows):
@@ -158,16 +167,23 @@
         [attended[pl.ds(j, rows, stride=heads_dev), :].astype(jnp.bfloat16) for j in range(heads_dev)], axis=1
     )
     left[...] = rounded
-    for x, out in enumerate(outs):
-        for i in range(per_out):
-            terms = jnp.dot(rounded, weight[(x + 1) * per_out + i], preferred_element_type=jnp.float32)
-            out[:, i * width : (i + 1) * width] = terms.astype(jnp.bfloat16)
-
-
-def project_own_kernel(left, weight, out):
-    width = weight.shape[2]
-    for i in range(out.shape[1] // width):
-        terms = jnp.dot(left[...], weight[i], preferred_element_type=jnp.float32)
+    for piece in range(per_out * len(outs)):
+        if piece >= ready:
+            copies[piece - ready].wait()
+        tile = fetched[piece] if piece < ready else buf[piece - ready]
+        terms = jnp.dot(rounded, tile, preferred_element_type=jnp.float32)
+        i = piece % per_out
+        outs[piece // per_out][:, i * width : (i + 1) * width] = terms.astype(jnp.bfloat16)
+
+
+def project_own_kernel(left, weight, out, buf, sems):
+    count, _, width = buf.shape
+    copies = piece_copies(weight, buf, sems, WEIGHT_PIECES // count, WEIGHT_PIECES, 0)
+    for copy in copies:
+        copy.start()
+    for i in range(count):
+        copies[i].wait()
+        terms = jnp.dot(left[...], buf[i], preferred_element_type=jnp.float32)
         out[:, i * width : (i + 1) * width] = terms.astype(jnp.bfloat16)
 
 
@@ -206,11 +222,17 @@
     inner = 4
     outer = devices // inner
     part = features // inner
-    packed = pl.pallas_call(
-        functools.partial(attend_kernel, heads_dev, devices),
-        out_shape=jax.ShapeDtypeStruct((devices, chunk, HD), jnp.bfloat16),
-        in_specs=[HBM] * 7,
-        out_specs=VMEM,
+    depth = heads_dev * HD
+    width = features // WEIGHT_PIECES
+    own_pieces = WEIGHT_PIECES // inner
+    packed, fetched = pl.pallas_call(
+        functools.partial(attend_kernel, heads_dev, devices, inner),
+        out_shape=[
+            jax.ShapeDtypeStruct((devices, chunk, HD), jnp.bfloat16),
+            pltpu.VMEM((FETCHED_PIECES, depth, width), jnp.bfloat16),
+        ],
+        in_specs=[HBM] * 8,
+        out_specs=[VMEM] * 2,
         scratch_shapes=[
             pltpu.SMEM((rows, pages), jnp.int32),
             pltpu.SMEM((rows,), jnp.int32),
@@ -223,6 +245,7 @@
             pltpu.VMEM((devices, chunk, HD), jnp.float32),
             pltpu.SemaphoreType.DMA((5,)),
             pltpu.SemaphoreType.DMA((2, 4)),
+            pltpu.SemaphoreType.DMA((FETCHED_PIECES,)),
         ],
         compiler_params=pltpu.CompilerParams(vmem_limit_bytes=ATTEND_VMEM),
         cost_estimate=pl.CostEstimate(
@@ -231,50 +254,45 @@
             transcendentals=heads * rows * pages * PAGE,
         ),
         name="attend",
-    )(*[in_hbm(a) for a in (page_table, lengths, key_scale.T, value_scale.T, queries, key_cache, value_cache)])
+    )(*[in_hbm(a) for a in (page_table, lengths, key_scale.T, value_scale.T, queries, key_cache, value_cache, out_weight)])
 
     received = lax.all_to_all(packed, "kvp", split_axis=0, concat_axis=0, tiled=True)
-
-    depth = heads_dev * HD
-    width = features // WEIGHT_PIECES
-    fetched = pl.pallas_call(
-        functools.partial(fetch_kernel, inner),
-        out_shape=pltpu.VMEM((WEIGHT_PIECES, depth, width), jnp.bfloat16),
-        in_specs=[ANY, HBM],
-        out_specs=VMEM,
-        scratch_shapes=[pltpu.SemaphoreType.DMA((WEIGHT_PIECES,))],
-        compiler_params=pltpu.CompilerParams(vmem_limit_bytes=SMALL_VMEM),
-        cost_estimate=pl.CostEstimate(flops=0, bytes_accessed=2 * out_weight.size, transcendentals=0),
-        name="fetch",
-    )(packed, in_hbm(out_weight))
 
     left, *others = pl.pallas_call(
         functools.partial(project_kernel, heads_dev),
         out_shape=[jax.ShapeDtypeStruct((rows, depth), jnp.bfloat16)]
         + [jax.ShapeDtypeStruct((rows, part), jnp.bfloat16)] * (inner - 1),
-        in_specs=[VMEM, VMEM],
+        in_specs=[VMEM, VMEM, HBM],
         out_specs=[VMEM] * inner,
-        scratch_shapes=[pltpu.VMEM((rows * heads_dev, HD), jnp.float32)],
-        compiler_params=pltpu.CompilerParams(vmem_limit_bytes=SMALL_VMEM),
+        scratch_shapes=[
+            pltpu.VMEM((rows * heads_dev, HD), jnp.float32),
+            pltpu.VMEM((WEIGHT_PIECES - own_pieces - FETCHED_PIECES, depth, width), jnp.bfloat16),
+            pltpu.SemaphoreType.DMA((WEIGHT_PIECES - own_pieces - FETCHED_PIECES,)),
+        ],
+        compiler_params=pltpu.CompilerParams(vmem_limit_bytes=PROJECT_VMEM),
         cost_estimate=pl.CostEstimate(
             flops=2 * rows * depth * part * (inner - 1),
             bytes_accessed=2 * depth * part * (inner - 1),
             transcendentals=0,
         ),
         name="project_others",
-    )(received, fetched)
+    )(received, fetched, in_hbm(out_weight))
     sent = [exchange(others[x - 1], x, devices) for x in range(1, inner)]
     own = pl.pallas_call(
         project_own_kernel,
         out_shape=jax.ShapeDtypeStruct((rows, part), jnp.bfloat16),
-        in_specs=[VMEM, VMEM],
+        in_specs=[VMEM, HBM],
         out_specs=VMEM,
-        compiler_params=pltpu.CompilerParams(vmem_limit_bytes=SMALL_VMEM),
+        scratch_shapes=[
+            pltpu.VMEM((own_pieces, depth, width), jnp.bfloat16),
+            pltpu.SemaphoreType.DMA((own_pieces,)),
+        ],
+        compiler_params=pltpu.CompilerParams(vmem_limit_bytes=PROJECT_VMEM),
         cost_estimate=pl.CostEstimate(
             flops=2 * rows * depth * part, bytes_accessed=2 * depth * part, transcendentals=0
         ),
         name="project_own",
-    )(left, fetched)
+    )(left, in_hbm(out_weight))
 
     def add(terms, name):
         return pl.pallas_call(

time: 51.1 us -> 41.3 us (0.81)
  blocking collectives: 0 us -> 14.6 us
  local copies, waits for them, and re-layouts: 11.5 us -> 0 us
  starting transfers between devices: 15.9 us -> 8.3 us
  waiting for transfers between devices: 8.85 us -> 4.57 us
  Pallas kernels: 14.6 us -> 13.6 us
    all_to_all x0 -> x1, blocking collectives: none -> 14.6 us  [body(): lax.all_to_all(packed, 'kvp', split_axis=0, concat_axis=0, tiled=True)]
    unnamed x4 -> x0, local copies, waits for them, and re-layouts: 11.5 us -> none
    all_to_all x1 -> x0, starting transfers between devices: 7.4 us -> none  [body(): lax.all_to_all(packed, 'kvp', split_axis=0, concat_axis=0, tiled=True)]
    pallas_call x2 -> x1, Pallas kernels: 11.2 us -> 6.13 us  [body(): pl.pallas_call(functools.partial(attend_kernel, heads_dev, devices, inner...]
    ppermute x9, waiting for transfers between devices: 8.85 us -> 4.57 us  [exchange(): lax.ppermute(array, 'kvp', [(i, i ^ partner) for i in range(devices)])]
    pallas_call x1, Pallas kernels: 2.07 us -> 4.25 us  [body(): pl.pallas_call(functools.partial(project_kernel, heads_dev), out_shape=[j...]
    pallas_call x1, Pallas kernels: 0.65 us -> 2.47 us  [body(): pl.pallas_call(project_own_kernel, out_shape=jax.ShapeDtypeStruct((rows,...]
  transfers between devices with their start and end apart: 10 -> 9, of which waited for: 6 -> 5; matrix products, arithmetic and copies ran while one was open for 0% -> 0% of each run, Pallas kernels for 13% -> 6%
where the time goes in v5:
time: 41.3 us; the launch traced here: 41.1 us
  blocking collectives  14.6 us (35%)
  Pallas kernels  13.6 us (33%)
  starting transfers between devices  8.3 us (20%)
  waiting for transfers between devices  4.57 us (11%)
    all_to_all x1, blocking collectives, body(): lax.all_to_all(packed, 'kvp', split_axis=0, concat_axis=0, tiled=True)  14.6 us
    ppermute x9, starting transfers between devices, exchange(): lax.ppermute(array, 'kvp', [(i, i ^ partner) for i in range(devices)])  8.3 us
    pallas_call x1, Pallas kernels, body(): pl.pallas_call(functools.partial(attend_kernel, heads_dev, devices, inner...  6.13 us
    ppermute x9, waiting for transfers between devices, exchange(): lax.ppermute(array, 'kvp', [(i, i ^ partner) for i in range(devices)])  4.57 us
    pallas_call x1, Pallas kernels, body(): pl.pallas_call(functools.partial(project_kernel, heads_dev), out_shape=[j...  4.25 us
    pallas_call x1, Pallas kernels, body(): pl.pallas_call(project_own_kernel, out_shape=jax.ShapeDtypeStruct((rows,...  2.47 us
  transfers between devices with their start and end apart: 9, of which 5 were waited for; matrix products, arithmetic and copies ran while one was open for 0% of the time, Pallas kernels for 6%

profile of v5, /device:TPU:0, one launch (start us, length us, event | category | flops | bytes accessed | tf_op | source)
XLA Modules:
  0.0 41.1 jit_solution(6443214109983083222)
XLA Ops:
  0.0 6.1 %attend.1 = (bf16[16,24,128]{2,1,0:T(8,128)(2,1)S(1)}, bf16[6,512,1024]{2,1,0:T(8,128)(2,1)S(1)}) custom-call(s32[4,12]{1,0:T(4,128)} %refs_0_.1, s32[4]{0:T(128)} %refs_1_.1, f32[4,48]{1,0:T(4,128)} %bitcast.2, f32[4,48]{1,0:T(4,128)} %bitcast.3, bf16[4,8192]{1,0:T(4,128)(2,1)} %refs_4_.1, bf16[48,64,512]{2,1,0:T(8,128)(2,1)} %refs_5_.1, ...), custom_call_target="tpu_custom_call" | custom-call | flops 100663296 | bytes 6291456 | tf_op jit(solution)/shard_map/attend/pallas_call | solution.py:228
  6.1 14.6 %all_to_all.5.packed = bf16[16,24,128]{2,1,0:T(8,128)(2,1)S(1)} all-to-all(bf16[16,24,128]{2,1,0:T(8,128)(2,1)S(1)} %get-tuple-element.11), channel_id=1, replica_groups=mesh['group'=2,'kvp'=16] {'kvp'}, dimensions={0} | all-to-all | bytes 196608 | tf_op jit(solution)/shard_map/all_to_all | solution.py:259
  20.7 4.3 %project_others.1 = (bf16[4,512]{1,0:T(4,128)(2,1)S(1)}, bf16[4,4096]{1,0:T(4,128)(2,1)S(1)}, bf16[4,4096]{1,0:T(4,128)(2,1)S(1)}, bf16[4,4096]{1,0:T(4,128)(2,1)S(1)}) custom-call(bf16[16,24,128]{2,1,0:T(8,128)(2,1)S(1)} %all_to_all.5.packed, bf16[6,512,1024]{2,1,0:T(8,128)(2,1)S(1)} %get-tuple-element.12.fetched, bf16[512,16384]{1,0:T(8,128)(2,1)} %weight.3), custom_call_target="tpu_custom_call" | custom-call | flops 50331648 | bytes 12582912 | tf_op jit(solution)/shard_map/project_others/pallas_call | solution.py:261
  25.0 0.1 collective-permute-start
  25.1 0.1 collective-permute-start.1
  25.2 1.8 %collective-permute-start.2 = (bf16[4,4096]{1,0:T(4,128)(2,1)S(1)}, bf16[4,4096]{1,0:T(4,128)(2,1)S(1)}, u32[]{:S(2)}, u32[]{:S(2)}) collective-permute-start(bf16[4,4096]{1,0:T(4,128)(2,1)S(1)} %get-tuple-element.16), channel_id=1, source_target_pairs={{0,3},{1,2},{2,1},{3,0},{4,7},{5,6},{6,5},{7,4},{8,11},{9,10},{10,... | collective-permute-start | bytes 98312 | tf_op jit(solution)/shard_map/ppermute | solution.py:207
  26.9 2.5 %project_own.1.refs_0_ = bf16[4,4096]{1,0:T(4,128)(2,1)S(1)} custom-call(bf16[4,512]{1,0:T(4,128)(2,1)S(1)} %get-tuple-element.13.left, bf16[512,16384]{1,0:T(8,128)(2,1)} %weight.3), custom_call_target="tpu_custom_call" | custom-call | flops 16777216 | bytes 4194304 | tf_op jit(solution)/shard_map/project_own/pallas_call | solution.py:281
  29.4 0.0 collective-permute-done.refs_1_
  29.4 0.0 collective-permute-done.1.refs_2_
  29.4 0.0 collective-permute-done.2.refs_3_
  29.5 0.9 %collective-permute-start.5 = (bf16[4,4096]{1,0:T(4,128)(2,1)S(1)}, bf16[4,4096]{1,0:T(4,128)(2,1)S(1)}, u32[]{:S(2)}, u32[]{:S(2)}) collective-permute-start(bf16[4,4096]{1,0:T(4,128)(2,1)S(1)} %add_near.1.refs_0_), channel_id=1, source_target_pairs={{0,12},{1,13},{2,14},{3,15},{4,8},{5,9},{6,10},{7,11},{8,4},{9,5},... | collective-permute-start | bytes 98312 | tf_op jit(solution)/shard_map/ppermute | solution.py:207
  30.4 0.8 %collective-permute-start.4 = (bf16[4,4096]{1,0:T(4,128)(2,1)S(1)}, bf16[4,4096]{1,0:T(4,128)(2,1)S(1)}, u32[]{:S(2)}, u32[]{:S(2)}) collective-permute-start(bf16[4,4096]{1,0:T(4,128)(2,1)S(1)} %add_near.1.refs_0_), channel_id=1, source_target_pairs={{0,8},{1,9},{2,10},{3,11},{4,12},{5,13},{6,14},{7,15},{8,0},{9,1},... | collective-permute-start | bytes 98312 | tf_op jit(solution)/shard_map/ppermute | solution.py:207
  31.1 2.8 %collective-permute-start.3 = (bf16[4,4096]{1,0:T(4,128)(2,1)S(1)}, bf16[4,4096]{1,0:T(4,128)(2,1)S(1)}, u32[]{:S(2)}, u32[]{:S(2)}) collective-permute-start(bf16[4,4096]{1,0:T(4,128)(2,1)S(1)} %add_near.1.refs_0_), channel_id=1, source_target_pairs={{0,4},{1,5},{2,6},{3,7},{4,0},{5,1},{6,2},{7,3},{8,12},{9,13},{10,... | collective-permute-start | bytes 98312 | tf_op jit(solution)/shard_map/ppermute | solution.py:207
  33.9 1.6 %collective-permute-done.5.refs_3_ = bf16[4,4096]{1,0:T(4,128)(2,1)S(1)} collective-permute-done((bf16[4,4096]{1,0:T(4,128)(2,1)S(1)}, bf16[4,4096]{1,0:T(4,128)(2,1)S(1)}, u32[]{:S(2)}, u32[]{:S(2)}) %collective-permute-start.5) | collective-permute-done | bytes 32800 | tf_op jit(solution)/shard_map/ppermute | solution.py:207
  35.6 0.3 collective-permute-done.4.refs_2_
  35.8 0.2 collective-permute-done.3.refs_1_
  36.1 0.1 collective-permute-start.8
  36.2 1.0 %collective-permute-start.7 = (bf16[4,4096]{1,0:T(4,128)(2,1)S(1)}, bf16[4,4096]{1,0:T(4,128)(2,1)S(1)}, u32[]{:S(2)}, u32[]{:S(2)}) collective-permute-start(bf16[4,4096]{1,0:T(4,128)(2,1)S(1)} %add_far.1.refs_0_), channel_id=1, source_target_pairs={{0,2},{1,3},{2,0},{3,1},{4,6},{5,7},{6,4},{7,5},{8,10},{9,11},{10,... | collective-permute-start | bytes 98312 | tf_op jit(solution)/shard_map/ppermute | solution.py:207
  37.1 0.9 %collective-permute-start.6 = (bf16[4,4096]{1,0:T(4,128)(2,1)S(1)}, bf16[4,4096]{1,0:T(4,128)(2,1)S(1)}, u32[]{:S(2)}, u32[]{:S(2)}) collective-permute-start(bf16[4,4096]{1,0:T(4,128)(2,1)S(1)} %add_far.1.refs_0_), channel_id=1, source_target_pairs={{0,1},{1,0},{2,3},{3,2},{4,5},{5,4},{6,7},{7,6},{8,9},{9,8},{10,11... | collective-permute-start | bytes 98312 | tf_op jit(solution)/shard_map/ppermute | solution.py:207
  38.0 1.5 %collective-permute-done.8.refs_3_ = bf16[4,4096]{1,0:T(4,128)(2,1)S(1)} collective-permute-done((bf16[4,4096]{1,0:T(4,128)(2,1)S(1)}, bf16[4,4096]{1,0:T(4,128)(2,1)S(1)}, u32[]{:S(2)}, u32[]{:S(2)}) %collective-permute-start.8) | collective-permute-done | bytes 32800 | tf_op jit(solution)/shard_map/ppermute | solution.py:207
  39.5 1.0 %collective-permute-done.7.refs_2_ = bf16[4,4096]{1,0:T(4,128)(2,1)S(1)} collective-permute-done((bf16[4,4096]{1,0:T(4,128)(2,1)S(1)}, bf16[4,4096]{1,0:T(4,128)(2,1)S(1)}, u32[]{:S(2)}, u32[]{:S(2)}) %collective-permute-start.7) | collective-permute-done | bytes 32800 | tf_op jit(solution)/shard_map/ppermute | solution.py:207
  40.5 0.0 collective-permute-done.6.refs_1_
  40.5 0.7 %lay.1 = bf16[4,16384]{1,0:T(4,128)(2,1)} custom-call(bf16[4,4096]{1,0:T(4,128)(2,1)S(1)} %add_far.1.refs_0_, bf16[4,4096]{1,0:T(4,128)(2,1)S(1)} %collective-permute-done.6.refs_1_, bf16[4,4096]{1,0:T(4,128)(2,1)S(1)} %collective-permute-done.7.refs_2_, bf16[4,4096]{1,0:T(4,128)(2,1)S(1)} %collective-permute-done.8.refs_3_), custom_call_target="tpu_custom_call" | custom-call | tf_op jit(solution)/shard_map/lay/pallas_call | solution.py:310
  (2 shorter events, 0.1 us)
Async XLA Ops:
  25.0 4.4 %collective-permute-start = (bf16[4,4096]{1,0:T(4,128)(2,1)S(1)}, bf16[4,4096]{1,0:T(4,128)(2,1)S(1)}, u32[]{:S(2)}, u32[]{:S(2)}) collective-permute-start(bf16[4,4096]{1,0:T(4,128)(2,1)S(1)} %get-tuple-element.14), channel_id=1, source_target_pairs={{0,1},{1,0},{2,3},{3,2},{4,5},{5,4},{6,7},{7,6},{8,9},{9,8},{10,11... | collective-permute-start | bytes 98312 | tf_op jit(solution)/shard_map/ppermute | solution.py:207
  25.1 4.4 %collective-permute-start.1 = (bf16[4,4096]{1,0:T(4,128)(2,1)S(1)}, bf16[4,4096]{1,0:T(4,128)(2,1)S(1)}, u32[]{:S(2)}, u32[]{:S(2)}) collective-permute-start(bf16[4,4096]{1,0:T(4,128)(2,1)S(1)} %get-tuple-element.15), channel_id=1, source_target_pairs={{0,2},{1,3},{2,0},{3,1},{4,6},{5,7},{6,4},{7,5},{8,10},{9,11},{10,... | collective-permute-start | bytes 98312 | tf_op jit(solution)/shard_map/ppermute | solution.py:207
  25.2 4.3 %collective-permute-start.2 = (bf16[4,4096]{1,0:T(4,128)(2,1)S(1)}, bf16[4,4096]{1,0:T(4,128)(2,1)S(1)}, u32[]{:S(2)}, u32[]{:S(2)}) collective-permute-start(bf16[4,4096]{1,0:T(4,128)(2,1)S(1)} %get-tuple-element.16), channel_id=1, source_target_pairs={{0,3},{1,2},{2,1},{3,0},{4,7},{5,6},{6,5},{7,4},{8,11},{9,10},{10,... | collective-permute-start | bytes 98312 | tf_op jit(solution)/shard_map/ppermute | solution.py:207
  29.5 6.1 %collective-permute-start.5 = (bf16[4,4096]{1,0:T(4,128)(2,1)S(1)}, bf16[4,4096]{1,0:T(4,128)(2,1)S(1)}, u32[]{:S(2)}, u32[]{:S(2)}) collective-permute-start(bf16[4,4096]{1,0:T(4,128)(2,1)S(1)} %add_near.1.refs_0_), channel_id=1, source_target_pairs={{0,12},{1,13},{2,14},{3,15},{4,8},{5,9},{6,10},{7,11},{8,4},{9,5},... | collective-permute-start | bytes 98312 | tf_op jit(solution)/shard_map/ppermute | solution.py:207
  30.4 5.5 %collective-permute-start.4 = (bf16[4,4096]{1,0:T(4,128)(2,1)S(1)}, bf16[4,4096]{1,0:T(4,128)(2,1)S(1)}, u32[]{:S(2)}, u32[]{:S(2)}) collective-permute-start(bf16[4,4096]{1,0:T(4,128)(2,1)S(1)} %add_near.1.refs_0_), channel_id=1, source_target_pairs={{0,8},{1,9},{2,10},{3,11},{4,12},{5,13},{6,14},{7,15},{8,0},{9,1},... | collective-permute-start | bytes 98312 | tf_op jit(solution)/shard_map/ppermute | solution.py:207
  31.1 4.9 %collective-permute-start.3 = (bf16[4,4096]{1,0:T(4,128)(2,1)S(1)}, bf16[4,4096]{1,0:T(4,128)(2,1)S(1)}, u32[]{:S(2)}, u32[]{:S(2)}) collective-permute-start(bf16[4,4096]{1,0:T(4,128)(2,1)S(1)} %add_near.1.refs_0_), channel_id=1, source_target_pairs={{0,4},{1,5},{2,6},{3,7},{4,0},{5,1},{6,2},{7,3},{8,12},{9,13},{10,... | collective-permute-start | bytes 98312 | tf_op jit(solution)/shard_map/ppermute | solution.py:207
  36.1 3.4 %collective-permute-start.8 = (bf16[4,4096]{1,0:T(4,128)(2,1)S(1)}, bf16[4,4096]{1,0:T(4,128)(2,1)S(1)}, u32[]{:S(2)}, u32[]{:S(2)}) collective-permute-start(bf16[4,4096]{1,0:T(4,128)(2,1)S(1)} %add_far.1.refs_0_), channel_id=1, source_target_pairs={{0,3},{1,2},{2,1},{3,0},{4,7},{5,6},{6,5},{7,4},{8,11},{9,10},{10,... | collective-permute-start | bytes 98312 | tf_op jit(solution)/shard_map/ppermute | solution.py:207
  36.2 4.3 %collective-permute-start.7 = (bf16[4,4096]{1,0:T(4,128)(2,1)S(1)}, bf16[4,4096]{1,0:T(4,128)(2,1)S(1)}, u32[]{:S(2)}, u32[]{:S(2)}) collective-permute-start(bf16[4,4096]{1,0:T(4,128)(2,1)S(1)} %add_far.1.refs_0_), channel_id=1, source_target_pairs={{0,2},{1,3},{2,0},{3,1},{4,6},{5,7},{6,4},{7,5},{8,10},{9,11},{10,... | collective-permute-start | bytes 98312 | tf_op jit(solution)/shard_map/ppermute | solution.py:207
  37.1 3.3 %collective-permute-start.6 = (bf16[4,4096]{1,0:T(4,128)(2,1)S(1)}, bf16[4,4096]{1,0:T(4,128)(2,1)S(1)}, u32[]{:S(2)}, u32[]{:S(2)}) collective-permute-start(bf16[4,4096]{1,0:T(4,128)(2,1)S(1)} %add_far.1.refs_0_), channel_id=1, source_target_pairs={{0,1},{1,0},{2,3},{3,2},{4,5},{5,4},{6,7},{7,6},{8,9},{9,8},{10,11... | collective-permute-start | bytes 98312 | tf_op jit(solution)/shard_map/ppermute | solution.py:207

commit v6 on v5

--- a/solution.py
+++ b/solution.py
@@ -13,7 +13,8 @@
 ATTEND_VMEM = 24 * 1024 * 1024
 PROJECT_VMEM = 12 * 1024 * 1024
 WEIGHT_PIECES = 16
-FETCHED_PIECES = 6
+FETCHED_PIECES = 5
+IN_FLIGHT = 3
 SMALL_VMEM = 8 * 1024 * 1024
 VMEM = pl.BlockSpec(memory_space=pltpu.VMEM)
 HBM = pl.BlockSpec(memory_space=pltpu.HBM)
@@ -37,6 +38,12 @@
     return copies
 
 
+def take(copies, i):
+    copies[i].wait()
+    if i + IN_FLIGHT < len(copies):
+        copies[i + IN_FLIGHT].start()
+
+
 def attend_kernel(heads_dev, devices, parts, *refs):
     table_hbm, lengths_hbm, key_scale_hbm, value_scale_hbm, queries_hbm, keys, values, weight = refs[:8]
     packed, fetched = refs[8:10]
@@ -46,7 +53,6 @@
     kv_heads = key_scale.shape[0]
     heads = queries.shape[1] // HD
     group = heads // kv_heads
-    part_rows = rows * heads_dev
     context = pages * PAGE
     pieces = sems.shape[1]
     piece = keys.shape[0] // pieces
@@ -69,12 +75,10 @@
         for i in range(pieces):
             here = pl.ds(i * piece, piece)
             large[-1].append(pltpu.make_async_copy(source.at[here], target.at[here], sems.at[which, i]))
-            large[-1][-1].start()
+    for copy in large[0]:
+        copy.start()
     ahead = piece_copies(weight, fetched, weight_sems, parts, WEIGHT_PIECES, WEIGHT_PIECES // parts)
-    for copy in ahead:
-        copy.start()
-
-    staged[:, part_rows:, :] = jnp.zeros((devices, staged.shape[1] - part_rows, HD), jnp.float32)
+
     me = lax.axis_index("kvp")
     place = me * context + lax.broadcasted_iota(jnp.int32, (group, context), 1)
     lane = lax.broadcasted_iota(jnp.int32, (group, HD), 1)
@@ -83,8 +87,12 @@
         copy.wait()
     for h in range(heads):
         query_rows[h * rows : (h + 1) * rows, :] = queries[:, h * HD : (h + 1) * HD].astype(jnp.float32)
+    for copy in large[1]:
+        copy.start()
     for copy in large[0]:
         copy.wait()
+    for copy in ahead:
+        copy.start()
 
     def factors(scales, r, k, times):
         columns = []
@@ -135,11 +143,11 @@
                 partial = both[i * group : (i + 1) * group, i * HD : (i + 1) * HD]
                 for start in range(0, group, heads_dev):
                     d = ((k + i) * group + start) // heads_dev
-                    staged[d, r * heads_dev : (r + 1) * heads_dev, :] = partial[start : start + heads_dev]
+                    staged[d, r] = partial[start : start + heads_dev]
     for k in range(kv_heads):
         for start in range(0, group, heads_dev):
             d = (k * group + start) // heads_dev
-            staged[d, part_rows : part_rows + heads_dev, :] = stats[k][start : start + heads_dev]
+            staged[d, rows] = stats[k][start : start + heads_dev]
     packed[...] = staged[...].astype(jnp.bfloat16)
     for copy in ahead:
         copy.wait()
@@ -151,12 +159,12 @@
     ready, _, width = fetched.shape
     per_out = WEIGHT_PIECES // (len(outs) + 1)
     copies = piece_copies(weight, buf, sems, len(outs) + 1, WEIGHT_PIECES, per_out + ready)
-    for copy in copies:
+    for copy in copies[:IN_FLIGHT]:
         copy.start()
     blocks = packed[...].astype(jnp.float32)
-    stats = blocks[:, rows * heads_dev : (rows + 1) * heads_dev, :]
+    stats = blocks[:, rows]
     for r in range(rows):
-        partial = blocks[:, r * heads_dev : (r + 1) * heads_dev, :]
+        partial = blocks[:, r]
         maxima = stats[:, :, 4 * r : 4 * r + 1] + stats[:, :, 4 * r + 1 : 4 * r + 2]
         totals = stats[:, :, 4 * r + 2 : 4 * r + 3] + stats[:, :, 4 * r + 3 : 4 * r + 4]
         rescale = jnp.exp(maxima - jnp.max(maxima, axis=0, keepdims=True))
@@ -169,7 +177,7 @@
     left[...] = rounded
     for piece in range(per_out * len(outs)):
         if piece >= ready:
-            copies[piece - ready].wait()
+            take(copies, piece - ready)
         tile = fetched[piece] if piece < ready else buf[piece - ready]
         terms = jnp.dot(rounded, tile, preferred_element_type=jnp.float32)
         i = piece % per_out
@@ -179,10 +187,10 @@
 def project_own_kernel(left, weight, out, buf, sems):
     count, _, width = buf.shape
     copies = piece_copies(weight, buf, sems, WEIGHT_PIECES // count, WEIGHT_PIECES, 0)
-    for copy in copies:
+    for copy in copies[:IN_FLIGHT]:
         copy.start()
     for i in range(count):
-        copies[i].wait()
+        take(copies, i)
         terms = jnp.dot(left[...], buf[i], preferred_element_type=jnp.float32)
         out[:, i * width : (i + 1) * width] = terms.astype(jnp.bfloat16)
 
@@ -218,7 +226,6 @@
     heads_dev = out_weight.shape[0] // HD
     heads = queries.shape[1] // HD
     features = out_weight.shape[1]
-    chunk = -(-(rows + 1) * heads_dev // 8) * 8
     inner = 4
     outer = devices // inner
     part = features // inner
@@ -228,7 +235,7 @@
     packed, fetched = pl.pallas_call(
         functools.partial(attend_kernel, heads_dev, devices, inner),
         out_shape=[
-            jax.ShapeDtypeStruct((devices, chunk, HD), jnp.bfloat16),
+            jax.ShapeDtypeStruct((devices, rows + 1, heads_dev, HD), jnp.bfloat16),
             pltpu.VMEM((FETCHED_PIECES, depth, width), jnp.bfloat16),
         ],
         in_specs=[HBM] * 8,
@@ -242,7 +249,7 @@
             pltpu.VMEM((slots, PAGE, columns), jnp.bfloat16),
             pltpu.VMEM((slots, PAGE, columns), jnp.bfloat16),
             pltpu.VMEM((heads * rows, HD), jnp.float32),
-            pltpu.VMEM((devices, chunk, HD), jnp.float32),
+            pltpu.VMEM((devices, rows + 1, heads_dev, HD), jnp.float32),
             pltpu.SemaphoreType.DMA((5,)),
             pltpu.SemaphoreType.DMA((2, 4)),
             pltpu.SemaphoreType.DMA((FETCHED_PIECES,)),

time: 41.3 us -> 41.8 us (1.012)
  Pallas kernels: 13.6 us -> 14.6 us
    pallas_call x1, Pallas kernels: 4.25 us -> 5.28 us  [body(): pl.pallas_call(functools.partial(project_kernel, heads_dev), out_shape=[j...]
    pallas_call x1, Pallas kernels: 2.47 us -> 2.89 us  [body(): pl.pallas_call(project_own_kernel, out_shape=jax.ShapeDtypeStruct((rows,...]
  transfers between devices with their start and end apart: 9 -> 9, of which waited for: 5 -> 5; matrix products, arithmetic and copies ran while one was open for 0% -> 0% of each run, Pallas kernels for 6% -> 7%
where the time goes in v6:
time: 41.8 us; the launch traced here: 41.6 us
  Pallas kernels  14.6 us (35%)
  blocking collectives  14.3 us (34%)
  starting transfers between devices  8.3 us (20%)
  waiting for transfers between devices  4.29 us (10%)
    all_to_all x1, blocking collectives, body(): lax.all_to_all(packed, 'kvp', split_axis=0, concat_axis=0, tiled=True)  14.3 us
    ppermute x9, starting transfers between devices, exchange(): lax.ppermute(array, 'kvp', [(i, i ^ partner) for i in range(devices)])  8.3 us
    pallas_call x1, Pallas kernels, body(): pl.pallas_call(functools.partial(attend_kernel, heads_dev, devices, inner...  5.72 us
    pallas_call x1, Pallas kernels, body(): pl.pallas_call(functools.partial(project_kernel, heads_dev), out_shape=[j...  5.28 us
    ppermute x9, waiting for transfers between devices, exchange(): lax.ppermute(array, 'kvp', [(i, i ^ partner) for i in range(devices)])  4.29 us
    pallas_call x1, Pallas kernels, body(): pl.pallas_call(project_own_kernel, out_shape=jax.ShapeDtypeStruct((rows,...  2.89 us
  transfers between devices with their start and end apart: 9, of which 5 were waited for; matrix products, arithmetic and copies ran while one was open for 0% of the time, Pallas kernels for 7%

profile of v6, /device:TPU:0, one launch (start us, length us, event | category | flops | bytes accessed | tf_op | source)
XLA Modules:
  0.0 41.6 jit_solution(10763818619875561474)
XLA Ops:
  0.0 5.7 %attend.1 = (bf16[16,5,4,128]{3,2,1,0:T(4,128)(2,1)S(1)}, bf16[5,512,1024]{2,1,0:T(8,128)(2,1)S(1)}) custom-call(s32[4,12]{1,0:T(4,128)} %refs_0_.1, s32[4]{0:T(128)} %refs_1_.1, f32[4,48]{1,0:T(4,128)} %bitcast.2, f32[4,48]{1,0:T(4,128)} %bitcast.3, bf16[4,8192]{1,0:T(4,128)(2,1)} %refs_4_.1, bf16[48,64,512]{2,1,0:T(8,128)(2,1)} %refs_5_.1, ...), custom_call_target="tpu_custom_call" | custom-call | flops 100663296 | bytes 6291456 | tf_op jit(solution)/shard_map/attend/pallas_call | solution.py:235
  5.7 14.3 %all_to_all.5.packed = bf16[16,5,4,128]{3,2,1,0:T(4,128)(2,1)S(1)} all-to-all(bf16[16,5,4,128]{3,2,1,0:T(4,128)(2,1)S(1)} %get-tuple-element.11), channel_id=1, replica_groups=mesh['group'=2,'kvp'=16] {'kvp'}, dimensions={0} | all-to-all | bytes 163840 | tf_op jit(solution)/shard_map/all_to_all | solution.py:266
  20.1 5.3 %project_others.1 = (bf16[4,512]{1,0:T(4,128)(2,1)S(1)}, bf16[4,4096]{1,0:T(4,128)(2,1)S(1)}, bf16[4,4096]{1,0:T(4,128)(2,1)S(1)}, bf16[4,4096]{1,0:T(4,128)(2,1)S(1)}) custom-call(bf16[16,5,4,128]{3,2,1,0:T(4,128)(2,1)S(1)} %all_to_all.5.packed, bf16[5,512,1024]{2,1,0:T(8,128)(2,1)S(1)} %get-tuple-element.12.fetched, bf16[512,16384]{1,0:T(8,128)(2,1)} %weight.3), custom_call_target="tpu_custom_call" | custom-call | flops 50331648 | bytes 12582912 | tf_op jit(solution)/shard_map/project_others/pallas_call | solution.py:268
  25.4 0.1 collective-permute-start
  25.4 0.2 collective-permute-start.1
  25.6 1.7 %collective-permute-start.2 = (bf16[4,4096]{1,0:T(4,128)(2,1)S(1)}, bf16[4,4096]{1,0:T(4,128)(2,1)S(1)}, u32[]{:S(2)}, u32[]{:S(2)}) collective-permute-start(bf16[4,4096]{1,0:T(4,128)(2,1)S(1)} %get-tuple-element.16), channel_id=1, source_target_pairs={{0,3},{1,2},{2,1},{3,0},{4,7},{5,6},{6,5},{7,4},{8,11},{9,10},{10,... | collective-permute-start | bytes 98312 | tf_op jit(solution)/shard_map/ppermute | solution.py:215
  27.3 2.9 %project_own.1.refs_0_ = bf16[4,4096]{1,0:T(4,128)(2,1)S(1)} custom-call(bf16[4,512]{1,0:T(4,128)(2,1)S(1)} %get-tuple-element.13.left, bf16[512,16384]{1,0:T(8,128)(2,1)} %weight.3), custom_call_target="tpu_custom_call" | custom-call | flops 16777216 | bytes 4194304 | tf_op jit(solution)/shard_map/project_own/pallas_call | solution.py:288
  30.2 0.0 collective-permute-done.refs_1_
  30.2 0.0 collective-permute-done.1.refs_2_
  30.2 0.0 collective-permute-done.2.refs_3_
  30.3 0.7 %collective-permute-start.5 = (bf16[4,4096]{1,0:T(4,128)(2,1)S(1)}, bf16[4,4096]{1,0:T(4,128)(2,1)S(1)}, u32[]{:S(2)}, u32[]{:S(2)}) collective-permute-start(bf16[4,4096]{1,0:T(4,128)(2,1)S(1)} %add_near.1.refs_0_), channel_id=1, source_target_pairs={{0,12},{1,13},{2,14},{3,15},{4,8},{5,9},{6,10},{7,11},{8,4},{9,5},... | collective-permute-start | bytes 98312 | tf_op jit(solution)/shard_map/ppermute | solution.py:215
  30.9 0.8 %collective-permute-start.4 = (bf16[4,4096]{1,0:T(4,128)(2,1)S(1)}, bf16[4,4096]{1,0:T(4,128)(2,1)S(1)}, u32[]{:S(2)}, u32[]{:S(2)}) collective-permute-start(bf16[4,4096]{1,0:T(4,128)(2,1)S(1)} %add_near.1.refs_0_), channel_id=1, source_target_pairs={{0,8},{1,9},{2,10},{3,11},{4,12},{5,13},{6,14},{7,15},{8,0},{9,1},... | collective-permute-start | bytes 98312 | tf_op jit(solution)/shard_map/ppermute | solution.py:215
  31.7 3.0 %collective-permute-start.3 = (bf16[4,4096]{1,0:T(4,128)(2,1)S(1)}, bf16[4,4096]{1,0:T(4,128)(2,1)S(1)}, u32[]{:S(2)}, u32[]{:S(2)}) collective-permute-start(bf16[4,4096]{1,0:T(4,128)(2,1)S(1)} %add_near.1.refs_0_), channel_id=1, source_target_pairs={{0,4},{1,5},{2,6},{3,7},{4,0},{5,1},{6,2},{7,3},{8,12},{9,13},{10,... | collective-permute-start | bytes 98312 | tf_op jit(solution)/shard_map/ppermute | solution.py:215
  34.7 1.6 %collective-permute-done.5.refs_3_ = bf16[4,4096]{1,0:T(4,128)(2,1)S(1)} collective-permute-done((bf16[4,4096]{1,0:T(4,128)(2,1)S(1)}, bf16[4,4096]{1,0:T(4,128)(2,1)S(1)}, u32[]{:S(2)}, u32[]{:S(2)}) %collective-permute-start.5) | collective-permute-done | bytes 32800 | tf_op jit(solution)/shard_map/ppermute | solution.py:215
  36.3 0.3 collective-permute-done.4.refs_2_
  36.6 0.2 collective-permute-done.3.refs_1_
  36.9 0.1 collective-permute-start.8
  36.9 0.9 %collective-permute-start.7 = (bf16[4,4096]{1,0:T(4,128)(2,1)S(1)}, bf16[4,4096]{1,0:T(4,128)(2,1)S(1)}, u32[]{:S(2)}, u32[]{:S(2)}) collective-permute-start(bf16[4,4096]{1,0:T(4,128)(2,1)S(1)} %add_far.1.refs_0_), channel_id=1, source_target_pairs={{0,2},{1,3},{2,0},{3,1},{4,6},{5,7},{6,4},{7,5},{8,10},{9,11},{10,... | collective-permute-start | bytes 98312 | tf_op jit(solution)/shard_map/ppermute | solution.py:215
  37.8 1.0 %collective-permute-start.6 = (bf16[4,4096]{1,0:T(4,128)(2,1)S(1)}, bf16[4,4096]{1,0:T(4,128)(2,1)S(1)}, u32[]{:S(2)}, u32[]{:S(2)}) collective-permute-start(bf16[4,4096]{1,0:T(4,128)(2,1)S(1)} %add_far.1.refs_0_), channel_id=1, source_target_pairs={{0,1},{1,0},{2,3},{3,2},{4,5},{5,4},{6,7},{7,6},{8,9},{9,8},{10,11... | collective-permute-start | bytes 98312 | tf_op jit(solution)/shard_map/ppermute | solution.py:215
  38.8 1.5 %collective-permute-done.8.refs_3_ = bf16[4,4096]{1,0:T(4,128)(2,1)S(1)} collective-permute-done((bf16[4,4096]{1,0:T(4,128)(2,1)S(1)}, bf16[4,4096]{1,0:T(4,128)(2,1)S(1)}, u32[]{:S(2)}, u32[]{:S(2)}) %collective-permute-start.8) | collective-permute-done | bytes 32800 | tf_op jit(solution)/shard_map/ppermute | solution.py:215
  40.3 0.7 %collective-permute-done.7.refs_2_ = bf16[4,4096]{1,0:T(4,128)(2,1)S(1)} collective-permute-done((bf16[4,4096]{1,0:T(4,128)(2,1)S(1)}, bf16[4,4096]{1,0:T(4,128)(2,1)S(1)}, u32[]{:S(2)}, u32[]{:S(2)}) %collective-permute-start.7) | collective-permute-done | bytes 32800 | tf_op jit(solution)/shard_map/ppermute | solution.py:215
  41.0 0.0 collective-permute-done.6.refs_1_
  41.0 0.7 %lay.1 = bf16[4,16384]{1,0:T(4,128)(2,1)} custom-call(bf16[4,4096]{1,0:T(4,128)(2,1)S(1)} %add_far.1.refs_0_, bf16[4,4096]{1,0:T(4,128)(2,1)S(1)} %collective-permute-done.6.refs_1_, bf16[4,4096]{1,0:T(4,128)(2,1)S(1)} %collective-permute-done.7.refs_2_, bf16[4,4096]{1,0:T(4,128)(2,1)S(1)} %collective-permute-done.8.refs_3_), custom_call_target="tpu_custom_call" | custom-call | tf_op jit(solution)/shard_map/lay/pallas_call | solution.py:317
  (2 shorter events, 0.1 us)
Async XLA Ops:
  25.4 4.8 %collective-permute-start = (bf16[4,4096]{1,0:T(4,128)(2,1)S(1)}, bf16[4,4096]{1,0:T(4,128)(2,1)S(1)}, u32[]{:S(2)}, u32[]{:S(2)}) collective-permute-start(bf16[4,4096]{1,0:T(4,128)(2,1)S(1)} %get-tuple-element.14), channel_id=1, source_target_pairs={{0,1},{1,0},{2,3},{3,2},{4,5},{5,4},{6,7},{7,6},{8,9},{9,8},{10,11... | collective-permute-start | bytes 98312 | tf_op jit(solution)/shard_map/ppermute | solution.py:215
  25.4 4.8 %collective-permute-start.1 = (bf16[4,4096]{1,0:T(4,128)(2,1)S(1)}, bf16[4,4096]{1,0:T(4,128)(2,1)S(1)}, u32[]{:S(2)}, u32[]{:S(2)}) collective-permute-start(bf16[4,4096]{1,0:T(4,128)(2,1)S(1)} %get-tuple-element.15), channel_id=1, source_target_pairs={{0,2},{1,3},{2,0},{3,1},{4,6},{5,7},{6,4},{7,5},{8,10},{9,11},{10,... | collective-permute-start | bytes 98312 | tf_op jit(solution)/shard_map/ppermute | solution.py:215
  25.6 4.6 %collective-permute-start.2 = (bf16[4,4096]{1,0:T(4,128)(2,1)S(1)}, bf16[4,4096]{1,0:T(4,128)(2,1)S(1)}, u32[]{:S(2)}, u32[]{:S(2)}) collective-permute-start(bf16[4,4096]{1,0:T(4,128)(2,1)S(1)} %get-tuple-element.16), channel_id=1, source_target_pairs={{0,3},{1,2},{2,1},{3,0},{4,7},{5,6},{6,5},{7,4},{8,11},{9,10},{10,... | collective-permute-start | bytes 98312 | tf_op jit(solution)/shard_map/ppermute | solution.py:215
  30.3 6.1 %collective-permute-start.5 = (bf16[4,4096]{1,0:T(4,128)(2,1)S(1)}, bf16[4,4096]{1,0:T(4,128)(2,1)S(1)}, u32[]{:S(2)}, u32[]{:S(2)}) collective-permute-start(bf16[4,4096]{1,0:T(4,128)(2,1)S(1)} %add_near.1.refs_0_), channel_id=1, source_target_pairs={{0,12},{1,13},{2,14},{3,15},{4,8},{5,9},{6,10},{7,11},{8,4},{9,5},... | collective-permute-start | bytes 98312 | tf_op jit(solution)/shard_map/ppermute | solution.py:215
  30.9 5.7 %collective-permute-start.4 = (bf16[4,4096]{1,0:T(4,128)(2,1)S(1)}, bf16[4,4096]{1,0:T(4,128)(2,1)S(1)}, u32[]{:S(2)}, u32[]{:S(2)}) collective-permute-start(bf16[4,4096]{1,0:T(4,128)(2,1)S(1)} %add_near.1.refs_0_), channel_id=1, source_target_pairs={{0,8},{1,9},{2,10},{3,11},{4,12},{5,13},{6,14},{7,15},{8,0},{9,1},... | collective-permute-start | bytes 98312 | tf_op jit(solution)/shard_map/ppermute | solution.py:215
  31.7 5.1 %collective-permute-start.3 = (bf16[4,4096]{1,0:T(4,128)(2,1)S(1)}, bf16[4,4096]{1,0:T(4,128)(2,1)S(1)}, u32[]{:S(2)}, u32[]{:S(2)}) collective-permute-start(bf16[4,4096]{1,0:T(4,128)(2,1)S(1)} %add_near.1.refs_0_), channel_id=1, source_target_pairs={{0,4},{1,5},{2,6},{3,7},{4,0},{5,1},{6,2},{7,3},{8,12},{9,13},{10,... | collective-permute-start | bytes 98312 | tf_op jit(solution)/shard_map/ppermute | solution.py:215
  36.9 3.4 %collective-permute-start.8 = (bf16[4,4096]{1,0:T(4,128)(2,1)S(1)}, bf16[4,4096]{1,0:T(4,128)(2,1)S(1)}, u32[]{:S(2)}, u32[]{:S(2)}) collective-permute-start(bf16[4,4096]{1,0:T(4,128)(2,1)S(1)} %add_far.1.refs_0_), channel_id=1, source_target_pairs={{0,3},{1,2},{2,1},{3,0},{4,7},{5,6},{6,5},{7,4},{8,11},{9,10},{10,... | collective-permute-start | bytes 98312 | tf_op jit(solution)/shard_map/ppermute | solution.py:215
  36.9 4.0 %collective-permute-start.7 = (bf16[4,4096]{1,0:T(4,128)(2,1)S(1)}, bf16[4,4096]{1,0:T(4,128)(2,1)S(1)}, u32[]{:S(2)}, u32[]{:S(2)}) collective-permute-start(bf16[4,4096]{1,0:T(4,128)(2,1)S(1)} %add_far.1.refs_0_), channel_id=1, source_target_pairs={{0,2},{1,3},{2,0},{3,1},{4,6},{5,7},{6,4},{7,5},{8,10},{9,11},{10,... | collective-permute-start | bytes 98312 | tf_op jit(solution)/shard_map/ppermute | solution.py:215
  37.8 3.2 %collective-permute-start.6 = (bf16[4,4096]{1,0:T(4,128)(2,1)S(1)}, bf16[4,4096]{1,0:T(4,128)(2,1)S(1)}, u32[]{:S(2)}, u32[]{:S(2)}) collective-permute-start(bf16[4,4096]{1,0:T(4,128)(2,1)S(1)} %add_far.1.refs_0_), channel_id=1, source_target_pairs={{0,1},{1,0},{2,3},{3,2},{4,5},{5,4},{6,7},{7,6},{8,9},{9,8},{10,11... | collective-permute-start | bytes 98312 | tf_op jit(solution)/shard_map/ppermute | solution.py:215

commit v7 on v5

--- a/solution.py
+++ b/solution.py
@@ -194,13 +194,14 @@
     refs[-1][...] = terms[0].astype(refs[-1].dtype)
 
 
-def lay_kernel(*refs):
-    parts, out = refs[:-1], refs[-1]
-    quarter = lax.rem(lax.axis_index("kvp"), len(parts))
-    width = parts[0].shape[1]
-    for x, part in enumerate(parts):
-        start = pl.multiple_of(jnp.bitwise_xor(quarter, x) * width, width)
-        out[:, pl.ds(start, width)] = part[...]
+def add_far_kernel(terms, out):
+    out[...] = jnp.sum(terms[...].astype(jnp.float32), axis=0).astype(out.dtype)
+
+
+def lay_kernel(parts, out):
+    count, _, width = parts.shape
+    for i in range(count):
+        out[:, i * width : (i + 1) * width] = parts[i]
 
 
 def exchange(array, partner, devices):
@@ -305,16 +306,26 @@
         )(*terms)
 
     mine = add([own] + sent, "add_near")
-    mine = add([mine] + [exchange(mine, x * inner, devices) for x in range(1, outer)], "add_far")
-    parts = [mine] + [exchange(mine, x, devices) for x in range(1, inner)]
+    far = [[x * inner + i for x in range(outer)] for i in range(inner)]
+    near = [[x * inner + i for i in range(inner)] for x in range(outer)]
+    terms = lax.all_gather(mine, "kvp", axis_index_groups=far)
+    mine = pl.pallas_call(
+        add_far_kernel,
+        out_shape=jax.ShapeDtypeStruct((rows, part), jnp.bfloat16),
+        in_specs=[VMEM],
+        out_specs=VMEM,
+        compiler_params=pltpu.CompilerParams(vmem_limit_bytes=SMALL_VMEM),
+        name="add_far",
+    )(terms)
+    parts = lax.all_gather(mine, "kvp", axis_index_groups=near)
     return pl.pallas_call(
         lay_kernel,
         out_shape=jax.ShapeDtypeStruct((rows, features), jnp.bfloat16),
-        in_specs=[VMEM] * inner,
+        in_specs=[VMEM],
         out_specs=VMEM,
         compiler_params=pltpu.CompilerParams(vmem_limit_bytes=SMALL_VMEM),
         name="lay",
-    )(*parts)
+    )(parts)
 
 
 def solution(mesh):

time: 41.3 us -> 49.4 us (1.20)
  blocking collectives: 14.6 us -> 33.6 us
  starting transfers between devices: 8.3 us -> 1.93 us
  waiting for transfers between devices: 4.57 us -> 0.01 us
    all_gather x0 -> x2, blocking collectives: none -> 19.1 us  [the longest x1 13.6 us: body(): terms = lax.all_gather(mine, 'kvp', axis_index_groups=far)]
    ppermute x9 -> x3, starting transfers between devices: 8.3 us -> 1.93 us  [exchange(): lax.ppermute(array, 'kvp', [(i, i ^ partner) for i in range(devices)])]
    ppermute x9 -> x3, waiting for transfers between devices: 4.57 us -> 0.01 us  [exchange(): lax.ppermute(array, 'kvp', [(i, i ^ partner) for i in range(devices)])]
  transfers between devices with their start and end apart: 9 -> 3, of which waited for: 5 -> 0; matrix products, arithmetic and copies ran while one was open for 0% -> 0% of each run, Pallas kernels for 6% -> 5%
where the time goes in v7:
time: 49.4 us; the launch traced here: 49.3 us
  blocking collectives  33.6 us (68%)
  Pallas kernels  13.6 us (28%)
  starting transfers between devices  1.93 us (4%)
    all_to_all x1, blocking collectives, body(): lax.all_to_all(packed, 'kvp', split_axis=0, concat_axis=0, tiled=True)  14.6 us
    all_gather x1, blocking collectives, body(): terms = lax.all_gather(mine, 'kvp', axis_index_groups=far)  13.6 us
    pallas_call x1, Pallas kernels, body(): pl.pallas_call(functools.partial(attend_kernel, heads_dev, devices, inner...  6.13 us
    all_gather x1, blocking collectives, body(): parts = lax.all_gather(mine, 'kvp', axis_index_groups=near)  5.43 us
    pallas_call x1, Pallas kernels, body(): pl.pallas_call(functools.partial(project_kernel, heads_dev), out_shape=[j...  4.25 us
    pallas_call x1, Pallas kernels, body(): pl.pallas_call(project_own_kernel, out_shape=jax.ShapeDtypeStruct((rows,...  2.47 us
    ppermute x3, starting transfers between devices, exchange(): lax.ppermute(array, 'kvp', [(i, i ^ partner) for i in range(devices)])  1.93 us
  transfers between devices with their start and end apart: 3, of which 0 were waited for; matrix products, arithmetic and copies ran while one was open for 0% of the time, Pallas kernels for 5%

profile of v7, /device:TPU:0, one launch (start us, length us, event | category | flops | bytes accessed | tf_op | source)
XLA Modules:
  0.0 49.3 jit_solution(9857162646789940592)
XLA Ops:
  0.0 6.1 %attend.1 = (bf16[16,24,128]{2,1,0:T(8,128)(2,1)S(1)}, bf16[6,512,1024]{2,1,0:T(8,128)(2,1)S(1)}) custom-call(s32[4,12]{1,0:T(4,128)} %refs_0_.1, s32[4]{0:T(128)} %refs_1_.1, f32[4,48]{1,0:T(4,128)} %bitcast.6, f32[4,48]{1,0:T(4,128)} %bitcast.7, bf16[4,8192]{1,0:T(4,128)(2,1)} %refs_4_.1, bf16[48,64,512]{2,1,0:T(8,128)(2,1)} %refs_5_.1, ...), custom_call_target="tpu_custom_call" | custom-call | flops 100663296 | bytes 6291456 | tf_op jit(solution)/shard_map/attend/pallas_call | solution.py:229
  6.1 14.6 %all_to_all.5.packed = bf16[16,24,128]{2,1,0:T(8,128)(2,1)S(1)} all-to-all(bf16[16,24,128]{2,1,0:T(8,128)(2,1)S(1)} %get-tuple-element.11), channel_id=1, replica_groups=mesh['group'=2,'kvp'=16] {'kvp'}, dimensions={0} | all-to-all | bytes 196608 | tf_op jit(solution)/shard_map/all_to_all | solution.py:260
  20.7 4.3 %project_others.1 = (bf16[4,512]{1,0:T(4,128)(2,1)S(1)}, bf16[4,4096]{1,0:T(4,128)(2,1)S(1)}, bf16[4,4096]{1,0:T(4,128)(2,1)S(1)}, bf16[4,4096]{1,0:T(4,128)(2,1)S(1)}) custom-call(bf16[16,24,128]{2,1,0:T(8,128)(2,1)S(1)} %all_to_all.5.packed, bf16[6,512,1024]{2,1,0:T(8,128)(2,1)S(1)} %get-tuple-element.12.fetched, bf16[512,16384]{1,0:T(8,128)(2,1)} %weight.3), custom_call_target="tpu_custom_call" | custom-call | flops 50331648 | bytes 12582912 | tf_op jit(solution)/shard_map/project_others/pallas_call | solution.py:262
  25.0 0.1 collective-permute-start
  25.1 0.1 collective-permute-start.1
  25.2 1.8 %collective-permute-start.2 = (bf16[4,4096]{1,0:T(4,128)(2,1)S(1)}, bf16[4,4096]{1,0:T(4,128)(2,1)S(1)}, u32[]{:S(2)}, u32[]{:S(2)}) collective-permute-start(bf16[4,4096]{1,0:T(4,128)(2,1)S(1)} %get-tuple-element.16), channel_id=1, source_target_pairs={{0,3},{1,2},{2,1},{3,0},{4,7},{5,6},{6,5},{7,4},{8,11},{9,10},{10,... | collective-permute-start | bytes 98312 | tf_op jit(solution)/shard_map/ppermute | solution.py:208
  26.9 2.5 %project_own.1.refs_0_ = bf16[4,4096]{1,0:T(4,128)(2,1)S(1)} custom-call(bf16[4,512]{1,0:T(4,128)(2,1)S(1)} %get-tuple-element.13.left, bf16[512,16384]{1,0:T(8,128)(2,1)} %weight.3), custom_call_target="tpu_custom_call" | custom-call | flops 16777216 | bytes 4194304 | tf_op jit(solution)/shard_map/project_own/pallas_call | solution.py:282
  29.4 0.0 collective-permute-done.refs_1_
  29.4 0.0 collective-permute-done.1.refs_2_
  29.4 0.0 collective-permute-done.2.refs_3_
  29.5 13.6 %all-gather.2.terms = bf16[4,4,4096]{2,1,0:T(4,128)(2,1)S(1)} all-gather(bf16[1,4,4096]{2,1,0:T(4,128)(2,1)S(1)} %bitcast.4), channel_id=2, replica_groups={{0,4,8,12},{1,5,9,13},{2,6,10,14},{3,7,11,15},{16,20,24,28},{17,21,25,2..., dimensions={0}, use_global_device_ids=true | all-gather | bytes 163840 | tf_op jit(solution)/shard_map/all_gather | solution.py:311
  43.1 0.1 add_far.1
  43.2 5.4 %all-gather.3.parts = bf16[4,4,4096]{2,1,0:T(4,128)(2,1)S(1)} all-gather(bf16[1,4,4096]{2,1,0:T(4,128)(2,1)S(1)} %bitcast.5), channel_id=3, replica_groups={{0,1,2,3},{4,5,6,7},{8,9,10,11},{12,13,14,15},{16,17,18,19},{20,21,22,2..., dimensions={0}, use_global_device_ids=true | all-gather | bytes 163840 | tf_op jit(solution)/shard_map/all_gather | solution.py:320
  48.6 0.7 %lay.1 = bf16[4,16384]{1,0:T(4,128)(2,1)} custom-call(bf16[4,4,4096]{2,1,0:T(4,128)(2,1)S(1)} %all-gather.3.parts), custom_call_target="tpu_custom_call" | custom-call | tf_op jit(solution)/shard_map/lay/pallas_call | solution.py:321
  (1 shorter events, 0.0 us)
Async XLA Ops:
  25.0 4.4 %collective-permute-start = (bf16[4,4096]{1,0:T(4,128)(2,1)S(1)}, bf16[4,4096]{1,0:T(4,128)(2,1)S(1)}, u32[]{:S(2)}, u32[]{:S(2)}) collective-permute-start(bf16[4,4096]{1,0:T(4,128)(2,1)S(1)} %get-tuple-element.14), channel_id=1, source_target_pairs={{0,1},{1,0},{2,3},{3,2},{4,5},{5,4},{6,7},{7,6},{8,9},{9,8},{10,11... | collective-permute-start | bytes 98312 | tf_op jit(solution)/shard_map/ppermute | solution.py:208
  25.1 4.4 %collective-permute-start.1 = (bf16[4,4096]{1,0:T(4,128)(2,1)S(1)}, bf16[4,4096]{1,0:T(4,128)(2,1)S(1)}, u32[]{:S(2)}, u32[]{:S(2)}) collective-permute-start(bf16[4,4096]{1,0:T(4,128)(2,1)S(1)} %get-tuple-element.15), channel_id=1, source_target_pairs={{0,2},{1,3},{2,0},{3,1},{4,6},{5,7},{6,4},{7,5},{8,10},{9,11},{10,... | collective-permute-start | bytes 98312 | tf_op jit(solution)/shard_map/ppermute | solution.py:208
  25.2 4.3 %collective-permute-start.2 = (bf16[4,4096]{1,0:T(4,128)(2,1)S(1)}, bf16[4,4096]{1,0:T(4,128)(2,1)S(1)}, u32[]{:S(2)}, u32[]{:S(2)}) collective-permute-start(bf16[4,4096]{1,0:T(4,128)(2,1)S(1)} %get-tuple-element.16), channel_id=1, source_target_pairs={{0,3},{1,2},{2,1},{3,0},{4,7},{5,6},{6,5},{7,4},{8,11},{9,10},{10,... | collective-permute-start | bytes 98312 | tf_op jit(solution)/shard_map/ppermute | solution.py:208

commit v8 on v4

--- a/solution.py
+++ b/solution.py
@@ -11,11 +11,11 @@
 HD = 128
 PAGE = 64
 ATTEND_VMEM = 24 * 1024 * 1024
-WEIGHT_PIECES = 8
+PROJECT_VMEM = 8 * 1024 * 1024
+EXCHANGE_FLOPS = 40_000_000_000
 SMALL_VMEM = 8 * 1024 * 1024
 VMEM = pl.BlockSpec(memory_space=pltpu.VMEM)
 HBM = pl.BlockSpec(memory_space=pltpu.HBM)
-ANY = pl.BlockSpec(memory_space=pl.ANY)
 
 
 def split_two(value):
@@ -26,12 +26,11 @@
 
 def attend_kernel(heads_dev, devices, *refs):
     table_hbm, lengths_hbm, key_scale_hbm, value_scale_hbm, queries_hbm, keys, values = refs[:7]
-    (packed, table, lengths, key_scale, value_scale, queries, key_buf, value_buf, query_rows, staged, small_sems, sems) = refs[7:]
+    (staged, table, lengths, key_scale, value_scale, queries, key_buf, value_buf, query_rows, small_sems, sems) = refs[7:]
     rows, pages = table.shape
     kv_heads = key_scale.shape[0]
     heads = queries.shape[1] // HD
     group = heads // kv_heads
-    part_rows = rows * heads_dev
     context = pages * PAGE
     pieces = sems.shape[1]
     piece = keys.shape[0] // pieces
@@ -54,9 +53,9 @@
         for i in range(pieces):
             here = pl.ds(i * piece, piece)
             large[-1].append(pltpu.make_async_copy(source.at[here], target.at[here], sems.at[which, i]))
-            large[-1][-1].start()
-
-    staged[:, part_rows:, :] = jnp.zeros((devices, staged.shape[1] - part_rows, HD), jnp.float32)
+    for copy in large[0]:
+        copy.start()
+
     me = lax.axis_index("kvp")
     place = me * context + lax.broadcasted_iota(jnp.int32, (group, context), 1)
     lane = lax.broadcasted_iota(jnp.int32, (group, HD), 1)
@@ -65,6 +64,8 @@
         copy.wait()
     for h in range(heads):
         query_rows[h * rows : (h + 1) * rows, :] = queries[:, h * HD : (h + 1) * HD].astype(jnp.float32)
+    for copy in large[1]:
+        copy.start()
     for copy in large[0]:
         copy.wait()
 
@@ -117,37 +118,26 @@
                 partial = both[i * group : (i + 1) * group, i * HD : (i + 1) * HD]
                 for start in range(0, group, heads_dev):
                     d = ((k + i) * group + start) // heads_dev
-                    staged[d, r * heads_dev : (r + 1) * heads_dev, :] = partial[start : start + heads_dev]
+                    staged[d, r] = partial[start : start + heads_dev]
     for k in range(kv_heads):
         for start in range(0, group, heads_dev):
             d = (k * group + start) // heads_dev
-            staged[d, part_rows : part_rows + heads_dev, :] = stats[k][start : start + heads_dev]
+            staged[d, rows] = stats[k][start : start + heads_dev]
+
+
+def pack_kernel(staged, packed):
     packed[...] = staged[...].astype(jnp.bfloat16)
-
-
-def fetch_kernel(parts, _, weight, buf, sems):
-    pieces, _, width = buf.shape
-    per_part = pieces // parts
-    quarter = lax.rem(lax.axis_index("kvp"), parts)
-    copies = []
-    for piece in range(pieces):
-        start = (jnp.bitwise_xor(quarter, piece // per_part) * per_part + piece % per_part) * width
-        source = weight.at[:, pl.ds(pl.multiple_of(start, width), width)]
-        copies.append(pltpu.make_async_copy(source, buf.at[piece], sems.at[piece]))
-        copies[-1].start()
-    for copy in copies:
-        copy.wait()
 
 
 def project_kernel(heads_dev, packed, weight, left, *refs):
     outs, attended = refs[:-1], refs[-1]
     rows = left.shape[0]
-    width = weight.shape[2]
-    per_out = weight.shape[0] // (len(outs) + 1)
+    part = outs[0].shape[1]
+    quarter = lax.rem(lax.axis_index("kvp"), len(outs) + 1)
     blocks = packed[...].astype(jnp.float32)
-    stats = blocks[:, rows * heads_dev : (rows + 1) * heads_dev, :]
+    stats = blocks[:, rows]
     for r in range(rows):
-        partial = blocks[:, r * heads_dev : (r + 1) * heads_dev, :]
+        partial = blocks[:, r]
         maxima = stats[:, :, 4 * r : 4 * r + 1] + stats[:, :, 4 * r + 1 : 4 * r + 2]
         totals = stats[:, :, 4 * r + 2 : 4 * r + 3] + stats[:, :, 4 * r + 3 : 4 * r + 4]
         rescale = jnp.exp(maxima - jnp.max(maxima, axis=0, keepdims=True))
@@ -159,16 +149,17 @@
     )
     left[...] = rounded
     for x, out in enumerate(outs):
-        for i in range(per_out):
-            terms = jnp.dot(rounded, weight[(x + 1) * per_out + i], preferred_element_type=jnp.float32)
-            out[:, i * width : (i + 1) * width] = terms.astype(jnp.bfloat16)
+        start = pl.multiple_of(jnp.bitwise_xor(quarter, x + 1) * part, part)
+        terms = jnp.dot(rounded, weight[:, pl.ds(start, part)], preferred_element_type=jnp.float32)
+        out[...] = terms.astype(jnp.bfloat16)
 
 
 def project_own_kernel(left, weight, out):
-    width = weight.shape[2]
-    for i in range(out.shape[1] // width):
-        terms = jnp.dot(left[...], weight[i], preferred_element_type=jnp.float32)
-        out[:, i * width : (i + 1) * width] = terms.astype(jnp.bfloat16)
+    part = out.shape[1]
+    quarter = lax.rem(lax.axis_index("kvp"), weight.shape[1] // part)
+    start = pl.multiple_of(quarter * part, part)
+    terms = jnp.dot(left[...], weight[:, pl.ds(start, part)], preferred_element_type=jnp.float32)
+    out[...] = terms.astype(jnp.bfloat16)
 
 
 def add_kernel(*refs):
@@ -202,13 +193,12 @@
     heads_dev = out_weight.shape[0] // HD
     heads = queries.shape[1] // HD
     features = out_weight.shape[1]
-    chunk = -(-(rows + 1) * heads_dev // 8) * 8
     inner = 4
     outer = devices // inner
     part = features // inner
-    packed = pl.pallas_call(
+    staged = pl.pallas_call(
         functools.partial(attend_kernel, heads_dev, devices),
-        out_shape=jax.ShapeDtypeStruct((devices, chunk, HD), jnp.bfloat16),
+        out_shape=jax.ShapeDtypeStruct((devices, rows + 1, heads_dev, HD), jnp.float32),
         in_specs=[HBM] * 7,
         out_specs=VMEM,
         scratch_shapes=[
@@ -220,7 +210,6 @@
             pltpu.VMEM((slots, PAGE, columns), jnp.bfloat16),
             pltpu.VMEM((slots, PAGE, columns), jnp.bfloat16),
             pltpu.VMEM((heads * rows, HD), jnp.float32),
-            pltpu.VMEM((devices, chunk, HD), jnp.float32),
             pltpu.SemaphoreType.DMA((5,)),
             pltpu.SemaphoreType.DMA((2, 4)),
         ],
@@ -233,21 +222,20 @@
         name="attend",
     )(*[in_hbm(a) for a in (page_table, lengths, key_scale.T, value_scale.T, queries, key_cache, value_cache)])
 
+    packed = pl.pallas_call(
+        pack_kernel,
+        out_shape=jax.ShapeDtypeStruct(staged.shape, jnp.bfloat16),
+        in_specs=[VMEM],
+        out_specs=VMEM,
+        compiler_params=pltpu.CompilerParams(vmem_limit_bytes=SMALL_VMEM),
+        cost_estimate=pl.CostEstimate(flops=EXCHANGE_FLOPS, bytes_accessed=6 * staged.size, transcendentals=0),
+        name="pack",
+    )(staged)
+
     received = lax.all_to_all(packed, "kvp", split_axis=0, concat_axis=0, tiled=True)
 
+    resident = pltpu.with_memory_space_constraint(out_weight, pltpu.VMEM)
     depth = heads_dev * HD
-    width = features // WEIGHT_PIECES
-    fetched = pl.pallas_call(
-        functools.partial(fetch_kernel, inner),
-        out_shape=pltpu.VMEM((WEIGHT_PIECES, depth, width), jnp.bfloat16),
-        in_specs=[ANY, HBM],
-        out_specs=VMEM,
-        scratch_shapes=[pltpu.SemaphoreType.DMA((WEIGHT_PIECES,))],
-        compiler_params=pltpu.CompilerParams(vmem_limit_bytes=SMALL_VMEM),
-        cost_estimate=pl.CostEstimate(flops=0, bytes_accessed=2 * out_weight.size, transcendentals=0),
-        name="fetch",
-    )(packed, in_hbm(out_weight))
-
     left, *others = pl.pallas_call(
         functools.partial(project_kernel, heads_dev),
         out_shape=[jax.ShapeDtypeStruct((rows, depth), jnp.bfloat16)]
@@ -255,26 +243,26 @@
         in_specs=[VMEM, VMEM],
         out_specs=[VMEM] * inner,
         scratch_shapes=[pltpu.VMEM((rows * heads_dev, HD), jnp.float32)],
-        compiler_params=pltpu.CompilerParams(vmem_limit_bytes=SMALL_VMEM),
+        compiler_params=pltpu.CompilerParams(vmem_limit_bytes=PROJECT_VMEM),
         cost_estimate=pl.CostEstimate(
             flops=2 * rows * depth * part * (inner - 1),
             bytes_accessed=2 * depth * part * (inner - 1),
             transcendentals=0,
         ),
         name="project_others",
-    )(received, fetched)
+    )(received, resident)
     sent = [exchange(others[x - 1], x, devices) for x in range(1, inner)]
     own = pl.pallas_call(
         project_own_kernel,
         out_shape=jax.ShapeDtypeStruct((rows, part), jnp.bfloat16),
         in_specs=[VMEM, VMEM],
         out_specs=VMEM,
-        compiler_params=pltpu.CompilerParams(vmem_limit_bytes=SMALL_VMEM),
+        compiler_params=pltpu.CompilerParams(vmem_limit_bytes=PROJECT_VMEM),
         cost_estimate=pl.CostEstimate(
             flops=2 * rows * depth * part, bytes_accessed=2 * depth * part, transcendentals=0
         ),
         name="project_own",
-    )(left, fetched)
+    )(left, resident)
 
     def add(terms, name):
         return pl.pallas_call(

time: 51.1 us -> 37 us (0.72)
  blocking collectives: 0 us -> 14.6 us
  local copies, waits for them, and re-layouts: 11.5 us -> 0.02 us
  starting transfers between devices: 15.9 us -> 8.24 us
  Pallas kernels: 14.6 us -> 8 us
  waiting for transfers between devices: 8.85 us -> 5.89 us
    all_to_all x0 -> x1, blocking collectives: none -> 14.6 us  [body(): lax.all_to_all(packed, 'kvp', split_axis=0, concat_axis=0, tiled=True)]
    unnamed x4 -> x8, local copies, waits for them, and re-layouts: 11.5 us -> 0.02 us
    all_to_all x1 -> x0, starting transfers between devices: 7.4 us -> none  [body(): lax.all_to_all(packed, 'kvp', split_axis=0, concat_axis=0, tiled=True)]
    pallas_call x1, Pallas kernels: 5.96 us -> 0.03 us  [body(): pl.pallas_call(pack_kernel, out_shape=jax.ShapeDtypeStruct(staged.shape,...]
    ppermute x9, waiting for transfers between devices: 8.85 us -> 5.89 us  [exchange(): lax.ppermute(array, 'kvp', [(i, i ^ partner) for i in range(devices)])]
    pallas_call x1, Pallas kernels: 5.19 us -> 4.51 us  [body(): pl.pallas_call(functools.partial(attend_kernel, heads_dev, devices), out_...]
  transfers between devices with their start and end apart: 10 -> 9, of which waited for: 6 -> 6; matrix products, arithmetic and copies ran while one was open for 0% -> 0% of each run, Pallas kernels for 13% -> 2%
where the time goes in v8:
time: 37 us; the launch traced here: 36.8 us
  blocking collectives  14.6 us (39%)
  starting transfers between devices  8.24 us (22%)
  Pallas kernels  8 us (22%)
  waiting for transfers between devices  5.89 us (16%)
    all_to_all x1, blocking collectives, body(): lax.all_to_all(packed, 'kvp', split_axis=0, concat_axis=0, tiled=True)  14.6 us
    ppermute x9, starting transfers between devices, exchange(): lax.ppermute(array, 'kvp', [(i, i ^ partner) for i in range(devices)])  8.24 us
    ppermute x9, waiting for transfers between devices, exchange(): lax.ppermute(array, 'kvp', [(i, i ^ partner) for i in range(devices)])  5.89 us
    pallas_call x1, Pallas kernels, body(): pl.pallas_call(functools.partial(attend_kernel, heads_dev, devices), out_...  4.51 us
    pallas_call x1, Pallas kernels, body(): pl.pallas_call(functools.partial(project_kernel, heads_dev), out_shape=[j...  2.08 us
  transfers between devices with their start and end apart: 9, of which 6 were waited for; matrix products, arithmetic and copies ran while one was open for 0% of the time, Pallas kernels for 2%

profile of v8, /device:TPU:0, one launch (start us, length us, event | category | flops | bytes accessed | tf_op | source)
XLA Modules:
  0.0 36.8 jit_solution(5413192092774961622)
XLA Ops:
  0.0 0.0 slice-start
  0.0 4.5 %attend.1.staged = f32[16,5,4,128]{3,2,1,0:T(4,128)S(1)} custom-call(s32[4,12]{1,0:T(4,128)} %refs_0_.1, s32[4]{0:T(128)} %refs_1_.1, f32[4,48]{1,0:T(4,128)} %bitcast.4, f32[4,48]{1,0:T(4,128)} %bitcast.5, bf16[4,8192]{1,0:T(4,128)(2,1)} %refs_4_.1, bf16[48,64,512]{2,1,0:T(8,128)(2,1)} %refs_5_.1, bf16[48,64,512]{2,1,0:T(8,128)(2,1)} %refs_6_.1), custom_call_target="tpu_custom_call" | custom-call | flops 100663296 | bytes 6291456 | tf_op jit(solution)/shard_map/attend/pallas_call | solution.py:199
  4.5 0.0 slice-start.1
  4.5 0.0 slice-start.2
  4.5 0.0 slice-start.3
  4.6 14.6 %all_to_all.5.packed = bf16[16,5,4,128]{3,2,1,0:T(4,128)(2,1)S(1)} all-to-all(bf16[16,5,4,128]{3,2,1,0:T(4,128)(2,1)S(1)} %pack.1), channel_id=1, replica_groups=mesh['group'=2,'kvp'=16] {'kvp'}, dimensions={0} | all-to-all | bytes 163840 | tf_op jit(solution)/shard_map/all_to_all | solution.py:235
  19.2 0.0 slice-done
  19.2 0.0 slice-done.1
  19.2 0.0 slice-done.2
  19.2 0.0 slice-done.3
  19.2 2.1 %project_others.1 = (bf16[4,512]{1,0:T(4,128)(2,1)S(1)}, bf16[4,4096]{1,0:T(4,128)(2,1)S(1)}, bf16[4,4096]{1,0:T(4,128)(2,1)S(1)}, bf16[4,4096]{1,0:T(4,128)(2,1)S(1)}) custom-call(bf16[16,5,4,128]{3,2,1,0:T(4,128)(2,1)S(1)} %all_to_all.5.packed, bf16[512,16384]{1,0:T(8,128)(2,1)S(1)} %bitcast.3), custom_call_target="tpu_custom_call" | custom-call | flops 50331648 | bytes 12582912 | tf_op jit(solution)/shard_map/project_others/pallas_call | solution.py:239
  21.3 0.0 collective-permute-start
  21.3 0.2 collective-permute-start.1
  21.5 1.7 %collective-permute-start.2 = (bf16[4,4096]{1,0:T(4,128)(2,1)S(1)}, bf16[4,4096]{1,0:T(4,128)(2,1)S(1)}, u32[]{:S(2)}, u32[]{:S(2)}) collective-permute-start(bf16[4,4096]{1,0:T(4,128)(2,1)S(1)} %get-tuple-element.12), channel_id=1, source_target_pairs={{0,3},{1,2},{2,1},{3,0},{4,7},{5,6},{6,5},{7,4},{8,11},{9,10},{10,... | collective-permute-start | bytes 98312 | tf_op jit(solution)/shard_map/ppermute | solution.py:182
  23.2 0.7 %project_own.1.refs_0_ = bf16[4,4096]{1,0:T(4,128)(2,1)S(1)} custom-call(bf16[4,512]{1,0:T(4,128)(2,1)S(1)} %get-tuple-element.9.left, bf16[512,16384]{1,0:T(8,128)(2,1)S(1)} %bitcast.3), custom_call_target="tpu_custom_call" | custom-call | flops 16777216 | bytes 4194304 | tf_op jit(solution)/shard_map/project_own/pallas_call | solution.py:255
  23.8 0.0 collective-permute-done.refs_1_
  23.8 1.6 %collective-permute-done.1.refs_2_ = bf16[4,4096]{1,0:T(4,128)(2,1)S(1)} collective-permute-done((bf16[4,4096]{1,0:T(4,128)(2,1)S(1)}, bf16[4,4096]{1,0:T(4,128)(2,1)S(1)}, u32[]{:S(2)}, u32[]{:S(2)}) %collective-permute-start.1) | collective-permute-done | bytes 32800 | tf_op jit(solution)/shard_map/ppermute | solution.py:182
  25.5 0.0 collective-permute-done.2.refs_3_
  25.5 1.0 %collective-permute-start.5 = (bf16[4,4096]{1,0:T(4,128)(2,1)S(1)}, bf16[4,4096]{1,0:T(4,128)(2,1)S(1)}, u32[]{:S(2)}, u32[]{:S(2)}) collective-permute-start(bf16[4,4096]{1,0:T(4,128)(2,1)S(1)} %add_near.1.refs_0_), channel_id=1, source_target_pairs={{0,12},{1,13},{2,14},{3,15},{4,8},{5,9},{6,10},{7,11},{8,4},{9,5},... | collective-permute-start | bytes 98312 | tf_op jit(solution)/shard_map/ppermute | solution.py:182
  26.5 0.9 %collective-permute-start.4 = (bf16[4,4096]{1,0:T(4,128)(2,1)S(1)}, bf16[4,4096]{1,0:T(4,128)(2,1)S(1)}, u32[]{:S(2)}, u32[]{:S(2)}) collective-permute-start(bf16[4,4096]{1,0:T(4,128)(2,1)S(1)} %add_near.1.refs_0_), channel_id=1, source_target_pairs={{0,8},{1,9},{2,10},{3,11},{4,12},{5,13},{6,14},{7,15},{8,0},{9,1},... | collective-permute-start | bytes 98312 | tf_op jit(solution)/shard_map/ppermute | solution.py:182
  27.4 2.5 %collective-permute-start.3 = (bf16[4,4096]{1,0:T(4,128)(2,1)S(1)}, bf16[4,4096]{1,0:T(4,128)(2,1)S(1)}, u32[]{:S(2)}, u32[]{:S(2)}) collective-permute-start(bf16[4,4096]{1,0:T(4,128)(2,1)S(1)} %add_near.1.refs_0_), channel_id=1, source_target_pairs={{0,4},{1,5},{2,6},{3,7},{4,0},{5,1},{6,2},{7,3},{8,12},{9,13},{10,... | collective-permute-start | bytes 98312 | tf_op jit(solution)/shard_map/ppermute | solution.py:182
  30.0 1.6 %collective-permute-done.5.refs_3_ = bf16[4,4096]{1,0:T(4,128)(2,1)S(1)} collective-permute-done((bf16[4,4096]{1,0:T(4,128)(2,1)S(1)}, bf16[4,4096]{1,0:T(4,128)(2,1)S(1)}, u32[]{:S(2)}, u32[]{:S(2)}) %collective-permute-start.5) | collective-permute-done | bytes 32800 | tf_op jit(solution)/shard_map/ppermute | solution.py:182
  31.5 0.2 collective-permute-done.4.refs_2_
  31.7 0.2 collective-permute-done.3.refs_1_
  32.0 0.1 collective-permute-start.8
  32.1 1.3 %collective-permute-start.7 = (bf16[4,4096]{1,0:T(4,128)(2,1)S(1)}, bf16[4,4096]{1,0:T(4,128)(2,1)S(1)}, u32[]{:S(2)}, u32[]{:S(2)}) collective-permute-start(bf16[4,4096]{1,0:T(4,128)(2,1)S(1)} %add_far.1.refs_0_), channel_id=1, source_target_pairs={{0,2},{1,3},{2,0},{3,1},{4,6},{5,7},{6,4},{7,5},{8,10},{9,11},{10,... | collective-permute-start | bytes 98312 | tf_op jit(solution)/shard_map/ppermute | solution.py:182
  33.3 0.6 %collective-permute-start.6 = (bf16[4,4096]{1,0:T(4,128)(2,1)S(1)}, bf16[4,4096]{1,0:T(4,128)(2,1)S(1)}, u32[]{:S(2)}, u32[]{:S(2)}) collective-permute-start(bf16[4,4096]{1,0:T(4,128)(2,1)S(1)} %add_far.1.refs_0_), channel_id=1, source_target_pairs={{0,1},{1,0},{2,3},{3,2},{4,5},{5,4},{6,7},{7,6},{8,9},{9,8},{10,11... | collective-permute-start | bytes 98312 | tf_op jit(solution)/shard_map/ppermute | solution.py:182
  33.9 1.6 %collective-permute-done.8.refs_3_ = bf16[4,4096]{1,0:T(4,128)(2,1)S(1)} collective-permute-done((bf16[4,4096]{1,0:T(4,128)(2,1)S(1)}, bf16[4,4096]{1,0:T(4,128)(2,1)S(1)}, u32[]{:S(2)}, u32[]{:S(2)}) %collective-permute-start.8) | collective-permute-done | bytes 32800 | tf_op jit(solution)/shard_map/ppermute | solution.py:182
  35.5 0.6 %collective-permute-done.7.refs_2_ = bf16[4,4096]{1,0:T(4,128)(2,1)S(1)} collective-permute-done((bf16[4,4096]{1,0:T(4,128)(2,1)S(1)}, bf16[4,4096]{1,0:T(4,128)(2,1)S(1)}, u32[]{:S(2)}, u32[]{:S(2)}) %collective-permute-start.7) | collective-permute-done | bytes 32800 | tf_op jit(solution)/shard_map/ppermute | solution.py:182
  36.2 0.0 collective-permute-done.6.refs_1_
  36.2 0.7 %lay.1 = bf16[4,16384]{1,0:T(4,128)(2,1)} custom-call(bf16[4,4096]{1,0:T(4,128)(2,1)S(1)} %add_far.1.refs_0_, bf16[4,4096]{1,0:T(4,128)(2,1)S(1)} %collective-permute-done.6.refs_1_, bf16[4,4096]{1,0:T(4,128)(2,1)S(1)} %collective-permute-done.7.refs_2_, bf16[4,4096]{1,0:T(4,128)(2,1)S(1)} %collective-permute-done.8.refs_3_), custom_call_target="tpu_custom_call" | custom-call | tf_op jit(solution)/shard_map/lay/pallas_call | solution.py:280
  (4 shorter events, 0.1 us)
Async XLA Ops:
  0.0 19.2 %slice-start = ((s8[16777216]{0:T(1024)(128)(4,1)}), s8[4194304]{0:T(1024)(128)(4,1)S(1)}, s32[]{:S(2)}) async-start(s8[16777216]{0:T(1024)(128)(4,1)} %bitcast.2), calls=%async_computation.1 | async-start | bytes 8388608
  4.5 14.7 %slice-start.1 = ((s8[16777216]{0:T(1024)(128)(4,1)}), s8[4194304]{0:T(1024)(128)(4,1)S(1)}, s32[]{:S(2)}) async-start(s8[16777216]{0:T(1024)(128)(4,1)} %bitcast.2), calls=%async_computation.2 | async-start | bytes 8388608
  4.5 14.7 %slice-start.2 = ((s8[16777216]{0:T(1024)(128)(4,1)}), s8[4194304]{0:T(1024)(128)(4,1)S(1)}, s32[]{:S(2)}) async-start(s8[16777216]{0:T(1024)(128)(4,1)} %bitcast.2), calls=%async_computation.3 | async-start | bytes 8388608
  4.5 14.7 %slice-start.3 = ((s8[16777216]{0:T(1024)(128)(4,1)}), s8[4194304]{0:T(1024)(128)(4,1)S(1)}, s32[]{:S(2)}) async-start(s8[16777216]{0:T(1024)(128)(4,1)} %bitcast.2), calls=%async_computation.4 | async-start | bytes 8388608
  21.3 2.5 %collective-permute-start = (bf16[4,4096]{1,0:T(4,128)(2,1)S(1)}, bf16[4,4096]{1,0:T(4,128)(2,1)S(1)}, u32[]{:S(2)}, u32[]{:S(2)}) collective-permute-start(bf16[4,4096]{1,0:T(4,128)(2,1)S(1)} %get-tuple-element.10), channel_id=1, source_target_pairs={{0,1},{1,0},{2,3},{3,2},{4,5},{5,4},{6,7},{7,6},{8,9},{9,8},{10,11... | collective-permute-start | bytes 98312 | tf_op jit(solution)/shard_map/ppermute | solution.py:182
  21.3 4.2 %collective-permute-start.1 = (bf16[4,4096]{1,0:T(4,128)(2,1)S(1)}, bf16[4,4096]{1,0:T(4,128)(2,1)S(1)}, u32[]{:S(2)}, u32[]{:S(2)}) collective-permute-start(bf16[4,4096]{1,0:T(4,128)(2,1)S(1)} %get-tuple-element.11), channel_id=1, source_target_pairs={{0,2},{1,3},{2,0},{3,1},{4,6},{5,7},{6,4},{7,5},{8,10},{9,11},{10,... | collective-permute-start | bytes 98312 | tf_op jit(solution)/shard_map/ppermute | solution.py:182
  21.5 4.0 %collective-permute-start.2 = (bf16[4,4096]{1,0:T(4,128)(2,1)S(1)}, bf16[4,4096]{1,0:T(4,128)(2,1)S(1)}, u32[]{:S(2)}, u32[]{:S(2)}) collective-permute-start(bf16[4,4096]{1,0:T(4,128)(2,1)S(1)} %get-tuple-element.12), channel_id=1, source_target_pairs={{0,3},{1,2},{2,1},{3,0},{4,7},{5,6},{6,5},{7,4},{8,11},{9,10},{10,... | collective-permute-start | bytes 98312 | tf_op jit(solution)/shard_map/ppermute | solution.py:182
  25.5 6.0 %collective-permute-start.5 = (bf16[4,4096]{1,0:T(4,128)(2,1)S(1)}, bf16[4,4096]{1,0:T(4,128)(2,1)S(1)}, u32[]{:S(2)}, u32[]{:S(2)}) collective-permute-start(bf16[4,4096]{1,0:T(4,128)(2,1)S(1)} %add_near.1.refs_0_), channel_id=1, source_target_pairs={{0,12},{1,13},{2,14},{3,15},{4,8},{5,9},{6,10},{7,11},{8,4},{9,5},... | collective-permute-start | bytes 98312 | tf_op jit(solution)/shard_map/ppermute | solution.py:182
  26.5 5.2 %collective-permute-start.4 = (bf16[4,4096]{1,0:T(4,128)(2,1)S(1)}, bf16[4,4096]{1,0:T(4,128)(2,1)S(1)}, u32[]{:S(2)}, u32[]{:S(2)}) collective-permute-start(bf16[4,4096]{1,0:T(4,128)(2,1)S(1)} %add_near.1.refs_0_), channel_id=1, source_target_pairs={{0,8},{1,9},{2,10},{3,11},{4,12},{5,13},{6,14},{7,15},{8,0},{9,1},... | collective-permute-start | bytes 98312 | tf_op jit(solution)/shard_map/ppermute | solution.py:182
  27.4 4.6 %collective-permute-start.3 = (bf16[4,4096]{1,0:T(4,128)(2,1)S(1)}, bf16[4,4096]{1,0:T(4,128)(2,1)S(1)}, u32[]{:S(2)}, u32[]{:S(2)}) collective-permute-start(bf16[4,4096]{1,0:T(4,128)(2,1)S(1)} %add_near.1.refs_0_), channel_id=1, source_target_pairs={{0,4},{1,5},{2,6},{3,7},{4,0},{5,1},{6,2},{7,3},{8,12},{9,13},{10,... | collective-permute-start | bytes 98312 | tf_op jit(solution)/shard_map/ppermute | solution.py:182
  32.0 3.5 %collective-permute-start.8 = (bf16[4,4096]{1,0:T(4,128)(2,1)S(1)}, bf16[4,4096]{1,0:T(4,128)(2,1)S(1)}, u32[]{:S(2)}, u32[]{:S(2)}) collective-permute-start(bf16[4,4096]{1,0:T(4,128)(2,1)S(1)} %add_far.1.refs_0_), channel_id=1, source_target_pairs={{0,3},{1,2},{2,1},{3,0},{4,7},{5,6},{6,5},{7,4},{8,11},{9,10},{10,... | collective-permute-start | bytes 98312 | tf_op jit(solution)/shard_map/ppermute | solution.py:182
  32.1 4.1 %collective-permute-start.7 = (bf16[4,4096]{1,0:T(4,128)(2,1)S(1)}, bf16[4,4096]{1,0:T(4,128)(2,1)S(1)}, u32[]{:S(2)}, u32[]{:S(2)}) collective-permute-start(bf16[4,4096]{1,0:T(4,128)(2,1)S(1)} %add_far.1.refs_0_), channel_id=1, source_target_pairs={{0,2},{1,3},{2,0},{3,1},{4,6},{5,7},{6,4},{7,5},{8,10},{9,11},{10,... | collective-permute-start | bytes 98312 | tf_op jit(solution)/shard_map/ppermute | solution.py:182
  33.3 2.8 %collective-permute-start.6 = (bf16[4,4096]{1,0:T(4,128)(2,1)S(1)}, bf16[4,4096]{1,0:T(4,128)(2,1)S(1)}, u32[]{:S(2)}, u32[]{:S(2)}) collective-permute-start(bf16[4,4096]{1,0:T(4,128)(2,1)S(1)} %add_far.1.refs_0_), channel_id=1, source_target_pairs={{0,1},{1,0},{2,3},{3,2},{4,5},{5,4},{6,7},{7,6},{8,9},{9,8},{10,11... | collective-permute-start | bytes 98312 | tf_op jit(solution)/shard_map/ppermute | solution.py:182

commit v9 on v8

--- a/solution.py
+++ b/solution.py
@@ -129,11 +129,8 @@
     packed[...] = staged[...].astype(jnp.bfloat16)
 
 
-def project_kernel(heads_dev, packed, weight, left, *refs):
-    outs, attended = refs[:-1], refs[-1]
+def project_kernel(heads_dev, count, packed, weight, left, out, attended):
     rows = left.shape[0]
-    part = outs[0].shape[1]
-    quarter = lax.rem(lax.axis_index("kvp"), len(outs) + 1)
     blocks = packed[...].astype(jnp.float32)
     stats = blocks[:, rows]
     for r in range(rows):
@@ -148,18 +145,25 @@
         [attended[pl.ds(j, rows, stride=heads_dev), :].astype(jnp.bfloat16) for j in range(heads_dev)], axis=1
     )
     left[...] = rounded
-    for x, out in enumerate(outs):
-        start = pl.multiple_of(jnp.bitwise_xor(quarter, x + 1) * part, part)
-        terms = jnp.dot(rounded, weight[:, pl.ds(start, part)], preferred_element_type=jnp.float32)
-        out[...] = terms.astype(jnp.bfloat16)
-
-
-def project_own_kernel(left, weight, out):
-    part = out.shape[1]
-    quarter = lax.rem(lax.axis_index("kvp"), weight.shape[1] // part)
-    start = pl.multiple_of(quarter * part, part)
-    terms = jnp.dot(left[...], weight[:, pl.ds(start, part)], preferred_element_type=jnp.float32)
-    out[...] = terms.astype(jnp.bfloat16)
+    project_quarters(count, (1, 3), rounded, weight, out)
+
+
+def project_quarters(count, partners, left, weight, out):
+    part = out.shape[2]
+    quarter = lax.rem(lax.axis_index("kvp"), count)
+    for i, x in enumerate(partners):
+        start = pl.multiple_of(jnp.bitwise_xor(quarter, x) * part, part)
+        terms = jnp.dot(left, weight[:, pl.ds(start, part)], preferred_element_type=jnp.float32)
+        out[i] = terms.astype(out.dtype)
+
+
+def project_own_kernel(count, left, weight, out):
+    project_quarters(count, (0, 2), left[...], weight, out)
+
+
+def add_core_kernel(own, arrived, keep, send):
+    keep[...] = own[0] + arrived[0].astype(jnp.float32)
+    send[...] = (own[1] + arrived[1].astype(jnp.float32)).astype(send.dtype)
 
 
 def add_kernel(*refs):
@@ -236,33 +240,46 @@
 
     resident = pltpu.with_memory_space_constraint(out_weight, pltpu.VMEM)
     depth = heads_dev * HD
-    left, *others = pl.pallas_call(
-        functools.partial(project_kernel, heads_dev),
-        out_shape=[jax.ShapeDtypeStruct((rows, depth), jnp.bfloat16)]
-        + [jax.ShapeDtypeStruct((rows, part), jnp.bfloat16)] * (inner - 1),
-        in_specs=[VMEM, VMEM],
-        out_specs=[VMEM] * inner,
+    def cost(count):
+        return pl.CostEstimate(
+            flops=2 * rows * depth * part * count, bytes_accessed=2 * depth * part * count, transcendentals=0
+        )
+
+    small = pltpu.CompilerParams(vmem_limit_bytes=SMALL_VMEM)
+    left, others = pl.pallas_call(
+        functools.partial(project_kernel, heads_dev, inner),
+        out_shape=[
+            jax.ShapeDtypeStruct((rows, depth), jnp.bfloat16),
+            jax.ShapeDtypeStruct((2, rows, part), jnp.bfloat16),
+        ],
+        in_specs=[VMEM] * 2,
+        out_specs=[VMEM] * 2,
         scratch_shapes=[pltpu.VMEM((rows * heads_dev, HD), jnp.float32)],
-        compiler_params=pltpu.CompilerParams(vmem_limit_bytes=PROJECT_VMEM),
-        cost_estimate=pl.CostEstimate(
-            flops=2 * rows * depth * part * (inner - 1),
-            bytes_accessed=2 * depth * part * (inner - 1),
-            transcendentals=0,
-        ),
+        compiler_params=small,
+        cost_estimate=cost(2),
         name="project_others",
     )(received, resident)
-    sent = [exchange(others[x - 1], x, devices) for x in range(1, inner)]
+    arrived = exchange(others, 1, devices)
     own = pl.pallas_call(
-        project_own_kernel,
-        out_shape=jax.ShapeDtypeStruct((rows, part), jnp.bfloat16),
-        in_specs=[VMEM, VMEM],
+        functools.partial(project_own_kernel, inner),
+        out_shape=jax.ShapeDtypeStruct((2, rows, part), jnp.float32),
+        in_specs=[VMEM] * 2,
         out_specs=VMEM,
-        compiler_params=pltpu.CompilerParams(vmem_limit_bytes=PROJECT_VMEM),
-        cost_estimate=pl.CostEstimate(
-            flops=2 * rows * depth * part, bytes_accessed=2 * depth * part, transcendentals=0
-        ),
+        compiler_params=small,
+        cost_estimate=cost(2),
         name="project_own",
     )(left, resident)
+    keep, send = pl.pallas_call(
+        add_core_kernel,
+        out_shape=[
+            jax.ShapeDtypeStruct((rows, part), jnp.float32),
+            jax.ShapeDtypeStruct((rows, part), jnp.bfloat16),
+        ],
+        in_specs=[VMEM] * 2,
+        out_specs=[VMEM] * 2,
+        compiler_params=small,
+        name="add_core",
+    )(own, arrived)
 
     def add(terms, name):
         return pl.pallas_call(
@@ -270,13 +287,14 @@
             out_shape=jax.ShapeDtypeStruct((rows, part), jnp.bfloat16),
             in_specs=[VMEM] * len(terms),
             out_specs=VMEM,
-            compiler_params=pltpu.CompilerParams(vmem_limit_bytes=SMALL_VMEM),
+            compiler_params=small,
             name=name,
         )(*terms)
 
-    mine = add([own] + sent, "add_near")
+    mine = add([keep, exchange(send, 2, devices)], "add_near")
     mine = add([mine] + [exchange(mine, x * inner, devices) for x in range(1, outer)], "add_far")
-    parts = [mine] + [exchange(mine, x, devices) for x in range(1, inner)]
+    across = exchange(mine, 2, devices)
+    parts = [mine, exchange(mine, 1, devices), across, exchange(across, 1, devices)]
     return pl.pallas_call(
         lay_kernel,
         out_shape=jax.ShapeDtypeStruct((rows, features), jnp.bfloat16),

time: 37 us -> 38.5 us (1.041)
  waiting for transfers between devices: 5.89 us -> 10.5 us
  starting transfers between devices: 8.24 us -> 5.13 us
    ppermute x9 -> x8, waiting for transfers between devices: 5.89 us -> 10.5 us  [exchange(): lax.ppermute(array, 'kvp', [(i, i ^ partner) for i in range(devices)])]
    ppermute x9 -> x8, starting transfers between devices: 8.24 us -> 5.13 us  [exchange(): lax.ppermute(array, 'kvp', [(i, i ^ partner) for i in range(devices)])]
    pallas_call x2 -> x3, Pallas kernels: 2.73 us -> 2.76 us  [the longest x1 1.53 us: body(): pl.pallas_call(functools.partial(project_kernel, heads_dev, inner), out_s...]
  transfers between devices with their start and end apart: 9 -> 8, of which waited for: 6 -> 6; matrix products, arithmetic and copies ran while one was open for 0% -> 0% of each run, Pallas kernels for 2% -> 3%
where the time goes in v9:
time: 38.5 us; the launch traced here: 38.4 us
  blocking collectives  14.6 us (38%)
  waiting for transfers between devices  10.5 us (27%)
  Pallas kernels  8.02 us (21%)
  starting transfers between devices  5.13 us (13%)
    all_to_all x1, blocking collectives, body(): lax.all_to_all(packed, 'kvp', split_axis=0, concat_axis=0, tiled=True)  14.6 us
    ppermute x8, waiting for transfers between devices, exchange(): lax.ppermute(array, 'kvp', [(i, i ^ partner) for i in range(devices)])  10.5 us
    ppermute x8, starting transfers between devices, exchange(): lax.ppermute(array, 'kvp', [(i, i ^ partner) for i in range(devices)])  5.13 us
    pallas_call x1, Pallas kernels, body(): pl.pallas_call(functools.partial(attend_kernel, heads_dev, devices), out_...  4.51 us
    pallas_call x1, Pallas kernels, body(): pl.pallas_call(functools.partial(project_kernel, heads_dev, inner), out_s...  1.53 us
    pallas_call x1, Pallas kernels, body(): pl.pallas_call(functools.partial(project_own_kernel, inner), out_shape=ja...  1.21 us
  transfers between devices with their start and end apart: 8, of which 6 were waited for; matrix products, arithmetic and copies ran while one was open for 0% of the time, Pallas kernels for 3%

profile of v9, /device:TPU:0, one launch (start us, length us, event | category | flops | bytes accessed | tf_op | source)
XLA Modules:
  0.0 38.4 jit_solution(6928817089735748244)
XLA Ops:
  0.0 0.0 slice-start
  0.0 4.5 %attend.1.staged = f32[16,5,4,128]{3,2,1,0:T(4,128)S(1)} custom-call(s32[4,12]{1,0:T(4,128)} %refs_0_.1, s32[4]{0:T(128)} %refs_1_.1, f32[4,48]{1,0:T(4,128)} %bitcast.4, f32[4,48]{1,0:T(4,128)} %bitcast.5, bf16[4,8192]{1,0:T(4,128)(2,1)} %refs_4_.1, bf16[48,64,512]{2,1,0:T(8,128)(2,1)} %refs_5_.1, bf16[48,64,512]{2,1,0:T(8,128)(2,1)} %refs_6_.1), custom_call_target="tpu_custom_call" | custom-call | flops 100663296 | bytes 6291456 | tf_op jit(solution)/shard_map/attend/pallas_call | solution.py:203
  4.5 0.0 slice-start.1
  4.5 0.0 slice-start.2
  4.5 0.0 slice-start.3
  4.6 14.6 %all_to_all.5.packed = bf16[16,5,4,128]{3,2,1,0:T(4,128)(2,1)S(1)} all-to-all(bf16[16,5,4,128]{3,2,1,0:T(4,128)(2,1)S(1)} %pack.1), channel_id=1, replica_groups=mesh['group'=2,'kvp'=16] {'kvp'}, dimensions={0} | all-to-all | bytes 163840 | tf_op jit(solution)/shard_map/all_to_all | solution.py:239
  19.2 0.0 slice-done
  19.2 0.0 slice-done.1
  19.2 0.0 slice-done.2
  19.2 0.0 slice-done.3
  19.2 1.5 %project_others.1 = (bf16[4,512]{1,0:T(4,128)(2,1)S(1)}, bf16[2,4,4096]{2,1,0:T(4,128)(2,1)S(1)}) custom-call(bf16[16,5,4,128]{3,2,1,0:T(4,128)(2,1)S(1)} %all_to_all.5.packed, bf16[512,16384]{1,0:T(8,128)(2,1)S(1)} %bitcast.3), custom_call_target="tpu_custom_call" | custom-call | flops 33554432 | bytes 8388608 | tf_op jit(solution)/shard_map/project_others/pallas_call | solution.py:249
  20.7 0.0 collective-permute-start
  20.8 1.2 %project_own.1.own = f32[2,4,4096]{2,1,0:T(4,128)S(1)} custom-call(bf16[4,512]{1,0:T(4,128)(2,1)S(1)} %get-tuple-element.9.left, bf16[512,16384]{1,0:T(8,128)(2,1)S(1)} %bitcast.3), custom_call_target="tpu_custom_call" | custom-call | flops 33554432 | bytes 8388608 | tf_op jit(solution)/shard_map/project_own/pallas_call | solution.py:263
  22.0 0.1 collective-permute-done.arrived
  22.0 0.2 collective-permute-start.1
  22.2 3.8 %collective-permute-done.1.refs_1_ = bf16[4,4096]{1,0:T(4,128)(2,1)S(1)} collective-permute-done((bf16[4,4096]{1,0:T(4,128)(2,1)S(1)}, bf16[4,4096]{1,0:T(4,128)(2,1)S(1)}, u32[]{:S(2)}, u32[]{:S(2)}) %collective-permute-start.1) | collective-permute-done | bytes 32800 | tf_op jit(solution)/shard_map/ppermute | solution.py:186
  26.0 0.8 %collective-permute-start.4 = (bf16[4,4096]{1,0:T(4,128)(2,1)S(1)}, bf16[4,4096]{1,0:T(4,128)(2,1)S(1)}, u32[]{:S(2)}, u32[]{:S(2)}) collective-permute-start(bf16[4,4096]{1,0:T(4,128)(2,1)S(1)} %add_near.1.refs_0_), channel_id=1, source_target_pairs={{0,12},{1,13},{2,14},{3,15},{4,8},{5,9},{6,10},{7,11},{8,4},{9,5},... | collective-permute-start | bytes 98312 | tf_op jit(solution)/shard_map/ppermute | solution.py:186
  26.8 0.9 %collective-permute-start.3 = (bf16[4,4096]{1,0:T(4,128)(2,1)S(1)}, bf16[4,4096]{1,0:T(4,128)(2,1)S(1)}, u32[]{:S(2)}, u32[]{:S(2)}) collective-permute-start(bf16[4,4096]{1,0:T(4,128)(2,1)S(1)} %add_near.1.refs_0_), channel_id=1, source_target_pairs={{0,8},{1,9},{2,10},{3,11},{4,12},{5,13},{6,14},{7,15},{8,0},{9,1},... | collective-permute-start | bytes 98312 | tf_op jit(solution)/shard_map/ppermute | solution.py:186
  27.7 2.8 %collective-permute-start.2 = (bf16[4,4096]{1,0:T(4,128)(2,1)S(1)}, bf16[4,4096]{1,0:T(4,128)(2,1)S(1)}, u32[]{:S(2)}, u32[]{:S(2)}) collective-permute-start(bf16[4,4096]{1,0:T(4,128)(2,1)S(1)} %add_near.1.refs_0_), channel_id=1, source_target_pairs={{0,4},{1,5},{2,6},{3,7},{4,0},{5,1},{6,2},{7,3},{8,12},{9,13},{10,... | collective-permute-start | bytes 98312 | tf_op jit(solution)/shard_map/ppermute | solution.py:186
  30.5 1.4 %collective-permute-done.4.refs_3_ = bf16[4,4096]{1,0:T(4,128)(2,1)S(1)} collective-permute-done((bf16[4,4096]{1,0:T(4,128)(2,1)S(1)}, bf16[4,4096]{1,0:T(4,128)(2,1)S(1)}, u32[]{:S(2)}, u32[]{:S(2)}) %collective-permute-start.4) | collective-permute-done | bytes 32800 | tf_op jit(solution)/shard_map/ppermute | solution.py:186
  31.9 0.5 %collective-permute-done.3.refs_2_ = bf16[4,4096]{1,0:T(4,128)(2,1)S(1)} collective-permute-done((bf16[4,4096]{1,0:T(4,128)(2,1)S(1)}, bf16[4,4096]{1,0:T(4,128)(2,1)S(1)}, u32[]{:S(2)}, u32[]{:S(2)}) %collective-permute-start.3) | collective-permute-done | bytes 32800 | tf_op jit(solution)/shard_map/ppermute | solution.py:186
  32.5 0.0 collective-permute-done.2.refs_1_
  32.5 0.5 %collective-permute-start.6 = (bf16[4,4096]{1,0:T(4,128)(2,1)S(1)}, bf16[4,4096]{1,0:T(4,128)(2,1)S(1)}, u32[]{:S(2)}, u32[]{:S(2)}) collective-permute-start(bf16[4,4096]{1,0:T(4,128)(2,1)S(1)} %add_far.1.refs_0_), channel_id=1, source_target_pairs={{0,2},{1,3},{2,0},{3,1},{4,6},{5,7},{6,4},{7,5},{8,10},{9,11},{10,... | collective-permute-start | bytes 98312 | tf_op jit(solution)/shard_map/ppermute | solution.py:186
  33.0 0.0 collective-permute-start.5
  33.0 3.5 %collective-permute-done.6.refs_2_ = bf16[4,4096]{1,0:T(4,128)(2,1)S(1)} collective-permute-done((bf16[4,4096]{1,0:T(4,128)(2,1)S(1)}, bf16[4,4096]{1,0:T(4,128)(2,1)S(1)}, u32[]{:S(2)}, u32[]{:S(2)}) %collective-permute-start.6) | collective-permute-done | bytes 32800 | tf_op jit(solution)/shard_map/ppermute | solution.py:186
  36.5 0.0 collective-permute-start.7
  36.5 0.0 collective-permute-done.5.refs_1_
  36.5 1.2 %collective-permute-done.7.refs_3_ = bf16[4,4096]{1,0:T(4,128)(2,1)S(1)} collective-permute-done((bf16[4,4096]{1,0:T(4,128)(2,1)S(1)}, bf16[4,4096]{1,0:T(4,128)(2,1)S(1)}, u32[]{:S(2)}, u32[]{:S(2)}) %collective-permute-start.7) | collective-permute-done | bytes 32800 | tf_op jit(solution)/shard_map/ppermute | solution.py:186
  37.7 0.7 %lay.1 = bf16[4,16384]{1,0:T(4,128)(2,1)} custom-call(bf16[4,4096]{1,0:T(4,128)(2,1)S(1)} %add_far.1.refs_0_, bf16[4,4096]{1,0:T(4,128)(2,1)S(1)} %collective-permute-done.5.refs_1_, bf16[4,4096]{1,0:T(4,128)(2,1)S(1)} %collective-permute-done.6.refs_2_, bf16[4,4096]{1,0:T(4,128)(2,1)S(1)} %collective-permute-done.7.refs_3_), custom_call_target="tpu_custom_call" | custom-call | tf_op jit(solution)/shard_map/lay/pallas_call | solution.py:298
  (5 shorter events, 0.1 us)
Async XLA Ops:
  0.0 19.2 %slice-start = ((s8[16777216]{0:T(1024)(128)(4,1)}), s8[4194304]{0:T(1024)(128)(4,1)S(1)}, s32[]{:S(2)}) async-start(s8[16777216]{0:T(1024)(128)(4,1)} %bitcast.2), calls=%async_computation.1 | async-start | bytes 8388608
  4.5 14.7 %slice-start.1 = ((s8[16777216]{0:T(1024)(128)(4,1)}), s8[4194304]{0:T(1024)(128)(4,1)S(1)}, s32[]{:S(2)}) async-start(s8[16777216]{0:T(1024)(128)(4,1)} %bitcast.2), calls=%async_computation.2 | async-start | bytes 8388608
  4.5 14.7 %slice-start.2 = ((s8[16777216]{0:T(1024)(128)(4,1)}), s8[4194304]{0:T(1024)(128)(4,1)S(1)}, s32[]{:S(2)}) async-start(s8[16777216]{0:T(1024)(128)(4,1)} %bitcast.2), calls=%async_computation.3 | async-start | bytes 8388608
  4.5 14.7 %slice-start.3 = ((s8[16777216]{0:T(1024)(128)(4,1)}), s8[4194304]{0:T(1024)(128)(4,1)S(1)}, s32[]{:S(2)}) async-start(s8[16777216]{0:T(1024)(128)(4,1)} %bitcast.2), calls=%async_computation.4 | async-start | bytes 8388608
  20.7 1.3 %collective-permute-start = (bf16[2,4,4096]{2,1,0:T(4,128)(2,1)S(1)}, bf16[2,4,4096]{2,1,0:T(4,128)(2,1)S(1)}, u32[]{:S(2)}, u32[]{:S(2)}) collective-permute-start(bf16[2,4,4096]{2,1,0:T(4,128)(2,1)S(1)} %get-tuple-element.10), channel_id=1, source_target_pairs={{0,1},{1,0},{2,3},{3,2},{4,5},{5,4},{6,7},{7,6},{8,9},{9,8},{10,11... | collective-permute-start | bytes 196616 | tf_op jit(solution)/shard_map/ppermute | solution.py:186
  22.0 4.0 %collective-permute-start.1 = (bf16[4,4096]{1,0:T(4,128)(2,1)S(1)}, bf16[4,4096]{1,0:T(4,128)(2,1)S(1)}, u32[]{:S(2)}, u32[]{:S(2)}) collective-permute-start(bf16[4,4096]{1,0:T(4,128)(2,1)S(1)} %get-tuple-element.12), channel_id=1, source_target_pairs={{0,2},{1,3},{2,0},{3,1},{4,6},{5,7},{6,4},{7,5},{8,10},{9,11},{10,... | collective-permute-start | bytes 98312 | tf_op jit(solution)/shard_map/ppermute | solution.py:186
  26.0 5.9 %collective-permute-start.4 = (bf16[4,4096]{1,0:T(4,128)(2,1)S(1)}, bf16[4,4096]{1,0:T(4,128)(2,1)S(1)}, u32[]{:S(2)}, u32[]{:S(2)}) collective-permute-start(bf16[4,4096]{1,0:T(4,128)(2,1)S(1)} %add_near.1.refs_0_), channel_id=1, source_target_pairs={{0,12},{1,13},{2,14},{3,15},{4,8},{5,9},{6,10},{7,11},{8,4},{9,5},... | collective-permute-start | bytes 98312 | tf_op jit(solution)/shard_map/ppermute | solution.py:186
  26.8 5.6 %collective-permute-start.3 = (bf16[4,4096]{1,0:T(4,128)(2,1)S(1)}, bf16[4,4096]{1,0:T(4,128)(2,1)S(1)}, u32[]{:S(2)}, u32[]{:S(2)}) collective-permute-start(bf16[4,4096]{1,0:T(4,128)(2,1)S(1)} %add_near.1.refs_0_), channel_id=1, source_target_pairs={{0,8},{1,9},{2,10},{3,11},{4,12},{5,13},{6,14},{7,15},{8,0},{9,1},... | collective-permute-start | bytes 98312 | tf_op jit(solution)/shard_map/ppermute | solution.py:186
  27.7 4.8 %collective-permute-start.2 = (bf16[4,4096]{1,0:T(4,128)(2,1)S(1)}, bf16[4,4096]{1,0:T(4,128)(2,1)S(1)}, u32[]{:S(2)}, u32[]{:S(2)}) collective-permute-start(bf16[4,4096]{1,0:T(4,128)(2,1)S(1)} %add_near.1.refs_0_), channel_id=1, source_target_pairs={{0,4},{1,5},{2,6},{3,7},{4,0},{5,1},{6,2},{7,3},{8,12},{9,13},{10,... | collective-permute-start | bytes 98312 | tf_op jit(solution)/shard_map/ppermute | solution.py:186
  32.5 4.0 %collective-permute-start.6 = (bf16[4,4096]{1,0:T(4,128)(2,1)S(1)}, bf16[4,4096]{1,0:T(4,128)(2,1)S(1)}, u32[]{:S(2)}, u32[]{:S(2)}) collective-permute-start(bf16[4,4096]{1,0:T(4,128)(2,1)S(1)} %add_far.1.refs_0_), channel_id=1, source_target_pairs={{0,2},{1,3},{2,0},{3,1},{4,6},{5,7},{6,4},{7,5},{8,10},{9,11},{10,... | collective-permute-start | bytes 98312 | tf_op jit(solution)/shard_map/ppermute | solution.py:186
  33.0 3.5 %collective-permute-start.5 = (bf16[4,4096]{1,0:T(4,128)(2,1)S(1)}, bf16[4,4096]{1,0:T(4,128)(2,1)S(1)}, u32[]{:S(2)}, u32[]{:S(2)}) collective-permute-start(bf16[4,4096]{1,0:T(4,128)(2,1)S(1)} %add_far.1.refs_0_), channel_id=1, source_target_pairs={{0,1},{1,0},{2,3},{3,2},{4,5},{5,4},{6,7},{7,6},{8,9},{9,8},{10,11... | collective-permute-start | bytes 98312 | tf_op jit(solution)/shard_map/ppermute | solution.py:186
  36.5 1.2 %collective-permute-start.7 = (bf16[4,4096]{1,0:T(4,128)(2,1)S(1)}, bf16[4,4096]{1,0:T(4,128)(2,1)S(1)}, u32[]{:S(2)}, u32[]{:S(2)}) collective-permute-start(bf16[4,4096]{1,0:T(4,128)(2,1)S(1)} %collective-permute-done.6.refs_2_), channel_id=1, source_target_pairs={{0,1},{1,0},{2,3},{3,2},{4,5},{5,4},{6,7},{7,6},{8,9},{9,8},{10,11... | collective-permute-start | bytes 98312 | tf_op jit(solution)/shard_map/ppermute | solution.py:186

commit v10 on v9

--- a/solution.py
+++ b/solution.py
@@ -12,6 +12,7 @@
 PAGE = 64
 ATTEND_VMEM = 24 * 1024 * 1024
 PROJECT_VMEM = 8 * 1024 * 1024
+EVEN, ODD = 0, 1
 EXCHANGE_FLOPS = 40_000_000_000
 SMALL_VMEM = 8 * 1024 * 1024
 VMEM = pl.BlockSpec(memory_space=pltpu.VMEM)
@@ -129,7 +130,7 @@
     packed[...] = staged[...].astype(jnp.bfloat16)
 
 
-def project_kernel(heads_dev, count, packed, weight, left, out, attended):
+def project_kernel(heads_dev, packed, weight, left, out, attended):
     rows = left.shape[0]
     blocks = packed[...].astype(jnp.float32)
     stats = blocks[:, rows]
@@ -145,25 +146,26 @@
         [attended[pl.ds(j, rows, stride=heads_dev), :].astype(jnp.bfloat16) for j in range(heads_dev)], axis=1
     )
     left[...] = rounded
-    project_quarters(count, (1, 3), rounded, weight, out)
-
-
-def project_quarters(count, partners, left, weight, out):
-    part = out.shape[2]
-    quarter = lax.rem(lax.axis_index("kvp"), count)
-    for i, x in enumerate(partners):
-        start = pl.multiple_of(jnp.bitwise_xor(quarter, x) * part, part)
-        terms = jnp.dot(left, weight[:, pl.ds(start, part)], preferred_element_type=jnp.float32)
-        out[i] = terms.astype(out.dtype)
-
-
-def project_own_kernel(count, left, weight, out):
-    project_quarters(count, (0, 2), left[...], weight, out)
-
-
-def add_core_kernel(own, arrived, keep, send):
-    keep[...] = own[0] + arrived[0].astype(jnp.float32)
-    send[...] = (own[1] + arrived[1].astype(jnp.float32)).astype(send.dtype)
+    project_half(1, rounded, weight, out)
+
+
+def half_of_device():
+    return lax.rem(lax.div(lax.axis_index("kvp"), 2), 2)
+
+
+def project_half(other, left, weight, *outs):
+    part = outs[0].shape[1]
+    width = part // 2
+    half = jnp.bitwise_xor(half_of_device(), other)
+    for i in range(2):
+        start = pl.multiple_of(half * part + i * width, width)
+        terms = jnp.dot(left, weight[:, pl.ds(start, width)], preferred_element_type=jnp.float32)
+        for out in outs:
+            out[:, i * width : (i + 1) * width] = terms.astype(out.dtype)
+
+
+def project_own_kernel(left, weight, keep, send):
+    project_half(0, left[...], weight, keep, send)
 
 
 def add_kernel(*refs):
@@ -173,17 +175,26 @@
     refs[-1][...] = terms[0].astype(refs[-1].dtype)
 
 
-def lay_kernel(*refs):
-    parts, out = refs[:-1], refs[-1]
-    quarter = lax.rem(lax.axis_index("kvp"), len(parts))
-    width = parts[0].shape[1]
-    for x, part in enumerate(parts):
-        start = pl.multiple_of(jnp.bitwise_xor(quarter, x) * width, width)
-        out[:, pl.ds(start, width)] = part[...]
-
-
-def exchange(array, partner, devices):
-    return lax.ppermute(array, "kvp", [(i, i ^ partner) for i in range(devices)])
+def lay_kernel(mine, from_odd, from_core, from_far, out):
+    part = mine.shape[1]
+    odd = lax.rem(lax.axis_index("kvp"), 2) == 1
+    half = half_of_device()
+    here = pl.multiple_of(half * part, part)
+    there = pl.multiple_of((1 - half) * part, part)
+
+    @pl.when(odd)
+    def _():
+        out[:, pl.ds(here, part)] = mine[...]
+        out[:, pl.ds(there, part)] = from_odd[...]
+
+    @pl.when(jnp.logical_not(odd))
+    def _():
+        out[:, pl.ds(here, part)] = from_core[...]
+        out[:, pl.ds(there, part)] = from_far[...]
+
+
+def exchange(array, partner, devices, sources):
+    return lax.ppermute(array, "kvp", [(i, i ^ partner) for i in range(devices) if i % 2 == sources])
 
 
 def in_hbm(array):
@@ -197,9 +208,6 @@
     heads_dev = out_weight.shape[0] // HD
     heads = queries.shape[1] // HD
     features = out_weight.shape[1]
-    inner = 4
-    outer = devices // inner
-    part = features // inner
     staged = pl.pallas_call(
         functools.partial(attend_kernel, heads_dev, devices),
         out_shape=jax.ShapeDtypeStruct((devices, rows + 1, heads_dev, HD), jnp.float32),
@@ -240,69 +248,61 @@
 
     resident = pltpu.with_memory_space_constraint(out_weight, pltpu.VMEM)
     depth = heads_dev * HD
+    part = features // 2
+
     def cost(count):
         return pl.CostEstimate(
             flops=2 * rows * depth * part * count, bytes_accessed=2 * depth * part * count, transcendentals=0
         )
 
     small = pltpu.CompilerParams(vmem_limit_bytes=SMALL_VMEM)
+    rounded = jax.ShapeDtypeStruct((rows, part), jnp.bfloat16)
     left, others = pl.pallas_call(
-        functools.partial(project_kernel, heads_dev, inner),
-        out_shape=[
-            jax.ShapeDtypeStruct((rows, depth), jnp.bfloat16),
-            jax.ShapeDtypeStruct((2, rows, part), jnp.bfloat16),
-        ],
+        functools.partial(project_kernel, heads_dev),
+        out_shape=[jax.ShapeDtypeStruct((rows, depth), jnp.bfloat16), rounded],
         in_specs=[VMEM] * 2,
         out_specs=[VMEM] * 2,
         scratch_shapes=[pltpu.VMEM((rows * heads_dev, HD), jnp.float32)],
         compiler_params=small,
-        cost_estimate=cost(2),
+        cost_estimate=cost(1),
         name="project_others",
     )(received, resident)
-    arrived = exchange(others, 1, devices)
-    own = pl.pallas_call(
-        functools.partial(project_own_kernel, inner),
-        out_shape=jax.ShapeDtypeStruct((2, rows, part), jnp.float32),
-        in_specs=[VMEM] * 2,
-        out_specs=VMEM,
-        compiler_params=small,
-        cost_estimate=cost(2),
-        name="project_own",
-    )(left, resident)
+    from_far = exchange(others, 3, devices, EVEN)
+    from_odd = exchange(others, 2, devices, ODD)
     keep, send = pl.pallas_call(
-        add_core_kernel,
-        out_shape=[
-            jax.ShapeDtypeStruct((rows, part), jnp.float32),
-            jax.ShapeDtypeStruct((rows, part), jnp.bfloat16),
-        ],
+        project_own_kernel,
+        out_shape=[jax.ShapeDtypeStruct((rows, part), jnp.float32), rounded],
         in_specs=[VMEM] * 2,
         out_specs=[VMEM] * 2,
         compiler_params=small,
-        name="add_core",
-    )(own, arrived)
+        cost_estimate=cost(1),
+        name="project_own",
+    )(left, resident)
+    from_core = exchange(send, 1, devices, EVEN)
 
     def add(terms, name):
         return pl.pallas_call(
             add_kernel,
-            out_shape=jax.ShapeDtypeStruct((rows, part), jnp.bfloat16),
+            out_shape=rounded,
             in_specs=[VMEM] * len(terms),
             out_specs=VMEM,
             compiler_params=small,
             name=name,
         )(*terms)
 
-    mine = add([keep, exchange(send, 2, devices)], "add_near")
-    mine = add([mine] + [exchange(mine, x * inner, devices) for x in range(1, outer)], "add_far")
-    across = exchange(mine, 2, devices)
-    parts = [mine, exchange(mine, 1, devices), across, exchange(across, 1, devices)]
+    mine = add([keep, from_core, from_odd, from_far], "add_near")
+    mine = add([mine] + [exchange(mine, x * 4, devices, ODD) for x in range(1, devices // 4)], "add_far")
+    from_odd = exchange(mine, 2, devices, ODD)
+    from_core = exchange(mine, 1, devices, ODD)
+    from_far = exchange(mine, 3, devices, ODD)
     return pl.pallas_call(
         lay_kernel,
         out_shape=jax.ShapeDtypeStruct((rows, features), jnp.bfloat16),
-        in_specs=[VMEM] * inner,
+        in_specs=[VMEM] * 4,
         out_specs=VMEM,
-        compiler_params=pltpu.CompilerParams(vmem_limit_bytes=SMALL_VMEM),
+        compiler_params=small,
         name="lay",
-    )(*parts)
+    )(mine, from_odd, from_core, from_far)
 
 
 def solution(mesh):

time: 38.5 us -> 47.4 us (1.23)
  the two profiles are of different devices: /device:TPU:0 before, /device:TPU:1 now
where the time goes in v10:
time: 47.4 us; the launch traced here: 47.1 us
  starting transfers between devices  19.7 us (42%)
  blocking collectives  13.6 us (29%)
  Pallas kernels  8.06 us (17%)
  waiting for transfers between devices  5.48 us (12%)
    ppermute x9, starting transfers between devices, exchange(): lax.ppermute(array, 'kvp', [(i, i ^ partner) for i in range(devices) if i...  19.7 us
    all_to_all x1, blocking collectives, body(): lax.all_to_all(packed, 'kvp', split_axis=0, concat_axis=0, tiled=True)  13.6 us
    ppermute x9, waiting for transfers between devices, exchange(): lax.ppermute(array, 'kvp', [(i, i ^ partner) for i in range(devices) if i...  5.48 us
    pallas_call x1, Pallas kernels, body(): pl.pallas_call(functools.partial(attend_kernel, heads_dev, devices), out_...  4.51 us
    pallas_call x1, Pallas kernels, body(): pl.pallas_call(functools.partial(project_kernel, heads_dev), out_shape=[j...  1.53 us
    pallas_call x1, Pallas kernels, body(): pl.pallas_call(project_own_kernel, out_shape=[jax.ShapeDtypeStruct((rows,...  1.22 us
  transfers between devices with their start and end apart: 9, of which 5 were waited for; matrix products, arithmetic and copies ran while one was open for 0% of the time, Pallas kernels for 3%

profile of v10, /device:TPU:1, one launch (start us, length us, event | category | flops | bytes accessed | tf_op | source)
XLA Modules:
  0.0 47.1 jit_solution(11965354381712241911)
XLA Ops:
  0.0 4.5 %attend.1.staged = f32[16,5,4,128]{3,2,1,0:T(4,128)S(1)} custom-call(s32[4,12]{1,0:T(4,128)} %refs_0_.1, s32[4]{0:T(128)} %refs_1_.1, f32[4,48]{1,0:T(4,128)} %bitcast.4, f32[4,48]{1,0:T(4,128)} %bitcast.5, bf16[4,8192]{1,0:T(4,128)(2,1)} %refs_4_.1, bf16[48,64,512]{2,1,0:T(8,128)(2,1)} %refs_5_.1, bf16[48,64,512]{2,1,0:T(8,128)(2,1)} %refs_6_.1), custom_call_target="tpu_custom_call" | custom-call | flops 100663296 | bytes 6291456 | tf_op jit(solution)/shard_map/attend/pallas_call | solution.py:211
  4.5 0.0 slice-start.1
  4.5 0.0 slice-start.2
  4.5 0.0 slice-start.3
  4.6 13.6 %all_to_all.5.packed = bf16[16,5,4,128]{3,2,1,0:T(4,128)(2,1)S(1)} all-to-all(bf16[16,5,4,128]{3,2,1,0:T(4,128)(2,1)S(1)} %pack.1), channel_id=1, replica_groups=mesh['group'=2,'kvp'=16] {'kvp'}, dimensions={0} | all-to-all | bytes 163840 | tf_op jit(solution)/shard_map/all_to_all | solution.py:247
  18.2 0.0 slice-done
  18.2 0.0 slice-done.1
  18.2 0.0 slice-done.2
  18.2 0.0 slice-done.3
  18.3 1.5 %project_others.1 = (bf16[4,512]{1,0:T(4,128)(2,1)S(1)}, bf16[4,8192]{1,0:T(4,128)(2,1)S(1)}) custom-call(bf16[16,5,4,128]{3,2,1,0:T(4,128)(2,1)S(1)} %all_to_all.5.packed, bf16[512,16384]{1,0:T(8,128)(2,1)S(1)} %bitcast.3), custom_call_target="tpu_custom_call" | custom-call | flops 33554432 | bytes 8388608 | tf_op jit(solution)/shard_map/project_others/pallas_call | solution.py:260
  19.8 1.3 %collective-permute-start.2 = (bf16[4,8192]{1,0:T(4,128)(2,1)S(1)}, bf16[4,8192]{1,0:T(4,128)(2,1)S(1)}, u32[]{:S(2)}, u32[]{:S(2)}) collective-permute-start(bf16[4,8192]{1,0:T(4,128)(2,1)S(1)} %get-tuple-element.12), channel_id=1, source_target_pairs={{0,3},{2,1},{4,7},{6,5},{8,11},{10,9},{12,15},{14,13},{16,19},{18,... | collective-permute-start | bytes 196616 | tf_op jit(solution)/shard_map/ppermute | solution.py:197
  21.1 2.3 %collective-permute-start.1 = (bf16[4,8192]{1,0:T(4,128)(2,1)S(1)}, bf16[4,8192]{1,0:T(4,128)(2,1)S(1)}, u32[]{:S(2)}, u32[]{:S(2)}) collective-permute-start(bf16[4,8192]{1,0:T(4,128)(2,1)S(1)} %get-tuple-element.12), channel_id=1, source_target_pairs={{1,3},{3,1},{5,7},{7,5},{9,11},{11,9},{13,15},{15,13},{17,19},{19,... | collective-permute-start | bytes 196616 | tf_op jit(solution)/shard_map/ppermute | solution.py:197
  23.4 1.2 %project_own.1 = (f32[4,8192]{1,0:T(4,128)S(1)}, bf16[4,8192]{1,0:T(4,128)(2,1)S(1)}) custom-call(bf16[4,512]{1,0:T(4,128)(2,1)S(1)} %get-tuple-element.9.left, bf16[512,16384]{1,0:T(8,128)(2,1)S(1)} %bitcast.3), custom_call_target="tpu_custom_call" | custom-call | flops 33554432 | bytes 8388608 | tf_op jit(solution)/shard_map/project_own/pallas_call | solution.py:272
  24.6 1.3 %collective-permute-start = (bf16[4,8192]{1,0:T(4,128)(2,1)S(1)}, bf16[4,8192]{1,0:T(4,128)(2,1)S(1)}, u32[]{:S(2)}, u32[]{:S(2)}) collective-permute-start(bf16[4,8192]{1,0:T(4,128)(2,1)S(1)} %get-tuple-element.11), channel_id=1, source_target_pairs={{0,1},{2,3},{4,5},{6,7},{8,9},{10,11},{12,13},{14,15},{16,17},{18,... | collective-permute-start | bytes 196616 | tf_op jit(solution)/shard_map/ppermute | solution.py:197
  25.9 0.0 collective-permute-done.2.refs_3_
  25.9 0.2 collective-permute-done.1.refs_2_
  26.1 1.7 %collective-permute-done.refs_1_ = bf16[4,8192]{1,0:T(4,128)(2,1)S(1)} collective-permute-done((bf16[4,8192]{1,0:T(4,128)(2,1)S(1)}, bf16[4,8192]{1,0:T(4,128)(2,1)S(1)}, u32[]{:S(2)}, u32[]{:S(2)}) %collective-permute-start) | collective-permute-done | bytes 65568 | tf_op jit(solution)/shard_map/ppermute | solution.py:197
  27.8 0.1 add_near.1.refs_0_
  27.8 2.9 %collective-permute-start.5 = (bf16[4,8192]{1,0:T(4,128)(2,1)S(1)}, bf16[4,8192]{1,0:T(4,128)(2,1)S(1)}, u32[]{:S(2)}, u32[]{:S(2)}) collective-permute-start(bf16[4,8192]{1,0:T(4,128)(2,1)S(1)} %add_near.1.refs_0_), channel_id=1, source_target_pairs={{1,13},{3,15},{5,9},{7,11},{9,5},{11,7},{13,1},{15,3},{17,29},{19,... | collective-permute-start | bytes 196616 | tf_op jit(solution)/shard_map/ppermute | solution.py:197
  30.7 2.5 %collective-permute-start.4 = (bf16[4,8192]{1,0:T(4,128)(2,1)S(1)}, bf16[4,8192]{1,0:T(4,128)(2,1)S(1)}, u32[]{:S(2)}, u32[]{:S(2)}) collective-permute-start(bf16[4,8192]{1,0:T(4,128)(2,1)S(1)} %add_near.1.refs_0_), channel_id=1, source_target_pairs={{1,9},{3,11},{5,13},{7,15},{9,1},{11,3},{13,5},{15,7},{17,25},{19,... | collective-permute-start | bytes 196616 | tf_op jit(solution)/shard_map/ppermute | solution.py:197
  33.2 3.9 %collective-permute-start.3 = (bf16[4,8192]{1,0:T(4,128)(2,1)S(1)}, bf16[4,8192]{1,0:T(4,128)(2,1)S(1)}, u32[]{:S(2)}, u32[]{:S(2)}) collective-permute-start(bf16[4,8192]{1,0:T(4,128)(2,1)S(1)} %add_near.1.refs_0_), channel_id=1, source_target_pairs={{1,5},{3,7},{5,1},{7,3},{9,13},{11,15},{13,9},{15,11},{17,21},{19,... | collective-permute-start | bytes 196616 | tf_op jit(solution)/shard_map/ppermute | solution.py:197
  37.1 0.0 collective-permute-done.5.refs_3_
  37.1 0.1 collective-permute-done.4.refs_2_
  37.2 1.5 %collective-permute-done.3.refs_1_ = bf16[4,8192]{1,0:T(4,128)(2,1)S(1)} collective-permute-done((bf16[4,8192]{1,0:T(4,128)(2,1)S(1)}, bf16[4,8192]{1,0:T(4,128)(2,1)S(1)}, u32[]{:S(2)}, u32[]{:S(2)}) %collective-permute-start.3) | collective-permute-done | bytes 65568 | tf_op jit(solution)/shard_map/ppermute | solution.py:197
  38.7 0.1 add_far.1.mine
  38.8 1.3 %collective-permute-start.8 = (bf16[4,8192]{1,0:T(4,128)(2,1)S(1)}, bf16[4,8192]{1,0:T(4,128)(2,1)S(1)}, u32[]{:S(2)}, u32[]{:S(2)}) collective-permute-start(bf16[4,8192]{1,0:T(4,128)(2,1)S(1)} %add_far.1.mine), channel_id=1, source_target_pairs={{1,2},{3,0},{5,6},{7,4},{9,10},{11,8},{13,14},{15,12},{17,18},{19,... | collective-permute-start | bytes 196616 | tf_op jit(solution)/shard_map/ppermute | solution.py:197
  40.1 1.3 %collective-permute-start.7 = (bf16[4,8192]{1,0:T(4,128)(2,1)S(1)}, bf16[4,8192]{1,0:T(4,128)(2,1)S(1)}, u32[]{:S(2)}, u32[]{:S(2)}) collective-permute-start(bf16[4,8192]{1,0:T(4,128)(2,1)S(1)} %add_far.1.mine), channel_id=1, source_target_pairs={{1,0},{3,2},{5,4},{7,6},{9,8},{11,10},{13,12},{15,14},{17,16},{19,... | collective-permute-start | bytes 196616 | tf_op jit(solution)/shard_map/ppermute | solution.py:197
  41.4 3.0 %collective-permute-start.6 = (bf16[4,8192]{1,0:T(4,128)(2,1)S(1)}, bf16[4,8192]{1,0:T(4,128)(2,1)S(1)}, u32[]{:S(2)}, u32[]{:S(2)}) collective-permute-start(bf16[4,8192]{1,0:T(4,128)(2,1)S(1)} %add_far.1.mine), channel_id=1, source_target_pairs={{1,3},{3,1},{5,7},{7,5},{9,11},{11,9},{13,15},{15,13},{17,19},{19,... | collective-permute-start | bytes 196616 | tf_op jit(solution)/shard_map/ppermute | solution.py:197
  44.4 0.0 collective-permute-done.8.from_far
  44.4 0.0 collective-permute-done.7.from_core
  44.4 2.0 %collective-permute-done.6.from_odd = bf16[4,8192]{1,0:T(4,128)(2,1)S(1)} collective-permute-done((bf16[4,8192]{1,0:T(4,128)(2,1)S(1)}, bf16[4,8192]{1,0:T(4,128)(2,1)S(1)}, u32[]{:S(2)}, u32[]{:S(2)}) %collective-permute-start.6) | collective-permute-done | bytes 65568 | tf_op jit(solution)/shard_map/ppermute | solution.py:197
  46.4 0.7 %lay.1 = bf16[4,16384]{1,0:T(4,128)(2,1)} custom-call(bf16[4,8192]{1,0:T(4,128)(2,1)S(1)} %add_far.1.mine, bf16[4,8192]{1,0:T(4,128)(2,1)S(1)} %collective-permute-done.6.from_odd, bf16[4,8192]{1,0:T(4,128)(2,1)S(1)} %collective-permute-done.7.from_core, bf16[4,8192]{1,0:T(4,128)(2,1)S(1)} %collective-permute-done.8.from_far), custom_call_target="tpu_custom_call" | custom-call | tf_op jit(solution)/shard_map/lay/pallas_call | solution.py:298
  (3 shorter events, 0.0 us)
Async XLA Ops:
  0.0 18.2 %slice-start = ((s8[16777216]{0:T(1024)(128)(4,1)}), s8[4194304]{0:T(1024)(128)(4,1)S(1)}, s32[]{:S(2)}) async-start(s8[16777216]{0:T(1024)(128)(4,1)} %bitcast.2), calls=%async_computation.1 | async-start | bytes 8388608
  4.5 13.7 %slice-start.1 = ((s8[16777216]{0:T(1024)(128)(4,1)}), s8[4194304]{0:T(1024)(128)(4,1)S(1)}, s32[]{:S(2)}) async-start(s8[16777216]{0:T(1024)(128)(4,1)} %bitcast.2), calls=%async_computation.2 | async-start | bytes 8388608
  4.5 13.7 %slice-start.2 = ((s8[16777216]{0:T(1024)(128)(4,1)}), s8[4194304]{0:T(1024)(128)(4,1)S(1)}, s32[]{:S(2)}) async-start(s8[16777216]{0:T(1024)(128)(4,1)} %bitcast.2), calls=%async_computation.3 | async-start | bytes 8388608
  4.5 13.7 %slice-start.3 = ((s8[16777216]{0:T(1024)(128)(4,1)}), s8[4194304]{0:T(1024)(128)(4,1)S(1)}, s32[]{:S(2)}) async-start(s8[16777216]{0:T(1024)(128)(4,1)} %bitcast.2), calls=%async_computation.4 | async-start | bytes 8388608
  19.8 6.1 %collective-permute-start.2 = (bf16[4,8192]{1,0:T(4,128)(2,1)S(1)}, bf16[4,8192]{1,0:T(4,128)(2,1)S(1)}, u32[]{:S(2)}, u32[]{:S(2)}) collective-permute-start(bf16[4,8192]{1,0:T(4,128)(2,1)S(1)} %get-tuple-element.12), channel_id=1, source_target_pairs={{0,3},{2,1},{4,7},{6,5},{8,11},{10,9},{12,15},{14,13},{16,19},{18,... | collective-permute-start | bytes 196616 | tf_op jit(solution)/shard_map/ppermute | solution.py:197
  21.1 5.0 %collective-permute-start.1 = (bf16[4,8192]{1,0:T(4,128)(2,1)S(1)}, bf16[4,8192]{1,0:T(4,128)(2,1)S(1)}, u32[]{:S(2)}, u32[]{:S(2)}) collective-permute-start(bf16[4,8192]{1,0:T(4,128)(2,1)S(1)} %get-tuple-element.12), channel_id=1, source_target_pairs={{1,3},{3,1},{5,7},{7,5},{9,11},{11,9},{13,15},{15,13},{17,19},{19,... | collective-permute-start | bytes 196616 | tf_op jit(solution)/shard_map/ppermute | solution.py:197
  24.6 3.1 %collective-permute-start = (bf16[4,8192]{1,0:T(4,128)(2,1)S(1)}, bf16[4,8192]{1,0:T(4,128)(2,1)S(1)}, u32[]{:S(2)}, u32[]{:S(2)}) collective-permute-start(bf16[4,8192]{1,0:T(4,128)(2,1)S(1)} %get-tuple-element.11), channel_id=1, source_target_pairs={{0,1},{2,3},{4,5},{6,7},{8,9},{10,11},{12,13},{14,15},{16,17},{18,... | collective-permute-start | bytes 196616 | tf_op jit(solution)/shard_map/ppermute | solution.py:197
  27.8 9.3 %collective-permute-start.5 = (bf16[4,8192]{1,0:T(4,128)(2,1)S(1)}, bf16[4,8192]{1,0:T(4,128)(2,1)S(1)}, u32[]{:S(2)}, u32[]{:S(2)}) collective-permute-start(bf16[4,8192]{1,0:T(4,128)(2,1)S(1)} %add_near.1.refs_0_), channel_id=1, source_target_pairs={{1,13},{3,15},{5,9},{7,11},{9,5},{11,7},{13,1},{15,3},{17,29},{19,... | collective-permute-start | bytes 196616 | tf_op jit(solution)/shard_map/ppermute | solution.py:197
  30.7 6.6 %collective-permute-start.4 = (bf16[4,8192]{1,0:T(4,128)(2,1)S(1)}, bf16[4,8192]{1,0:T(4,128)(2,1)S(1)}, u32[]{:S(2)}, u32[]{:S(2)}) collective-permute-start(bf16[4,8192]{1,0:T(4,128)(2,1)S(1)} %add_near.1.refs_0_), channel_id=1, source_target_pairs={{1,9},{3,11},{5,13},{7,15},{9,1},{11,3},{13,5},{15,7},{17,25},{19,... | collective-permute-start | bytes 196616 | tf_op jit(solution)/shard_map/ppermute | solution.py:197
  33.2 5.5 %collective-permute-start.3 = (bf16[4,8192]{1,0:T(4,128)(2,1)S(1)}, bf16[4,8192]{1,0:T(4,128)(2,1)S(1)}, u32[]{:S(2)}, u32[]{:S(2)}) collective-permute-start(bf16[4,8192]{1,0:T(4,128)(2,1)S(1)} %add_near.1.refs_0_), channel_id=1, source_target_pairs={{1,5},{3,7},{5,1},{7,3},{9,13},{11,15},{13,9},{15,11},{17,21},{19,... | collective-permute-start | bytes 196616 | tf_op jit(solution)/shard_map/ppermute | solution.py:197
  38.8 5.6 %collective-permute-start.8 = (bf16[4,8192]{1,0:T(4,128)(2,1)S(1)}, bf16[4,8192]{1,0:T(4,128)(2,1)S(1)}, u32[]{:S(2)}, u32[]{:S(2)}) collective-permute-start(bf16[4,8192]{1,0:T(4,128)(2,1)S(1)} %add_far.1.mine), channel_id=1, source_target_pairs={{1,2},{3,0},{5,6},{7,4},{9,10},{11,8},{13,14},{15,12},{17,18},{19,... | collective-permute-start | bytes 196616 | tf_op jit(solution)/shard_map/ppermute | solution.py:197
  40.1 4.3 %collective-permute-start.7 = (bf16[4,8192]{1,0:T(4,128)(2,1)S(1)}, bf16[4,8192]{1,0:T(4,128)(2,1)S(1)}, u32[]{:S(2)}, u32[]{:S(2)}) collective-permute-start(bf16[4,8192]{1,0:T(4,128)(2,1)S(1)} %add_far.1.mine), channel_id=1, source_target_pairs={{1,0},{3,2},{5,4},{7,6},{9,8},{11,10},{13,12},{15,14},{17,16},{19,... | collective-permute-start | bytes 196616 | tf_op jit(solution)/shard_map/ppermute | solution.py:197
  41.4 5.0 %collective-permute-start.6 = (bf16[4,8192]{1,0:T(4,128)(2,1)S(1)}, bf16[4,8192]{1,0:T(4,128)(2,1)S(1)}, u32[]{:S(2)}, u32[]{:S(2)}) collective-permute-start(bf16[4,8192]{1,0:T(4,128)(2,1)S(1)} %add_far.1.mine), channel_id=1, source_target_pairs={{1,3},{3,1},{5,7},{7,5},{9,11},{11,9},{13,15},{15,13},{17,19},{19,... | collective-permute-start | bytes 196616 | tf_op jit(solution)/shard_map/ppermute | solution.py:197

commit v11 on v8

--- a/solution.py
+++ b/solution.py
@@ -12,6 +12,8 @@
 PAGE = 64
 ATTEND_VMEM = 24 * 1024 * 1024
 PROJECT_VMEM = 8 * 1024 * 1024
+HIDDEN = -1e30
+LOWEST = -1e20
 EXCHANGE_FLOPS = 40_000_000_000
 SMALL_VMEM = 8 * 1024 * 1024
 VMEM = pl.BlockSpec(memory_space=pltpu.VMEM)
@@ -26,7 +28,8 @@
 
 def attend_kernel(heads_dev, devices, *refs):
     table_hbm, lengths_hbm, key_scale_hbm, value_scale_hbm, queries_hbm, keys, values = refs[:7]
-    (staged, table, lengths, key_scale, value_scale, queries, key_buf, value_buf, query_rows, small_sems, sems) = refs[7:]
+    staged, table, lengths, key_scale, value_scale, queries, key_buf, value_buf, query_rows = refs[7:16]
+    key_factor, value_factor, bias, weights, small_sems, sems = refs[16:]
     rows, pages = table.shape
     kv_heads = key_scale.shape[0]
     heads = queries.shape[1] // HD
@@ -57,35 +60,39 @@
         copy.start()
 
     me = lax.axis_index("kvp")
-    place = me * context + lax.broadcasted_iota(jnp.int32, (group, context), 1)
+    place = me * context + lax.broadcasted_iota(jnp.int32, (1, context), 1)
     lane = lax.broadcasted_iota(jnp.int32, (group, HD), 1)
+    left_page = lax.broadcasted_iota(jnp.int32, (8, HD), 1) < PAGE
     zeros = jnp.zeros((group, HD), jnp.bfloat16)
     for copy in small:
         copy.wait()
+    for copy in large[1]:
+        copy.start()
     for h in range(heads):
         query_rows[h * rows : (h + 1) * rows, :] = queries[:, h * HD : (h + 1) * HD].astype(jnp.float32)
-    for copy in large[1]:
-        copy.start()
+    for r in range(rows):
+        bias[r] = jnp.broadcast_to(jnp.where(place < lengths[r], 0.0, HIDDEN), (8, context))
+        for p in range(0, pages, 2):
+            slots = table[r, p], table[r, p + 1]
+            here = slice(p * PAGE, (p + 2) * PAGE)
+            for k in range(kv_heads):
+                key_factor[r, k, :, here] = jnp.where(left_page, key_scale[k, slots[0]], key_scale[k, slots[1]]) * (
+                    math.log2(math.e) / math.sqrt(HD)
+                )
+                value_factor[r, k, :, here] = jnp.where(left_page, value_scale[k, slots[0]], value_scale[k, slots[1]])
     for copy in large[0]:
         copy.wait()
-
-    def factors(scales, r, k, times):
-        columns = []
-        for p in range(0, pages, 2):
-            left = scales[k, table[r, p]] * times
-            right = scales[k, table[r, p + 1]] * times
-            columns.append(jnp.where(lane < PAGE, left, right))
-        return jnp.concatenate(columns, axis=1)
 
     def pages_of(buf, r, k):
         return jnp.concatenate(
             [buf[table[r, p], :, k * HD : (k + 2) * HD] for p in range(pages)], axis=0
         )
 
-    probs = {}
+    def on_rows(row):
+        return jnp.concatenate([row] * (group // 8), axis=0)
+
     stats = [jnp.zeros((group, HD), jnp.float32)] * kv_heads
     for r in range(rows):
-        visible = place < lengths[r]
         query = query_rows[pl.ds(r, heads, stride=rows), :].astype(jnp.bfloat16)
         for k in range(0, kv_heads, 2):
             left = jnp.concatenate(
@@ -98,22 +105,24 @@
             both = lax.dot_general(
                 left, pages_of(key_buf, r, k), (((1,), (1,)), ((), ())), preferred_element_type=jnp.float32
             )
-            weights = []
             for i in (0, 1):
-                scores = both[i * group : (i + 1) * group] * factors(key_scale, r, k + i, 1.0 / math.sqrt(HD))
-                highest = jnp.max(jnp.where(visible, scores, -1e30), axis=1, keepdims=True)
+                scores = both[i * group : (i + 1) * group] * on_rows(key_factor[r, k + i]) + on_rows(bias[r])
+                highest = jnp.maximum(jnp.max(scores, axis=1, keepdims=True), LOWEST)
                 high, low = split_two(highest)
-                prob = jnp.where(visible, jnp.exp(scores - (high + low)), 0.0)
+                prob = jnp.exp2(scores - (high + low))
                 total_high, total_low = split_two(jnp.sum(prob, axis=1, keepdims=True))
                 for at, value in enumerate((high, low, total_high, total_low)):
                     stats[k + i] = jnp.where(lane == 4 * r + at, value, stats[k + i])
-                weights.append((prob * factors(value_scale, r, k + i, 1.0)).astype(jnp.bfloat16))
-            probs[r, k] = jnp.concatenate(weights, axis=0)
+                weights[r, (k + i) * group : (k + i + 1) * group] = (prob * on_rows(value_factor[r, k + i])).astype(
+                    jnp.bfloat16
+                )
     for copy in large[1]:
         copy.wait()
     for r in range(rows):
         for k in range(0, kv_heads, 2):
-            both = jnp.dot(probs[r, k], pages_of(value_buf, r, k), preferred_element_type=jnp.float32)
+            both = jnp.dot(
+                weights[r, k * group : (k + 2) * group], pages_of(value_buf, r, k), preferred_element_type=jnp.float32
+            )
             for i in (0, 1):
                 partial = both[i * group : (i + 1) * group, i * HD : (i + 1) * HD]
                 for start in range(0, group, heads_dev):
@@ -134,16 +143,20 @@
     rows = left.shape[0]
     part = outs[0].shape[1]
     quarter = lax.rem(lax.axis_index("kvp"), len(outs) + 1)
-    blocks = packed[...].astype(jnp.float32)
-    stats = blocks[:, rows]
+    stats = packed[:, rows].astype(jnp.float32)
+    lanes = stats.shape[-1]
+
+    def lanes_ahead(value, by):
+        return pltpu.roll(value, lanes - by, axis=2)
+
+    maxima = stats + lanes_ahead(stats, 1)
+    rescale = jnp.exp2(maxima - jnp.max(maxima, axis=0, keepdims=True))
+    totals = lanes_ahead(stats, 2) + lanes_ahead(stats, 3)
+    denominator = jnp.sum(totals * rescale, axis=0)
     for r in range(rows):
-        partial = blocks[:, r]
-        maxima = stats[:, :, 4 * r : 4 * r + 1] + stats[:, :, 4 * r + 1 : 4 * r + 2]
-        totals = stats[:, :, 4 * r + 2 : 4 * r + 3] + stats[:, :, 4 * r + 3 : 4 * r + 4]
-        rescale = jnp.exp(maxima - jnp.max(maxima, axis=0, keepdims=True))
-        attended[r * heads_dev : (r + 1) * heads_dev, :] = jnp.sum(partial * rescale, axis=0) / jnp.sum(
-            totals * rescale, axis=0
-        )
+        partial = packed[:, r].astype(jnp.float32)
+        numerator = jnp.sum(partial * rescale[:, :, 4 * r : 4 * r + 1], axis=0)
+        attended[r * heads_dev : (r + 1) * heads_dev, :] = numerator / denominator[:, 4 * r : 4 * r + 1]
     rounded = jnp.concatenate(
         [attended[pl.ds(j, rows, stride=heads_dev), :].astype(jnp.bfloat16) for j in range(heads_dev)], axis=1
     )
@@ -210,6 +223,10 @@
             pltpu.VMEM((slots, PAGE, columns), jnp.bfloat16),
             pltpu.VMEM((slots, PAGE, columns), jnp.bfloat16),
             pltpu.VMEM((heads * rows, HD), jnp.float32),
+            pltpu.VMEM((rows, kv_heads, 8, pages * PAGE), jnp.float32),
+            pltpu.VMEM((rows, kv_heads, 8, pages * PAGE), jnp.float32),
+            pltpu.VMEM((rows, 8, pages * PAGE), jnp.float32),
+            pltpu.VMEM((rows, heads, pages * PAGE), jnp.bfloat16),
             pltpu.SemaphoreType.DMA((5,)),
             pltpu.SemaphoreType.DMA((2, 4)),
         ],

time: 37 us -> 37.2 us (level)
  no operation moved by 1% of the time
where the time goes in v11:
time: 37.2 us; the launch traced here: 37.1 us
  blocking collectives  14.6 us (39%)
  starting transfers between devices  8.24 us (22%)
  Pallas kernels  8.22 us (22%)
  waiting for transfers between devices  5.89 us (16%)
    all_to_all x1, blocking collectives, body(): lax.all_to_all(packed, 'kvp', split_axis=0, concat_axis=0, tiled=True)  14.6 us
    ppermute x9, starting transfers between devices, exchange(): lax.ppermute(array, 'kvp', [(i, i ^ partner) for i in range(devices)])  8.24 us
    ppermute x9, waiting for transfers between devices, exchange(): lax.ppermute(array, 'kvp', [(i, i ^ partner) for i in range(devices)])  5.89 us
    pallas_call x1, Pallas kernels, body(): pl.pallas_call(functools.partial(attend_kernel, heads_dev, devices), out_...  4.81 us
    pallas_call x1, Pallas kernels, body(): pl.pallas_call(functools.partial(project_kernel, heads_dev), out_shape=[j...  2 us
  transfers between devices with their start and end apart: 9, of which 6 were waited for; matrix products, arithmetic and copies ran while one was open for 0% of the time, Pallas kernels for 2%

profile of v11, /device:TPU:0, one launch (start us, length us, event | category | flops | bytes accessed | tf_op | source)
XLA Modules:
  0.0 37.1 jit_solution(7040124556442593274)
XLA Ops:
  0.0 0.0 slice-start
  0.0 4.8 %attend.1.staged = f32[16,5,4,128]{3,2,1,0:T(4,128)S(1)} custom-call(s32[4,12]{1,0:T(4,128)} %refs_0_.1, s32[4]{0:T(128)} %refs_1_.1, f32[4,48]{1,0:T(4,128)} %bitcast.4, f32[4,48]{1,0:T(4,128)} %bitcast.5, bf16[4,8192]{1,0:T(4,128)(2,1)} %refs_4_.1, bf16[48,64,512]{2,1,0:T(8,128)(2,1)} %refs_5_.1, bf16[48,64,512]{2,1,0:T(8,128)(2,1)} %refs_6_.1), custom_call_target="tpu_custom_call" | custom-call | flops 100663296 | bytes 6291456 | tf_op jit(solution)/shard_map/attend/pallas_call | solution.py:212
  4.8 0.0 slice-start.1
  4.8 0.0 slice-start.2
  4.8 0.0 slice-start.3
  4.9 14.6 %all_to_all.5.packed = bf16[16,5,4,128]{3,2,1,0:T(4,128)(2,1)S(1)} all-to-all(bf16[16,5,4,128]{3,2,1,0:T(4,128)(2,1)S(1)} %pack.1), channel_id=1, replica_groups=mesh['group'=2,'kvp'=16] {'kvp'}, dimensions={0} | all-to-all | bytes 163840 | tf_op jit(solution)/shard_map/all_to_all | solution.py:252
  19.5 0.0 slice-done
  19.5 0.0 slice-done.1
  19.5 0.0 slice-done.2
  19.5 0.0 slice-done.3
  19.5 2.0 %project_others.1 = (bf16[4,512]{1,0:T(4,128)(2,1)S(1)}, bf16[4,4096]{1,0:T(4,128)(2,1)S(1)}, bf16[4,4096]{1,0:T(4,128)(2,1)S(1)}, bf16[4,4096]{1,0:T(4,128)(2,1)S(1)}) custom-call(bf16[16,5,4,128]{3,2,1,0:T(4,128)(2,1)S(1)} %all_to_all.5.packed, bf16[512,16384]{1,0:T(8,128)(2,1)S(1)} %bitcast.3), custom_call_target="tpu_custom_call" | custom-call | flops 50331648 | bytes 12582912 | tf_op jit(solution)/shard_map/project_others/pallas_call | solution.py:256
  21.5 0.0 collective-permute-start
  21.5 0.2 collective-permute-start.1
  21.7 1.7 %collective-permute-start.2 = (bf16[4,4096]{1,0:T(4,128)(2,1)S(1)}, bf16[4,4096]{1,0:T(4,128)(2,1)S(1)}, u32[]{:S(2)}, u32[]{:S(2)}) collective-permute-start(bf16[4,4096]{1,0:T(4,128)(2,1)S(1)} %get-tuple-element.12), channel_id=1, source_target_pairs={{0,3},{1,2},{2,1},{3,0},{4,7},{5,6},{6,5},{7,4},{8,11},{9,10},{10,... | collective-permute-start | bytes 98312 | tf_op jit(solution)/shard_map/ppermute | solution.py:195
  23.4 0.7 %project_own.1.refs_0_ = bf16[4,4096]{1,0:T(4,128)(2,1)S(1)} custom-call(bf16[4,512]{1,0:T(4,128)(2,1)S(1)} %get-tuple-element.9.left, bf16[512,16384]{1,0:T(8,128)(2,1)S(1)} %bitcast.3), custom_call_target="tpu_custom_call" | custom-call | flops 16777216 | bytes 4194304 | tf_op jit(solution)/shard_map/project_own/pallas_call | solution.py:272
  24.0 0.0 collective-permute-done.refs_1_
  24.0 1.6 %collective-permute-done.1.refs_2_ = bf16[4,4096]{1,0:T(4,128)(2,1)S(1)} collective-permute-done((bf16[4,4096]{1,0:T(4,128)(2,1)S(1)}, bf16[4,4096]{1,0:T(4,128)(2,1)S(1)}, u32[]{:S(2)}, u32[]{:S(2)}) %collective-permute-start.1) | collective-permute-done | bytes 32800 | tf_op jit(solution)/shard_map/ppermute | solution.py:195
  25.7 0.0 collective-permute-done.2.refs_3_
  25.7 1.0 %collective-permute-start.5 = (bf16[4,4096]{1,0:T(4,128)(2,1)S(1)}, bf16[4,4096]{1,0:T(4,128)(2,1)S(1)}, u32[]{:S(2)}, u32[]{:S(2)}) collective-permute-start(bf16[4,4096]{1,0:T(4,128)(2,1)S(1)} %add_near.1.refs_0_), channel_id=1, source_target_pairs={{0,12},{1,13},{2,14},{3,15},{4,8},{5,9},{6,10},{7,11},{8,4},{9,5},... | collective-permute-start | bytes 98312 | tf_op jit(solution)/shard_map/ppermute | solution.py:195
  26.8 0.9 %collective-permute-start.4 = (bf16[4,4096]{1,0:T(4,128)(2,1)S(1)}, bf16[4,4096]{1,0:T(4,128)(2,1)S(1)}, u32[]{:S(2)}, u32[]{:S(2)}) collective-permute-start(bf16[4,4096]{1,0:T(4,128)(2,1)S(1)} %add_near.1.refs_0_), channel_id=1, source_target_pairs={{0,8},{1,9},{2,10},{3,11},{4,12},{5,13},{6,14},{7,15},{8,0},{9,1},... | collective-permute-start | bytes 98312 | tf_op jit(solution)/shard_map/ppermute | solution.py:195
  27.6 2.5 %collective-permute-start.3 = (bf16[4,4096]{1,0:T(4,128)(2,1)S(1)}, bf16[4,4096]{1,0:T(4,128)(2,1)S(1)}, u32[]{:S(2)}, u32[]{:S(2)}) collective-permute-start(bf16[4,4096]{1,0:T(4,128)(2,1)S(1)} %add_near.1.refs_0_), channel_id=1, source_target_pairs={{0,4},{1,5},{2,6},{3,7},{4,0},{5,1},{6,2},{7,3},{8,12},{9,13},{10,... | collective-permute-start | bytes 98312 | tf_op jit(solution)/shard_map/ppermute | solution.py:195
  30.2 1.6 %collective-permute-done.5.refs_3_ = bf16[4,4096]{1,0:T(4,128)(2,1)S(1)} collective-permute-done((bf16[4,4096]{1,0:T(4,128)(2,1)S(1)}, bf16[4,4096]{1,0:T(4,128)(2,1)S(1)}, u32[]{:S(2)}, u32[]{:S(2)}) %collective-permute-start.5) | collective-permute-done | bytes 32800 | tf_op jit(solution)/shard_map/ppermute | solution.py:195
  31.7 0.2 collective-permute-done.4.refs_2_
  32.0 0.2 collective-permute-done.3.refs_1_
  32.2 0.1 collective-permute-start.8
  32.3 1.3 %collective-permute-start.7 = (bf16[4,4096]{1,0:T(4,128)(2,1)S(1)}, bf16[4,4096]{1,0:T(4,128)(2,1)S(1)}, u32[]{:S(2)}, u32[]{:S(2)}) collective-permute-start(bf16[4,4096]{1,0:T(4,128)(2,1)S(1)} %add_far.1.refs_0_), channel_id=1, source_target_pairs={{0,2},{1,3},{2,0},{3,1},{4,6},{5,7},{6,4},{7,5},{8,10},{9,11},{10,... | collective-permute-start | bytes 98312 | tf_op jit(solution)/shard_map/ppermute | solution.py:195
  33.6 0.6 %collective-permute-start.6 = (bf16[4,4096]{1,0:T(4,128)(2,1)S(1)}, bf16[4,4096]{1,0:T(4,128)(2,1)S(1)}, u32[]{:S(2)}, u32[]{:S(2)}) collective-permute-start(bf16[4,4096]{1,0:T(4,128)(2,1)S(1)} %add_far.1.refs_0_), channel_id=1, source_target_pairs={{0,1},{1,0},{2,3},{3,2},{4,5},{5,4},{6,7},{7,6},{8,9},{9,8},{10,11... | collective-permute-start | bytes 98312 | tf_op jit(solution)/shard_map/ppermute | solution.py:195
  34.2 1.6 %collective-permute-done.8.refs_3_ = bf16[4,4096]{1,0:T(4,128)(2,1)S(1)} collective-permute-done((bf16[4,4096]{1,0:T(4,128)(2,1)S(1)}, bf16[4,4096]{1,0:T(4,128)(2,1)S(1)}, u32[]{:S(2)}, u32[]{:S(2)}) %collective-permute-start.8) | collective-permute-done | bytes 32800 | tf_op jit(solution)/shard_map/ppermute | solution.py:195
  35.7 0.6 %collective-permute-done.7.refs_2_ = bf16[4,4096]{1,0:T(4,128)(2,1)S(1)} collective-permute-done((bf16[4,4096]{1,0:T(4,128)(2,1)S(1)}, bf16[4,4096]{1,0:T(4,128)(2,1)S(1)}, u32[]{:S(2)}, u32[]{:S(2)}) %collective-permute-start.7) | collective-permute-done | bytes 32800 | tf_op jit(solution)/shard_map/ppermute | solution.py:195
  36.4 0.0 collective-permute-done.6.refs_1_
  36.4 0.7 %lay.1 = bf16[4,16384]{1,0:T(4,128)(2,1)} custom-call(bf16[4,4096]{1,0:T(4,128)(2,1)S(1)} %add_far.1.refs_0_, bf16[4,4096]{1,0:T(4,128)(2,1)S(1)} %collective-permute-done.6.refs_1_, bf16[4,4096]{1,0:T(4,128)(2,1)S(1)} %collective-permute-done.7.refs_2_, bf16[4,4096]{1,0:T(4,128)(2,1)S(1)} %collective-permute-done.8.refs_3_), custom_call_target="tpu_custom_call" | custom-call | tf_op jit(solution)/shard_map/lay/pallas_call | solution.py:297
  (4 shorter events, 0.1 us)
Async XLA Ops:
  0.0 19.5 %slice-start = ((s8[16777216]{0:T(1024)(128)(4,1)}), s8[4194304]{0:T(1024)(128)(4,1)S(1)}, s32[]{:S(2)}) async-start(s8[16777216]{0:T(1024)(128)(4,1)} %bitcast.2), calls=%async_computation.1 | async-start | bytes 8388608
  4.8 14.7 %slice-start.1 = ((s8[16777216]{0:T(1024)(128)(4,1)}), s8[4194304]{0:T(1024)(128)(4,1)S(1)}, s32[]{:S(2)}) async-start(s8[16777216]{0:T(1024)(128)(4,1)} %bitcast.2), calls=%async_computation.2 | async-start | bytes 8388608
  4.8 14.7 %slice-start.2 = ((s8[16777216]{0:T(1024)(128)(4,1)}), s8[4194304]{0:T(1024)(128)(4,1)S(1)}, s32[]{:S(2)}) async-start(s8[16777216]{0:T(1024)(128)(4,1)} %bitcast.2), calls=%async_computation.3 | async-start | bytes 8388608
  4.8 14.7 %slice-start.3 = ((s8[16777216]{0:T(1024)(128)(4,1)}), s8[4194304]{0:T(1024)(128)(4,1)S(1)}, s32[]{:S(2)}) async-start(s8[16777216]{0:T(1024)(128)(4,1)} %bitcast.2), calls=%async_computation.4 | async-start | bytes 8388608
  21.5 2.5 %collective-permute-start = (bf16[4,4096]{1,0:T(4,128)(2,1)S(1)}, bf16[4,4096]{1,0:T(4,128)(2,1)S(1)}, u32[]{:S(2)}, u32[]{:S(2)}) collective-permute-start(bf16[4,4096]{1,0:T(4,128)(2,1)S(1)} %get-tuple-element.10), channel_id=1, source_target_pairs={{0,1},{1,0},{2,3},{3,2},{4,5},{5,4},{6,7},{7,6},{8,9},{9,8},{10,11... | collective-permute-start | bytes 98312 | tf_op jit(solution)/shard_map/ppermute | solution.py:195
  21.5 4.2 %collective-permute-start.1 = (bf16[4,4096]{1,0:T(4,128)(2,1)S(1)}, bf16[4,4096]{1,0:T(4,128)(2,1)S(1)}, u32[]{:S(2)}, u32[]{:S(2)}) collective-permute-start(bf16[4,4096]{1,0:T(4,128)(2,1)S(1)} %get-tuple-element.11), channel_id=1, source_target_pairs={{0,2},{1,3},{2,0},{3,1},{4,6},{5,7},{6,4},{7,5},{8,10},{9,11},{10,... | collective-permute-start | bytes 98312 | tf_op jit(solution)/shard_map/ppermute | solution.py:195
  21.7 4.0 %collective-permute-start.2 = (bf16[4,4096]{1,0:T(4,128)(2,1)S(1)}, bf16[4,4096]{1,0:T(4,128)(2,1)S(1)}, u32[]{:S(2)}, u32[]{:S(2)}) collective-permute-start(bf16[4,4096]{1,0:T(4,128)(2,1)S(1)} %get-tuple-element.12), channel_id=1, source_target_pairs={{0,3},{1,2},{2,1},{3,0},{4,7},{5,6},{6,5},{7,4},{8,11},{9,10},{10,... | collective-permute-start | bytes 98312 | tf_op jit(solution)/shard_map/ppermute | solution.py:195
  25.7 6.0 %collective-permute-start.5 = (bf16[4,4096]{1,0:T(4,128)(2,1)S(1)}, bf16[4,4096]{1,0:T(4,128)(2,1)S(1)}, u32[]{:S(2)}, u32[]{:S(2)}) collective-permute-start(bf16[4,4096]{1,0:T(4,128)(2,1)S(1)} %add_near.1.refs_0_), channel_id=1, source_target_pairs={{0,12},{1,13},{2,14},{3,15},{4,8},{5,9},{6,10},{7,11},{8,4},{9,5},... | collective-permute-start | bytes 98312 | tf_op jit(solution)/shard_map/ppermute | solution.py:195
  26.8 5.2 %collective-permute-start.4 = (bf16[4,4096]{1,0:T(4,128)(2,1)S(1)}, bf16[4,4096]{1,0:T(4,128)(2,1)S(1)}, u32[]{:S(2)}, u32[]{:S(2)}) collective-permute-start(bf16[4,4096]{1,0:T(4,128)(2,1)S(1)} %add_near.1.refs_0_), channel_id=1, source_target_pairs={{0,8},{1,9},{2,10},{3,11},{4,12},{5,13},{6,14},{7,15},{8,0},{9,1},... | collective-permute-start | bytes 98312 | tf_op jit(solution)/shard_map/ppermute | solution.py:195
  27.6 4.6 %collective-permute-start.3 = (bf16[4,4096]{1,0:T(4,128)(2,1)S(1)}, bf16[4,4096]{1,0:T(4,128)(2,1)S(1)}, u32[]{:S(2)}, u32[]{:S(2)}) collective-permute-start(bf16[4,4096]{1,0:T(4,128)(2,1)S(1)} %add_near.1.refs_0_), channel_id=1, source_target_pairs={{0,4},{1,5},{2,6},{3,7},{4,0},{5,1},{6,2},{7,3},{8,12},{9,13},{10,... | collective-permute-start | bytes 98312 | tf_op jit(solution)/shard_map/ppermute | solution.py:195
  32.2 3.5 %collective-permute-start.8 = (bf16[4,4096]{1,0:T(4,128)(2,1)S(1)}, bf16[4,4096]{1,0:T(4,128)(2,1)S(1)}, u32[]{:S(2)}, u32[]{:S(2)}) collective-permute-start(bf16[4,4096]{1,0:T(4,128)(2,1)S(1)} %add_far.1.refs_0_), channel_id=1, source_target_pairs={{0,3},{1,2},{2,1},{3,0},{4,7},{5,6},{6,5},{7,4},{8,11},{9,10},{10,... | collective-permute-start | bytes 98312 | tf_op jit(solution)/shard_map/ppermute | solution.py:195
  32.3 4.1 %collective-permute-start.7 = (bf16[4,4096]{1,0:T(4,128)(2,1)S(1)}, bf16[4,4096]{1,0:T(4,128)(2,1)S(1)}, u32[]{:S(2)}, u32[]{:S(2)}) collective-permute-start(bf16[4,4096]{1,0:T(4,128)(2,1)S(1)} %add_far.1.refs_0_), channel_id=1, source_target_pairs={{0,2},{1,3},{2,0},{3,1},{4,6},{5,7},{6,4},{7,5},{8,10},{9,11},{10,... | collective-permute-start | bytes 98312 | tf_op jit(solution)/shard_map/ppermute | solution.py:195
  33.6 2.8 %collective-permute-start.6 = (bf16[4,4096]{1,0:T(4,128)(2,1)S(1)}, bf16[4,4096]{1,0:T(4,128)(2,1)S(1)}, u32[]{:S(2)}, u32[]{:S(2)}) collective-permute-start(bf16[4,4096]{1,0:T(4,128)(2,1)S(1)} %add_far.1.refs_0_), channel_id=1, source_target_pairs={{0,1},{1,0},{2,3},{3,2},{4,5},{5,4},{6,7},{7,6},{8,9},{9,8},{10,11... | collective-permute-start | bytes 98312 | tf_op jit(solution)/shard_map/ppermute | solution.py:195

commit v12 on v11

--- a/solution.py
+++ b/solution.py
@@ -29,7 +29,7 @@
 def attend_kernel(heads_dev, devices, *refs):
     table_hbm, lengths_hbm, key_scale_hbm, value_scale_hbm, queries_hbm, keys, values = refs[:7]
     staged, table, lengths, key_scale, value_scale, queries, key_buf, value_buf, query_rows = refs[7:16]
-    key_factor, value_factor, bias, weights, small_sems, sems = refs[16:]
+    query_blocks, key_rows, value_rows, scores, weight_rows, stats, small_sems, sems = refs[16:]
     rows, pages = table.shape
     kv_heads = key_scale.shape[0]
     heads = queries.shape[1] // HD
@@ -60,78 +60,91 @@
         copy.start()
 
     me = lax.axis_index("kvp")
-    place = me * context + lax.broadcasted_iota(jnp.int32, (1, context), 1)
-    lane = lax.broadcasted_iota(jnp.int32, (group, HD), 1)
-    left_page = lax.broadcasted_iota(jnp.int32, (8, HD), 1) < PAGE
-    zeros = jnp.zeros((group, HD), jnp.bfloat16)
+    lane = lax.broadcasted_iota(jnp.int32, (1, HD), 1)
+    first_of_pair = lane < heads
+    of_lane = lax.rem(lax.div(lane, group), kv_heads)
+    spread = (of_lane == lax.broadcasted_iota(jnp.int32, (kv_heads, HD), 0)).astype(jnp.float32)
+    place = lax.broadcasted_iota(jnp.int32, (PAGE, HD), 0)
+    stats[...] = jnp.zeros_like(stats)
     for copy in small:
         copy.wait()
     for copy in large[1]:
         copy.start()
+
+    def by_slot(scales):
+        return lax.dot_general(
+            scales[...], spread, (((0,), (0,)), ((), ())),
+            precision=lax.Precision.HIGHEST, preferred_element_type=jnp.float32,
+        )
+
+    key_rows[...] = by_slot(key_scale) * (math.log2(math.e) / math.sqrt(HD))
+    value_rows[...] = by_slot(value_scale)
     for h in range(heads):
         query_rows[h * rows : (h + 1) * rows, :] = queries[:, h * HD : (h + 1) * HD].astype(jnp.float32)
-    for r in range(rows):
-        bias[r] = jnp.broadcast_to(jnp.where(place < lengths[r], 0.0, HIDDEN), (8, context))
-        for p in range(0, pages, 2):
-            slots = table[r, p], table[r, p + 1]
-            here = slice(p * PAGE, (p + 2) * PAGE)
+    for r in range(0, rows, 2):
+        both = jnp.concatenate([query_rows[pl.ds(r + i, heads, stride=rows), :] for i in (0, 1)], axis=0)
+        turned = both.T
+        for i in (0, 1):
             for k in range(kv_heads):
-                key_factor[r, k, :, here] = jnp.where(left_page, key_scale[k, slots[0]], key_scale[k, slots[1]]) * (
-                    math.log2(math.e) / math.sqrt(HD)
-                )
-                value_factor[r, k, :, here] = jnp.where(left_page, value_scale[k, slots[0]], value_scale[k, slots[1]])
+                mine = lax.div(lane, group) == i * kv_heads + k
+                query_blocks[r + i, k * HD : (k + 1) * HD, :] = jnp.where(mine, turned, 0.0).astype(jnp.bfloat16)
+
+    def pages_of(buf, r, columns):
+        return jnp.concatenate([buf[table[r, p], :, columns] for p in range(pages)], axis=0)
+
+    def factor(scale_rows, r, p):
+        left, right = (scale_rows[pl.ds(table[r + i, p], 1), :] for i in (0, 1))
+        return jnp.where(first_of_pair, left, right)
+
     for copy in large[0]:
         copy.wait()
-
-    def pages_of(buf, r, k):
-        return jnp.concatenate(
-            [buf[table[r, p], :, k * HD : (k + 2) * HD] for p in range(pages)], axis=0
-        )
-
-    def on_rows(row):
-        return jnp.concatenate([row] * (group // 8), axis=0)
-
-    stats = [jnp.zeros((group, HD), jnp.float32)] * kv_heads
     for r in range(rows):
-        query = query_rows[pl.ds(r, heads, stride=rows), :].astype(jnp.bfloat16)
-        for k in range(0, kv_heads, 2):
-            left = jnp.concatenate(
-                [
-                    jnp.concatenate([query[k * group : (k + 1) * group], zeros], axis=1),
-                    jnp.concatenate([zeros, query[(k + 1) * group : (k + 2) * group]], axis=1),
-                ],
-                axis=0,
-            )
-            both = lax.dot_general(
-                left, pages_of(key_buf, r, k), (((1,), (1,)), ((), ())), preferred_element_type=jnp.float32
-            )
+        both = jnp.dot(pages_of(key_buf, r, slice(None)), query_blocks[r], preferred_element_type=jnp.float32)
+        if r % 2 == 0:
+            scores[r // 2] = both
+        else:
+            scores[r // 2] += both
+    for r in range(0, rows, 2):
+        length = jnp.where(first_of_pair, lengths[r], lengths[r + 1]) - me * context
+        highest = jnp.full((PAGE, HD), LOWEST, jnp.float32)
+        for p in range(pages):
+            here = slice(p * PAGE, (p + 1) * PAGE)
+            scaled = jnp.where(place < length - p * PAGE, scores[r // 2, here] * factor(key_rows, r, p), HIDDEN)
+            scores[r // 2, here] = scaled
+            highest = jnp.maximum(highest, scaled)
+        high, low = split_two(jnp.max(highest, axis=0, keepdims=True))
+        total = jnp.zeros((PAGE, HD), jnp.float32)
+        for p in range(0, pages, 2):
+            weights = []
             for i in (0, 1):
-                scores = both[i * group : (i + 1) * group] * on_rows(key_factor[r, k + i]) + on_rows(bias[r])
-                highest = jnp.maximum(jnp.max(scores, axis=1, keepdims=True), LOWEST)
-                high, low = split_two(highest)
-                prob = jnp.exp2(scores - (high + low))
-                total_high, total_low = split_two(jnp.sum(prob, axis=1, keepdims=True))
-                for at, value in enumerate((high, low, total_high, total_low)):
-                    stats[k + i] = jnp.where(lane == 4 * r + at, value, stats[k + i])
-                weights[r, (k + i) * group : (k + i + 1) * group] = (prob * on_rows(value_factor[r, k + i])).astype(
-                    jnp.bfloat16
-                )
+                here = slice((p + i) * PAGE, (p + i + 1) * PAGE)
+                prob = jnp.exp2(scores[r // 2, here] - (high + low))
+                total += prob
+                weights.append(prob * factor(value_rows, r, p + i))
+            turned = jnp.concatenate(weights, axis=0).T
+            weight_rows[r // 2, :, p * PAGE : (p + 2) * PAGE] = turned.astype(jnp.bfloat16)
+        total_high, total_low = split_two(jnp.sum(total, axis=0, keepdims=True))
+        for at, value in enumerate((high, low, total_high, total_low)):
+            stats[4 * r + at : 4 * r + at + 1, :] = value
+            stats[4 * r + 4 + at : 4 * r + 5 + at, :] = pltpu.roll(value, HD - heads, axis=1)
+    by_head = stats[...].T
+    for d in range(devices):
+        staged[d, rows] = by_head[d * heads_dev : (d + 1) * heads_dev]
     for copy in large[1]:
         copy.wait()
     for r in range(rows):
         for k in range(0, kv_heads, 2):
+            first = r % 2 * heads + k * group
             both = jnp.dot(
-                weights[r, k * group : (k + 2) * group], pages_of(value_buf, r, k), preferred_element_type=jnp.float32
+                weight_rows[r // 2, first : first + 2 * group, :],
+                pages_of(value_buf, r, slice(k * HD, (k + 2) * HD)),
+                preferred_element_type=jnp.float32,
             )
             for i in (0, 1):
                 partial = both[i * group : (i + 1) * group, i * HD : (i + 1) * HD]
                 for start in range(0, group, heads_dev):
                     d = ((k + i) * group + start) // heads_dev
                     staged[d, r] = partial[start : start + heads_dev]
-    for k in range(kv_heads):
-        for start in range(0, group, heads_dev):
-            d = (k * group + start) // heads_dev
-            staged[d, rows] = stats[k][start : start + heads_dev]
 
 
 def pack_kernel(staged, packed):
@@ -217,16 +230,18 @@
         scratch_shapes=[
             pltpu.SMEM((rows, pages), jnp.int32),
             pltpu.SMEM((rows,), jnp.int32),
-            pltpu.SMEM((kv_heads, slots), jnp.float32),
-            pltpu.SMEM((kv_heads, slots), jnp.float32),
+            pltpu.VMEM((kv_heads, slots), jnp.float32),
+            pltpu.VMEM((kv_heads, slots), jnp.float32),
             pltpu.VMEM((rows, heads * HD), jnp.bfloat16),
             pltpu.VMEM((slots, PAGE, columns), jnp.bfloat16),
             pltpu.VMEM((slots, PAGE, columns), jnp.bfloat16),
             pltpu.VMEM((heads * rows, HD), jnp.float32),
-            pltpu.VMEM((rows, kv_heads, 8, pages * PAGE), jnp.float32),
-            pltpu.VMEM((rows, kv_heads, 8, pages * PAGE), jnp.float32),
-            pltpu.VMEM((rows, 8, pages * PAGE), jnp.float32),
-            pltpu.VMEM((rows, heads, pages * PAGE), jnp.bfloat16),
+            pltpu.VMEM((rows, columns, HD), jnp.bfloat16),
+            pltpu.VMEM((slots, HD), jnp.float32),
+            pltpu.VMEM((slots, HD), jnp.float32),
+            pltpu.VMEM((rows // 2, pages * PAGE, HD), jnp.float32),
+            pltpu.VMEM((rows // 2, HD, pages * PAGE), jnp.bfloat16),
+            pltpu.VMEM((HD, HD), jnp.float32),
             pltpu.SemaphoreType.DMA((5,)),
             pltpu.SemaphoreType.DMA((2, 4)),
         ],

time: 37.2 us -> 37 us (level)
  no operation moved by 1% of the time
where the time goes in v12:
time: 37 us; the launch traced here: 36.8 us
  blocking collectives  14.6 us (39%)
  starting transfers between devices  8.24 us (22%)
  Pallas kernels  7.97 us (22%)
  waiting for transfers between devices  5.89 us (16%)
    all_to_all x1, blocking collectives, body(): lax.all_to_all(packed, 'kvp', split_axis=0, concat_axis=0, tiled=True)  14.6 us
    ppermute x9, starting transfers between devices, exchange(): lax.ppermute(array, 'kvp', [(i, i ^ partner) for i in range(devices)])  8.24 us
    ppermute x9, waiting for transfers between devices, exchange(): lax.ppermute(array, 'kvp', [(i, i ^ partner) for i in range(devices)])  5.89 us
    pallas_call x1, Pallas kernels, body(): pl.pallas_call(functools.partial(attend_kernel, heads_dev, devices), out_...  4.56 us
    pallas_call x1, Pallas kernels, body(): pl.pallas_call(functools.partial(project_kernel, heads_dev), out_shape=[j...  2 us
  transfers between devices with their start and end apart: 9, of which 6 were waited for; matrix products, arithmetic and copies ran while one was open for 0% of the time, Pallas kernels for 2%

profile of v12, /device:TPU:0, one launch (start us, length us, event | category | flops | bytes accessed | tf_op | source)
XLA Modules:
  0.0 36.8 jit_solution(17916400460442256668)
XLA Ops:
  0.0 0.0 slice-start
  0.0 4.6 %attend.1.staged = f32[16,5,4,128]{3,2,1,0:T(4,128)S(1)} custom-call(s32[4,12]{1,0:T(4,128)} %refs_0_.1, s32[4]{0:T(128)} %refs_1_.1, f32[4,48]{1,0:T(4,128)} %bitcast.4, f32[4,48]{1,0:T(4,128)} %bitcast.5, bf16[4,8192]{1,0:T(4,128)(2,1)} %refs_4_.1, bf16[48,64,512]{2,1,0:T(8,128)(2,1)} %refs_5_.1, bf16[48,64,512]{2,1,0:T(8,128)(2,1)} %refs_6_.1), custom_call_target="tpu_custom_call" | custom-call | flops 100663296 | bytes 6291456 | tf_op jit(solution)/shard_map/attend/pallas_call | solution.py:225
  4.6 0.0 slice-start.1
  4.6 0.0 slice-start.2
  4.6 0.0 slice-start.3
  4.6 14.6 %all_to_all.5.packed = bf16[16,5,4,128]{3,2,1,0:T(4,128)(2,1)S(1)} all-to-all(bf16[16,5,4,128]{3,2,1,0:T(4,128)(2,1)S(1)} %pack.1), channel_id=1, replica_groups=mesh['group'=2,'kvp'=16] {'kvp'}, dimensions={0} | all-to-all | bytes 163840 | tf_op jit(solution)/shard_map/all_to_all | solution.py:267
  19.2 0.0 slice-done
  19.2 0.0 slice-done.1
  19.2 0.0 slice-done.2
  19.3 0.0 slice-done.3
  19.3 2.0 %project_others.1 = (bf16[4,512]{1,0:T(4,128)(2,1)S(1)}, bf16[4,4096]{1,0:T(4,128)(2,1)S(1)}, bf16[4,4096]{1,0:T(4,128)(2,1)S(1)}, bf16[4,4096]{1,0:T(4,128)(2,1)S(1)}) custom-call(bf16[16,5,4,128]{3,2,1,0:T(4,128)(2,1)S(1)} %all_to_all.5.packed, bf16[512,16384]{1,0:T(8,128)(2,1)S(1)} %bitcast.3), custom_call_target="tpu_custom_call" | custom-call | flops 50331648 | bytes 12582912 | tf_op jit(solution)/shard_map/project_others/pallas_call | solution.py:271
  21.3 0.0 collective-permute-start
  21.3 0.2 collective-permute-start.1
  21.4 1.7 %collective-permute-start.2 = (bf16[4,4096]{1,0:T(4,128)(2,1)S(1)}, bf16[4,4096]{1,0:T(4,128)(2,1)S(1)}, u32[]{:S(2)}, u32[]{:S(2)}) collective-permute-start(bf16[4,4096]{1,0:T(4,128)(2,1)S(1)} %get-tuple-element.12), channel_id=1, source_target_pairs={{0,3},{1,2},{2,1},{3,0},{4,7},{5,6},{6,5},{7,4},{8,11},{9,10},{10,... | collective-permute-start | bytes 98312 | tf_op jit(solution)/shard_map/ppermute | solution.py:208
  23.1 0.7 %project_own.1.refs_0_ = bf16[4,4096]{1,0:T(4,128)(2,1)S(1)} custom-call(bf16[4,512]{1,0:T(4,128)(2,1)S(1)} %get-tuple-element.9.left, bf16[512,16384]{1,0:T(8,128)(2,1)S(1)} %bitcast.3), custom_call_target="tpu_custom_call" | custom-call | flops 16777216 | bytes 4194304 | tf_op jit(solution)/shard_map/project_own/pallas_call | solution.py:287
  23.8 0.0 collective-permute-done.refs_1_
  23.8 1.6 %collective-permute-done.1.refs_2_ = bf16[4,4096]{1,0:T(4,128)(2,1)S(1)} collective-permute-done((bf16[4,4096]{1,0:T(4,128)(2,1)S(1)}, bf16[4,4096]{1,0:T(4,128)(2,1)S(1)}, u32[]{:S(2)}, u32[]{:S(2)}) %collective-permute-start.1) | collective-permute-done | bytes 32800 | tf_op jit(solution)/shard_map/ppermute | solution.py:208
  25.4 0.0 collective-permute-done.2.refs_3_
  25.5 1.0 %collective-permute-start.5 = (bf16[4,4096]{1,0:T(4,128)(2,1)S(1)}, bf16[4,4096]{1,0:T(4,128)(2,1)S(1)}, u32[]{:S(2)}, u32[]{:S(2)}) collective-permute-start(bf16[4,4096]{1,0:T(4,128)(2,1)S(1)} %add_near.1.refs_0_), channel_id=1, source_target_pairs={{0,12},{1,13},{2,14},{3,15},{4,8},{5,9},{6,10},{7,11},{8,4},{9,5},... | collective-permute-start | bytes 98312 | tf_op jit(solution)/shard_map/ppermute | solution.py:208
  26.5 0.9 %collective-permute-start.4 = (bf16[4,4096]{1,0:T(4,128)(2,1)S(1)}, bf16[4,4096]{1,0:T(4,128)(2,1)S(1)}, u32[]{:S(2)}, u32[]{:S(2)}) collective-permute-start(bf16[4,4096]{1,0:T(4,128)(2,1)S(1)} %add_near.1.refs_0_), channel_id=1, source_target_pairs={{0,8},{1,9},{2,10},{3,11},{4,12},{5,13},{6,14},{7,15},{8,0},{9,1},... | collective-permute-start | bytes 98312 | tf_op jit(solution)/shard_map/ppermute | solution.py:208
  27.4 2.5 %collective-permute-start.3 = (bf16[4,4096]{1,0:T(4,128)(2,1)S(1)}, bf16[4,4096]{1,0:T(4,128)(2,1)S(1)}, u32[]{:S(2)}, u32[]{:S(2)}) collective-permute-start(bf16[4,4096]{1,0:T(4,128)(2,1)S(1)} %add_near.1.refs_0_), channel_id=1, source_target_pairs={{0,4},{1,5},{2,6},{3,7},{4,0},{5,1},{6,2},{7,3},{8,12},{9,13},{10,... | collective-permute-start | bytes 98312 | tf_op jit(solution)/shard_map/ppermute | solution.py:208
  29.9 1.6 %collective-permute-done.5.refs_3_ = bf16[4,4096]{1,0:T(4,128)(2,1)S(1)} collective-permute-done((bf16[4,4096]{1,0:T(4,128)(2,1)S(1)}, bf16[4,4096]{1,0:T(4,128)(2,1)S(1)}, u32[]{:S(2)}, u32[]{:S(2)}) %collective-permute-start.5) | collective-permute-done | bytes 32800 | tf_op jit(solution)/shard_map/ppermute | solution.py:208
  31.5 0.2 collective-permute-done.4.refs_2_
  31.7 0.2 collective-permute-done.3.refs_1_
  32.0 0.1 collective-permute-start.8
  32.1 1.3 %collective-permute-start.7 = (bf16[4,4096]{1,0:T(4,128)(2,1)S(1)}, bf16[4,4096]{1,0:T(4,128)(2,1)S(1)}, u32[]{:S(2)}, u32[]{:S(2)}) collective-permute-start(bf16[4,4096]{1,0:T(4,128)(2,1)S(1)} %add_far.1.refs_0_), channel_id=1, source_target_pairs={{0,2},{1,3},{2,0},{3,1},{4,6},{5,7},{6,4},{7,5},{8,10},{9,11},{10,... | collective-permute-start | bytes 98312 | tf_op jit(solution)/shard_map/ppermute | solution.py:208
  33.3 0.6 %collective-permute-start.6 = (bf16[4,4096]{1,0:T(4,128)(2,1)S(1)}, bf16[4,4096]{1,0:T(4,128)(2,1)S(1)}, u32[]{:S(2)}, u32[]{:S(2)}) collective-permute-start(bf16[4,4096]{1,0:T(4,128)(2,1)S(1)} %add_far.1.refs_0_), channel_id=1, source_target_pairs={{0,1},{1,0},{2,3},{3,2},{4,5},{5,4},{6,7},{7,6},{8,9},{9,8},{10,11... | collective-permute-start | bytes 98312 | tf_op jit(solution)/shard_map/ppermute | solution.py:208
  33.9 1.6 %collective-permute-done.8.refs_3_ = bf16[4,4096]{1,0:T(4,128)(2,1)S(1)} collective-permute-done((bf16[4,4096]{1,0:T(4,128)(2,1)S(1)}, bf16[4,4096]{1,0:T(4,128)(2,1)S(1)}, u32[]{:S(2)}, u32[]{:S(2)}) %collective-permute-start.8) | collective-permute-done | bytes 32800 | tf_op jit(solution)/shard_map/ppermute | solution.py:208
  35.5 0.6 %collective-permute-done.7.refs_2_ = bf16[4,4096]{1,0:T(4,128)(2,1)S(1)} collective-permute-done((bf16[4,4096]{1,0:T(4,128)(2,1)S(1)}, bf16[4,4096]{1,0:T(4,128)(2,1)S(1)}, u32[]{:S(2)}, u32[]{:S(2)}) %collective-permute-start.7) | collective-permute-done | bytes 32800 | tf_op jit(solution)/shard_map/ppermute | solution.py:208
  36.1 0.0 collective-permute-done.6.refs_1_
  36.1 0.7 %lay.1 = bf16[4,16384]{1,0:T(4,128)(2,1)} custom-call(bf16[4,4096]{1,0:T(4,128)(2,1)S(1)} %add_far.1.refs_0_, bf16[4,4096]{1,0:T(4,128)(2,1)S(1)} %collective-permute-done.6.refs_1_, bf16[4,4096]{1,0:T(4,128)(2,1)S(1)} %collective-permute-done.7.refs_2_, bf16[4,4096]{1,0:T(4,128)(2,1)S(1)} %collective-permute-done.8.refs_3_), custom_call_target="tpu_custom_call" | custom-call | tf_op jit(solution)/shard_map/lay/pallas_call | solution.py:312
  (4 shorter events, 0.1 us)
Async XLA Ops:
  0.0 19.2 %slice-start = ((s8[16777216]{0:T(1024)(128)(4,1)}), s8[4194304]{0:T(1024)(128)(4,1)S(1)}, s32[]{:S(2)}) async-start(s8[16777216]{0:T(1024)(128)(4,1)} %bitcast.2), calls=%async_computation.1 | async-start | bytes 8388608
  4.6 14.7 %slice-start.1 = ((s8[16777216]{0:T(1024)(128)(4,1)}), s8[4194304]{0:T(1024)(128)(4,1)S(1)}, s32[]{:S(2)}) async-start(s8[16777216]{0:T(1024)(128)(4,1)} %bitcast.2), calls=%async_computation.2 | async-start | bytes 8388608
  4.6 14.7 %slice-start.2 = ((s8[16777216]{0:T(1024)(128)(4,1)}), s8[4194304]{0:T(1024)(128)(4,1)S(1)}, s32[]{:S(2)}) async-start(s8[16777216]{0:T(1024)(128)(4,1)} %bitcast.2), calls=%async_computation.3 | async-start | bytes 8388608
  4.6 14.7 %slice-start.3 = ((s8[16777216]{0:T(1024)(128)(4,1)}), s8[4194304]{0:T(1024)(128)(4,1)S(1)}, s32[]{:S(2)}) async-start(s8[16777216]{0:T(1024)(128)(4,1)} %bitcast.2), calls=%async_computation.4 | async-start | bytes 8388608
  21.3 2.5 %collective-permute-start = (bf16[4,4096]{1,0:T(4,128)(2,1)S(1)}, bf16[4,4096]{1,0:T(4,128)(2,1)S(1)}, u32[]{:S(2)}, u32[]{:S(2)}) collective-permute-start(bf16[4,4096]{1,0:T(4,128)(2,1)S(1)} %get-tuple-element.10), channel_id=1, source_target_pairs={{0,1},{1,0},{2,3},{3,2},{4,5},{5,4},{6,7},{7,6},{8,9},{9,8},{10,11... | collective-permute-start | bytes 98312 | tf_op jit(solution)/shard_map/ppermute | solution.py:208
  21.3 4.2 %collective-permute-start.1 = (bf16[4,4096]{1,0:T(4,128)(2,1)S(1)}, bf16[4,4096]{1,0:T(4,128)(2,1)S(1)}, u32[]{:S(2)}, u32[]{:S(2)}) collective-permute-start(bf16[4,4096]{1,0:T(4,128)(2,1)S(1)} %get-tuple-element.11), channel_id=1, source_target_pairs={{0,2},{1,3},{2,0},{3,1},{4,6},{5,7},{6,4},{7,5},{8,10},{9,11},{10,... | collective-permute-start | bytes 98312 | tf_op jit(solution)/shard_map/ppermute | solution.py:208
  21.4 4.0 %collective-permute-start.2 = (bf16[4,4096]{1,0:T(4,128)(2,1)S(1)}, bf16[4,4096]{1,0:T(4,128)(2,1)S(1)}, u32[]{:S(2)}, u32[]{:S(2)}) collective-permute-start(bf16[4,4096]{1,0:T(4,128)(2,1)S(1)} %get-tuple-element.12), channel_id=1, source_target_pairs={{0,3},{1,2},{2,1},{3,0},{4,7},{5,6},{6,5},{7,4},{8,11},{9,10},{10,... | collective-permute-start | bytes 98312 | tf_op jit(solution)/shard_map/ppermute | solution.py:208
  25.5 6.0 %collective-permute-start.5 = (bf16[4,4096]{1,0:T(4,128)(2,1)S(1)}, bf16[4,4096]{1,0:T(4,128)(2,1)S(1)}, u32[]{:S(2)}, u32[]{:S(2)}) collective-permute-start(bf16[4,4096]{1,0:T(4,128)(2,1)S(1)} %add_near.1.refs_0_), channel_id=1, source_target_pairs={{0,12},{1,13},{2,14},{3,15},{4,8},{5,9},{6,10},{7,11},{8,4},{9,5},... | collective-permute-start | bytes 98312 | tf_op jit(solution)/shard_map/ppermute | solution.py:208
  26.5 5.2 %collective-permute-start.4 = (bf16[4,4096]{1,0:T(4,128)(2,1)S(1)}, bf16[4,4096]{1,0:T(4,128)(2,1)S(1)}, u32[]{:S(2)}, u32[]{:S(2)}) collective-permute-start(bf16[4,4096]{1,0:T(4,128)(2,1)S(1)} %add_near.1.refs_0_), channel_id=1, source_target_pairs={{0,8},{1,9},{2,10},{3,11},{4,12},{5,13},{6,14},{7,15},{8,0},{9,1},... | collective-permute-start | bytes 98312 | tf_op jit(solution)/shard_map/ppermute | solution.py:208
  27.4 4.6 %collective-permute-start.3 = (bf16[4,4096]{1,0:T(4,128)(2,1)S(1)}, bf16[4,4096]{1,0:T(4,128)(2,1)S(1)}, u32[]{:S(2)}, u32[]{:S(2)}) collective-permute-start(bf16[4,4096]{1,0:T(4,128)(2,1)S(1)} %add_near.1.refs_0_), channel_id=1, source_target_pairs={{0,4},{1,5},{2,6},{3,7},{4,0},{5,1},{6,2},{7,3},{8,12},{9,13},{10,... | collective-permute-start | bytes 98312 | tf_op jit(solution)/shard_map/ppermute | solution.py:208
  32.0 3.5 %collective-permute-start.8 = (bf16[4,4096]{1,0:T(4,128)(2,1)S(1)}, bf16[4,4096]{1,0:T(4,128)(2,1)S(1)}, u32[]{:S(2)}, u32[]{:S(2)}) collective-permute-start(bf16[4,4096]{1,0:T(4,128)(2,1)S(1)} %add_far.1.refs_0_), channel_id=1, source_target_pairs={{0,3},{1,2},{2,1},{3,0},{4,7},{5,6},{6,5},{7,4},{8,11},{9,10},{10,... | collective-permute-start | bytes 98312 | tf_op jit(solution)/shard_map/ppermute | solution.py:208
  32.1 4.1 %collective-permute-start.7 = (bf16[4,4096]{1,0:T(4,128)(2,1)S(1)}, bf16[4,4096]{1,0:T(4,128)(2,1)S(1)}, u32[]{:S(2)}, u32[]{:S(2)}) collective-permute-start(bf16[4,4096]{1,0:T(4,128)(2,1)S(1)} %add_far.1.refs_0_), channel_id=1, source_target_pairs={{0,2},{1,3},{2,0},{3,1},{4,6},{5,7},{6,4},{7,5},{8,10},{9,11},{10,... | collective-permute-start | bytes 98312 | tf_op jit(solution)/shard_map/ppermute | solution.py:208
  33.3 2.8 %collective-permute-start.6 = (bf16[4,4096]{1,0:T(4,128)(2,1)S(1)}, bf16[4,4096]{1,0:T(4,128)(2,1)S(1)}, u32[]{:S(2)}, u32[]{:S(2)}) collective-permute-start(bf16[4,4096]{1,0:T(4,128)(2,1)S(1)} %add_far.1.refs_0_), channel_id=1, source_target_pairs={{0,1},{1,0},{2,3},{3,2},{4,5},{5,4},{6,7},{7,6},{8,9},{9,8},{10,11... | collective-permute-start | bytes 98312 | tf_op jit(solution)/shard_map/ppermute | solution.py:208

commit v13 on v12

--- a/solution.py
+++ b/solution.py
@@ -10,7 +10,7 @@
 
 HD = 128
 PAGE = 64
-ATTEND_VMEM = 24 * 1024 * 1024
+ATTEND_VMEM = 60 * 1024 * 1024
 PROJECT_VMEM = 8 * 1024 * 1024
 HIDDEN = -1e30
 LOWEST = -1e20
@@ -224,7 +224,7 @@
     part = features // inner
     staged = pl.pallas_call(
         functools.partial(attend_kernel, heads_dev, devices),
-        out_shape=jax.ShapeDtypeStruct((devices, rows + 1, heads_dev, HD), jnp.float32),
+        out_shape=pltpu.VMEM((devices, rows + 1, heads_dev, HD), jnp.float32),
         in_specs=[HBM] * 7,
         out_specs=VMEM,
         scratch_shapes=[

time: 37 us -> 36.7 us (level)
  no operation moved by 1% of the time
where the time goes in v13:
time: 36.7 us; the launch traced here: 36.5 us
  blocking collectives  14.6 us (40%)
  starting transfers between devices  8.24 us (22%)
  Pallas kernels  7.67 us (21%)
  waiting for transfers between devices  5.89 us (16%)
    all_to_all x1, blocking collectives, body(): lax.all_to_all(packed, 'kvp', split_axis=0, concat_axis=0, tiled=True)  14.6 us
    ppermute x9, starting transfers between devices, exchange(): lax.ppermute(array, 'kvp', [(i, i ^ partner) for i in range(devices)])  8.24 us
    ppermute x9, waiting for transfers between devices, exchange(): lax.ppermute(array, 'kvp', [(i, i ^ partner) for i in range(devices)])  5.89 us
    pallas_call x1, Pallas kernels, body(): pl.pallas_call(functools.partial(attend_kernel, heads_dev, devices), out_...  4.27 us
    pallas_call x1, Pallas kernels, body(): pl.pallas_call(functools.partial(project_kernel, heads_dev), out_shape=[j...  1.99 us
  transfers between devices with their start and end apart: 9, of which 6 were waited for; matrix products, arithmetic and copies ran while one was open for 0% of the time, Pallas kernels for 2%

profile of v13, /device:TPU:0, one launch (start us, length us, event | category | flops | bytes accessed | tf_op | source)
XLA Modules:
  0.0 36.5 jit_solution(1608766503648258496)
XLA Ops:
  0.0 4.3 %attend.1.staged = f32[16,5,4,128]{3,2,1,0:T(4,128)S(1)} custom-call(s32[4,12]{1,0:T(4,128)} %refs_0_.1, s32[4]{0:T(128)} %refs_1_.1, f32[4,48]{1,0:T(4,128)} %bitcast.2, f32[4,48]{1,0:T(4,128)} %bitcast.3, bf16[4,8192]{1,0:T(4,128)(2,1)} %refs_4_.1, bf16[48,64,512]{2,1,0:T(8,128)(2,1)} %refs_5_.1, bf16[48,64,512]{2,1,0:T(8,128)(2,1)} %refs_6_.1), custom_call_target="tpu_custom_call" | custom-call | flops 100663296 | bytes 6291456 | tf_op jit(solution)/shard_map/attend/pallas_call | solution.py:225
  4.3 0.0 copy-start
  4.3 14.6 %all_to_all.5.packed = bf16[16,5,4,128]{3,2,1,0:T(4,128)(2,1)S(1)} all-to-all(bf16[16,5,4,128]{3,2,1,0:T(4,128)(2,1)S(1)} %pack.1), channel_id=1, replica_groups=mesh['group'=2,'kvp'=16] {'kvp'}, dimensions={0} | all-to-all | bytes 163840 | tf_op jit(solution)/shard_map/all_to_all | solution.py:267
  18.9 0.0 copy-done
  18.9 2.0 %project_others.1 = (bf16[4,512]{1,0:T(4,128)(2,1)S(1)}, bf16[4,4096]{1,0:T(4,128)(2,1)S(1)}, bf16[4,4096]{1,0:T(4,128)(2,1)S(1)}, bf16[4,4096]{1,0:T(4,128)(2,1)S(1)}) custom-call(bf16[16,5,4,128]{3,2,1,0:T(4,128)(2,1)S(1)} %all_to_all.5.packed, bf16[512,16384]{1,0:T(8,128)(2,1)S(1)} %copy-done), custom_call_target="tpu_custom_call" | custom-call | flops 50331648 | bytes 12582912 | tf_op jit(solution)/shard_map/project_others/pallas_call | solution.py:271
  20.9 0.0 collective-permute-start
  20.9 0.2 collective-permute-start.1
  21.1 1.7 %collective-permute-start.2 = (bf16[4,4096]{1,0:T(4,128)(2,1)S(1)}, bf16[4,4096]{1,0:T(4,128)(2,1)S(1)}, u32[]{:S(2)}, u32[]{:S(2)}) collective-permute-start(bf16[4,4096]{1,0:T(4,128)(2,1)S(1)} %get-tuple-element.12), channel_id=1, source_target_pairs={{0,3},{1,2},{2,1},{3,0},{4,7},{5,6},{6,5},{7,4},{8,11},{9,10},{10,... | collective-permute-start | bytes 98312 | tf_op jit(solution)/shard_map/ppermute | solution.py:208
  22.8 0.7 %project_own.1.refs_0_ = bf16[4,4096]{1,0:T(4,128)(2,1)S(1)} custom-call(bf16[4,512]{1,0:T(4,128)(2,1)S(1)} %get-tuple-element.9.left, bf16[512,16384]{1,0:T(8,128)(2,1)S(1)} %copy-done), custom_call_target="tpu_custom_call" | custom-call | flops 16777216 | bytes 4194304 | tf_op jit(solution)/shard_map/project_own/pallas_call | solution.py:287
  23.4 0.0 collective-permute-done.refs_1_
  23.4 1.6 %collective-permute-done.1.refs_2_ = bf16[4,4096]{1,0:T(4,128)(2,1)S(1)} collective-permute-done((bf16[4,4096]{1,0:T(4,128)(2,1)S(1)}, bf16[4,4096]{1,0:T(4,128)(2,1)S(1)}, u32[]{:S(2)}, u32[]{:S(2)}) %collective-permute-start.1) | collective-permute-done | bytes 32800 | tf_op jit(solution)/shard_map/ppermute | solution.py:208
  25.1 0.0 collective-permute-done.2.refs_3_
  25.1 1.0 %collective-permute-start.5 = (bf16[4,4096]{1,0:T(4,128)(2,1)S(1)}, bf16[4,4096]{1,0:T(4,128)(2,1)S(1)}, u32[]{:S(2)}, u32[]{:S(2)}) collective-permute-start(bf16[4,4096]{1,0:T(4,128)(2,1)S(1)} %add_near.1.refs_0_), channel_id=1, source_target_pairs={{0,12},{1,13},{2,14},{3,15},{4,8},{5,9},{6,10},{7,11},{8,4},{9,5},... | collective-permute-start | bytes 98312 | tf_op jit(solution)/shard_map/ppermute | solution.py:208
  26.2 0.9 %collective-permute-start.4 = (bf16[4,4096]{1,0:T(4,128)(2,1)S(1)}, bf16[4,4096]{1,0:T(4,128)(2,1)S(1)}, u32[]{:S(2)}, u32[]{:S(2)}) collective-permute-start(bf16[4,4096]{1,0:T(4,128)(2,1)S(1)} %add_near.1.refs_0_), channel_id=1, source_target_pairs={{0,8},{1,9},{2,10},{3,11},{4,12},{5,13},{6,14},{7,15},{8,0},{9,1},... | collective-permute-start | bytes 98312 | tf_op jit(solution)/shard_map/ppermute | solution.py:208
  27.0 2.5 %collective-permute-start.3 = (bf16[4,4096]{1,0:T(4,128)(2,1)S(1)}, bf16[4,4096]{1,0:T(4,128)(2,1)S(1)}, u32[]{:S(2)}, u32[]{:S(2)}) collective-permute-start(bf16[4,4096]{1,0:T(4,128)(2,1)S(1)} %add_near.1.refs_0_), channel_id=1, source_target_pairs={{0,4},{1,5},{2,6},{3,7},{4,0},{5,1},{6,2},{7,3},{8,12},{9,13},{10,... | collective-permute-start | bytes 98312 | tf_op jit(solution)/shard_map/ppermute | solution.py:208
  29.6 1.6 %collective-permute-done.5.refs_3_ = bf16[4,4096]{1,0:T(4,128)(2,1)S(1)} collective-permute-done((bf16[4,4096]{1,0:T(4,128)(2,1)S(1)}, bf16[4,4096]{1,0:T(4,128)(2,1)S(1)}, u32[]{:S(2)}, u32[]{:S(2)}) %collective-permute-start.5) | collective-permute-done | bytes 32800 | tf_op jit(solution)/shard_map/ppermute | solution.py:208
  31.1 0.2 collective-permute-done.4.refs_2_
  31.4 0.2 collective-permute-done.3.refs_1_
  31.6 0.1 collective-permute-start.8
  31.7 1.3 %collective-permute-start.7 = (bf16[4,4096]{1,0:T(4,128)(2,1)S(1)}, bf16[4,4096]{1,0:T(4,128)(2,1)S(1)}, u32[]{:S(2)}, u32[]{:S(2)}) collective-permute-start(bf16[4,4096]{1,0:T(4,128)(2,1)S(1)} %add_far.1.refs_0_), channel_id=1, source_target_pairs={{0,2},{1,3},{2,0},{3,1},{4,6},{5,7},{6,4},{7,5},{8,10},{9,11},{10,... | collective-permute-start | bytes 98312 | tf_op jit(solution)/shard_map/ppermute | solution.py:208
  33.0 0.6 %collective-permute-start.6 = (bf16[4,4096]{1,0:T(4,128)(2,1)S(1)}, bf16[4,4096]{1,0:T(4,128)(2,1)S(1)}, u32[]{:S(2)}, u32[]{:S(2)}) collective-permute-start(bf16[4,4096]{1,0:T(4,128)(2,1)S(1)} %add_far.1.refs_0_), channel_id=1, source_target_pairs={{0,1},{1,0},{2,3},{3,2},{4,5},{5,4},{6,7},{7,6},{8,9},{9,8},{10,11... | collective-permute-start | bytes 98312 | tf_op jit(solution)/shard_map/ppermute | solution.py:208
  33.6 1.6 %collective-permute-done.8.refs_3_ = bf16[4,4096]{1,0:T(4,128)(2,1)S(1)} collective-permute-done((bf16[4,4096]{1,0:T(4,128)(2,1)S(1)}, bf16[4,4096]{1,0:T(4,128)(2,1)S(1)}, u32[]{:S(2)}, u32[]{:S(2)}) %collective-permute-start.8) | collective-permute-done | bytes 32800 | tf_op jit(solution)/shard_map/ppermute | solution.py:208
  35.1 0.6 %collective-permute-done.7.refs_2_ = bf16[4,4096]{1,0:T(4,128)(2,1)S(1)} collective-permute-done((bf16[4,4096]{1,0:T(4,128)(2,1)S(1)}, bf16[4,4096]{1,0:T(4,128)(2,1)S(1)}, u32[]{:S(2)}, u32[]{:S(2)}) %collective-permute-start.7) | collective-permute-done | bytes 32800 | tf_op jit(solution)/shard_map/ppermute | solution.py:208
  35.8 0.0 collective-permute-done.6.refs_1_
  35.8 0.7 %lay.1 = bf16[4,16384]{1,0:T(4,128)(2,1)} custom-call(bf16[4,4096]{1,0:T(4,128)(2,1)S(1)} %add_far.1.refs_0_, bf16[4,4096]{1,0:T(4,128)(2,1)S(1)} %collective-permute-done.6.refs_1_, bf16[4,4096]{1,0:T(4,128)(2,1)S(1)} %collective-permute-done.7.refs_2_, bf16[4,4096]{1,0:T(4,128)(2,1)S(1)} %collective-permute-done.8.refs_3_), custom_call_target="tpu_custom_call" | custom-call | tf_op jit(solution)/shard_map/lay/pallas_call | solution.py:312
  (3 shorter events, 0.1 us)
Async XLA Ops:
  4.3 14.6 %copy-start = (bf16[512,16384]{1,0:T(8,128)(2,1)S(1)}, bf16[512,16384]{1,0:T(8,128)(2,1)}, u32[]{:S(2)}) copy-start(bf16[512,16384]{1,0:T(8,128)(2,1)} %weight.3) | copy-start | bytes 50331652
  20.9 2.5 %collective-permute-start = (bf16[4,4096]{1,0:T(4,128)(2,1)S(1)}, bf16[4,4096]{1,0:T(4,128)(2,1)S(1)}, u32[]{:S(2)}, u32[]{:S(2)}) collective-permute-start(bf16[4,4096]{1,0:T(4,128)(2,1)S(1)} %get-tuple-element.10), channel_id=1, source_target_pairs={{0,1},{1,0},{2,3},{3,2},{4,5},{5,4},{6,7},{7,6},{8,9},{9,8},{10,11... | collective-permute-start | bytes 98312 | tf_op jit(solution)/shard_map/ppermute | solution.py:208
  20.9 4.2 %collective-permute-start.1 = (bf16[4,4096]{1,0:T(4,128)(2,1)S(1)}, bf16[4,4096]{1,0:T(4,128)(2,1)S(1)}, u32[]{:S(2)}, u32[]{:S(2)}) collective-permute-start(bf16[4,4096]{1,0:T(4,128)(2,1)S(1)} %get-tuple-element.11), channel_id=1, source_target_pairs={{0,2},{1,3},{2,0},{3,1},{4,6},{5,7},{6,4},{7,5},{8,10},{9,11},{10,... | collective-permute-start | bytes 98312 | tf_op jit(solution)/shard_map/ppermute | solution.py:208
  21.1 4.0 %collective-permute-start.2 = (bf16[4,4096]{1,0:T(4,128)(2,1)S(1)}, bf16[4,4096]{1,0:T(4,128)(2,1)S(1)}, u32[]{:S(2)}, u32[]{:S(2)}) collective-permute-start(bf16[4,4096]{1,0:T(4,128)(2,1)S(1)} %get-tuple-element.12), channel_id=1, source_target_pairs={{0,3},{1,2},{2,1},{3,0},{4,7},{5,6},{6,5},{7,4},{8,11},{9,10},{10,... | collective-permute-start | bytes 98312 | tf_op jit(solution)/shard_map/ppermute | solution.py:208
  25.1 6.0 %collective-permute-start.5 = (bf16[4,4096]{1,0:T(4,128)(2,1)S(1)}, bf16[4,4096]{1,0:T(4,128)(2,1)S(1)}, u32[]{:S(2)}, u32[]{:S(2)}) collective-permute-start(bf16[4,4096]{1,0:T(4,128)(2,1)S(1)} %add_near.1.refs_0_), channel_id=1, source_target_pairs={{0,12},{1,13},{2,14},{3,15},{4,8},{5,9},{6,10},{7,11},{8,4},{9,5},... | collective-permute-start | bytes 98312 | tf_op jit(solution)/shard_map/ppermute | solution.py:208
  26.2 5.2 %collective-permute-start.4 = (bf16[4,4096]{1,0:T(4,128)(2,1)S(1)}, bf16[4,4096]{1,0:T(4,128)(2,1)S(1)}, u32[]{:S(2)}, u32[]{:S(2)}) collective-permute-start(bf16[4,4096]{1,0:T(4,128)(2,1)S(1)} %add_near.1.refs_0_), channel_id=1, source_target_pairs={{0,8},{1,9},{2,10},{3,11},{4,12},{5,13},{6,14},{7,15},{8,0},{9,1},... | collective-permute-start | bytes 98312 | tf_op jit(solution)/shard_map/ppermute | solution.py:208
  27.0 4.6 %collective-permute-start.3 = (bf16[4,4096]{1,0:T(4,128)(2,1)S(1)}, bf16[4,4096]{1,0:T(4,128)(2,1)S(1)}, u32[]{:S(2)}, u32[]{:S(2)}) collective-permute-start(bf16[4,4096]{1,0:T(4,128)(2,1)S(1)} %add_near.1.refs_0_), channel_id=1, source_target_pairs={{0,4},{1,5},{2,6},{3,7},{4,0},{5,1},{6,2},{7,3},{8,12},{9,13},{10,... | collective-permute-start | bytes 98312 | tf_op jit(solution)/shard_map/ppermute | solution.py:208
  31.6 3.5 %collective-permute-start.8 = (bf16[4,4096]{1,0:T(4,128)(2,1)S(1)}, bf16[4,4096]{1,0:T(4,128)(2,1)S(1)}, u32[]{:S(2)}, u32[]{:S(2)}) collective-permute-start(bf16[4,4096]{1,0:T(4,128)(2,1)S(1)} %add_far.1.refs_0_), channel_id=1, source_target_pairs={{0,3},{1,2},{2,1},{3,0},{4,7},{5,6},{6,5},{7,4},{8,11},{9,10},{10,... | collective-permute-start | bytes 98312 | tf_op jit(solution)/shard_map/ppermute | solution.py:208
  31.7 4.1 %collective-permute-start.7 = (bf16[4,4096]{1,0:T(4,128)(2,1)S(1)}, bf16[4,4096]{1,0:T(4,128)(2,1)S(1)}, u32[]{:S(2)}, u32[]{:S(2)}) collective-permute-start(bf16[4,4096]{1,0:T(4,128)(2,1)S(1)} %add_far.1.refs_0_), channel_id=1, source_target_pairs={{0,2},{1,3},{2,0},{3,1},{4,6},{5,7},{6,4},{7,5},{8,10},{9,11},{10,... | collective-permute-start | bytes 98312 | tf_op jit(solution)/shard_map/ppermute | solution.py:208
  33.0 2.8 %collective-permute-start.6 = (bf16[4,4096]{1,0:T(4,128)(2,1)S(1)}, bf16[4,4096]{1,0:T(4,128)(2,1)S(1)}, u32[]{:S(2)}, u32[]{:S(2)}) collective-permute-start(bf16[4,4096]{1,0:T(4,128)(2,1)S(1)} %add_far.1.refs_0_), channel_id=1, source_target_pairs={{0,1},{1,0},{2,3},{3,2},{4,5},{5,4},{6,7},{7,6},{8,9},{9,8},{10,11... | collective-permute-start | bytes 98312 | tf_op jit(solution)/shard_map/ppermute | solution.py:208

commit v14 on v13

--- a/solution.py
+++ b/solution.py
@@ -11,7 +11,6 @@
 HD = 128
 PAGE = 64
 ATTEND_VMEM = 60 * 1024 * 1024
-PROJECT_VMEM = 8 * 1024 * 1024
 HIDDEN = -1e30
 LOWEST = -1e20
 EXCHANGE_FLOPS = 40_000_000_000
@@ -151,11 +150,8 @@
     packed[...] = staged[...].astype(jnp.bfloat16)
 
 
-def project_kernel(heads_dev, packed, weight, left, *refs):
-    outs, attended = refs[:-1], refs[-1]
+def combine_kernel(heads_dev, packed, left, attended):
     rows = left.shape[0]
-    part = outs[0].shape[1]
-    quarter = lax.rem(lax.axis_index("kvp"), len(outs) + 1)
     stats = packed[:, rows].astype(jnp.float32)
     lanes = stats.shape[-1]
 
@@ -174,18 +170,14 @@
         [attended[pl.ds(j, rows, stride=heads_dev), :].astype(jnp.bfloat16) for j in range(heads_dev)], axis=1
     )
     left[...] = rounded
-    for x, out in enumerate(outs):
-        start = pl.multiple_of(jnp.bitwise_xor(quarter, x + 1) * part, part)
-        terms = jnp.dot(rounded, weight[:, pl.ds(start, part)], preferred_element_type=jnp.float32)
-        out[...] = terms.astype(jnp.bfloat16)
-
-
-def project_own_kernel(left, weight, out):
+
+
+def project_kernel(partner, left, weight, out):
     part = out.shape[1]
     quarter = lax.rem(lax.axis_index("kvp"), weight.shape[1] // part)
-    start = pl.multiple_of(quarter * part, part)
+    start = pl.multiple_of(jnp.bitwise_xor(quarter, partner) * part, part)
     terms = jnp.dot(left[...], weight[:, pl.ds(start, part)], preferred_element_type=jnp.float32)
-    out[...] = terms.astype(jnp.bfloat16)
+    out[...] = terms.astype(out.dtype)
 
 
 def add_kernel(*refs):
@@ -268,33 +260,29 @@
 
     resident = pltpu.with_memory_space_constraint(out_weight, pltpu.VMEM)
     depth = heads_dev * HD
-    left, *others = pl.pallas_call(
-        functools.partial(project_kernel, heads_dev),
-        out_shape=[jax.ShapeDtypeStruct((rows, depth), jnp.bfloat16)]
-        + [jax.ShapeDtypeStruct((rows, part), jnp.bfloat16)] * (inner - 1),
-        in_specs=[VMEM, VMEM],
-        out_specs=[VMEM] * inner,
+    cost = pl.CostEstimate(flops=2 * rows * depth * part, bytes_accessed=2 * depth * part, transcendentals=0)
+    small = pltpu.CompilerParams(vmem_limit_bytes=SMALL_VMEM)
+    left = pl.pallas_call(
+        functools.partial(combine_kernel, heads_dev),
+        out_shape=jax.ShapeDtypeStruct((rows, depth), jnp.bfloat16),
+        in_specs=[VMEM],
+        out_specs=VMEM,
         scratch_shapes=[pltpu.VMEM((rows * heads_dev, HD), jnp.float32)],
-        compiler_params=pltpu.CompilerParams(vmem_limit_bytes=PROJECT_VMEM),
-        cost_estimate=pl.CostEstimate(
-            flops=2 * rows * depth * part * (inner - 1),
-            bytes_accessed=2 * depth * part * (inner - 1),
-            transcendentals=0,
-        ),
-        name="project_others",
-    )(received, resident)
-    sent = [exchange(others[x - 1], x, devices) for x in range(1, inner)]
-    own = pl.pallas_call(
-        project_own_kernel,
-        out_shape=jax.ShapeDtypeStruct((rows, part), jnp.bfloat16),
-        in_specs=[VMEM, VMEM],
-        out_specs=VMEM,
-        compiler_params=pltpu.CompilerParams(vmem_limit_bytes=PROJECT_VMEM),
-        cost_estimate=pl.CostEstimate(
-            flops=2 * rows * depth * part, bytes_accessed=2 * depth * part, transcendentals=0
-        ),
-        name="project_own",
-    )(left, resident)
+        compiler_params=small,
+        name="combine",
+    )(received)
+    arrived = []
+    for x in reversed(range(inner)):
+        terms = pl.pallas_call(
+            functools.partial(project_kernel, x),
+            out_shape=jax.ShapeDtypeStruct((rows, part), jnp.bfloat16 if x else jnp.float32),
+            in_specs=[VMEM] * 2,
+            out_specs=VMEM,
+            compiler_params=small,
+            cost_estimate=cost,
+            name=f"project_{x}",
+        )(left, resident)
+        arrived.append(exchange(terms, x, devices) if x else terms)
 
     def add(terms, name):
         return pl.pallas_call(
@@ -306,7 +294,7 @@
             name=name,
         )(*terms)
 
-    mine = add([own] + sent, "add_near")
+    mine = add(arrived, "add_near")
     mine = add([mine] + [exchange(mine, x * inner, devices) for x in range(1, outer)], "add_far")
     parts = [mine] + [exchange(mine, x, devices) for x in range(1, inner)]
     return pl.pallas_call(

time: 36.7 us -> 36.9 us (level)
    pallas_call x2 -> x5, Pallas kernels: 2.65 us -> 2.9 us  [the longest x4 2.65 us: body(): pl.pallas_call(functools.partial(project_kernel, x), out_shape=jax.ShapeD...]
where the time goes in v14:
time: 36.9 us; the launch traced here: 36.7 us
  blocking collectives  14.6 us (40%)
  starting transfers between devices  8.25 us (22%)
  Pallas kernels  7.93 us (21%)
  waiting for transfers between devices  5.86 us (16%)
    all_to_all x1, blocking collectives, body(): lax.all_to_all(packed, 'kvp', split_axis=0, concat_axis=0, tiled=True)  14.6 us
    ppermute x9, starting transfers between devices, exchange(): lax.ppermute(array, 'kvp', [(i, i ^ partner) for i in range(devices)])  8.25 us
    ppermute x9, waiting for transfers between devices, exchange(): lax.ppermute(array, 'kvp', [(i, i ^ partner) for i in range(devices)])  5.86 us
    pallas_call x1, Pallas kernels, body(): pl.pallas_call(functools.partial(attend_kernel, heads_dev, devices), out_...  4.27 us
    pallas_call x4, Pallas kernels, body(): pl.pallas_call(functools.partial(project_kernel, x), out_shape=jax.ShapeD...  2.65 us
  transfers between devices with their start and end apart: 9, of which 6 were waited for; matrix products, arithmetic and copies ran while one was open for 0% of the time, Pallas kernels for 2%

profile of v14, /device:TPU:0, one launch (start us, length us, event | category | flops | bytes accessed | tf_op | source)
XLA Modules:
  0.0 36.7 jit_solution(5567769071127949590)
XLA Ops:
  0.0 4.3 %attend.1.staged = f32[16,5,4,128]{3,2,1,0:T(4,128)S(1)} custom-call(s32[4,12]{1,0:T(4,128)} %refs_0_.1, s32[4]{0:T(128)} %refs_1_.1, f32[4,48]{1,0:T(4,128)} %bitcast.2, f32[4,48]{1,0:T(4,128)} %bitcast.3, bf16[4,8192]{1,0:T(4,128)(2,1)} %refs_4_.1, bf16[48,64,512]{2,1,0:T(8,128)(2,1)} %refs_5_.1, bf16[48,64,512]{2,1,0:T(8,128)(2,1)} %refs_6_.1), custom_call_target="tpu_custom_call" | custom-call | flops 100663296 | bytes 6291456 | tf_op jit(solution)/shard_map/attend/pallas_call | solution.py:217
  4.3 0.0 copy-start
  4.3 14.6 %all_to_all.5.packed = bf16[16,5,4,128]{3,2,1,0:T(4,128)(2,1)S(1)} all-to-all(bf16[16,5,4,128]{3,2,1,0:T(4,128)(2,1)S(1)} %pack.1), channel_id=1, replica_groups=mesh['group'=2,'kvp'=16] {'kvp'}, dimensions={0} | all-to-all | bytes 163840 | tf_op jit(solution)/shard_map/all_to_all | solution.py:259
  18.9 0.3 combine.1.left
  19.2 0.0 copy-done
  19.2 0.7 %project_1.1 = bf16[4,4096]{1,0:T(4,128)(2,1)S(1)} custom-call(bf16[4,512]{1,0:T(4,128)(2,1)S(1)} %combine.1.left, bf16[512,16384]{1,0:T(8,128)(2,1)S(1)} %copy-done), custom_call_target="tpu_custom_call" | custom-call | flops 16777216 | bytes 4194304 | tf_op jit(solution)/shard_map/project_1/pallas_call | solution.py:276
  19.9 0.7 %project_2.1 = bf16[4,4096]{1,0:T(4,128)(2,1)S(1)} custom-call(bf16[4,512]{1,0:T(4,128)(2,1)S(1)} %combine.1.left, bf16[512,16384]{1,0:T(8,128)(2,1)S(1)} %copy-done), custom_call_target="tpu_custom_call" | custom-call | flops 16777216 | bytes 4194304 | tf_op jit(solution)/shard_map/project_2/pallas_call | solution.py:276
  20.5 0.7 %project_3.1 = bf16[4,4096]{1,0:T(4,128)(2,1)S(1)} custom-call(bf16[4,512]{1,0:T(4,128)(2,1)S(1)} %combine.1.left, bf16[512,16384]{1,0:T(8,128)(2,1)S(1)} %copy-done), custom_call_target="tpu_custom_call" | custom-call | flops 16777216 | bytes 4194304 | tf_op jit(solution)/shard_map/project_3/pallas_call | solution.py:276
  21.2 0.0 collective-permute-start
  21.2 1.1 %collective-permute-start.1 = (bf16[4,4096]{1,0:T(4,128)(2,1)S(1)}, bf16[4,4096]{1,0:T(4,128)(2,1)S(1)}, u32[]{:S(2)}, u32[]{:S(2)}) collective-permute-start(bf16[4,4096]{1,0:T(4,128)(2,1)S(1)} %project_2.1), channel_id=1, source_target_pairs={{0,2},{1,3},{2,0},{3,1},{4,6},{5,7},{6,4},{7,5},{8,10},{9,11},{10,... | collective-permute-start | bytes 98312 | tf_op jit(solution)/shard_map/ppermute | solution.py:200
  22.3 0.7 %collective-permute-start.2 = (bf16[4,4096]{1,0:T(4,128)(2,1)S(1)}, bf16[4,4096]{1,0:T(4,128)(2,1)S(1)}, u32[]{:S(2)}, u32[]{:S(2)}) collective-permute-start(bf16[4,4096]{1,0:T(4,128)(2,1)S(1)} %project_1.1), channel_id=1, source_target_pairs={{0,1},{1,0},{2,3},{3,2},{4,5},{5,4},{6,7},{7,6},{8,9},{9,8},{10,11... | collective-permute-start | bytes 98312 | tf_op jit(solution)/shard_map/ppermute | solution.py:200
  23.1 0.7 %project_0.1.refs_3_ = f32[4,4096]{1,0:T(4,128)S(1)} custom-call(bf16[4,512]{1,0:T(4,128)(2,1)S(1)} %combine.1.left, bf16[512,16384]{1,0:T(8,128)(2,1)S(1)} %copy-done), custom_call_target="tpu_custom_call" | custom-call | flops 16777216 | bytes 4194304 | tf_op jit(solution)/shard_map/project_0/pallas_call | solution.py:276
  23.7 0.8 %collective-permute-done.refs_0_ = bf16[4,4096]{1,0:T(4,128)(2,1)S(1)} collective-permute-done((bf16[4,4096]{1,0:T(4,128)(2,1)S(1)}, bf16[4,4096]{1,0:T(4,128)(2,1)S(1)}, u32[]{:S(2)}, u32[]{:S(2)}) %collective-permute-start) | collective-permute-done | bytes 32800 | tf_op jit(solution)/shard_map/ppermute | solution.py:200
  24.6 0.7 %collective-permute-done.1.refs_1_ = bf16[4,4096]{1,0:T(4,128)(2,1)S(1)} collective-permute-done((bf16[4,4096]{1,0:T(4,128)(2,1)S(1)}, bf16[4,4096]{1,0:T(4,128)(2,1)S(1)}, u32[]{:S(2)}, u32[]{:S(2)}) %collective-permute-start.1) | collective-permute-done | bytes 32800 | tf_op jit(solution)/shard_map/ppermute | solution.py:200
  25.3 0.0 collective-permute-done.2.refs_2_
  25.3 1.0 %collective-permute-start.5 = (bf16[4,4096]{1,0:T(4,128)(2,1)S(1)}, bf16[4,4096]{1,0:T(4,128)(2,1)S(1)}, u32[]{:S(2)}, u32[]{:S(2)}) collective-permute-start(bf16[4,4096]{1,0:T(4,128)(2,1)S(1)} %add_near.1.refs_0_), channel_id=1, source_target_pairs={{0,12},{1,13},{2,14},{3,15},{4,8},{5,9},{6,10},{7,11},{8,4},{9,5},... | collective-permute-start | bytes 98312 | tf_op jit(solution)/shard_map/ppermute | solution.py:200
  26.3 0.8 %collective-permute-start.4 = (bf16[4,4096]{1,0:T(4,128)(2,1)S(1)}, bf16[4,4096]{1,0:T(4,128)(2,1)S(1)}, u32[]{:S(2)}, u32[]{:S(2)}) collective-permute-start(bf16[4,4096]{1,0:T(4,128)(2,1)S(1)} %add_near.1.refs_0_), channel_id=1, source_target_pairs={{0,8},{1,9},{2,10},{3,11},{4,12},{5,13},{6,14},{7,15},{8,0},{9,1},... | collective-permute-start | bytes 98312 | tf_op jit(solution)/shard_map/ppermute | solution.py:200
  27.2 2.6 %collective-permute-start.3 = (bf16[4,4096]{1,0:T(4,128)(2,1)S(1)}, bf16[4,4096]{1,0:T(4,128)(2,1)S(1)}, u32[]{:S(2)}, u32[]{:S(2)}) collective-permute-start(bf16[4,4096]{1,0:T(4,128)(2,1)S(1)} %add_near.1.refs_0_), channel_id=1, source_target_pairs={{0,4},{1,5},{2,6},{3,7},{4,0},{5,1},{6,2},{7,3},{8,12},{9,13},{10,... | collective-permute-start | bytes 98312 | tf_op jit(solution)/shard_map/ppermute | solution.py:200
  29.8 1.5 %collective-permute-done.5.refs_3_ = bf16[4,4096]{1,0:T(4,128)(2,1)S(1)} collective-permute-done((bf16[4,4096]{1,0:T(4,128)(2,1)S(1)}, bf16[4,4096]{1,0:T(4,128)(2,1)S(1)}, u32[]{:S(2)}, u32[]{:S(2)}) %collective-permute-start.5) | collective-permute-done | bytes 32800 | tf_op jit(solution)/shard_map/ppermute | solution.py:200
  31.2 0.6 %collective-permute-done.4.refs_2_ = bf16[4,4096]{1,0:T(4,128)(2,1)S(1)} collective-permute-done((bf16[4,4096]{1,0:T(4,128)(2,1)S(1)}, bf16[4,4096]{1,0:T(4,128)(2,1)S(1)}, u32[]{:S(2)}, u32[]{:S(2)}) %collective-permute-start.4) | collective-permute-done | bytes 32800 | tf_op jit(solution)/shard_map/ppermute | solution.py:200
  31.9 0.0 collective-permute-done.3.refs_1_
  31.9 0.1 collective-permute-start.8
  32.0 1.3 %collective-permute-start.7 = (bf16[4,4096]{1,0:T(4,128)(2,1)S(1)}, bf16[4,4096]{1,0:T(4,128)(2,1)S(1)}, u32[]{:S(2)}, u32[]{:S(2)}) collective-permute-start(bf16[4,4096]{1,0:T(4,128)(2,1)S(1)} %add_far.1.refs_0_), channel_id=1, source_target_pairs={{0,2},{1,3},{2,0},{3,1},{4,6},{5,7},{6,4},{7,5},{8,10},{9,11},{10,... | collective-permute-start | bytes 98312 | tf_op jit(solution)/shard_map/ppermute | solution.py:200
  33.2 0.6 %collective-permute-start.6 = (bf16[4,4096]{1,0:T(4,128)(2,1)S(1)}, bf16[4,4096]{1,0:T(4,128)(2,1)S(1)}, u32[]{:S(2)}, u32[]{:S(2)}) collective-permute-start(bf16[4,4096]{1,0:T(4,128)(2,1)S(1)} %add_far.1.refs_0_), channel_id=1, source_target_pairs={{0,1},{1,0},{2,3},{3,2},{4,5},{5,4},{6,7},{7,6},{8,9},{9,8},{10,11... | collective-permute-start | bytes 98312 | tf_op jit(solution)/shard_map/ppermute | solution.py:200
  33.8 1.6 %collective-permute-done.8.refs_3_ = bf16[4,4096]{1,0:T(4,128)(2,1)S(1)} collective-permute-done((bf16[4,4096]{1,0:T(4,128)(2,1)S(1)}, bf16[4,4096]{1,0:T(4,128)(2,1)S(1)}, u32[]{:S(2)}, u32[]{:S(2)}) %collective-permute-start.8) | collective-permute-done | bytes 32800 | tf_op jit(solution)/shard_map/ppermute | solution.py:200
  35.4 0.6 %collective-permute-done.7.refs_2_ = bf16[4,4096]{1,0:T(4,128)(2,1)S(1)} collective-permute-done((bf16[4,4096]{1,0:T(4,128)(2,1)S(1)}, bf16[4,4096]{1,0:T(4,128)(2,1)S(1)}, u32[]{:S(2)}, u32[]{:S(2)}) %collective-permute-start.7) | collective-permute-done | bytes 32800 | tf_op jit(solution)/shard_map/ppermute | solution.py:200
  36.0 0.0 collective-permute-done.6.refs_1_
  36.0 0.7 %lay.1 = bf16[4,16384]{1,0:T(4,128)(2,1)} custom-call(bf16[4,4096]{1,0:T(4,128)(2,1)S(1)} %add_far.1.refs_0_, bf16[4,4096]{1,0:T(4,128)(2,1)S(1)} %collective-permute-done.6.refs_1_, bf16[4,4096]{1,0:T(4,128)(2,1)S(1)} %collective-permute-done.7.refs_2_, bf16[4,4096]{1,0:T(4,128)(2,1)S(1)} %collective-permute-done.8.refs_3_), custom_call_target="tpu_custom_call" | custom-call | tf_op jit(solution)/shard_map/lay/pallas_call | solution.py:300
  (3 shorter events, 0.1 us)
Async XLA Ops:
  4.3 14.9 %copy-start = (bf16[512,16384]{1,0:T(8,128)(2,1)S(1)}, bf16[512,16384]{1,0:T(8,128)(2,1)}, u32[]{:S(2)}) copy-start(bf16[512,16384]{1,0:T(8,128)(2,1)} %weight.7) | copy-start | bytes 50331652
  21.2 3.4 %collective-permute-start = (bf16[4,4096]{1,0:T(4,128)(2,1)S(1)}, bf16[4,4096]{1,0:T(4,128)(2,1)S(1)}, u32[]{:S(2)}, u32[]{:S(2)}) collective-permute-start(bf16[4,4096]{1,0:T(4,128)(2,1)S(1)} %project_3.1), channel_id=1, source_target_pairs={{0,3},{1,2},{2,1},{3,0},{4,7},{5,6},{6,5},{7,4},{8,11},{9,10},{10,... | collective-permute-start | bytes 98312 | tf_op jit(solution)/shard_map/ppermute | solution.py:200
  21.2 4.1 %collective-permute-start.1 = (bf16[4,4096]{1,0:T(4,128)(2,1)S(1)}, bf16[4,4096]{1,0:T(4,128)(2,1)S(1)}, u32[]{:S(2)}, u32[]{:S(2)}) collective-permute-start(bf16[4,4096]{1,0:T(4,128)(2,1)S(1)} %project_2.1), channel_id=1, source_target_pairs={{0,2},{1,3},{2,0},{3,1},{4,6},{5,7},{6,4},{7,5},{8,10},{9,11},{10,... | collective-permute-start | bytes 98312 | tf_op jit(solution)/shard_map/ppermute | solution.py:200
  22.3 2.9 %collective-permute-start.2 = (bf16[4,4096]{1,0:T(4,128)(2,1)S(1)}, bf16[4,4096]{1,0:T(4,128)(2,1)S(1)}, u32[]{:S(2)}, u32[]{:S(2)}) collective-permute-start(bf16[4,4096]{1,0:T(4,128)(2,1)S(1)} %project_1.1), channel_id=1, source_target_pairs={{0,1},{1,0},{2,3},{3,2},{4,5},{5,4},{6,7},{7,6},{8,9},{9,8},{10,11... | collective-permute-start | bytes 98312 | tf_op jit(solution)/shard_map/ppermute | solution.py:200
  25.3 5.9 %collective-permute-start.5 = (bf16[4,4096]{1,0:T(4,128)(2,1)S(1)}, bf16[4,4096]{1,0:T(4,128)(2,1)S(1)}, u32[]{:S(2)}, u32[]{:S(2)}) collective-permute-start(bf16[4,4096]{1,0:T(4,128)(2,1)S(1)} %add_near.1.refs_0_), channel_id=1, source_target_pairs={{0,12},{1,13},{2,14},{3,15},{4,8},{5,9},{6,10},{7,11},{8,4},{9,5},... | collective-permute-start | bytes 98312 | tf_op jit(solution)/shard_map/ppermute | solution.py:200
  26.3 5.5 %collective-permute-start.4 = (bf16[4,4096]{1,0:T(4,128)(2,1)S(1)}, bf16[4,4096]{1,0:T(4,128)(2,1)S(1)}, u32[]{:S(2)}, u32[]{:S(2)}) collective-permute-start(bf16[4,4096]{1,0:T(4,128)(2,1)S(1)} %add_near.1.refs_0_), channel_id=1, source_target_pairs={{0,8},{1,9},{2,10},{3,11},{4,12},{5,13},{6,14},{7,15},{8,0},{9,1},... | collective-permute-start | bytes 98312 | tf_op jit(solution)/shard_map/ppermute | solution.py:200
  27.2 4.7 %collective-permute-start.3 = (bf16[4,4096]{1,0:T(4,128)(2,1)S(1)}, bf16[4,4096]{1,0:T(4,128)(2,1)S(1)}, u32[]{:S(2)}, u32[]{:S(2)}) collective-permute-start(bf16[4,4096]{1,0:T(4,128)(2,1)S(1)} %add_near.1.refs_0_), channel_id=1, source_target_pairs={{0,4},{1,5},{2,6},{3,7},{4,0},{5,1},{6,2},{7,3},{8,12},{9,13},{10,... | collective-permute-start | bytes 98312 | tf_op jit(solution)/shard_map/ppermute | solution.py:200
  31.9 3.5 %collective-permute-start.8 = (bf16[4,4096]{1,0:T(4,128)(2,1)S(1)}, bf16[4,4096]{1,0:T(4,128)(2,1)S(1)}, u32[]{:S(2)}, u32[]{:S(2)}) collective-permute-start(bf16[4,4096]{1,0:T(4,128)(2,1)S(1)} %add_far.1.refs_0_), channel_id=1, source_target_pairs={{0,3},{1,2},{2,1},{3,0},{4,7},{5,6},{6,5},{7,4},{8,11},{9,10},{10,... | collective-permute-start | bytes 98312 | tf_op jit(solution)/shard_map/ppermute | solution.py:200
  32.0 4.1 %collective-permute-start.7 = (bf16[4,4096]{1,0:T(4,128)(2,1)S(1)}, bf16[4,4096]{1,0:T(4,128)(2,1)S(1)}, u32[]{:S(2)}, u32[]{:S(2)}) collective-permute-start(bf16[4,4096]{1,0:T(4,128)(2,1)S(1)} %add_far.1.refs_0_), channel_id=1, source_target_pairs={{0,2},{1,3},{2,0},{3,1},{4,6},{5,7},{6,4},{7,5},{8,10},{9,11},{10,... | collective-permute-start | bytes 98312 | tf_op jit(solution)/shard_map/ppermute | solution.py:200
  33.2 2.8 %collective-permute-start.6 = (bf16[4,4096]{1,0:T(4,128)(2,1)S(1)}, bf16[4,4096]{1,0:T(4,128)(2,1)S(1)}, u32[]{:S(2)}, u32[]{:S(2)}) collective-permute-start(bf16[4,4096]{1,0:T(4,128)(2,1)S(1)} %add_far.1.refs_0_), channel_id=1, source_target_pairs={{0,1},{1,0},{2,3},{3,2},{4,5},{5,4},{6,7},{7,6},{8,9},{9,8},{10,11... | collective-permute-start | bytes 98312 | tf_op jit(solution)/shard_map/ppermute | solution.py:200

commit v15 on v14

--- a/solution.py
+++ b/solution.py
@@ -260,7 +260,7 @@
 
     resident = pltpu.with_memory_space_constraint(out_weight, pltpu.VMEM)
     depth = heads_dev * HD
-    cost = pl.CostEstimate(flops=2 * rows * depth * part, bytes_accessed=2 * depth * part, transcendentals=0)
+    cost = pl.CostEstimate(flops=1024, bytes_accessed=1024, transcendentals=0)
     small = pltpu.CompilerParams(vmem_limit_bytes=SMALL_VMEM)
     left = pl.pallas_call(
         functools.partial(combine_kernel, heads_dev),

time: 36.9 us -> 36.2 us (0.981)
  waiting for transfers between devices: 5.86 us -> 5.19 us
    ppermute x9, waiting for transfers between devices: 5.86 us -> 5.19 us  [exchange(): lax.ppermute(array, 'kvp', [(i, i ^ partner) for i in range(devices)])]
  transfers between devices with their start and end apart: 9 -> 9, of which waited for: 6 -> 6; matrix products, arithmetic and copies ran while one was open for 0% -> 0% of each run, Pallas kernels for 2% -> 4%
where the time goes in v15:
time: 36.2 us; the launch traced here: 36 us
  blocking collectives  14.6 us (40%)
  starting transfers between devices  8.27 us (23%)
  Pallas kernels  7.91 us (22%)
  waiting for transfers between devices  5.19 us (14%)
    all_to_all x1, blocking collectives, body(): lax.all_to_all(packed, 'kvp', split_axis=0, concat_axis=0, tiled=True)  14.6 us
    ppermute x9, starting transfers between devices, exchange(): lax.ppermute(array, 'kvp', [(i, i ^ partner) for i in range(devices)])  8.27 us
    ppermute x9, waiting for transfers between devices, exchange(): lax.ppermute(array, 'kvp', [(i, i ^ partner) for i in range(devices)])  5.19 us
    pallas_call x1, Pallas kernels, body(): pl.pallas_call(functools.partial(attend_kernel, heads_dev, devices), out_...  4.27 us
    pallas_call x4, Pallas kernels, body(): pl.pallas_call(functools.partial(project_kernel, x), out_shape=jax.ShapeD...  2.63 us
  transfers between devices with their start and end apart: 9, of which 6 were waited for; matrix products, arithmetic and copies ran while one was open for 0% of the time, Pallas kernels for 4%

profile of v15, /device:TPU:0, one launch (start us, length us, event | category | flops | bytes accessed | tf_op | source)
XLA Modules:
  0.0 36.0 jit_solution(15201403460907835283)
XLA Ops:
  0.0 4.3 %attend.1.staged = f32[16,5,4,128]{3,2,1,0:T(4,128)S(1)} custom-call(s32[4,12]{1,0:T(4,128)} %refs_0_.1, s32[4]{0:T(128)} %refs_1_.1, f32[4,48]{1,0:T(4,128)} %bitcast.2, f32[4,48]{1,0:T(4,128)} %bitcast.3, bf16[4,8192]{1,0:T(4,128)(2,1)} %refs_4_.1, bf16[48,64,512]{2,1,0:T(8,128)(2,1)} %refs_5_.1, bf16[48,64,512]{2,1,0:T(8,128)(2,1)} %refs_6_.1), custom_call_target="tpu_custom_call" | custom-call | flops 100663296 | bytes 6291456 | tf_op jit(solution)/shard_map/attend/pallas_call | solution.py:217
  4.3 0.0 copy-start
  4.3 14.6 %all_to_all.5.packed = bf16[16,5,4,128]{3,2,1,0:T(4,128)(2,1)S(1)} all-to-all(bf16[16,5,4,128]{3,2,1,0:T(4,128)(2,1)S(1)} %pack.1), channel_id=1, replica_groups=mesh['group'=2,'kvp'=16] {'kvp'}, dimensions={0} | all-to-all | bytes 163840 | tf_op jit(solution)/shard_map/all_to_all | solution.py:259
  18.9 0.3 combine.1.left
  19.2 0.0 copy-done
  19.2 0.7 %project_2.1 = bf16[4,4096]{1,0:T(4,128)(2,1)S(1)} custom-call(bf16[4,512]{1,0:T(4,128)(2,1)S(1)} %combine.1.left, bf16[512,16384]{1,0:T(8,128)(2,1)S(1)} %copy-done), custom_call_target="tpu_custom_call" | custom-call | flops 1024 | bytes 1024 | tf_op jit(solution)/shard_map/project_2/pallas_call | solution.py:276
  19.9 0.7 %project_3.1 = bf16[4,4096]{1,0:T(4,128)(2,1)S(1)} custom-call(bf16[4,512]{1,0:T(4,128)(2,1)S(1)} %combine.1.left, bf16[512,16384]{1,0:T(8,128)(2,1)S(1)} %copy-done), custom_call_target="tpu_custom_call" | custom-call | flops 1024 | bytes 1024 | tf_op jit(solution)/shard_map/project_3/pallas_call | solution.py:276
  20.5 0.0 collective-permute-start
  20.5 1.1 %collective-permute-start.1 = (bf16[4,4096]{1,0:T(4,128)(2,1)S(1)}, bf16[4,4096]{1,0:T(4,128)(2,1)S(1)}, u32[]{:S(2)}, u32[]{:S(2)}) collective-permute-start(bf16[4,4096]{1,0:T(4,128)(2,1)S(1)} %project_2.1), channel_id=1, source_target_pairs={{0,2},{1,3},{2,0},{3,1},{4,6},{5,7},{6,4},{7,5},{8,10},{9,11},{10,... | collective-permute-start | bytes 98312 | tf_op jit(solution)/shard_map/ppermute | solution.py:200
  21.7 0.7 %project_1.1 = bf16[4,4096]{1,0:T(4,128)(2,1)S(1)} custom-call(bf16[4,512]{1,0:T(4,128)(2,1)S(1)} %combine.1.left, bf16[512,16384]{1,0:T(8,128)(2,1)S(1)} %copy-done), custom_call_target="tpu_custom_call" | custom-call | flops 1024 | bytes 1024 | tf_op jit(solution)/shard_map/project_1/pallas_call | solution.py:276
  22.3 0.8 %collective-permute-start.2 = (bf16[4,4096]{1,0:T(4,128)(2,1)S(1)}, bf16[4,4096]{1,0:T(4,128)(2,1)S(1)}, u32[]{:S(2)}, u32[]{:S(2)}) collective-permute-start(bf16[4,4096]{1,0:T(4,128)(2,1)S(1)} %project_1.1), channel_id=1, source_target_pairs={{0,1},{1,0},{2,3},{3,2},{4,5},{5,4},{6,7},{7,6},{8,9},{9,8},{10,11... | collective-permute-start | bytes 98312 | tf_op jit(solution)/shard_map/ppermute | solution.py:200
  23.1 0.7 %project_0.1.refs_3_ = f32[4,4096]{1,0:T(4,128)S(1)} custom-call(bf16[4,512]{1,0:T(4,128)(2,1)S(1)} %combine.1.left, bf16[512,16384]{1,0:T(8,128)(2,1)S(1)} %copy-done), custom_call_target="tpu_custom_call" | custom-call | flops 1024 | bytes 1024 | tf_op jit(solution)/shard_map/project_0/pallas_call | solution.py:276
  23.7 0.2 collective-permute-done.refs_0_
  23.9 0.7 %collective-permute-done.1.refs_1_ = bf16[4,4096]{1,0:T(4,128)(2,1)S(1)} collective-permute-done((bf16[4,4096]{1,0:T(4,128)(2,1)S(1)}, bf16[4,4096]{1,0:T(4,128)(2,1)S(1)}, u32[]{:S(2)}, u32[]{:S(2)}) %collective-permute-start.1) | collective-permute-done | bytes 32800 | tf_op jit(solution)/shard_map/ppermute | solution.py:200
  24.6 0.0 collective-permute-done.2.refs_2_
  24.6 1.0 %collective-permute-start.5 = (bf16[4,4096]{1,0:T(4,128)(2,1)S(1)}, bf16[4,4096]{1,0:T(4,128)(2,1)S(1)}, u32[]{:S(2)}, u32[]{:S(2)}) collective-permute-start(bf16[4,4096]{1,0:T(4,128)(2,1)S(1)} %add_near.1.refs_0_), channel_id=1, source_target_pairs={{0,12},{1,13},{2,14},{3,15},{4,8},{5,9},{6,10},{7,11},{8,4},{9,5},... | collective-permute-start | bytes 98312 | tf_op jit(solution)/shard_map/ppermute | solution.py:200
  25.6 0.8 %collective-permute-start.4 = (bf16[4,4096]{1,0:T(4,128)(2,1)S(1)}, bf16[4,4096]{1,0:T(4,128)(2,1)S(1)}, u32[]{:S(2)}, u32[]{:S(2)}) collective-permute-start(bf16[4,4096]{1,0:T(4,128)(2,1)S(1)} %add_near.1.refs_0_), channel_id=1, source_target_pairs={{0,8},{1,9},{2,10},{3,11},{4,12},{5,13},{6,14},{7,15},{8,0},{9,1},... | collective-permute-start | bytes 98312 | tf_op jit(solution)/shard_map/ppermute | solution.py:200
  26.5 2.6 %collective-permute-start.3 = (bf16[4,4096]{1,0:T(4,128)(2,1)S(1)}, bf16[4,4096]{1,0:T(4,128)(2,1)S(1)}, u32[]{:S(2)}, u32[]{:S(2)}) collective-permute-start(bf16[4,4096]{1,0:T(4,128)(2,1)S(1)} %add_near.1.refs_0_), channel_id=1, source_target_pairs={{0,4},{1,5},{2,6},{3,7},{4,0},{5,1},{6,2},{7,3},{8,12},{9,13},{10,... | collective-permute-start | bytes 98312 | tf_op jit(solution)/shard_map/ppermute | solution.py:200
  29.1 1.5 %collective-permute-done.5.refs_3_ = bf16[4,4096]{1,0:T(4,128)(2,1)S(1)} collective-permute-done((bf16[4,4096]{1,0:T(4,128)(2,1)S(1)}, bf16[4,4096]{1,0:T(4,128)(2,1)S(1)}, u32[]{:S(2)}, u32[]{:S(2)}) %collective-permute-start.5) | collective-permute-done | bytes 32800 | tf_op jit(solution)/shard_map/ppermute | solution.py:200
  30.6 0.6 %collective-permute-done.4.refs_2_ = bf16[4,4096]{1,0:T(4,128)(2,1)S(1)} collective-permute-done((bf16[4,4096]{1,0:T(4,128)(2,1)S(1)}, bf16[4,4096]{1,0:T(4,128)(2,1)S(1)}, u32[]{:S(2)}, u32[]{:S(2)}) %collective-permute-start.4) | collective-permute-done | bytes 32800 | tf_op jit(solution)/shard_map/ppermute | solution.py:200
  31.2 0.0 collective-permute-done.3.refs_1_
  31.2 0.1 collective-permute-start.8
  31.3 1.3 %collective-permute-start.7 = (bf16[4,4096]{1,0:T(4,128)(2,1)S(1)}, bf16[4,4096]{1,0:T(4,128)(2,1)S(1)}, u32[]{:S(2)}, u32[]{:S(2)}) collective-permute-start(bf16[4,4096]{1,0:T(4,128)(2,1)S(1)} %add_far.1.refs_0_), channel_id=1, source_target_pairs={{0,2},{1,3},{2,0},{3,1},{4,6},{5,7},{6,4},{7,5},{8,10},{9,11},{10,... | collective-permute-start | bytes 98312 | tf_op jit(solution)/shard_map/ppermute | solution.py:200
  32.6 0.6 %collective-permute-start.6 = (bf16[4,4096]{1,0:T(4,128)(2,1)S(1)}, bf16[4,4096]{1,0:T(4,128)(2,1)S(1)}, u32[]{:S(2)}, u32[]{:S(2)}) collective-permute-start(bf16[4,4096]{1,0:T(4,128)(2,1)S(1)} %add_far.1.refs_0_), channel_id=1, source_target_pairs={{0,1},{1,0},{2,3},{3,2},{4,5},{5,4},{6,7},{7,6},{8,9},{9,8},{10,11... | collective-permute-start | bytes 98312 | tf_op jit(solution)/shard_map/ppermute | solution.py:200
  33.2 1.6 %collective-permute-done.8.refs_3_ = bf16[4,4096]{1,0:T(4,128)(2,1)S(1)} collective-permute-done((bf16[4,4096]{1,0:T(4,128)(2,1)S(1)}, bf16[4,4096]{1,0:T(4,128)(2,1)S(1)}, u32[]{:S(2)}, u32[]{:S(2)}) %collective-permute-start.8) | collective-permute-done | bytes 32800 | tf_op jit(solution)/shard_map/ppermute | solution.py:200
  34.7 0.6 %collective-permute-done.7.refs_2_ = bf16[4,4096]{1,0:T(4,128)(2,1)S(1)} collective-permute-done((bf16[4,4096]{1,0:T(4,128)(2,1)S(1)}, bf16[4,4096]{1,0:T(4,128)(2,1)S(1)}, u32[]{:S(2)}, u32[]{:S(2)}) %collective-permute-start.7) | collective-permute-done | bytes 32800 | tf_op jit(solution)/shard_map/ppermute | solution.py:200
  35.4 0.0 collective-permute-done.6.refs_1_
  35.4 0.7 %lay.1 = bf16[4,16384]{1,0:T(4,128)(2,1)} custom-call(bf16[4,4096]{1,0:T(4,128)(2,1)S(1)} %add_far.1.refs_0_, bf16[4,4096]{1,0:T(4,128)(2,1)S(1)} %collective-permute-done.6.refs_1_, bf16[4,4096]{1,0:T(4,128)(2,1)S(1)} %collective-permute-done.7.refs_2_, bf16[4,4096]{1,0:T(4,128)(2,1)S(1)} %collective-permute-done.8.refs_3_), custom_call_target="tpu_custom_call" | custom-call | tf_op jit(solution)/shard_map/lay/pallas_call | solution.py:300
  (3 shorter events, 0.1 us)
Async XLA Ops:
  4.3 14.9 %copy-start = (bf16[512,16384]{1,0:T(8,128)(2,1)S(1)}, bf16[512,16384]{1,0:T(8,128)(2,1)}, u32[]{:S(2)}) copy-start(bf16[512,16384]{1,0:T(8,128)(2,1)} %weight.7) | copy-start | bytes 50331652
  20.5 3.4 %collective-permute-start = (bf16[4,4096]{1,0:T(4,128)(2,1)S(1)}, bf16[4,4096]{1,0:T(4,128)(2,1)S(1)}, u32[]{:S(2)}, u32[]{:S(2)}) collective-permute-start(bf16[4,4096]{1,0:T(4,128)(2,1)S(1)} %project_3.1), channel_id=1, source_target_pairs={{0,3},{1,2},{2,1},{3,0},{4,7},{5,6},{6,5},{7,4},{8,11},{9,10},{10,... | collective-permute-start | bytes 98312 | tf_op jit(solution)/shard_map/ppermute | solution.py:200
  20.5 4.1 %collective-permute-start.1 = (bf16[4,4096]{1,0:T(4,128)(2,1)S(1)}, bf16[4,4096]{1,0:T(4,128)(2,1)S(1)}, u32[]{:S(2)}, u32[]{:S(2)}) collective-permute-start(bf16[4,4096]{1,0:T(4,128)(2,1)S(1)} %project_2.1), channel_id=1, source_target_pairs={{0,2},{1,3},{2,0},{3,1},{4,6},{5,7},{6,4},{7,5},{8,10},{9,11},{10,... | collective-permute-start | bytes 98312 | tf_op jit(solution)/shard_map/ppermute | solution.py:200
  22.3 2.3 %collective-permute-start.2 = (bf16[4,4096]{1,0:T(4,128)(2,1)S(1)}, bf16[4,4096]{1,0:T(4,128)(2,1)S(1)}, u32[]{:S(2)}, u32[]{:S(2)}) collective-permute-start(bf16[4,4096]{1,0:T(4,128)(2,1)S(1)} %project_1.1), channel_id=1, source_target_pairs={{0,1},{1,0},{2,3},{3,2},{4,5},{5,4},{6,7},{7,6},{8,9},{9,8},{10,11... | collective-permute-start | bytes 98312 | tf_op jit(solution)/shard_map/ppermute | solution.py:200
  24.6 5.9 %collective-permute-start.5 = (bf16[4,4096]{1,0:T(4,128)(2,1)S(1)}, bf16[4,4096]{1,0:T(4,128)(2,1)S(1)}, u32[]{:S(2)}, u32[]{:S(2)}) collective-permute-start(bf16[4,4096]{1,0:T(4,128)(2,1)S(1)} %add_near.1.refs_0_), channel_id=1, source_target_pairs={{0,12},{1,13},{2,14},{3,15},{4,8},{5,9},{6,10},{7,11},{8,4},{9,5},... | collective-permute-start | bytes 98312 | tf_op jit(solution)/shard_map/ppermute | solution.py:200
  25.6 5.5 %collective-permute-start.4 = (bf16[4,4096]{1,0:T(4,128)(2,1)S(1)}, bf16[4,4096]{1,0:T(4,128)(2,1)S(1)}, u32[]{:S(2)}, u32[]{:S(2)}) collective-permute-start(bf16[4,4096]{1,0:T(4,128)(2,1)S(1)} %add_near.1.refs_0_), channel_id=1, source_target_pairs={{0,8},{1,9},{2,10},{3,11},{4,12},{5,13},{6,14},{7,15},{8,0},{9,1},... | collective-permute-start | bytes 98312 | tf_op jit(solution)/shard_map/ppermute | solution.py:200
  26.5 4.7 %collective-permute-start.3 = (bf16[4,4096]{1,0:T(4,128)(2,1)S(1)}, bf16[4,4096]{1,0:T(4,128)(2,1)S(1)}, u32[]{:S(2)}, u32[]{:S(2)}) collective-permute-start(bf16[4,4096]{1,0:T(4,128)(2,1)S(1)} %add_near.1.refs_0_), channel_id=1, source_target_pairs={{0,4},{1,5},{2,6},{3,7},{4,0},{5,1},{6,2},{7,3},{8,12},{9,13},{10,... | collective-permute-start | bytes 98312 | tf_op jit(solution)/shard_map/ppermute | solution.py:200
  31.2 3.5 %collective-permute-start.8 = (bf16[4,4096]{1,0:T(4,128)(2,1)S(1)}, bf16[4,4096]{1,0:T(4,128)(2,1)S(1)}, u32[]{:S(2)}, u32[]{:S(2)}) collective-permute-start(bf16[4,4096]{1,0:T(4,128)(2,1)S(1)} %add_far.1.refs_0_), channel_id=1, source_target_pairs={{0,3},{1,2},{2,1},{3,0},{4,7},{5,6},{6,5},{7,4},{8,11},{9,10},{10,... | collective-permute-start | bytes 98312 | tf_op jit(solution)/shard_map/ppermute | solution.py:200
  31.3 4.1 %collective-permute-start.7 = (bf16[4,4096]{1,0:T(4,128)(2,1)S(1)}, bf16[4,4096]{1,0:T(4,128)(2,1)S(1)}, u32[]{:S(2)}, u32[]{:S(2)}) collective-permute-start(bf16[4,4096]{1,0:T(4,128)(2,1)S(1)} %add_far.1.refs_0_), channel_id=1, source_target_pairs={{0,2},{1,3},{2,0},{3,1},{4,6},{5,7},{6,4},{7,5},{8,10},{9,11},{10,... | collective-permute-start | bytes 98312 | tf_op jit(solution)/shard_map/ppermute | solution.py:200
  32.6 2.8 %collective-permute-start.6 = (bf16[4,4096]{1,0:T(4,128)(2,1)S(1)}, bf16[4,4096]{1,0:T(4,128)(2,1)S(1)}, u32[]{:S(2)}, u32[]{:S(2)}) collective-permute-start(bf16[4,4096]{1,0:T(4,128)(2,1)S(1)} %add_far.1.refs_0_), channel_id=1, source_target_pairs={{0,1},{1,0},{2,3},{3,2},{4,5},{5,4},{6,7},{7,6},{8,9},{9,8},{10,11... | collective-permute-start | bytes 98312 | tf_op jit(solution)/shard_map/ppermute | solution.py:200

commit v16 on v15

--- a/solution.py
+++ b/solution.py
@@ -97,13 +97,17 @@
 
     for copy in large[0]:
         copy.wait()
-    for r in range(rows):
-        both = jnp.dot(pages_of(key_buf, r, slice(None)), query_blocks[r], preferred_element_type=jnp.float32)
-        if r % 2 == 0:
-            scores[r // 2] = both
-        else:
-            scores[r // 2] += both
-    for r in range(0, rows, 2):
+    def score(r):
+        for i in (0, 1):
+            both = jnp.dot(
+                pages_of(key_buf, r + i, slice(None)), query_blocks[r + i], preferred_element_type=jnp.float32
+            )
+            if i == 0:
+                scores[r // 2] = both
+            else:
+                scores[r // 2] += both
+
+    def weigh(r):
         length = jnp.where(first_of_pair, lengths[r], lengths[r + 1]) - me * context
         highest = jnp.full((PAGE, HD), LOWEST, jnp.float32)
         for p in range(pages):
@@ -126,12 +130,8 @@
         for at, value in enumerate((high, low, total_high, total_low)):
             stats[4 * r + at : 4 * r + at + 1, :] = value
             stats[4 * r + 4 + at : 4 * r + 5 + at, :] = pltpu.roll(value, HD - heads, axis=1)
-    by_head = stats[...].T
-    for d in range(devices):
-        staged[d, rows] = by_head[d * heads_dev : (d + 1) * heads_dev]
-    for copy in large[1]:
-        copy.wait()
-    for r in range(rows):
+
+    def attend(r):
         for k in range(0, kv_heads, 2):
             first = r % 2 * heads + k * group
             both = jnp.dot(
@@ -144,6 +144,21 @@
                 for start in range(0, group, heads_dev):
                     d = ((k + i) * group + start) // heads_dev
                     staged[d, r] = partial[start : start + heads_dev]
+
+    score(0)
+    weigh(0)
+    for r in range(2, rows, 2):
+        score(r)
+    for copy in large[1]:
+        copy.wait()
+    for r in range(0, rows, 2):
+        attend(r)
+        attend(r + 1)
+        if r + 2 < rows:
+            weigh(r + 2)
+    by_head = stats[...].T
+    for d in range(devices):
+        staged[d, rows] = by_head[d * heads_dev : (d + 1) * heads_dev]
 
 
 def pack_kernel(staged, packed):

time: 36.2 us -> 36.3 us (level)
  no operation moved by 1% of the time
where the time goes in v16:
time: 36.3 us; the launch traced here: 36.1 us
  blocking collectives  14.6 us (40%)
  starting transfers between devices  8.27 us (23%)
  Pallas kernels  7.95 us (22%)
  waiting for transfers between devices  5.19 us (14%)
    all_to_all x1, blocking collectives, body(): lax.all_to_all(packed, 'kvp', split_axis=0, concat_axis=0, tiled=True)  14.6 us
    ppermute x9, starting transfers between devices, exchange(): lax.ppermute(array, 'kvp', [(i, i ^ partner) for i in range(devices)])  8.27 us
    ppermute x9, waiting for transfers between devices, exchange(): lax.ppermute(array, 'kvp', [(i, i ^ partner) for i in range(devices)])  5.19 us
    pallas_call x1, Pallas kernels, body(): pl.pallas_call(functools.partial(attend_kernel, heads_dev, devices), out_...  4.31 us
    pallas_call x4, Pallas kernels, body(): pl.pallas_call(functools.partial(project_kernel, x), out_shape=jax.ShapeD...  2.63 us
  transfers between devices with their start and end apart: 9, of which 6 were waited for; matrix products, arithmetic and copies ran while one was open for 0% of the time, Pallas kernels for 4%

profile of v16, /device:TPU:0, one launch (start us, length us, event | category | flops | bytes accessed | tf_op | source)
XLA Modules:
  0.0 36.1 jit_solution(12045281176518173939)
XLA Ops:
  0.0 4.3 %attend.1.staged = f32[16,5,4,128]{3,2,1,0:T(4,128)S(1)} custom-call(s32[4,12]{1,0:T(4,128)} %refs_0_.1, s32[4]{0:T(128)} %refs_1_.1, f32[4,48]{1,0:T(4,128)} %bitcast.2, f32[4,48]{1,0:T(4,128)} %bitcast.3, bf16[4,8192]{1,0:T(4,128)(2,1)} %refs_4_.1, bf16[48,64,512]{2,1,0:T(8,128)(2,1)} %refs_5_.1, bf16[48,64,512]{2,1,0:T(8,128)(2,1)} %refs_6_.1), custom_call_target="tpu_custom_call" | custom-call | flops 100663296 | bytes 6291456 | tf_op jit(solution)/shard_map/attend/pallas_call | solution.py:232
  4.3 0.0 copy-start
  4.4 14.6 %all_to_all.5.packed = bf16[16,5,4,128]{3,2,1,0:T(4,128)(2,1)S(1)} all-to-all(bf16[16,5,4,128]{3,2,1,0:T(4,128)(2,1)S(1)} %pack.1), channel_id=1, replica_groups=mesh['group'=2,'kvp'=16] {'kvp'}, dimensions={0} | all-to-all | bytes 163840 | tf_op jit(solution)/shard_map/all_to_all | solution.py:274
  19.0 0.3 combine.1.left
  19.2 0.0 copy-done
  19.2 0.7 %project_2.1 = bf16[4,4096]{1,0:T(4,128)(2,1)S(1)} custom-call(bf16[4,512]{1,0:T(4,128)(2,1)S(1)} %combine.1.left, bf16[512,16384]{1,0:T(8,128)(2,1)S(1)} %copy-done), custom_call_target="tpu_custom_call" | custom-call | flops 1024 | bytes 1024 | tf_op jit(solution)/shard_map/project_2/pallas_call | solution.py:291
  19.9 0.7 %project_3.1 = bf16[4,4096]{1,0:T(4,128)(2,1)S(1)} custom-call(bf16[4,512]{1,0:T(4,128)(2,1)S(1)} %combine.1.left, bf16[512,16384]{1,0:T(8,128)(2,1)S(1)} %copy-done), custom_call_target="tpu_custom_call" | custom-call | flops 1024 | bytes 1024 | tf_op jit(solution)/shard_map/project_3/pallas_call | solution.py:291
  20.6 0.0 collective-permute-start
  20.6 1.1 %collective-permute-start.1 = (bf16[4,4096]{1,0:T(4,128)(2,1)S(1)}, bf16[4,4096]{1,0:T(4,128)(2,1)S(1)}, u32[]{:S(2)}, u32[]{:S(2)}) collective-permute-start(bf16[4,4096]{1,0:T(4,128)(2,1)S(1)} %project_2.1), channel_id=1, source_target_pairs={{0,2},{1,3},{2,0},{3,1},{4,6},{5,7},{6,4},{7,5},{8,10},{9,11},{10,... | collective-permute-start | bytes 98312 | tf_op jit(solution)/shard_map/ppermute | solution.py:215
  21.7 0.7 %project_1.1 = bf16[4,4096]{1,0:T(4,128)(2,1)S(1)} custom-call(bf16[4,512]{1,0:T(4,128)(2,1)S(1)} %combine.1.left, bf16[512,16384]{1,0:T(8,128)(2,1)S(1)} %copy-done), custom_call_target="tpu_custom_call" | custom-call | flops 1024 | bytes 1024 | tf_op jit(solution)/shard_map/project_1/pallas_call | solution.py:291
  22.4 0.8 %collective-permute-start.2 = (bf16[4,4096]{1,0:T(4,128)(2,1)S(1)}, bf16[4,4096]{1,0:T(4,128)(2,1)S(1)}, u32[]{:S(2)}, u32[]{:S(2)}) collective-permute-start(bf16[4,4096]{1,0:T(4,128)(2,1)S(1)} %project_1.1), channel_id=1, source_target_pairs={{0,1},{1,0},{2,3},{3,2},{4,5},{5,4},{6,7},{7,6},{8,9},{9,8},{10,11... | collective-permute-start | bytes 98312 | tf_op jit(solution)/shard_map/ppermute | solution.py:215
  23.1 0.7 %project_0.1.refs_3_ = f32[4,4096]{1,0:T(4,128)S(1)} custom-call(bf16[4,512]{1,0:T(4,128)(2,1)S(1)} %combine.1.left, bf16[512,16384]{1,0:T(8,128)(2,1)S(1)} %copy-done), custom_call_target="tpu_custom_call" | custom-call | flops 1024 | bytes 1024 | tf_op jit(solution)/shard_map/project_0/pallas_call | solution.py:291
  23.8 0.2 collective-permute-done.refs_0_
  23.9 0.7 %collective-permute-done.1.refs_1_ = bf16[4,4096]{1,0:T(4,128)(2,1)S(1)} collective-permute-done((bf16[4,4096]{1,0:T(4,128)(2,1)S(1)}, bf16[4,4096]{1,0:T(4,128)(2,1)S(1)}, u32[]{:S(2)}, u32[]{:S(2)}) %collective-permute-start.1) | collective-permute-done | bytes 32800 | tf_op jit(solution)/shard_map/ppermute | solution.py:215
  24.6 0.0 collective-permute-done.2.refs_2_
  24.7 1.0 %collective-permute-start.5 = (bf16[4,4096]{1,0:T(4,128)(2,1)S(1)}, bf16[4,4096]{1,0:T(4,128)(2,1)S(1)}, u32[]{:S(2)}, u32[]{:S(2)}) collective-permute-start(bf16[4,4096]{1,0:T(4,128)(2,1)S(1)} %add_near.1.refs_0_), channel_id=1, source_target_pairs={{0,12},{1,13},{2,14},{3,15},{4,8},{5,9},{6,10},{7,11},{8,4},{9,5},... | collective-permute-start | bytes 98312 | tf_op jit(solution)/shard_map/ppermute | solution.py:215
  25.7 0.8 %collective-permute-start.4 = (bf16[4,4096]{1,0:T(4,128)(2,1)S(1)}, bf16[4,4096]{1,0:T(4,128)(2,1)S(1)}, u32[]{:S(2)}, u32[]{:S(2)}) collective-permute-start(bf16[4,4096]{1,0:T(4,128)(2,1)S(1)} %add_near.1.refs_0_), channel_id=1, source_target_pairs={{0,8},{1,9},{2,10},{3,11},{4,12},{5,13},{6,14},{7,15},{8,0},{9,1},... | collective-permute-start | bytes 98312 | tf_op jit(solution)/shard_map/ppermute | solution.py:215
  26.5 2.6 %collective-permute-start.3 = (bf16[4,4096]{1,0:T(4,128)(2,1)S(1)}, bf16[4,4096]{1,0:T(4,128)(2,1)S(1)}, u32[]{:S(2)}, u32[]{:S(2)}) collective-permute-start(bf16[4,4096]{1,0:T(4,128)(2,1)S(1)} %add_near.1.refs_0_), channel_id=1, source_target_pairs={{0,4},{1,5},{2,6},{3,7},{4,0},{5,1},{6,2},{7,3},{8,12},{9,13},{10,... | collective-permute-start | bytes 98312 | tf_op jit(solution)/shard_map/ppermute | solution.py:215
  29.1 1.5 %collective-permute-done.5.refs_3_ = bf16[4,4096]{1,0:T(4,128)(2,1)S(1)} collective-permute-done((bf16[4,4096]{1,0:T(4,128)(2,1)S(1)}, bf16[4,4096]{1,0:T(4,128)(2,1)S(1)}, u32[]{:S(2)}, u32[]{:S(2)}) %collective-permute-start.5) | collective-permute-done | bytes 32800 | tf_op jit(solution)/shard_map/ppermute | solution.py:215
  30.6 0.6 %collective-permute-done.4.refs_2_ = bf16[4,4096]{1,0:T(4,128)(2,1)S(1)} collective-permute-done((bf16[4,4096]{1,0:T(4,128)(2,1)S(1)}, bf16[4,4096]{1,0:T(4,128)(2,1)S(1)}, u32[]{:S(2)}, u32[]{:S(2)}) %collective-permute-start.4) | collective-permute-done | bytes 32800 | tf_op jit(solution)/shard_map/ppermute | solution.py:215
  31.2 0.0 collective-permute-done.3.refs_1_
  31.3 0.1 collective-permute-start.8
  31.3 1.3 %collective-permute-start.7 = (bf16[4,4096]{1,0:T(4,128)(2,1)S(1)}, bf16[4,4096]{1,0:T(4,128)(2,1)S(1)}, u32[]{:S(2)}, u32[]{:S(2)}) collective-permute-start(bf16[4,4096]{1,0:T(4,128)(2,1)S(1)} %add_far.1.refs_0_), channel_id=1, source_target_pairs={{0,2},{1,3},{2,0},{3,1},{4,6},{5,7},{6,4},{7,5},{8,10},{9,11},{10,... | collective-permute-start | bytes 98312 | tf_op jit(solution)/shard_map/ppermute | solution.py:215
  32.6 0.6 %collective-permute-start.6 = (bf16[4,4096]{1,0:T(4,128)(2,1)S(1)}, bf16[4,4096]{1,0:T(4,128)(2,1)S(1)}, u32[]{:S(2)}, u32[]{:S(2)}) collective-permute-start(bf16[4,4096]{1,0:T(4,128)(2,1)S(1)} %add_far.1.refs_0_), channel_id=1, source_target_pairs={{0,1},{1,0},{2,3},{3,2},{4,5},{5,4},{6,7},{7,6},{8,9},{9,8},{10,11... | collective-permute-start | bytes 98312 | tf_op jit(solution)/shard_map/ppermute | solution.py:215
  33.2 1.6 %collective-permute-done.8.refs_3_ = bf16[4,4096]{1,0:T(4,128)(2,1)S(1)} collective-permute-done((bf16[4,4096]{1,0:T(4,128)(2,1)S(1)}, bf16[4,4096]{1,0:T(4,128)(2,1)S(1)}, u32[]{:S(2)}, u32[]{:S(2)}) %collective-permute-start.8) | collective-permute-done | bytes 32800 | tf_op jit(solution)/shard_map/ppermute | solution.py:215
  34.8 0.6 %collective-permute-done.7.refs_2_ = bf16[4,4096]{1,0:T(4,128)(2,1)S(1)} collective-permute-done((bf16[4,4096]{1,0:T(4,128)(2,1)S(1)}, bf16[4,4096]{1,0:T(4,128)(2,1)S(1)}, u32[]{:S(2)}, u32[]{:S(2)}) %collective-permute-start.7) | collective-permute-done | bytes 32800 | tf_op jit(solution)/shard_map/ppermute | solution.py:215
  35.4 0.0 collective-permute-done.6.refs_1_
  35.4 0.7 %lay.1 = bf16[4,16384]{1,0:T(4,128)(2,1)} custom-call(bf16[4,4096]{1,0:T(4,128)(2,1)S(1)} %add_far.1.refs_0_, bf16[4,4096]{1,0:T(4,128)(2,1)S(1)} %collective-permute-done.6.refs_1_, bf16[4,4096]{1,0:T(4,128)(2,1)S(1)} %collective-permute-done.7.refs_2_, bf16[4,4096]{1,0:T(4,128)(2,1)S(1)} %collective-permute-done.8.refs_3_), custom_call_target="tpu_custom_call" | custom-call | tf_op jit(solution)/shard_map/lay/pallas_call | solution.py:315
  (3 shorter events, 0.1 us)
Async XLA Ops:
  4.3 14.9 %copy-start = (bf16[512,16384]{1,0:T(8,128)(2,1)S(1)}, bf16[512,16384]{1,0:T(8,128)(2,1)}, u32[]{:S(2)}) copy-start(bf16[512,16384]{1,0:T(8,128)(2,1)} %weight.7) | copy-start | bytes 50331652
  20.6 3.4 %collective-permute-start = (bf16[4,4096]{1,0:T(4,128)(2,1)S(1)}, bf16[4,4096]{1,0:T(4,128)(2,1)S(1)}, u32[]{:S(2)}, u32[]{:S(2)}) collective-permute-start(bf16[4,4096]{1,0:T(4,128)(2,1)S(1)} %project_3.1), channel_id=1, source_target_pairs={{0,3},{1,2},{2,1},{3,0},{4,7},{5,6},{6,5},{7,4},{8,11},{9,10},{10,... | collective-permute-start | bytes 98312 | tf_op jit(solution)/shard_map/ppermute | solution.py:215
  20.6 4.1 %collective-permute-start.1 = (bf16[4,4096]{1,0:T(4,128)(2,1)S(1)}, bf16[4,4096]{1,0:T(4,128)(2,1)S(1)}, u32[]{:S(2)}, u32[]{:S(2)}) collective-permute-start(bf16[4,4096]{1,0:T(4,128)(2,1)S(1)} %project_2.1), channel_id=1, source_target_pairs={{0,2},{1,3},{2,0},{3,1},{4,6},{5,7},{6,4},{7,5},{8,10},{9,11},{10,... | collective-permute-start | bytes 98312 | tf_op jit(solution)/shard_map/ppermute | solution.py:215
  22.4 2.3 %collective-permute-start.2 = (bf16[4,4096]{1,0:T(4,128)(2,1)S(1)}, bf16[4,4096]{1,0:T(4,128)(2,1)S(1)}, u32[]{:S(2)}, u32[]{:S(2)}) collective-permute-start(bf16[4,4096]{1,0:T(4,128)(2,1)S(1)} %project_1.1), channel_id=1, source_target_pairs={{0,1},{1,0},{2,3},{3,2},{4,5},{5,4},{6,7},{7,6},{8,9},{9,8},{10,11... | collective-permute-start | bytes 98312 | tf_op jit(solution)/shard_map/ppermute | solution.py:215
  24.7 5.9 %collective-permute-start.5 = (bf16[4,4096]{1,0:T(4,128)(2,1)S(1)}, bf16[4,4096]{1,0:T(4,128)(2,1)S(1)}, u32[]{:S(2)}, u32[]{:S(2)}) collective-permute-start(bf16[4,4096]{1,0:T(4,128)(2,1)S(1)} %add_near.1.refs_0_), channel_id=1, source_target_pairs={{0,12},{1,13},{2,14},{3,15},{4,8},{5,9},{6,10},{7,11},{8,4},{9,5},... | collective-permute-start | bytes 98312 | tf_op jit(solution)/shard_map/ppermute | solution.py:215
  25.7 5.5 %collective-permute-start.4 = (bf16[4,4096]{1,0:T(4,128)(2,1)S(1)}, bf16[4,4096]{1,0:T(4,128)(2,1)S(1)}, u32[]{:S(2)}, u32[]{:S(2)}) collective-permute-start(bf16[4,4096]{1,0:T(4,128)(2,1)S(1)} %add_near.1.refs_0_), channel_id=1, source_target_pairs={{0,8},{1,9},{2,10},{3,11},{4,12},{5,13},{6,14},{7,15},{8,0},{9,1},... | collective-permute-start | bytes 98312 | tf_op jit(solution)/shard_map/ppermute | solution.py:215
  26.5 4.7 %collective-permute-start.3 = (bf16[4,4096]{1,0:T(4,128)(2,1)S(1)}, bf16[4,4096]{1,0:T(4,128)(2,1)S(1)}, u32[]{:S(2)}, u32[]{:S(2)}) collective-permute-start(bf16[4,4096]{1,0:T(4,128)(2,1)S(1)} %add_near.1.refs_0_), channel_id=1, source_target_pairs={{0,4},{1,5},{2,6},{3,7},{4,0},{5,1},{6,2},{7,3},{8,12},{9,13},{10,... | collective-permute-start | bytes 98312 | tf_op jit(solution)/shard_map/ppermute | solution.py:215
  31.3 3.5 %collective-permute-start.8 = (bf16[4,4096]{1,0:T(4,128)(2,1)S(1)}, bf16[4,4096]{1,0:T(4,128)(2,1)S(1)}, u32[]{:S(2)}, u32[]{:S(2)}) collective-permute-start(bf16[4,4096]{1,0:T(4,128)(2,1)S(1)} %add_far.1.refs_0_), channel_id=1, source_target_pairs={{0,3},{1,2},{2,1},{3,0},{4,7},{5,6},{6,5},{7,4},{8,11},{9,10},{10,... | collective-permute-start | bytes 98312 | tf_op jit(solution)/shard_map/ppermute | solution.py:215
  31.3 4.1 %collective-permute-start.7 = (bf16[4,4096]{1,0:T(4,128)(2,1)S(1)}, bf16[4,4096]{1,0:T(4,128)(2,1)S(1)}, u32[]{:S(2)}, u32[]{:S(2)}) collective-permute-start(bf16[4,4096]{1,0:T(4,128)(2,1)S(1)} %add_far.1.refs_0_), channel_id=1, source_target_pairs={{0,2},{1,3},{2,0},{3,1},{4,6},{5,7},{6,4},{7,5},{8,10},{9,11},{10,... | collective-permute-start | bytes 98312 | tf_op jit(solution)/shard_map/ppermute | solution.py:215
  32.6 2.8 %collective-permute-start.6 = (bf16[4,4096]{1,0:T(4,128)(2,1)S(1)}, bf16[4,4096]{1,0:T(4,128)(2,1)S(1)}, u32[]{:S(2)}, u32[]{:S(2)}) collective-permute-start(bf16[4,4096]{1,0:T(4,128)(2,1)S(1)} %add_far.1.refs_0_), channel_id=1, source_target_pairs={{0,1},{1,0},{2,3},{3,2},{4,5},{5,4},{6,7},{7,6},{8,9},{9,8},{10,11... | collective-permute-start | bytes 98312 | tf_op jit(solution)/shard_map/ppermute | solution.py:215

commit v17 on v16

--- a/solution.py
+++ b/solution.py
@@ -55,7 +55,7 @@
         for i in range(pieces):
             here = pl.ds(i * piece, piece)
             large[-1].append(pltpu.make_async_copy(source.at[here], target.at[here], sems.at[which, i]))
-    for copy in large[0]:
+    for copy in large[0] + large[1]:
         copy.start()
 
     me = lax.axis_index("kvp")
@@ -67,8 +67,6 @@
     stats[...] = jnp.zeros_like(stats)
     for copy in small:
         copy.wait()
-    for copy in large[1]:
-        copy.start()
 
     def by_slot(scales):
         return lax.dot_general(

time: 36.3 us -> 36.7 us (1.011)
  Pallas kernels: 7.95 us -> 8.41 us
    pallas_call x1, Pallas kernels: 4.31 us -> 4.77 us  [body(): pl.pallas_call(functools.partial(attend_kernel, heads_dev, devices), out_...]
where the time goes in v17:
time: 36.7 us; the launch traced here: 36.5 us
  blocking collectives  14.6 us (40%)
  Pallas kernels  8.41 us (23%)
  starting transfers between devices  8.27 us (23%)
  waiting for transfers between devices  5.19 us (14%)
    all_to_all x1, blocking collectives, body(): lax.all_to_all(packed, 'kvp', split_axis=0, concat_axis=0, tiled=True)  14.6 us
    ppermute x9, starting transfers between devices, exchange(): lax.ppermute(array, 'kvp', [(i, i ^ partner) for i in range(devices)])  8.27 us
    ppermute x9, waiting for transfers between devices, exchange(): lax.ppermute(array, 'kvp', [(i, i ^ partner) for i in range(devices)])  5.19 us
    pallas_call x1, Pallas kernels, body(): pl.pallas_call(functools.partial(attend_kernel, heads_dev, devices), out_...  4.77 us
    pallas_call x4, Pallas kernels, body(): pl.pallas_call(functools.partial(project_kernel, x), out_shape=jax.ShapeD...  2.63 us
  transfers between devices with their start and end apart: 9, of which 6 were waited for; matrix products, arithmetic and copies ran while one was open for 0% of the time, Pallas kernels for 4%

profile of v17, /device:TPU:0, one launch (start us, length us, event | category | flops | bytes accessed | tf_op | source)
XLA Modules:
  0.0 36.5 jit_solution(12390034908372250523)
XLA Ops:
  0.0 4.8 %attend.1.staged = f32[16,5,4,128]{3,2,1,0:T(4,128)S(1)} custom-call(s32[4,12]{1,0:T(4,128)} %refs_0_.1, s32[4]{0:T(128)} %refs_1_.1, f32[4,48]{1,0:T(4,128)} %bitcast.2, f32[4,48]{1,0:T(4,128)} %bitcast.3, bf16[4,8192]{1,0:T(4,128)(2,1)} %refs_4_.1, bf16[48,64,512]{2,1,0:T(8,128)(2,1)} %refs_5_.1, bf16[48,64,512]{2,1,0:T(8,128)(2,1)} %refs_6_.1), custom_call_target="tpu_custom_call" | custom-call | flops 100663296 | bytes 6291456 | tf_op jit(solution)/shard_map/attend/pallas_call | solution.py:230
  4.8 0.0 copy-start
  4.8 14.6 %all_to_all.5.packed = bf16[16,5,4,128]{3,2,1,0:T(4,128)(2,1)S(1)} all-to-all(bf16[16,5,4,128]{3,2,1,0:T(4,128)(2,1)S(1)} %pack.1), channel_id=1, replica_groups=mesh['group'=2,'kvp'=16] {'kvp'}, dimensions={0} | all-to-all | bytes 163840 | tf_op jit(solution)/shard_map/all_to_all | solution.py:272
  19.4 0.3 combine.1.left
  19.7 0.0 copy-done
  19.7 0.7 %project_2.1 = bf16[4,4096]{1,0:T(4,128)(2,1)S(1)} custom-call(bf16[4,512]{1,0:T(4,128)(2,1)S(1)} %combine.1.left, bf16[512,16384]{1,0:T(8,128)(2,1)S(1)} %copy-done), custom_call_target="tpu_custom_call" | custom-call | flops 1024 | bytes 1024 | tf_op jit(solution)/shard_map/project_2/pallas_call | solution.py:289
  20.3 0.7 %project_3.1 = bf16[4,4096]{1,0:T(4,128)(2,1)S(1)} custom-call(bf16[4,512]{1,0:T(4,128)(2,1)S(1)} %combine.1.left, bf16[512,16384]{1,0:T(8,128)(2,1)S(1)} %copy-done), custom_call_target="tpu_custom_call" | custom-call | flops 1024 | bytes 1024 | tf_op jit(solution)/shard_map/project_3/pallas_call | solution.py:289
  21.0 0.0 collective-permute-start
  21.0 1.1 %collective-permute-start.1 = (bf16[4,4096]{1,0:T(4,128)(2,1)S(1)}, bf16[4,4096]{1,0:T(4,128)(2,1)S(1)}, u32[]{:S(2)}, u32[]{:S(2)}) collective-permute-start(bf16[4,4096]{1,0:T(4,128)(2,1)S(1)} %project_2.1), channel_id=1, source_target_pairs={{0,2},{1,3},{2,0},{3,1},{4,6},{5,7},{6,4},{7,5},{8,10},{9,11},{10,... | collective-permute-start | bytes 98312 | tf_op jit(solution)/shard_map/ppermute | solution.py:213
  22.2 0.7 %project_1.1 = bf16[4,4096]{1,0:T(4,128)(2,1)S(1)} custom-call(bf16[4,512]{1,0:T(4,128)(2,1)S(1)} %combine.1.left, bf16[512,16384]{1,0:T(8,128)(2,1)S(1)} %copy-done), custom_call_target="tpu_custom_call" | custom-call | flops 1024 | bytes 1024 | tf_op jit(solution)/shard_map/project_1/pallas_call | solution.py:289
  22.8 0.8 %collective-permute-start.2 = (bf16[4,4096]{1,0:T(4,128)(2,1)S(1)}, bf16[4,4096]{1,0:T(4,128)(2,1)S(1)}, u32[]{:S(2)}, u32[]{:S(2)}) collective-permute-start(bf16[4,4096]{1,0:T(4,128)(2,1)S(1)} %project_1.1), channel_id=1, source_target_pairs={{0,1},{1,0},{2,3},{3,2},{4,5},{5,4},{6,7},{7,6},{8,9},{9,8},{10,11... | collective-permute-start | bytes 98312 | tf_op jit(solution)/shard_map/ppermute | solution.py:213
  23.6 0.7 %project_0.1.refs_3_ = f32[4,4096]{1,0:T(4,128)S(1)} custom-call(bf16[4,512]{1,0:T(4,128)(2,1)S(1)} %combine.1.left, bf16[512,16384]{1,0:T(8,128)(2,1)S(1)} %copy-done), custom_call_target="tpu_custom_call" | custom-call | flops 1024 | bytes 1024 | tf_op jit(solution)/shard_map/project_0/pallas_call | solution.py:289
  24.2 0.2 collective-permute-done.refs_0_
  24.4 0.7 %collective-permute-done.1.refs_1_ = bf16[4,4096]{1,0:T(4,128)(2,1)S(1)} collective-permute-done((bf16[4,4096]{1,0:T(4,128)(2,1)S(1)}, bf16[4,4096]{1,0:T(4,128)(2,1)S(1)}, u32[]{:S(2)}, u32[]{:S(2)}) %collective-permute-start.1) | collective-permute-done | bytes 32800 | tf_op jit(solution)/shard_map/ppermute | solution.py:213
  25.1 0.0 collective-permute-done.2.refs_2_
  25.1 1.0 %collective-permute-start.5 = (bf16[4,4096]{1,0:T(4,128)(2,1)S(1)}, bf16[4,4096]{1,0:T(4,128)(2,1)S(1)}, u32[]{:S(2)}, u32[]{:S(2)}) collective-permute-start(bf16[4,4096]{1,0:T(4,128)(2,1)S(1)} %add_near.1.refs_0_), channel_id=1, source_target_pairs={{0,12},{1,13},{2,14},{3,15},{4,8},{5,9},{6,10},{7,11},{8,4},{9,5},... | collective-permute-start | bytes 98312 | tf_op jit(solution)/shard_map/ppermute | solution.py:213
  26.1 0.8 %collective-permute-start.4 = (bf16[4,4096]{1,0:T(4,128)(2,1)S(1)}, bf16[4,4096]{1,0:T(4,128)(2,1)S(1)}, u32[]{:S(2)}, u32[]{:S(2)}) collective-permute-start(bf16[4,4096]{1,0:T(4,128)(2,1)S(1)} %add_near.1.refs_0_), channel_id=1, source_target_pairs={{0,8},{1,9},{2,10},{3,11},{4,12},{5,13},{6,14},{7,15},{8,0},{9,1},... | collective-permute-start | bytes 98312 | tf_op jit(solution)/shard_map/ppermute | solution.py:213
  27.0 2.6 %collective-permute-start.3 = (bf16[4,4096]{1,0:T(4,128)(2,1)S(1)}, bf16[4,4096]{1,0:T(4,128)(2,1)S(1)}, u32[]{:S(2)}, u32[]{:S(2)}) collective-permute-start(bf16[4,4096]{1,0:T(4,128)(2,1)S(1)} %add_near.1.refs_0_), channel_id=1, source_target_pairs={{0,4},{1,5},{2,6},{3,7},{4,0},{5,1},{6,2},{7,3},{8,12},{9,13},{10,... | collective-permute-start | bytes 98312 | tf_op jit(solution)/shard_map/ppermute | solution.py:213
  29.6 1.5 %collective-permute-done.5.refs_3_ = bf16[4,4096]{1,0:T(4,128)(2,1)S(1)} collective-permute-done((bf16[4,4096]{1,0:T(4,128)(2,1)S(1)}, bf16[4,4096]{1,0:T(4,128)(2,1)S(1)}, u32[]{:S(2)}, u32[]{:S(2)}) %collective-permute-start.5) | collective-permute-done | bytes 32800 | tf_op jit(solution)/shard_map/ppermute | solution.py:213
  31.1 0.6 %collective-permute-done.4.refs_2_ = bf16[4,4096]{1,0:T(4,128)(2,1)S(1)} collective-permute-done((bf16[4,4096]{1,0:T(4,128)(2,1)S(1)}, bf16[4,4096]{1,0:T(4,128)(2,1)S(1)}, u32[]{:S(2)}, u32[]{:S(2)}) %collective-permute-start.4) | collective-permute-done | bytes 32800 | tf_op jit(solution)/shard_map/ppermute | solution.py:213
  31.7 0.0 collective-permute-done.3.refs_1_
  31.7 0.1 collective-permute-start.8
  31.8 1.3 %collective-permute-start.7 = (bf16[4,4096]{1,0:T(4,128)(2,1)S(1)}, bf16[4,4096]{1,0:T(4,128)(2,1)S(1)}, u32[]{:S(2)}, u32[]{:S(2)}) collective-permute-start(bf16[4,4096]{1,0:T(4,128)(2,1)S(1)} %add_far.1.refs_0_), channel_id=1, source_target_pairs={{0,2},{1,3},{2,0},{3,1},{4,6},{5,7},{6,4},{7,5},{8,10},{9,11},{10,... | collective-permute-start | bytes 98312 | tf_op jit(solution)/shard_map/ppermute | solution.py:213
  33.1 0.6 %collective-permute-start.6 = (bf16[4,4096]{1,0:T(4,128)(2,1)S(1)}, bf16[4,4096]{1,0:T(4,128)(2,1)S(1)}, u32[]{:S(2)}, u32[]{:S(2)}) collective-permute-start(bf16[4,4096]{1,0:T(4,128)(2,1)S(1)} %add_far.1.refs_0_), channel_id=1, source_target_pairs={{0,1},{1,0},{2,3},{3,2},{4,5},{5,4},{6,7},{7,6},{8,9},{9,8},{10,11... | collective-permute-start | bytes 98312 | tf_op jit(solution)/shard_map/ppermute | solution.py:213
  33.7 1.6 %collective-permute-done.8.refs_3_ = bf16[4,4096]{1,0:T(4,128)(2,1)S(1)} collective-permute-done((bf16[4,4096]{1,0:T(4,128)(2,1)S(1)}, bf16[4,4096]{1,0:T(4,128)(2,1)S(1)}, u32[]{:S(2)}, u32[]{:S(2)}) %collective-permute-start.8) | collective-permute-done | bytes 32800 | tf_op jit(solution)/shard_map/ppermute | solution.py:213
  35.2 0.6 %collective-permute-done.7.refs_2_ = bf16[4,4096]{1,0:T(4,128)(2,1)S(1)} collective-permute-done((bf16[4,4096]{1,0:T(4,128)(2,1)S(1)}, bf16[4,4096]{1,0:T(4,128)(2,1)S(1)}, u32[]{:S(2)}, u32[]{:S(2)}) %collective-permute-start.7) | collective-permute-done | bytes 32800 | tf_op jit(solution)/shard_map/ppermute | solution.py:213
  35.9 0.0 collective-permute-done.6.refs_1_
  35.9 0.7 %lay.1 = bf16[4,16384]{1,0:T(4,128)(2,1)} custom-call(bf16[4,4096]{1,0:T(4,128)(2,1)S(1)} %add_far.1.refs_0_, bf16[4,4096]{1,0:T(4,128)(2,1)S(1)} %collective-permute-done.6.refs_1_, bf16[4,4096]{1,0:T(4,128)(2,1)S(1)} %collective-permute-done.7.refs_2_, bf16[4,4096]{1,0:T(4,128)(2,1)S(1)} %collective-permute-done.8.refs_3_), custom_call_target="tpu_custom_call" | custom-call | tf_op jit(solution)/shard_map/lay/pallas_call | solution.py:313
  (3 shorter events, 0.1 us)
Async XLA Ops:
  4.8 14.9 %copy-start = (bf16[512,16384]{1,0:T(8,128)(2,1)S(1)}, bf16[512,16384]{1,0:T(8,128)(2,1)}, u32[]{:S(2)}) copy-start(bf16[512,16384]{1,0:T(8,128)(2,1)} %weight.7) | copy-start | bytes 50331652
  21.0 3.4 %collective-permute-start = (bf16[4,4096]{1,0:T(4,128)(2,1)S(1)}, bf16[4,4096]{1,0:T(4,128)(2,1)S(1)}, u32[]{:S(2)}, u32[]{:S(2)}) collective-permute-start(bf16[4,4096]{1,0:T(4,128)(2,1)S(1)} %project_3.1), channel_id=1, source_target_pairs={{0,3},{1,2},{2,1},{3,0},{4,7},{5,6},{6,5},{7,4},{8,11},{9,10},{10,... | collective-permute-start | bytes 98312 | tf_op jit(solution)/shard_map/ppermute | solution.py:213
  21.0 4.1 %collective-permute-start.1 = (bf16[4,4096]{1,0:T(4,128)(2,1)S(1)}, bf16[4,4096]{1,0:T(4,128)(2,1)S(1)}, u32[]{:S(2)}, u32[]{:S(2)}) collective-permute-start(bf16[4,4096]{1,0:T(4,128)(2,1)S(1)} %project_2.1), channel_id=1, source_target_pairs={{0,2},{1,3},{2,0},{3,1},{4,6},{5,7},{6,4},{7,5},{8,10},{9,11},{10,... | collective-permute-start | bytes 98312 | tf_op jit(solution)/shard_map/ppermute | solution.py:213
  22.8 2.3 %collective-permute-start.2 = (bf16[4,4096]{1,0:T(4,128)(2,1)S(1)}, bf16[4,4096]{1,0:T(4,128)(2,1)S(1)}, u32[]{:S(2)}, u32[]{:S(2)}) collective-permute-start(bf16[4,4096]{1,0:T(4,128)(2,1)S(1)} %project_1.1), channel_id=1, source_target_pairs={{0,1},{1,0},{2,3},{3,2},{4,5},{5,4},{6,7},{7,6},{8,9},{9,8},{10,11... | collective-permute-start | bytes 98312 | tf_op jit(solution)/shard_map/ppermute | solution.py:213
  25.1 5.9 %collective-permute-start.5 = (bf16[4,4096]{1,0:T(4,128)(2,1)S(1)}, bf16[4,4096]{1,0:T(4,128)(2,1)S(1)}, u32[]{:S(2)}, u32[]{:S(2)}) collective-permute-start(bf16[4,4096]{1,0:T(4,128)(2,1)S(1)} %add_near.1.refs_0_), channel_id=1, source_target_pairs={{0,12},{1,13},{2,14},{3,15},{4,8},{5,9},{6,10},{7,11},{8,4},{9,5},... | collective-permute-start | bytes 98312 | tf_op jit(solution)/shard_map/ppermute | solution.py:213
  26.1 5.5 %collective-permute-start.4 = (bf16[4,4096]{1,0:T(4,128)(2,1)S(1)}, bf16[4,4096]{1,0:T(4,128)(2,1)S(1)}, u32[]{:S(2)}, u32[]{:S(2)}) collective-permute-start(bf16[4,4096]{1,0:T(4,128)(2,1)S(1)} %add_near.1.refs_0_), channel_id=1, source_target_pairs={{0,8},{1,9},{2,10},{3,11},{4,12},{5,13},{6,14},{7,15},{8,0},{9,1},... | collective-permute-start | bytes 98312 | tf_op jit(solution)/shard_map/ppermute | solution.py:213
  27.0 4.7 %collective-permute-start.3 = (bf16[4,4096]{1,0:T(4,128)(2,1)S(1)}, bf16[4,4096]{1,0:T(4,128)(2,1)S(1)}, u32[]{:S(2)}, u32[]{:S(2)}) collective-permute-start(bf16[4,4096]{1,0:T(4,128)(2,1)S(1)} %add_near.1.refs_0_), channel_id=1, source_target_pairs={{0,4},{1,5},{2,6},{3,7},{4,0},{5,1},{6,2},{7,3},{8,12},{9,13},{10,... | collective-permute-start | bytes 98312 | tf_op jit(solution)/shard_map/ppermute | solution.py:213
  31.7 3.5 %collective-permute-start.8 = (bf16[4,4096]{1,0:T(4,128)(2,1)S(1)}, bf16[4,4096]{1,0:T(4,128)(2,1)S(1)}, u32[]{:S(2)}, u32[]{:S(2)}) collective-permute-start(bf16[4,4096]{1,0:T(4,128)(2,1)S(1)} %add_far.1.refs_0_), channel_id=1, source_target_pairs={{0,3},{1,2},{2,1},{3,0},{4,7},{5,6},{6,5},{7,4},{8,11},{9,10},{10,... | collective-permute-start | bytes 98312 | tf_op jit(solution)/shard_map/ppermute | solution.py:213
  31.8 4.1 %collective-permute-start.7 = (bf16[4,4096]{1,0:T(4,128)(2,1)S(1)}, bf16[4,4096]{1,0:T(4,128)(2,1)S(1)}, u32[]{:S(2)}, u32[]{:S(2)}) collective-permute-start(bf16[4,4096]{1,0:T(4,128)(2,1)S(1)} %add_far.1.refs_0_), channel_id=1, source_target_pairs={{0,2},{1,3},{2,0},{3,1},{4,6},{5,7},{6,4},{7,5},{8,10},{9,11},{10,... | collective-permute-start | bytes 98312 | tf_op jit(solution)/shard_map/ppermute | solution.py:213
  33.1 2.8 %collective-permute-start.6 = (bf16[4,4096]{1,0:T(4,128)(2,1)S(1)}, bf16[4,4096]{1,0:T(4,128)(2,1)S(1)}, u32[]{:S(2)}, u32[]{:S(2)}) collective-permute-start(bf16[4,4096]{1,0:T(4,128)(2,1)S(1)} %add_far.1.refs_0_), channel_id=1, source_target_pairs={{0,1},{1,0},{2,3},{3,2},{4,5},{5,4},{6,7},{7,6},{8,9},{9,8},{10,11... | collective-permute-start | bytes 98312 | tf_op jit(solution)/shard_map/ppermute | solution.py:213

commit v18 on v16

--- a/solution.py
+++ b/solution.py
@@ -13,6 +13,7 @@
 ATTEND_VMEM = 60 * 1024 * 1024
 HIDDEN = -1e30
 LOWEST = -1e20
+CACHE_PIECES = 6
 EXCHANGE_FLOPS = 40_000_000_000
 SMALL_VMEM = 8 * 1024 * 1024
 VMEM = pl.BlockSpec(memory_space=pltpu.VMEM)
@@ -28,12 +29,13 @@
 def attend_kernel(heads_dev, devices, *refs):
     table_hbm, lengths_hbm, key_scale_hbm, value_scale_hbm, queries_hbm, keys, values = refs[:7]
     staged, table, lengths, key_scale, value_scale, queries, key_buf, value_buf, query_rows = refs[7:16]
-    query_blocks, key_rows, value_rows, scores, weight_rows, stats, small_sems, sems = refs[16:]
+    query_blocks, key_rows, value_rows, by_slot_scores, scores, weight_rows, stats, small_sems, sems = refs[16:]
     rows, pages = table.shape
     kv_heads = key_scale.shape[0]
     heads = queries.shape[1] // HD
     group = heads // kv_heads
     context = pages * PAGE
+    columns = keys.shape[2]
     pieces = sems.shape[1]
     piece = keys.shape[0] // pieces
 
@@ -83,10 +85,10 @@
     for r in range(0, rows, 2):
         both = jnp.concatenate([query_rows[pl.ds(r + i, heads, stride=rows), :] for i in (0, 1)], axis=0)
         turned = both.T
-        for i in (0, 1):
-            for k in range(kv_heads):
-                mine = lax.div(lane, group) == i * kv_heads + k
-                query_blocks[r + i, k * HD : (k + 1) * HD, :] = jnp.where(mine, turned, 0.0).astype(jnp.bfloat16)
+        for k in range(kv_heads):
+            query_blocks[k * HD : (k + 1) * HD, r // 2 * HD : (r // 2 + 1) * HD] = jnp.where(
+                of_lane == k, turned, 0.0
+            ).astype(jnp.bfloat16)
 
     def pages_of(buf, r, columns):
         return jnp.concatenate([buf[table[r, p], :, columns] for p in range(pages)], axis=0)
@@ -94,25 +96,15 @@
     def factor(scale_rows, r, p):
         left, right = (scale_rows[pl.ds(table[r + i, p], 1), :] for i in (0, 1))
         return jnp.where(first_of_pair, left, right)
-
-    for copy in large[0]:
-        copy.wait()
-    def score(r):
-        for i in (0, 1):
-            both = jnp.dot(
-                pages_of(key_buf, r + i, slice(None)), query_blocks[r + i], preferred_element_type=jnp.float32
-            )
-            if i == 0:
-                scores[r // 2] = both
-            else:
-                scores[r // 2] += both
 
     def weigh(r):
         length = jnp.where(first_of_pair, lengths[r], lengths[r + 1]) - me * context
         highest = jnp.full((PAGE, HD), LOWEST, jnp.float32)
         for p in range(pages):
             here = slice(p * PAGE, (p + 1) * PAGE)
-            scaled = jnp.where(place < length - p * PAGE, scores[r // 2, here] * factor(key_rows, r, p), HIDDEN)
+            left, right = (by_slot_scores[table[r + i, p], :, r // 2 * HD : (r // 2 + 1) * HD] for i in (0, 1))
+            scaled = jnp.where(first_of_pair, left, right) * factor(key_rows, r, p)
+            scaled = jnp.where(place < length - p * PAGE, scaled, HIDDEN)
             scores[r // 2, here] = scaled
             highest = jnp.maximum(highest, scaled)
         high, low = split_two(jnp.max(highest, axis=0, keepdims=True))
@@ -145,10 +137,13 @@
                     d = ((k + i) * group + start) // heads_dev
                     staged[d, r] = partial[start : start + heads_dev]
 
-    score(0)
+    for i, copy in enumerate(large[0]):
+        copy.wait()
+        here = slice(i * piece, (i + 1) * piece)
+        arrived = key_buf[here].reshape(piece * PAGE, columns)
+        both = jnp.dot(arrived, query_blocks[...], preferred_element_type=jnp.float32)
+        by_slot_scores[here] = both.reshape(piece, PAGE, rows // 2 * HD)
     weigh(0)
-    for r in range(2, rows, 2):
-        score(r)
     for copy in large[1]:
         copy.wait()
     for r in range(0, rows, 2):
@@ -243,14 +238,15 @@
             pltpu.VMEM((slots, PAGE, columns), jnp.bfloat16),
             pltpu.VMEM((slots, PAGE, columns), jnp.bfloat16),
             pltpu.VMEM((heads * rows, HD), jnp.float32),
-            pltpu.VMEM((rows, columns, HD), jnp.bfloat16),
+            pltpu.VMEM((columns, rows // 2 * HD), jnp.bfloat16),
             pltpu.VMEM((slots, HD), jnp.float32),
             pltpu.VMEM((slots, HD), jnp.float32),
+            pltpu.VMEM((slots, PAGE, rows // 2 * HD), jnp.float32),
             pltpu.VMEM((rows // 2, pages * PAGE, HD), jnp.float32),
             pltpu.VMEM((rows // 2, HD, pages * PAGE), jnp.bfloat16),
             pltpu.VMEM((HD, HD), jnp.float32),
             pltpu.SemaphoreType.DMA((5,)),
-            pltpu.SemaphoreType.DMA((2, 4)),
+            pltpu.SemaphoreType.DMA((2, CACHE_PIECES)),
         ],
         compiler_params=pltpu.CompilerParams(vmem_limit_bytes=ATTEND_VMEM),
         cost_estimate=pl.CostEstimate(

time: 36.3 us -> 37.5 us (1.033)
  Pallas kernels: 7.95 us -> 9.22 us
    pallas_call x1, Pallas kernels: 4.31 us -> 5.58 us  [body(): pl.pallas_call(functools.partial(attend_kernel, heads_dev, devices), out_...]
  transfers between devices with their start and end apart: 9 -> 9, of which waited for: 6 -> 6; matrix products, arithmetic and copies ran while one was open for 0% -> 0% of each run, Pallas kernels for 4% -> 3%
where the time goes in v18:
time: 37.5 us; the launch traced here: 37.3 us
  blocking collectives  14.6 us (39%)
  Pallas kernels  9.22 us (25%)
  starting transfers between devices  8.27 us (22%)
  waiting for transfers between devices  5.19 us (14%)
    all_to_all x1, blocking collectives, body(): lax.all_to_all(packed, 'kvp', split_axis=0, concat_axis=0, tiled=True)  14.6 us
    ppermute x9, starting transfers between devices, exchange(): lax.ppermute(array, 'kvp', [(i, i ^ partner) for i in range(devices)])  8.27 us
    pallas_call x1, Pallas kernels, body(): pl.pallas_call(functools.partial(attend_kernel, heads_dev, devices), out_...  5.58 us
    ppermute x9, waiting for transfers between devices, exchange(): lax.ppermute(array, 'kvp', [(i, i ^ partner) for i in range(devices)])  5.19 us
    pallas_call x4, Pallas kernels, body(): pl.pallas_call(functools.partial(project_kernel, x), out_shape=jax.ShapeD...  2.63 us
  transfers between devices with their start and end apart: 9, of which 6 were waited for; matrix products, arithmetic and copies ran while one was open for 0% of the time, Pallas kernels for 3%

profile of v18, /device:TPU:0, one launch (start us, length us, event | category | flops | bytes accessed | tf_op | source)
XLA Modules:
  0.0 37.3 jit_solution(14108580823946356096)
XLA Ops:
  0.0 5.6 %attend.1.staged = f32[16,5,4,128]{3,2,1,0:T(4,128)S(1)} custom-call(s32[4,12]{1,0:T(4,128)} %refs_0_.1, s32[4]{0:T(128)} %refs_1_.1, f32[4,48]{1,0:T(4,128)} %bitcast.2, f32[4,48]{1,0:T(4,128)} %bitcast.3, bf16[4,8192]{1,0:T(4,128)(2,1)} %refs_4_.1, bf16[48,64,512]{2,1,0:T(8,128)(2,1)} %refs_5_.1, bf16[48,64,512]{2,1,0:T(8,128)(2,1)} %refs_6_.1), custom_call_target="tpu_custom_call" | custom-call | flops 100663296 | bytes 6291456 | tf_op jit(solution)/shard_map/attend/pallas_call | solution.py:227
  5.6 0.0 copy-start
  5.6 14.6 %all_to_all.5.packed = bf16[16,5,4,128]{3,2,1,0:T(4,128)(2,1)S(1)} all-to-all(bf16[16,5,4,128]{3,2,1,0:T(4,128)(2,1)S(1)} %pack.1), channel_id=1, replica_groups=mesh['group'=2,'kvp'=16] {'kvp'}, dimensions={0} | all-to-all | bytes 163840 | tf_op jit(solution)/shard_map/all_to_all | solution.py:270
  20.2 0.3 combine.1.left
  20.5 0.0 copy-done
  20.5 0.7 %project_2.1 = bf16[4,4096]{1,0:T(4,128)(2,1)S(1)} custom-call(bf16[4,512]{1,0:T(4,128)(2,1)S(1)} %combine.1.left, bf16[512,16384]{1,0:T(8,128)(2,1)S(1)} %copy-done), custom_call_target="tpu_custom_call" | custom-call | flops 1024 | bytes 1024 | tf_op jit(solution)/shard_map/project_2/pallas_call | solution.py:287
  21.2 0.7 %project_3.1 = bf16[4,4096]{1,0:T(4,128)(2,1)S(1)} custom-call(bf16[4,512]{1,0:T(4,128)(2,1)S(1)} %combine.1.left, bf16[512,16384]{1,0:T(8,128)(2,1)S(1)} %copy-done), custom_call_target="tpu_custom_call" | custom-call | flops 1024 | bytes 1024 | tf_op jit(solution)/shard_map/project_3/pallas_call | solution.py:287
  21.8 0.0 collective-permute-start
  21.8 1.1 %collective-permute-start.1 = (bf16[4,4096]{1,0:T(4,128)(2,1)S(1)}, bf16[4,4096]{1,0:T(4,128)(2,1)S(1)}, u32[]{:S(2)}, u32[]{:S(2)}) collective-permute-start(bf16[4,4096]{1,0:T(4,128)(2,1)S(1)} %project_2.1), channel_id=1, source_target_pairs={{0,2},{1,3},{2,0},{3,1},{4,6},{5,7},{6,4},{7,5},{8,10},{9,11},{10,... | collective-permute-start | bytes 98312 | tf_op jit(solution)/shard_map/ppermute | solution.py:210
  23.0 0.7 %project_1.1 = bf16[4,4096]{1,0:T(4,128)(2,1)S(1)} custom-call(bf16[4,512]{1,0:T(4,128)(2,1)S(1)} %combine.1.left, bf16[512,16384]{1,0:T(8,128)(2,1)S(1)} %copy-done), custom_call_target="tpu_custom_call" | custom-call | flops 1024 | bytes 1024 | tf_op jit(solution)/shard_map/project_1/pallas_call | solution.py:287
  23.6 0.8 %collective-permute-start.2 = (bf16[4,4096]{1,0:T(4,128)(2,1)S(1)}, bf16[4,4096]{1,0:T(4,128)(2,1)S(1)}, u32[]{:S(2)}, u32[]{:S(2)}) collective-permute-start(bf16[4,4096]{1,0:T(4,128)(2,1)S(1)} %project_1.1), channel_id=1, source_target_pairs={{0,1},{1,0},{2,3},{3,2},{4,5},{5,4},{6,7},{7,6},{8,9},{9,8},{10,11... | collective-permute-start | bytes 98312 | tf_op jit(solution)/shard_map/ppermute | solution.py:210
  24.4 0.7 %project_0.1.refs_3_ = f32[4,4096]{1,0:T(4,128)S(1)} custom-call(bf16[4,512]{1,0:T(4,128)(2,1)S(1)} %combine.1.left, bf16[512,16384]{1,0:T(8,128)(2,1)S(1)} %copy-done), custom_call_target="tpu_custom_call" | custom-call | flops 1024 | bytes 1024 | tf_op jit(solution)/shard_map/project_0/pallas_call | solution.py:287
  25.0 0.2 collective-permute-done.refs_0_
  25.2 0.7 %collective-permute-done.1.refs_1_ = bf16[4,4096]{1,0:T(4,128)(2,1)S(1)} collective-permute-done((bf16[4,4096]{1,0:T(4,128)(2,1)S(1)}, bf16[4,4096]{1,0:T(4,128)(2,1)S(1)}, u32[]{:S(2)}, u32[]{:S(2)}) %collective-permute-start.1) | collective-permute-done | bytes 32800 | tf_op jit(solution)/shard_map/ppermute | solution.py:210
  25.9 0.0 collective-permute-done.2.refs_2_
  25.9 1.0 %collective-permute-start.5 = (bf16[4,4096]{1,0:T(4,128)(2,1)S(1)}, bf16[4,4096]{1,0:T(4,128)(2,1)S(1)}, u32[]{:S(2)}, u32[]{:S(2)}) collective-permute-start(bf16[4,4096]{1,0:T(4,128)(2,1)S(1)} %add_near.1.refs_0_), channel_id=1, source_target_pairs={{0,12},{1,13},{2,14},{3,15},{4,8},{5,9},{6,10},{7,11},{8,4},{9,5},... | collective-permute-start | bytes 98312 | tf_op jit(solution)/shard_map/ppermute | solution.py:210
  26.9 0.8 %collective-permute-start.4 = (bf16[4,4096]{1,0:T(4,128)(2,1)S(1)}, bf16[4,4096]{1,0:T(4,128)(2,1)S(1)}, u32[]{:S(2)}, u32[]{:S(2)}) collective-permute-start(bf16[4,4096]{1,0:T(4,128)(2,1)S(1)} %add_near.1.refs_0_), channel_id=1, source_target_pairs={{0,8},{1,9},{2,10},{3,11},{4,12},{5,13},{6,14},{7,15},{8,0},{9,1},... | collective-permute-start | bytes 98312 | tf_op jit(solution)/shard_map/ppermute | solution.py:210
  27.8 2.6 %collective-permute-start.3 = (bf16[4,4096]{1,0:T(4,128)(2,1)S(1)}, bf16[4,4096]{1,0:T(4,128)(2,1)S(1)}, u32[]{:S(2)}, u32[]{:S(2)}) collective-permute-start(bf16[4,4096]{1,0:T(4,128)(2,1)S(1)} %add_near.1.refs_0_), channel_id=1, source_target_pairs={{0,4},{1,5},{2,6},{3,7},{4,0},{5,1},{6,2},{7,3},{8,12},{9,13},{10,... | collective-permute-start | bytes 98312 | tf_op jit(solution)/shard_map/ppermute | solution.py:210
  30.4 1.5 %collective-permute-done.5.refs_3_ = bf16[4,4096]{1,0:T(4,128)(2,1)S(1)} collective-permute-done((bf16[4,4096]{1,0:T(4,128)(2,1)S(1)}, bf16[4,4096]{1,0:T(4,128)(2,1)S(1)}, u32[]{:S(2)}, u32[]{:S(2)}) %collective-permute-start.5) | collective-permute-done | bytes 32800 | tf_op jit(solution)/shard_map/ppermute | solution.py:210
  31.9 0.6 %collective-permute-done.4.refs_2_ = bf16[4,4096]{1,0:T(4,128)(2,1)S(1)} collective-permute-done((bf16[4,4096]{1,0:T(4,128)(2,1)S(1)}, bf16[4,4096]{1,0:T(4,128)(2,1)S(1)}, u32[]{:S(2)}, u32[]{:S(2)}) %collective-permute-start.4) | collective-permute-done | bytes 32800 | tf_op jit(solution)/shard_map/ppermute | solution.py:210
  32.5 0.0 collective-permute-done.3.refs_1_
  32.5 0.1 collective-permute-start.8
  32.6 1.3 %collective-permute-start.7 = (bf16[4,4096]{1,0:T(4,128)(2,1)S(1)}, bf16[4,4096]{1,0:T(4,128)(2,1)S(1)}, u32[]{:S(2)}, u32[]{:S(2)}) collective-permute-start(bf16[4,4096]{1,0:T(4,128)(2,1)S(1)} %add_far.1.refs_0_), channel_id=1, source_target_pairs={{0,2},{1,3},{2,0},{3,1},{4,6},{5,7},{6,4},{7,5},{8,10},{9,11},{10,... | collective-permute-start | bytes 98312 | tf_op jit(solution)/shard_map/ppermute | solution.py:210
  33.9 0.6 %collective-permute-start.6 = (bf16[4,4096]{1,0:T(4,128)(2,1)S(1)}, bf16[4,4096]{1,0:T(4,128)(2,1)S(1)}, u32[]{:S(2)}, u32[]{:S(2)}) collective-permute-start(bf16[4,4096]{1,0:T(4,128)(2,1)S(1)} %add_far.1.refs_0_), channel_id=1, source_target_pairs={{0,1},{1,0},{2,3},{3,2},{4,5},{5,4},{6,7},{7,6},{8,9},{9,8},{10,11... | collective-permute-start | bytes 98312 | tf_op jit(solution)/shard_map/ppermute | solution.py:210
  34.5 1.6 %collective-permute-done.8.refs_3_ = bf16[4,4096]{1,0:T(4,128)(2,1)S(1)} collective-permute-done((bf16[4,4096]{1,0:T(4,128)(2,1)S(1)}, bf16[4,4096]{1,0:T(4,128)(2,1)S(1)}, u32[]{:S(2)}, u32[]{:S(2)}) %collective-permute-start.8) | collective-permute-done | bytes 32800 | tf_op jit(solution)/shard_map/ppermute | solution.py:210
  36.0 0.6 %collective-permute-done.7.refs_2_ = bf16[4,4096]{1,0:T(4,128)(2,1)S(1)} collective-permute-done((bf16[4,4096]{1,0:T(4,128)(2,1)S(1)}, bf16[4,4096]{1,0:T(4,128)(2,1)S(1)}, u32[]{:S(2)}, u32[]{:S(2)}) %collective-permute-start.7) | collective-permute-done | bytes 32800 | tf_op jit(solution)/shard_map/ppermute | solution.py:210
  36.7 0.0 collective-permute-done.6.refs_1_
  36.7 0.7 %lay.1 = bf16[4,16384]{1,0:T(4,128)(2,1)} custom-call(bf16[4,4096]{1,0:T(4,128)(2,1)S(1)} %add_far.1.refs_0_, bf16[4,4096]{1,0:T(4,128)(2,1)S(1)} %collective-permute-done.6.refs_1_, bf16[4,4096]{1,0:T(4,128)(2,1)S(1)} %collective-permute-done.7.refs_2_, bf16[4,4096]{1,0:T(4,128)(2,1)S(1)} %collective-permute-done.8.refs_3_), custom_call_target="tpu_custom_call" | custom-call | tf_op jit(solution)/shard_map/lay/pallas_call | solution.py:311
  (3 shorter events, 0.1 us)
Async XLA Ops:
  5.6 14.9 %copy-start = (bf16[512,16384]{1,0:T(8,128)(2,1)S(1)}, bf16[512,16384]{1,0:T(8,128)(2,1)}, u32[]{:S(2)}) copy-start(bf16[512,16384]{1,0:T(8,128)(2,1)} %weight.7) | copy-start | bytes 50331652
  21.8 3.4 %collective-permute-start = (bf16[4,4096]{1,0:T(4,128)(2,1)S(1)}, bf16[4,4096]{1,0:T(4,128)(2,1)S(1)}, u32[]{:S(2)}, u32[]{:S(2)}) collective-permute-start(bf16[4,4096]{1,0:T(4,128)(2,1)S(1)} %project_3.1), channel_id=1, source_target_pairs={{0,3},{1,2},{2,1},{3,0},{4,7},{5,6},{6,5},{7,4},{8,11},{9,10},{10,... | collective-permute-start | bytes 98312 | tf_op jit(solution)/shard_map/ppermute | solution.py:210
  21.8 4.1 %collective-permute-start.1 = (bf16[4,4096]{1,0:T(4,128)(2,1)S(1)}, bf16[4,4096]{1,0:T(4,128)(2,1)S(1)}, u32[]{:S(2)}, u32[]{:S(2)}) collective-permute-start(bf16[4,4096]{1,0:T(4,128)(2,1)S(1)} %project_2.1), channel_id=1, source_target_pairs={{0,2},{1,3},{2,0},{3,1},{4,6},{5,7},{6,4},{7,5},{8,10},{9,11},{10,... | collective-permute-start | bytes 98312 | tf_op jit(solution)/shard_map/ppermute | solution.py:210
  23.6 2.3 %collective-permute-start.2 = (bf16[4,4096]{1,0:T(4,128)(2,1)S(1)}, bf16[4,4096]{1,0:T(4,128)(2,1)S(1)}, u32[]{:S(2)}, u32[]{:S(2)}) collective-permute-start(bf16[4,4096]{1,0:T(4,128)(2,1)S(1)} %project_1.1), channel_id=1, source_target_pairs={{0,1},{1,0},{2,3},{3,2},{4,5},{5,4},{6,7},{7,6},{8,9},{9,8},{10,11... | collective-permute-start | bytes 98312 | tf_op jit(solution)/shard_map/ppermute | solution.py:210
  25.9 5.9 %collective-permute-start.5 = (bf16[4,4096]{1,0:T(4,128)(2,1)S(1)}, bf16[4,4096]{1,0:T(4,128)(2,1)S(1)}, u32[]{:S(2)}, u32[]{:S(2)}) collective-permute-start(bf16[4,4096]{1,0:T(4,128)(2,1)S(1)} %add_near.1.refs_0_), channel_id=1, source_target_pairs={{0,12},{1,13},{2,14},{3,15},{4,8},{5,9},{6,10},{7,11},{8,4},{9,5},... | collective-permute-start | bytes 98312 | tf_op jit(solution)/shard_map/ppermute | solution.py:210
  26.9 5.5 %collective-permute-start.4 = (bf16[4,4096]{1,0:T(4,128)(2,1)S(1)}, bf16[4,4096]{1,0:T(4,128)(2,1)S(1)}, u32[]{:S(2)}, u32[]{:S(2)}) collective-permute-start(bf16[4,4096]{1,0:T(4,128)(2,1)S(1)} %add_near.1.refs_0_), channel_id=1, source_target_pairs={{0,8},{1,9},{2,10},{3,11},{4,12},{5,13},{6,14},{7,15},{8,0},{9,1},... | collective-permute-start | bytes 98312 | tf_op jit(solution)/shard_map/ppermute | solution.py:210
  27.8 4.7 %collective-permute-start.3 = (bf16[4,4096]{1,0:T(4,128)(2,1)S(1)}, bf16[4,4096]{1,0:T(4,128)(2,1)S(1)}, u32[]{:S(2)}, u32[]{:S(2)}) collective-permute-start(bf16[4,4096]{1,0:T(4,128)(2,1)S(1)} %add_near.1.refs_0_), channel_id=1, source_target_pairs={{0,4},{1,5},{2,6},{3,7},{4,0},{5,1},{6,2},{7,3},{8,12},{9,13},{10,... | collective-permute-start | bytes 98312 | tf_op jit(solution)/shard_map/ppermute | solution.py:210
  32.5 3.5 %collective-permute-start.8 = (bf16[4,4096]{1,0:T(4,128)(2,1)S(1)}, bf16[4,4096]{1,0:T(4,128)(2,1)S(1)}, u32[]{:S(2)}, u32[]{:S(2)}) collective-permute-start(bf16[4,4096]{1,0:T(4,128)(2,1)S(1)} %add_far.1.refs_0_), channel_id=1, source_target_pairs={{0,3},{1,2},{2,1},{3,0},{4,7},{5,6},{6,5},{7,4},{8,11},{9,10},{10,... | collective-permute-start | bytes 98312 | tf_op jit(solution)/shard_map/ppermute | solution.py:210
  32.6 4.1 %collective-permute-start.7 = (bf16[4,4096]{1,0:T(4,128)(2,1)S(1)}, bf16[4,4096]{1,0:T(4,128)(2,1)S(1)}, u32[]{:S(2)}, u32[]{:S(2)}) collective-permute-start(bf16[4,4096]{1,0:T(4,128)(2,1)S(1)} %add_far.1.refs_0_), channel_id=1, source_target_pairs={{0,2},{1,3},{2,0},{3,1},{4,6},{5,7},{6,4},{7,5},{8,10},{9,11},{10,... | collective-permute-start | bytes 98312 | tf_op jit(solution)/shard_map/ppermute | solution.py:210
  33.9 2.8 %collective-permute-start.6 = (bf16[4,4096]{1,0:T(4,128)(2,1)S(1)}, bf16[4,4096]{1,0:T(4,128)(2,1)S(1)}, u32[]{:S(2)}, u32[]{:S(2)}) collective-permute-start(bf16[4,4096]{1,0:T(4,128)(2,1)S(1)} %add_far.1.refs_0_), channel_id=1, source_target_pairs={{0,1},{1,0},{2,3},{3,2},{4,5},{5,4},{6,7},{7,6},{8,9},{9,8},{10,11... | collective-permute-start | bytes 98312 | tf_op jit(solution)/shard_map/ppermute | solution.py:210

commit v19 on v15

--- a/solution.py
+++ b/solution.py
@@ -28,7 +28,7 @@
 def attend_kernel(heads_dev, devices, *refs):
     table_hbm, lengths_hbm, key_scale_hbm, value_scale_hbm, queries_hbm, keys, values = refs[:7]
     staged, table, lengths, key_scale, value_scale, queries, key_buf, value_buf, query_rows = refs[7:16]
-    query_blocks, key_rows, value_rows, scores, weight_rows, stats, small_sems, sems = refs[16:]
+    table_rows, factors, bias, weights, small_sems, sems = refs[16:]
     rows, pages = table.shape
     kv_heads = key_scale.shape[0]
     heads = queries.shape[1] // HD
@@ -41,6 +41,7 @@
     for i, (source, target) in enumerate(
         (
             (table_hbm, table),
+            (table_hbm, table_rows),
             (lengths_hbm, lengths),
             (key_scale_hbm, key_scale),
             (value_scale_hbm, value_scale),
@@ -59,91 +60,81 @@
         copy.start()
 
     me = lax.axis_index("kvp")
-    lane = lax.broadcasted_iota(jnp.int32, (1, HD), 1)
-    first_of_pair = lane < heads
-    of_lane = lax.rem(lax.div(lane, group), kv_heads)
-    spread = (of_lane == lax.broadcasted_iota(jnp.int32, (kv_heads, HD), 0)).astype(jnp.float32)
-    place = lax.broadcasted_iota(jnp.int32, (PAGE, HD), 0)
-    stats[...] = jnp.zeros_like(stats)
+    lane = lax.broadcasted_iota(jnp.int32, (group, HD), 1)
+    place = me * context + lax.broadcasted_iota(jnp.int32, (1, context), 1)
+    page_of = lax.div(lax.broadcasted_iota(jnp.int32, (pages, context), 1), PAGE)
+    spread = (page_of == lax.broadcasted_iota(jnp.int32, (pages, context), 0)).astype(jnp.float32).astype(jnp.bfloat16)
+    slot = lax.broadcasted_iota(jnp.int32, (keys.shape[0], context), 0).astype(jnp.float32)
+    zeros = jnp.zeros((group, HD), jnp.bfloat16)
     for copy in small:
         copy.wait()
     for copy in large[1]:
         copy.start()
 
-    def by_slot(scales):
-        return lax.dot_general(
-            scales[...], spread, (((0,), (0,)), ((), ())),
-            precision=lax.Precision.HIGHEST, preferred_element_type=jnp.float32,
-        )
-
-    key_rows[...] = by_slot(key_scale) * (math.log2(math.e) / math.sqrt(HD))
-    value_rows[...] = by_slot(value_scale)
+    scales = jnp.concatenate([key_scale[...] * (math.log2(math.e) / math.sqrt(HD)), value_scale[...]], axis=0)
+    high, low = split_two(scales)
+    parts = jnp.concatenate([high, low, scales - high - low], axis=0).astype(jnp.bfloat16)
+    slots = jnp.dot(
+        table_rows[...].astype(jnp.float32).astype(jnp.bfloat16), spread, preferred_element_type=jnp.float32
+    )
+    for r in range(rows):
+        chosen = (slots[r : r + 1] == slot).astype(jnp.float32).astype(jnp.bfloat16)
+        found = jnp.dot(parts, chosen, preferred_element_type=jnp.float32)
+        count = 2 * kv_heads
+        factors[r] = found[:count] + found[count : 2 * count] + found[2 * count :]
+        bias[r : r + 1] = jnp.where(place < lengths[r], 0.0, HIDDEN)
     for h in range(heads):
         query_rows[h * rows : (h + 1) * rows, :] = queries[:, h * HD : (h + 1) * HD].astype(jnp.float32)
-    for r in range(0, rows, 2):
-        both = jnp.concatenate([query_rows[pl.ds(r + i, heads, stride=rows), :] for i in (0, 1)], axis=0)
-        turned = both.T
-        for i in (0, 1):
-            for k in range(kv_heads):
-                mine = lax.div(lane, group) == i * kv_heads + k
-                query_blocks[r + i, k * HD : (k + 1) * HD, :] = jnp.where(mine, turned, 0.0).astype(jnp.bfloat16)
-
-    def pages_of(buf, r, columns):
-        return jnp.concatenate([buf[table[r, p], :, columns] for p in range(pages)], axis=0)
-
-    def factor(scale_rows, r, p):
-        left, right = (scale_rows[pl.ds(table[r + i, p], 1), :] for i in (0, 1))
-        return jnp.where(first_of_pair, left, right)
+
+    def pages_of(buf, r, k):
+        return jnp.concatenate(
+            [buf[table[r, p], :, k * HD : (k + 2) * HD] for p in range(pages)], axis=0
+        )
 
     for copy in large[0]:
         copy.wait()
+    stats = [jnp.zeros((group, HD), jnp.float32)] * kv_heads
     for r in range(rows):
-        both = jnp.dot(pages_of(key_buf, r, slice(None)), query_blocks[r], preferred_element_type=jnp.float32)
-        if r % 2 == 0:
-            scores[r // 2] = both
-        else:
-            scores[r // 2] += both
-    for r in range(0, rows, 2):
-        length = jnp.where(first_of_pair, lengths[r], lengths[r + 1]) - me * context
-        highest = jnp.full((PAGE, HD), LOWEST, jnp.float32)
-        for p in range(pages):
-            here = slice(p * PAGE, (p + 1) * PAGE)
-            scaled = jnp.where(place < length - p * PAGE, scores[r // 2, here] * factor(key_rows, r, p), HIDDEN)
-            scores[r // 2, here] = scaled
-            highest = jnp.maximum(highest, scaled)
-        high, low = split_two(jnp.max(highest, axis=0, keepdims=True))
-        total = jnp.zeros((PAGE, HD), jnp.float32)
-        for p in range(0, pages, 2):
-            weights = []
+        query = query_rows[pl.ds(r, heads, stride=rows), :].astype(jnp.bfloat16)
+        for k in range(0, kv_heads, 2):
+            left = jnp.concatenate(
+                [
+                    jnp.concatenate([query[k * group : (k + 1) * group], zeros], axis=1),
+                    jnp.concatenate([zeros, query[(k + 1) * group : (k + 2) * group]], axis=1),
+                ],
+                axis=0,
+            )
+            both = lax.dot_general(
+                left, pages_of(key_buf, r, k), (((1,), (1,)), ((), ())), preferred_element_type=jnp.float32
+            )
             for i in (0, 1):
-                here = slice((p + i) * PAGE, (p + i + 1) * PAGE)
-                prob = jnp.exp2(scores[r // 2, here] - (high + low))
-                total += prob
-                weights.append(prob * factor(value_rows, r, p + i))
-            turned = jnp.concatenate(weights, axis=0).T
-            weight_rows[r // 2, :, p * PAGE : (p + 2) * PAGE] = turned.astype(jnp.bfloat16)
-        total_high, total_low = split_two(jnp.sum(total, axis=0, keepdims=True))
-        for at, value in enumerate((high, low, total_high, total_low)):
-            stats[4 * r + at : 4 * r + at + 1, :] = value
-            stats[4 * r + 4 + at : 4 * r + 5 + at, :] = pltpu.roll(value, HD - heads, axis=1)
-    by_head = stats[...].T
-    for d in range(devices):
-        staged[d, rows] = by_head[d * heads_dev : (d + 1) * heads_dev]
+                at_key, at_value = k + i, kv_heads + k + i
+                scores = both[i * group : (i + 1) * group] * factors[r, at_key : at_key + 1] + bias[r : r + 1]
+                highest = jnp.maximum(jnp.max(scores, axis=1, keepdims=True), LOWEST)
+                high, low = split_two(highest)
+                prob = jnp.exp2(scores - (high + low))
+                total_high, total_low = split_two(jnp.sum(prob, axis=1, keepdims=True))
+                for at, value in enumerate((high, low, total_high, total_low)):
+                    stats[k + i] = jnp.where(lane == 4 * r + at, value, stats[k + i])
+                weights[r, (k + i) * group : (k + i + 1) * group] = (
+                    prob * factors[r, at_value : at_value + 1]
+                ).astype(jnp.bfloat16)
     for copy in large[1]:
         copy.wait()
     for r in range(rows):
         for k in range(0, kv_heads, 2):
-            first = r % 2 * heads + k * group
             both = jnp.dot(
-                weight_rows[r // 2, first : first + 2 * group, :],
-                pages_of(value_buf, r, slice(k * HD, (k + 2) * HD)),
-                preferred_element_type=jnp.float32,
+                weights[r, k * group : (k + 2) * group], pages_of(value_buf, r, k), preferred_element_type=jnp.float32
             )
             for i in (0, 1):
                 partial = both[i * group : (i + 1) * group, i * HD : (i + 1) * HD]
                 for start in range(0, group, heads_dev):
                     d = ((k + i) * group + start) // heads_dev
                     staged[d, r] = partial[start : start + heads_dev]
+    for k in range(kv_heads):
+        for start in range(0, group, heads_dev):
+            d = (k * group + start) // heads_dev
+            staged[d, rows] = stats[k][start : start + heads_dev]
 
 
 def pack_kernel(staged, packed):
@@ -228,13 +219,11 @@
             pltpu.VMEM((slots, PAGE, columns), jnp.bfloat16),
             pltpu.VMEM((slots, PAGE, columns), jnp.bfloat16),
             pltpu.VMEM((heads * rows, HD), jnp.float32),
-            pltpu.VMEM((rows, columns, HD), jnp.bfloat16),
-            pltpu.VMEM((slots, HD), jnp.float32),
-            pltpu.VMEM((slots, HD), jnp.float32),
-            pltpu.VMEM((rows // 2, pages * PAGE, HD), jnp.float32),
-            pltpu.VMEM((rows // 2, HD, pages * PAGE), jnp.bfloat16),
-            pltpu.VMEM((HD, HD), jnp.float32),
-            pltpu.SemaphoreType.DMA((5,)),
+            pltpu.VMEM((rows, pages), jnp.int32),
+            pltpu.VMEM((rows, 2 * kv_heads, pages * PAGE), jnp.float32),
+            pltpu.VMEM((rows, pages * PAGE), jnp.float32),
+            pltpu.VMEM((rows, heads, pages * PAGE), jnp.bfloat16),
+            pltpu.SemaphoreType.DMA((6,)),
             pltpu.SemaphoreType.DMA((2, 4)),
         ],
         compiler_params=pltpu.CompilerParams(vmem_limit_bytes=ATTEND_VMEM),

time: 36.2 us -> 36.3 us (level)
  no operation moved by 1% of the time
where the time goes in v19:
time: 36.3 us; the launch traced here: 36.1 us
  blocking collectives  14.6 us (40%)
  starting transfers between devices  8.27 us (23%)
  Pallas kernels  7.94 us (22%)
  waiting for transfers between devices  5.19 us (14%)
    all_to_all x1, blocking collectives, body(): lax.all_to_all(packed, 'kvp', split_axis=0, concat_axis=0, tiled=True)  14.6 us
    ppermute x9, starting transfers between devices, exchange(): lax.ppermute(array, 'kvp', [(i, i ^ partner) for i in range(devices)])  8.27 us
    ppermute x9, waiting for transfers between devices, exchange(): lax.ppermute(array, 'kvp', [(i, i ^ partner) for i in range(devices)])  5.19 us
    pallas_call x1, Pallas kernels, body(): pl.pallas_call(functools.partial(attend_kernel, heads_dev, devices), out_...  4.3 us
    pallas_call x4, Pallas kernels, body(): pl.pallas_call(functools.partial(project_kernel, x), out_shape=jax.ShapeD...  2.63 us
  transfers between devices with their start and end apart: 9, of which 6 were waited for; matrix products, arithmetic and copies ran while one was open for 0% of the time, Pallas kernels for 4%

profile of v19, /device:TPU:0, one launch (start us, length us, event | category | flops | bytes accessed | tf_op | source)
XLA Modules:
  0.0 36.1 jit_solution(3573560408467822171)
XLA Ops:
  0.0 4.3 %attend.1.staged = f32[16,5,4,128]{3,2,1,0:T(4,128)S(1)} custom-call(s32[4,12]{1,0:T(4,128)} %refs_0_.1, s32[4]{0:T(128)} %refs_1_.1, f32[4,48]{1,0:T(4,128)} %bitcast.2, f32[4,48]{1,0:T(4,128)} %bitcast.3, bf16[4,8192]{1,0:T(4,128)(2,1)} %refs_4_.1, bf16[48,64,512]{2,1,0:T(8,128)(2,1)} %refs_5_.1, bf16[48,64,512]{2,1,0:T(8,128)(2,1)} %refs_6_.1), custom_call_target="tpu_custom_call" | custom-call | flops 100663296 | bytes 6291456 | tf_op jit(solution)/shard_map/attend/pallas_call | solution.py:208
  4.3 0.0 copy-start
  4.4 14.6 %all_to_all.5.packed = bf16[16,5,4,128]{3,2,1,0:T(4,128)(2,1)S(1)} all-to-all(bf16[16,5,4,128]{3,2,1,0:T(4,128)(2,1)S(1)} %pack.1), channel_id=1, replica_groups=mesh['group'=2,'kvp'=16] {'kvp'}, dimensions={0} | all-to-all | bytes 163840 | tf_op jit(solution)/shard_map/all_to_all | solution.py:248
  19.0 0.3 combine.1.left
  19.2 0.0 copy-done
  19.2 0.7 %project_2.1 = bf16[4,4096]{1,0:T(4,128)(2,1)S(1)} custom-call(bf16[4,512]{1,0:T(4,128)(2,1)S(1)} %combine.1.left, bf16[512,16384]{1,0:T(8,128)(2,1)S(1)} %copy-done), custom_call_target="tpu_custom_call" | custom-call | flops 1024 | bytes 1024 | tf_op jit(solution)/shard_map/project_2/pallas_call | solution.py:265
  19.9 0.7 %project_3.1 = bf16[4,4096]{1,0:T(4,128)(2,1)S(1)} custom-call(bf16[4,512]{1,0:T(4,128)(2,1)S(1)} %combine.1.left, bf16[512,16384]{1,0:T(8,128)(2,1)S(1)} %copy-done), custom_call_target="tpu_custom_call" | custom-call | flops 1024 | bytes 1024 | tf_op jit(solution)/shard_map/project_3/pallas_call | solution.py:265
  20.5 0.0 collective-permute-start
  20.5 1.1 %collective-permute-start.1 = (bf16[4,4096]{1,0:T(4,128)(2,1)S(1)}, bf16[4,4096]{1,0:T(4,128)(2,1)S(1)}, u32[]{:S(2)}, u32[]{:S(2)}) collective-permute-start(bf16[4,4096]{1,0:T(4,128)(2,1)S(1)} %project_2.1), channel_id=1, source_target_pairs={{0,2},{1,3},{2,0},{3,1},{4,6},{5,7},{6,4},{7,5},{8,10},{9,11},{10,... | collective-permute-start | bytes 98312 | tf_op jit(solution)/shard_map/ppermute | solution.py:191
  21.7 0.7 %project_1.1 = bf16[4,4096]{1,0:T(4,128)(2,1)S(1)} custom-call(bf16[4,512]{1,0:T(4,128)(2,1)S(1)} %combine.1.left, bf16[512,16384]{1,0:T(8,128)(2,1)S(1)} %copy-done), custom_call_target="tpu_custom_call" | custom-call | flops 1024 | bytes 1024 | tf_op jit(solution)/shard_map/project_1/pallas_call | solution.py:265
  22.3 0.8 %collective-permute-start.2 = (bf16[4,4096]{1,0:T(4,128)(2,1)S(1)}, bf16[4,4096]{1,0:T(4,128)(2,1)S(1)}, u32[]{:S(2)}, u32[]{:S(2)}) collective-permute-start(bf16[4,4096]{1,0:T(4,128)(2,1)S(1)} %project_1.1), channel_id=1, source_target_pairs={{0,1},{1,0},{2,3},{3,2},{4,5},{5,4},{6,7},{7,6},{8,9},{9,8},{10,11... | collective-permute-start | bytes 98312 | tf_op jit(solution)/shard_map/ppermute | solution.py:191
  23.1 0.7 %project_0.1.refs_3_ = f32[4,4096]{1,0:T(4,128)S(1)} custom-call(bf16[4,512]{1,0:T(4,128)(2,1)S(1)} %combine.1.left, bf16[512,16384]{1,0:T(8,128)(2,1)S(1)} %copy-done), custom_call_target="tpu_custom_call" | custom-call | flops 1024 | bytes 1024 | tf_op jit(solution)/shard_map/project_0/pallas_call | solution.py:265
  23.7 0.2 collective-permute-done.refs_0_
  23.9 0.7 %collective-permute-done.1.refs_1_ = bf16[4,4096]{1,0:T(4,128)(2,1)S(1)} collective-permute-done((bf16[4,4096]{1,0:T(4,128)(2,1)S(1)}, bf16[4,4096]{1,0:T(4,128)(2,1)S(1)}, u32[]{:S(2)}, u32[]{:S(2)}) %collective-permute-start.1) | collective-permute-done | bytes 32800 | tf_op jit(solution)/shard_map/ppermute | solution.py:191
  24.6 0.0 collective-permute-done.2.refs_2_
  24.7 1.0 %collective-permute-start.5 = (bf16[4,4096]{1,0:T(4,128)(2,1)S(1)}, bf16[4,4096]{1,0:T(4,128)(2,1)S(1)}, u32[]{:S(2)}, u32[]{:S(2)}) collective-permute-start(bf16[4,4096]{1,0:T(4,128)(2,1)S(1)} %add_near.1.refs_0_), channel_id=1, source_target_pairs={{0,12},{1,13},{2,14},{3,15},{4,8},{5,9},{6,10},{7,11},{8,4},{9,5},... | collective-permute-start | bytes 98312 | tf_op jit(solution)/shard_map/ppermute | solution.py:191
  25.7 0.8 %collective-permute-start.4 = (bf16[4,4096]{1,0:T(4,128)(2,1)S(1)}, bf16[4,4096]{1,0:T(4,128)(2,1)S(1)}, u32[]{:S(2)}, u32[]{:S(2)}) collective-permute-start(bf16[4,4096]{1,0:T(4,128)(2,1)S(1)} %add_near.1.refs_0_), channel_id=1, source_target_pairs={{0,8},{1,9},{2,10},{3,11},{4,12},{5,13},{6,14},{7,15},{8,0},{9,1},... | collective-permute-start | bytes 98312 | tf_op jit(solution)/shard_map/ppermute | solution.py:191
  26.5 2.6 %collective-permute-start.3 = (bf16[4,4096]{1,0:T(4,128)(2,1)S(1)}, bf16[4,4096]{1,0:T(4,128)(2,1)S(1)}, u32[]{:S(2)}, u32[]{:S(2)}) collective-permute-start(bf16[4,4096]{1,0:T(4,128)(2,1)S(1)} %add_near.1.refs_0_), channel_id=1, source_target_pairs={{0,4},{1,5},{2,6},{3,7},{4,0},{5,1},{6,2},{7,3},{8,12},{9,13},{10,... | collective-permute-start | bytes 98312 | tf_op jit(solution)/shard_map/ppermute | solution.py:191
  29.1 1.5 %collective-permute-done.5.refs_3_ = bf16[4,4096]{1,0:T(4,128)(2,1)S(1)} collective-permute-done((bf16[4,4096]{1,0:T(4,128)(2,1)S(1)}, bf16[4,4096]{1,0:T(4,128)(2,1)S(1)}, u32[]{:S(2)}, u32[]{:S(2)}) %collective-permute-start.5) | collective-permute-done | bytes 32800 | tf_op jit(solution)/shard_map/ppermute | solution.py:191
  30.6 0.6 %collective-permute-done.4.refs_2_ = bf16[4,4096]{1,0:T(4,128)(2,1)S(1)} collective-permute-done((bf16[4,4096]{1,0:T(4,128)(2,1)S(1)}, bf16[4,4096]{1,0:T(4,128)(2,1)S(1)}, u32[]{:S(2)}, u32[]{:S(2)}) %collective-permute-start.4) | collective-permute-done | bytes 32800 | tf_op jit(solution)/shard_map/ppermute | solution.py:191
  31.2 0.0 collective-permute-done.3.refs_1_
  31.3 0.1 collective-permute-start.8
  31.3 1.3 %collective-permute-start.7 = (bf16[4,4096]{1,0:T(4,128)(2,1)S(1)}, bf16[4,4096]{1,0:T(4,128)(2,1)S(1)}, u32[]{:S(2)}, u32[]{:S(2)}) collective-permute-start(bf16[4,4096]{1,0:T(4,128)(2,1)S(1)} %add_far.1.refs_0_), channel_id=1, source_target_pairs={{0,2},{1,3},{2,0},{3,1},{4,6},{5,7},{6,4},{7,5},{8,10},{9,11},{10,... | collective-permute-start | bytes 98312 | tf_op jit(solution)/shard_map/ppermute | solution.py:191
  32.6 0.6 %collective-permute-start.6 = (bf16[4,4096]{1,0:T(4,128)(2,1)S(1)}, bf16[4,4096]{1,0:T(4,128)(2,1)S(1)}, u32[]{:S(2)}, u32[]{:S(2)}) collective-permute-start(bf16[4,4096]{1,0:T(4,128)(2,1)S(1)} %add_far.1.refs_0_), channel_id=1, source_target_pairs={{0,1},{1,0},{2,3},{3,2},{4,5},{5,4},{6,7},{7,6},{8,9},{9,8},{10,11... | collective-permute-start | bytes 98312 | tf_op jit(solution)/shard_map/ppermute | solution.py:191
  33.2 1.6 %collective-permute-done.8.refs_3_ = bf16[4,4096]{1,0:T(4,128)(2,1)S(1)} collective-permute-done((bf16[4,4096]{1,0:T(4,128)(2,1)S(1)}, bf16[4,4096]{1,0:T(4,128)(2,1)S(1)}, u32[]{:S(2)}, u32[]{:S(2)}) %collective-permute-start.8) | collective-permute-done | bytes 32800 | tf_op jit(solution)/shard_map/ppermute | solution.py:191
  34.8 0.6 %collective-permute-done.7.refs_2_ = bf16[4,4096]{1,0:T(4,128)(2,1)S(1)} collective-permute-done((bf16[4,4096]{1,0:T(4,128)(2,1)S(1)}, bf16[4,4096]{1,0:T(4,128)(2,1)S(1)}, u32[]{:S(2)}, u32[]{:S(2)}) %collective-permute-start.7) | collective-permute-done | bytes 32800 | tf_op jit(solution)/shard_map/ppermute | solution.py:191
  35.4 0.0 collective-permute-done.6.refs_1_
  35.4 0.7 %lay.1 = bf16[4,16384]{1,0:T(4,128)(2,1)} custom-call(bf16[4,4096]{1,0:T(4,128)(2,1)S(1)} %add_far.1.refs_0_, bf16[4,4096]{1,0:T(4,128)(2,1)S(1)} %collective-permute-done.6.refs_1_, bf16[4,4096]{1,0:T(4,128)(2,1)S(1)} %collective-permute-done.7.refs_2_, bf16[4,4096]{1,0:T(4,128)(2,1)S(1)} %collective-permute-done.8.refs_3_), custom_call_target="tpu_custom_call" | custom-call | tf_op jit(solution)/shard_map/lay/pallas_call | solution.py:289
  (3 shorter events, 0.1 us)
Async XLA Ops:
  4.3 14.9 %copy-start = (bf16[512,16384]{1,0:T(8,128)(2,1)S(1)}, bf16[512,16384]{1,0:T(8,128)(2,1)}, u32[]{:S(2)}) copy-start(bf16[512,16384]{1,0:T(8,128)(2,1)} %weight.7) | copy-start | bytes 50331652
  20.5 3.4 %collective-permute-start = (bf16[4,4096]{1,0:T(4,128)(2,1)S(1)}, bf16[4,4096]{1,0:T(4,128)(2,1)S(1)}, u32[]{:S(2)}, u32[]{:S(2)}) collective-permute-start(bf16[4,4096]{1,0:T(4,128)(2,1)S(1)} %project_3.1), channel_id=1, source_target_pairs={{0,3},{1,2},{2,1},{3,0},{4,7},{5,6},{6,5},{7,4},{8,11},{9,10},{10,... | collective-permute-start | bytes 98312 | tf_op jit(solution)/shard_map/ppermute | solution.py:191
  20.5 4.1 %collective-permute-start.1 = (bf16[4,4096]{1,0:T(4,128)(2,1)S(1)}, bf16[4,4096]{1,0:T(4,128)(2,1)S(1)}, u32[]{:S(2)}, u32[]{:S(2)}) collective-permute-start(bf16[4,4096]{1,0:T(4,128)(2,1)S(1)} %project_2.1), channel_id=1, source_target_pairs={{0,2},{1,3},{2,0},{3,1},{4,6},{5,7},{6,4},{7,5},{8,10},{9,11},{10,... | collective-permute-start | bytes 98312 | tf_op jit(solution)/shard_map/ppermute | solution.py:191
  22.3 2.3 %collective-permute-start.2 = (bf16[4,4096]{1,0:T(4,128)(2,1)S(1)}, bf16[4,4096]{1,0:T(4,128)(2,1)S(1)}, u32[]{:S(2)}, u32[]{:S(2)}) collective-permute-start(bf16[4,4096]{1,0:T(4,128)(2,1)S(1)} %project_1.1), channel_id=1, source_target_pairs={{0,1},{1,0},{2,3},{3,2},{4,5},{5,4},{6,7},{7,6},{8,9},{9,8},{10,11... | collective-permute-start | bytes 98312 | tf_op jit(solution)/shard_map/ppermute | solution.py:191
  24.7 5.9 %collective-permute-start.5 = (bf16[4,4096]{1,0:T(4,128)(2,1)S(1)}, bf16[4,4096]{1,0:T(4,128)(2,1)S(1)}, u32[]{:S(2)}, u32[]{:S(2)}) collective-permute-start(bf16[4,4096]{1,0:T(4,128)(2,1)S(1)} %add_near.1.refs_0_), channel_id=1, source_target_pairs={{0,12},{1,13},{2,14},{3,15},{4,8},{5,9},{6,10},{7,11},{8,4},{9,5},... | collective-permute-start | bytes 98312 | tf_op jit(solution)/shard_map/ppermute | solution.py:191
  25.7 5.5 %collective-permute-start.4 = (bf16[4,4096]{1,0:T(4,128)(2,1)S(1)}, bf16[4,4096]{1,0:T(4,128)(2,1)S(1)}, u32[]{:S(2)}, u32[]{:S(2)}) collective-permute-start(bf16[4,4096]{1,0:T(4,128)(2,1)S(1)} %add_near.1.refs_0_), channel_id=1, source_target_pairs={{0,8},{1,9},{2,10},{3,11},{4,12},{5,13},{6,14},{7,15},{8,0},{9,1},... | collective-permute-start | bytes 98312 | tf_op jit(solution)/shard_map/ppermute | solution.py:191
  26.5 4.7 %collective-permute-start.3 = (bf16[4,4096]{1,0:T(4,128)(2,1)S(1)}, bf16[4,4096]{1,0:T(4,128)(2,1)S(1)}, u32[]{:S(2)}, u32[]{:S(2)}) collective-permute-start(bf16[4,4096]{1,0:T(4,128)(2,1)S(1)} %add_near.1.refs_0_), channel_id=1, source_target_pairs={{0,4},{1,5},{2,6},{3,7},{4,0},{5,1},{6,2},{7,3},{8,12},{9,13},{10,... | collective-permute-start | bytes 98312 | tf_op jit(solution)/shard_map/ppermute | solution.py:191
  31.3 3.5 %collective-permute-start.8 = (bf16[4,4096]{1,0:T(4,128)(2,1)S(1)}, bf16[4,4096]{1,0:T(4,128)(2,1)S(1)}, u32[]{:S(2)}, u32[]{:S(2)}) collective-permute-start(bf16[4,4096]{1,0:T(4,128)(2,1)S(1)} %add_far.1.refs_0_), channel_id=1, source_target_pairs={{0,3},{1,2},{2,1},{3,0},{4,7},{5,6},{6,5},{7,4},{8,11},{9,10},{10,... | collective-permute-start | bytes 98312 | tf_op jit(solution)/shard_map/ppermute | solution.py:191
  31.3 4.1 %collective-permute-start.7 = (bf16[4,4096]{1,0:T(4,128)(2,1)S(1)}, bf16[4,4096]{1,0:T(4,128)(2,1)S(1)}, u32[]{:S(2)}, u32[]{:S(2)}) collective-permute-start(bf16[4,4096]{1,0:T(4,128)(2,1)S(1)} %add_far.1.refs_0_), channel_id=1, source_target_pairs={{0,2},{1,3},{2,0},{3,1},{4,6},{5,7},{6,4},{7,5},{8,10},{9,11},{10,... | collective-permute-start | bytes 98312 | tf_op jit(solution)/shard_map/ppermute | solution.py:191
  32.6 2.8 %collective-permute-start.6 = (bf16[4,4096]{1,0:T(4,128)(2,1)S(1)}, bf16[4,4096]{1,0:T(4,128)(2,1)S(1)}, u32[]{:S(2)}, u32[]{:S(2)}) collective-permute-start(bf16[4,4096]{1,0:T(4,128)(2,1)S(1)} %add_far.1.refs_0_), channel_id=1, source_target_pairs={{0,1},{1,0},{2,3},{3,2},{4,5},{5,4},{6,7},{7,6},{8,9},{9,8},{10,11... | collective-permute-start | bytes 98312 | tf_op jit(solution)/shard_map/ppermute | solution.py:191

commit v20 on v19

--- a/solution.py
+++ b/solution.py
@@ -13,6 +13,7 @@
 ATTEND_VMEM = 60 * 1024 * 1024
 HIDDEN = -1e30
 LOWEST = -1e20
+CACHE_PIECES = 12
 EXCHANGE_FLOPS = 40_000_000_000
 SMALL_VMEM = 8 * 1024 * 1024
 VMEM = pl.BlockSpec(memory_space=pltpu.VMEM)
@@ -224,7 +225,7 @@
             pltpu.VMEM((rows, pages * PAGE), jnp.float32),
             pltpu.VMEM((rows, heads, pages * PAGE), jnp.bfloat16),
             pltpu.SemaphoreType.DMA((6,)),
-            pltpu.SemaphoreType.DMA((2, 4)),
+            pltpu.SemaphoreType.DMA((2, CACHE_PIECES)),
         ],
         compiler_params=pltpu.CompilerParams(vmem_limit_bytes=ATTEND_VMEM),
         cost_estimate=pl.CostEstimate(

time: 36.3 us -> 36.4 us (level)
  no operation moved by 1% of the time
where the time goes in v20:
time: 36.4 us; the launch traced here: 36.3 us
  blocking collectives  14.6 us (40%)
  starting transfers between devices  8.27 us (23%)
  Pallas kernels  8.13 us (22%)
  waiting for transfers between devices  5.19 us (14%)
    all_to_all x1, blocking collectives, body(): lax.all_to_all(packed, 'kvp', split_axis=0, concat_axis=0, tiled=True)  14.6 us
    ppermute x9, starting transfers between devices, exchange(): lax.ppermute(array, 'kvp', [(i, i ^ partner) for i in range(devices)])  8.27 us
    ppermute x9, waiting for transfers between devices, exchange(): lax.ppermute(array, 'kvp', [(i, i ^ partner) for i in range(devices)])  5.19 us
    pallas_call x1, Pallas kernels, body(): pl.pallas_call(functools.partial(attend_kernel, heads_dev, devices), out_...  4.49 us
    pallas_call x4, Pallas kernels, body(): pl.pallas_call(functools.partial(project_kernel, x), out_shape=jax.ShapeD...  2.63 us
  transfers between devices with their start and end apart: 9, of which 6 were waited for; matrix products, arithmetic and copies ran while one was open for 0% of the time, Pallas kernels for 4%

profile of v20, /device:TPU:0, one launch (start us, length us, event | category | flops | bytes accessed | tf_op | source)
XLA Modules:
  0.0 36.3 jit_solution(9180164714269768055)
XLA Ops:
  0.0 4.5 %attend.1.staged = f32[16,5,4,128]{3,2,1,0:T(4,128)S(1)} custom-call(s32[4,12]{1,0:T(4,128)} %refs_0_.1, s32[4]{0:T(128)} %refs_1_.1, f32[4,48]{1,0:T(4,128)} %bitcast.2, f32[4,48]{1,0:T(4,128)} %bitcast.3, bf16[4,8192]{1,0:T(4,128)(2,1)} %refs_4_.1, bf16[48,64,512]{2,1,0:T(8,128)(2,1)} %refs_5_.1, bf16[48,64,512]{2,1,0:T(8,128)(2,1)} %refs_6_.1), custom_call_target="tpu_custom_call" | custom-call | flops 100663296 | bytes 6291456 | tf_op jit(solution)/shard_map/attend/pallas_call | solution.py:209
  4.5 0.0 copy-start
  4.5 14.6 %all_to_all.5.packed = bf16[16,5,4,128]{3,2,1,0:T(4,128)(2,1)S(1)} all-to-all(bf16[16,5,4,128]{3,2,1,0:T(4,128)(2,1)S(1)} %pack.1), channel_id=1, replica_groups=mesh['group'=2,'kvp'=16] {'kvp'}, dimensions={0} | all-to-all | bytes 163840 | tf_op jit(solution)/shard_map/all_to_all | solution.py:249
  19.1 0.3 combine.1.left
  19.4 0.0 copy-done
  19.4 0.7 %project_2.1 = bf16[4,4096]{1,0:T(4,128)(2,1)S(1)} custom-call(bf16[4,512]{1,0:T(4,128)(2,1)S(1)} %combine.1.left, bf16[512,16384]{1,0:T(8,128)(2,1)S(1)} %copy-done), custom_call_target="tpu_custom_call" | custom-call | flops 1024 | bytes 1024 | tf_op jit(solution)/shard_map/project_2/pallas_call | solution.py:266
  20.1 0.7 %project_3.1 = bf16[4,4096]{1,0:T(4,128)(2,1)S(1)} custom-call(bf16[4,512]{1,0:T(4,128)(2,1)S(1)} %combine.1.left, bf16[512,16384]{1,0:T(8,128)(2,1)S(1)} %copy-done), custom_call_target="tpu_custom_call" | custom-call | flops 1024 | bytes 1024 | tf_op jit(solution)/shard_map/project_3/pallas_call | solution.py:266
  20.7 0.0 collective-permute-start
  20.7 1.1 %collective-permute-start.1 = (bf16[4,4096]{1,0:T(4,128)(2,1)S(1)}, bf16[4,4096]{1,0:T(4,128)(2,1)S(1)}, u32[]{:S(2)}, u32[]{:S(2)}) collective-permute-start(bf16[4,4096]{1,0:T(4,128)(2,1)S(1)} %project_2.1), channel_id=1, source_target_pairs={{0,2},{1,3},{2,0},{3,1},{4,6},{5,7},{6,4},{7,5},{8,10},{9,11},{10,... | collective-permute-start | bytes 98312 | tf_op jit(solution)/shard_map/ppermute | solution.py:192
  21.9 0.7 %project_1.1 = bf16[4,4096]{1,0:T(4,128)(2,1)S(1)} custom-call(bf16[4,512]{1,0:T(4,128)(2,1)S(1)} %combine.1.left, bf16[512,16384]{1,0:T(8,128)(2,1)S(1)} %copy-done), custom_call_target="tpu_custom_call" | custom-call | flops 1024 | bytes 1024 | tf_op jit(solution)/shard_map/project_1/pallas_call | solution.py:266
  22.5 0.8 %collective-permute-start.2 = (bf16[4,4096]{1,0:T(4,128)(2,1)S(1)}, bf16[4,4096]{1,0:T(4,128)(2,1)S(1)}, u32[]{:S(2)}, u32[]{:S(2)}) collective-permute-start(bf16[4,4096]{1,0:T(4,128)(2,1)S(1)} %project_1.1), channel_id=1, source_target_pairs={{0,1},{1,0},{2,3},{3,2},{4,5},{5,4},{6,7},{7,6},{8,9},{9,8},{10,11... | collective-permute-start | bytes 98312 | tf_op jit(solution)/shard_map/ppermute | solution.py:192
  23.3 0.7 %project_0.1.refs_3_ = f32[4,4096]{1,0:T(4,128)S(1)} custom-call(bf16[4,512]{1,0:T(4,128)(2,1)S(1)} %combine.1.left, bf16[512,16384]{1,0:T(8,128)(2,1)S(1)} %copy-done), custom_call_target="tpu_custom_call" | custom-call | flops 1024 | bytes 1024 | tf_op jit(solution)/shard_map/project_0/pallas_call | solution.py:266
  23.9 0.2 collective-permute-done.refs_0_
  24.1 0.7 %collective-permute-done.1.refs_1_ = bf16[4,4096]{1,0:T(4,128)(2,1)S(1)} collective-permute-done((bf16[4,4096]{1,0:T(4,128)(2,1)S(1)}, bf16[4,4096]{1,0:T(4,128)(2,1)S(1)}, u32[]{:S(2)}, u32[]{:S(2)}) %collective-permute-start.1) | collective-permute-done | bytes 32800 | tf_op jit(solution)/shard_map/ppermute | solution.py:192
  24.8 0.0 collective-permute-done.2.refs_2_
  24.9 1.0 %collective-permute-start.5 = (bf16[4,4096]{1,0:T(4,128)(2,1)S(1)}, bf16[4,4096]{1,0:T(4,128)(2,1)S(1)}, u32[]{:S(2)}, u32[]{:S(2)}) collective-permute-start(bf16[4,4096]{1,0:T(4,128)(2,1)S(1)} %add_near.1.refs_0_), channel_id=1, source_target_pairs={{0,12},{1,13},{2,14},{3,15},{4,8},{5,9},{6,10},{7,11},{8,4},{9,5},... | collective-permute-start | bytes 98312 | tf_op jit(solution)/shard_map/ppermute | solution.py:192
  25.9 0.8 %collective-permute-start.4 = (bf16[4,4096]{1,0:T(4,128)(2,1)S(1)}, bf16[4,4096]{1,0:T(4,128)(2,1)S(1)}, u32[]{:S(2)}, u32[]{:S(2)}) collective-permute-start(bf16[4,4096]{1,0:T(4,128)(2,1)S(1)} %add_near.1.refs_0_), channel_id=1, source_target_pairs={{0,8},{1,9},{2,10},{3,11},{4,12},{5,13},{6,14},{7,15},{8,0},{9,1},... | collective-permute-start | bytes 98312 | tf_op jit(solution)/shard_map/ppermute | solution.py:192
  26.7 2.6 %collective-permute-start.3 = (bf16[4,4096]{1,0:T(4,128)(2,1)S(1)}, bf16[4,4096]{1,0:T(4,128)(2,1)S(1)}, u32[]{:S(2)}, u32[]{:S(2)}) collective-permute-start(bf16[4,4096]{1,0:T(4,128)(2,1)S(1)} %add_near.1.refs_0_), channel_id=1, source_target_pairs={{0,4},{1,5},{2,6},{3,7},{4,0},{5,1},{6,2},{7,3},{8,12},{9,13},{10,... | collective-permute-start | bytes 98312 | tf_op jit(solution)/shard_map/ppermute | solution.py:192
  29.3 1.5 %collective-permute-done.5.refs_3_ = bf16[4,4096]{1,0:T(4,128)(2,1)S(1)} collective-permute-done((bf16[4,4096]{1,0:T(4,128)(2,1)S(1)}, bf16[4,4096]{1,0:T(4,128)(2,1)S(1)}, u32[]{:S(2)}, u32[]{:S(2)}) %collective-permute-start.5) | collective-permute-done | bytes 32800 | tf_op jit(solution)/shard_map/ppermute | solution.py:192
  30.8 0.6 %collective-permute-done.4.refs_2_ = bf16[4,4096]{1,0:T(4,128)(2,1)S(1)} collective-permute-done((bf16[4,4096]{1,0:T(4,128)(2,1)S(1)}, bf16[4,4096]{1,0:T(4,128)(2,1)S(1)}, u32[]{:S(2)}, u32[]{:S(2)}) %collective-permute-start.4) | collective-permute-done | bytes 32800 | tf_op jit(solution)/shard_map/ppermute | solution.py:192
  31.4 0.0 collective-permute-done.3.refs_1_
  31.4 0.1 collective-permute-start.8
  31.5 1.3 %collective-permute-start.7 = (bf16[4,4096]{1,0:T(4,128)(2,1)S(1)}, bf16[4,4096]{1,0:T(4,128)(2,1)S(1)}, u32[]{:S(2)}, u32[]{:S(2)}) collective-permute-start(bf16[4,4096]{1,0:T(4,128)(2,1)S(1)} %add_far.1.refs_0_), channel_id=1, source_target_pairs={{0,2},{1,3},{2,0},{3,1},{4,6},{5,7},{6,4},{7,5},{8,10},{9,11},{10,... | collective-permute-start | bytes 98312 | tf_op jit(solution)/shard_map/ppermute | solution.py:192
  32.8 0.6 %collective-permute-start.6 = (bf16[4,4096]{1,0:T(4,128)(2,1)S(1)}, bf16[4,4096]{1,0:T(4,128)(2,1)S(1)}, u32[]{:S(2)}, u32[]{:S(2)}) collective-permute-start(bf16[4,4096]{1,0:T(4,128)(2,1)S(1)} %add_far.1.refs_0_), channel_id=1, source_target_pairs={{0,1},{1,0},{2,3},{3,2},{4,5},{5,4},{6,7},{7,6},{8,9},{9,8},{10,11... | collective-permute-start | bytes 98312 | tf_op jit(solution)/shard_map/ppermute | solution.py:192
  33.4 1.6 %collective-permute-done.8.refs_3_ = bf16[4,4096]{1,0:T(4,128)(2,1)S(1)} collective-permute-done((bf16[4,4096]{1,0:T(4,128)(2,1)S(1)}, bf16[4,4096]{1,0:T(4,128)(2,1)S(1)}, u32[]{:S(2)}, u32[]{:S(2)}) %collective-permute-start.8) | collective-permute-done | bytes 32800 | tf_op jit(solution)/shard_map/ppermute | solution.py:192
  35.0 0.6 %collective-permute-done.7.refs_2_ = bf16[4,4096]{1,0:T(4,128)(2,1)S(1)} collective-permute-done((bf16[4,4096]{1,0:T(4,128)(2,1)S(1)}, bf16[4,4096]{1,0:T(4,128)(2,1)S(1)}, u32[]{:S(2)}, u32[]{:S(2)}) %collective-permute-start.7) | collective-permute-done | bytes 32800 | tf_op jit(solution)/shard_map/ppermute | solution.py:192
  35.6 0.0 collective-permute-done.6.refs_1_
  35.6 0.7 %lay.1 = bf16[4,16384]{1,0:T(4,128)(2,1)} custom-call(bf16[4,4096]{1,0:T(4,128)(2,1)S(1)} %add_far.1.refs_0_, bf16[4,4096]{1,0:T(4,128)(2,1)S(1)} %collective-permute-done.6.refs_1_, bf16[4,4096]{1,0:T(4,128)(2,1)S(1)} %collective-permute-done.7.refs_2_, bf16[4,4096]{1,0:T(4,128)(2,1)S(1)} %collective-permute-done.8.refs_3_), custom_call_target="tpu_custom_call" | custom-call | tf_op jit(solution)/shard_map/lay/pallas_call | solution.py:290
  (3 shorter events, 0.1 us)
Async XLA Ops:
  4.5 14.9 %copy-start = (bf16[512,16384]{1,0:T(8,128)(2,1)S(1)}, bf16[512,16384]{1,0:T(8,128)(2,1)}, u32[]{:S(2)}) copy-start(bf16[512,16384]{1,0:T(8,128)(2,1)} %weight.7) | copy-start | bytes 50331652
  20.7 3.4 %collective-permute-start = (bf16[4,4096]{1,0:T(4,128)(2,1)S(1)}, bf16[4,4096]{1,0:T(4,128)(2,1)S(1)}, u32[]{:S(2)}, u32[]{:S(2)}) collective-permute-start(bf16[4,4096]{1,0:T(4,128)(2,1)S(1)} %project_3.1), channel_id=1, source_target_pairs={{0,3},{1,2},{2,1},{3,0},{4,7},{5,6},{6,5},{7,4},{8,11},{9,10},{10,... | collective-permute-start | bytes 98312 | tf_op jit(solution)/shard_map/ppermute | solution.py:192
  20.7 4.1 %collective-permute-start.1 = (bf16[4,4096]{1,0:T(4,128)(2,1)S(1)}, bf16[4,4096]{1,0:T(4,128)(2,1)S(1)}, u32[]{:S(2)}, u32[]{:S(2)}) collective-permute-start(bf16[4,4096]{1,0:T(4,128)(2,1)S(1)} %project_2.1), channel_id=1, source_target_pairs={{0,2},{1,3},{2,0},{3,1},{4,6},{5,7},{6,4},{7,5},{8,10},{9,11},{10,... | collective-permute-start | bytes 98312 | tf_op jit(solution)/shard_map/ppermute | solution.py:192
  22.5 2.3 %collective-permute-start.2 = (bf16[4,4096]{1,0:T(4,128)(2,1)S(1)}, bf16[4,4096]{1,0:T(4,128)(2,1)S(1)}, u32[]{:S(2)}, u32[]{:S(2)}) collective-permute-start(bf16[4,4096]{1,0:T(4,128)(2,1)S(1)} %project_1.1), channel_id=1, source_target_pairs={{0,1},{1,0},{2,3},{3,2},{4,5},{5,4},{6,7},{7,6},{8,9},{9,8},{10,11... | collective-permute-start | bytes 98312 | tf_op jit(solution)/shard_map/ppermute | solution.py:192
  24.9 5.9 %collective-permute-start.5 = (bf16[4,4096]{1,0:T(4,128)(2,1)S(1)}, bf16[4,4096]{1,0:T(4,128)(2,1)S(1)}, u32[]{:S(2)}, u32[]{:S(2)}) collective-permute-start(bf16[4,4096]{1,0:T(4,128)(2,1)S(1)} %add_near.1.refs_0_), channel_id=1, source_target_pairs={{0,12},{1,13},{2,14},{3,15},{4,8},{5,9},{6,10},{7,11},{8,4},{9,5},... | collective-permute-start | bytes 98312 | tf_op jit(solution)/shard_map/ppermute | solution.py:192
  25.9 5.5 %collective-permute-start.4 = (bf16[4,4096]{1,0:T(4,128)(2,1)S(1)}, bf16[4,4096]{1,0:T(4,128)(2,1)S(1)}, u32[]{:S(2)}, u32[]{:S(2)}) collective-permute-start(bf16[4,4096]{1,0:T(4,128)(2,1)S(1)} %add_near.1.refs_0_), channel_id=1, source_target_pairs={{0,8},{1,9},{2,10},{3,11},{4,12},{5,13},{6,14},{7,15},{8,0},{9,1},... | collective-permute-start | bytes 98312 | tf_op jit(solution)/shard_map/ppermute | solution.py:192
  26.7 4.7 %collective-permute-start.3 = (bf16[4,4096]{1,0:T(4,128)(2,1)S(1)}, bf16[4,4096]{1,0:T(4,128)(2,1)S(1)}, u32[]{:S(2)}, u32[]{:S(2)}) collective-permute-start(bf16[4,4096]{1,0:T(4,128)(2,1)S(1)} %add_near.1.refs_0_), channel_id=1, source_target_pairs={{0,4},{1,5},{2,6},{3,7},{4,0},{5,1},{6,2},{7,3},{8,12},{9,13},{10,... | collective-permute-start | bytes 98312 | tf_op jit(solution)/shard_map/ppermute | solution.py:192
  31.4 3.5 %collective-permute-start.8 = (bf16[4,4096]{1,0:T(4,128)(2,1)S(1)}, bf16[4,4096]{1,0:T(4,128)(2,1)S(1)}, u32[]{:S(2)}, u32[]{:S(2)}) collective-permute-start(bf16[4,4096]{1,0:T(4,128)(2,1)S(1)} %add_far.1.refs_0_), channel_id=1, source_target_pairs={{0,3},{1,2},{2,1},{3,0},{4,7},{5,6},{6,5},{7,4},{8,11},{9,10},{10,... | collective-permute-start | bytes 98312 | tf_op jit(solution)/shard_map/ppermute | solution.py:192
  31.5 4.1 %collective-permute-start.7 = (bf16[4,4096]{1,0:T(4,128)(2,1)S(1)}, bf16[4,4096]{1,0:T(4,128)(2,1)S(1)}, u32[]{:S(2)}, u32[]{:S(2)}) collective-permute-start(bf16[4,4096]{1,0:T(4,128)(2,1)S(1)} %add_far.1.refs_0_), channel_id=1, source_target_pairs={{0,2},{1,3},{2,0},{3,1},{4,6},{5,7},{6,4},{7,5},{8,10},{9,11},{10,... | collective-permute-start | bytes 98312 | tf_op jit(solution)/shard_map/ppermute | solution.py:192
  32.8 2.8 %collective-permute-start.6 = (bf16[4,4096]{1,0:T(4,128)(2,1)S(1)}, bf16[4,4096]{1,0:T(4,128)(2,1)S(1)}, u32[]{:S(2)}, u32[]{:S(2)}) collective-permute-start(bf16[4,4096]{1,0:T(4,128)(2,1)S(1)} %add_far.1.refs_0_), channel_id=1, source_target_pairs={{0,1},{1,0},{2,3},{3,2},{4,5},{5,4},{6,7},{7,6},{8,9},{9,8},{10,11... | collective-permute-start | bytes 98312 | tf_op jit(solution)/shard_map/ppermute | solution.py:192

commit v21 on v19

--- a/solution.py
+++ b/solution.py
@@ -13,7 +13,7 @@
 ATTEND_VMEM = 60 * 1024 * 1024
 HIDDEN = -1e30
 LOWEST = -1e20
-EXCHANGE_FLOPS = 40_000_000_000
+EXCHANGE_FLOPS = 5_000_000_000
 SMALL_VMEM = 8 * 1024 * 1024
 VMEM = pl.BlockSpec(memory_space=pltpu.VMEM)
 HBM = pl.BlockSpec(memory_space=pltpu.HBM)
@@ -171,20 +171,31 @@
     out[...] = terms.astype(out.dtype)
 
 
-def add_kernel(*refs):
-    terms = [ref[...].astype(jnp.float32) for ref in refs[:-1]]
-    while len(terms) > 1:
-        terms = [terms[i] + terms[i + 1] for i in range(0, len(terms), 2)]
-    refs[-1][...] = terms[0].astype(refs[-1].dtype)
-
-
-def lay_kernel(*refs):
-    parts, out = refs[:-1], refs[-1]
-    quarter = lax.rem(lax.axis_index("kvp"), len(parts))
-    width = parts[0].shape[1]
-    for x, part in enumerate(parts):
-        start = pl.multiple_of(jnp.bitwise_xor(quarter, x) * width, width)
-        out[:, pl.ds(start, width)] = part[...]
+def regroup_kernel(outer, inner, arrived, grouped):
+    for x in range(outer):
+        for i in range(inner):
+            grouped[i * outer + x] = arrived[x * inner + i]
+
+
+def spread_copies(value, copies):
+    for i in range(copies.shape[0]):
+        copies[i] = value
+
+
+def add_near_kernel(*refs):
+    terms, copies = refs[:-1], refs[-1]
+    spread_copies(sum(term[...].astype(jnp.float32) for term in terms).astype(copies.dtype), copies)
+
+
+def add_far_kernel(terms, copies):
+    total = sum(terms[i].astype(jnp.float32) for i in range(terms.shape[0]))
+    spread_copies(total.astype(copies.dtype), copies)
+
+
+def lay_kernel(parts, out):
+    count, _, width = parts.shape
+    for i in range(count):
+        out[:, i * width : (i + 1) * width] = parts[i]
 
 
 def exchange(array, partner, devices):
@@ -202,9 +213,6 @@
     heads_dev = out_weight.shape[0] // HD
     heads = queries.shape[1] // HD
     features = out_weight.shape[1]
-    inner = 4
-    outer = devices // inner
-    part = features // inner
     staged = pl.pallas_call(
         functools.partial(attend_kernel, heads_dev, devices),
         out_shape=pltpu.VMEM((devices, rows + 1, heads_dev, HD), jnp.float32),
@@ -235,6 +243,21 @@
         name="attend",
     )(*[in_hbm(a) for a in (page_table, lengths, key_scale.T, value_scale.T, queries, key_cache, value_cache)])
 
+    inner = 4
+    outer = devices // inner
+    part = features // inner
+
+    def small_kernel(kernel, out_shape, name, *operands, flops=1024):
+        return pl.pallas_call(
+            kernel,
+            out_shape=out_shape,
+            in_specs=[VMEM] * len(operands),
+            out_specs=VMEM,
+            compiler_params=pltpu.CompilerParams(vmem_limit_bytes=SMALL_VMEM),
+            cost_estimate=pl.CostEstimate(flops=flops, bytes_accessed=1024, transcendentals=0),
+            name=name,
+        )(*operands)
+
     packed = pl.pallas_call(
         pack_kernel,
         out_shape=jax.ShapeDtypeStruct(staged.shape, jnp.bfloat16),
@@ -245,7 +268,18 @@
         name="pack",
     )(staged)
 
-    received = lax.all_to_all(packed, "kvp", split_axis=0, concat_axis=0, tiled=True)
+    far = [[x * inner + i for x in range(outer)] for i in range(inner)]
+    near = [[x * inner + i for i in range(inner)] for x in range(outer)]
+
+    def exchange_all(array, groups):
+        return lax.all_to_all(array, "kvp", split_axis=0, concat_axis=0, axis_index_groups=groups, tiled=True)
+
+    arrived = exchange_all(packed, far)
+    grouped = small_kernel(
+        functools.partial(regroup_kernel, outer, inner), jax.ShapeDtypeStruct(arrived.shape, arrived.dtype),
+        "regroup", arrived,
+    )
+    received = exchange_all(grouped, near)
 
     resident = pltpu.with_memory_space_constraint(out_weight, pltpu.VMEM)
     depth = heads_dev * HD
@@ -273,27 +307,12 @@
         )(left, resident)
         arrived.append(exchange(terms, x, devices) if x else terms)
 
-    def add(terms, name):
-        return pl.pallas_call(
-            add_kernel,
-            out_shape=jax.ShapeDtypeStruct((rows, part), jnp.bfloat16),
-            in_specs=[VMEM] * len(terms),
-            out_specs=VMEM,
-            compiler_params=pltpu.CompilerParams(vmem_limit_bytes=SMALL_VMEM),
-            name=name,
-        )(*terms)
-
-    mine = add(arrived, "add_near")
-    mine = add([mine] + [exchange(mine, x * inner, devices) for x in range(1, outer)], "add_far")
-    parts = [mine] + [exchange(mine, x, devices) for x in range(1, inner)]
-    return pl.pallas_call(
-        lay_kernel,
-        out_shape=jax.ShapeDtypeStruct((rows, features), jnp.bfloat16),
-        in_specs=[VMEM] * inner,
-        out_specs=VMEM,
-        compiler_params=pltpu.CompilerParams(vmem_limit_bytes=SMALL_VMEM),
-        name="lay",
-    )(*parts)
+    copies = jax.ShapeDtypeStruct((outer, rows, part), jnp.bfloat16)
+    mine = small_kernel(add_near_kernel, copies, "add_near", *arrived)
+    copies = jax.ShapeDtypeStruct((inner, rows, part), jnp.bfloat16)
+    mine = small_kernel(add_far_kernel, copies, "add_far", exchange_all(mine, far))
+    whole = jax.ShapeDtypeStruct((rows, features), jnp.bfloat16)
+    return small_kernel(lay_kernel, whole, "lay", exchange_all(mine, near))
 
 
 def solution(mesh):

time: 36.3 us -> 45.9 us (1.26)
  blocking collectives: 14.6 us -> 34.8 us
  starting transfers between devices: 8.27 us -> 1.91 us
  waiting for transfers between devices: 5.19 us -> 0.98 us
    all_to_all x1 -> x4, blocking collectives: 14.6 us -> 34.8 us  [exchange_all(): lax.all_to_all(array, 'kvp', split_axis=0, concat_axis=0, axis_index_grou...]
    ppermute x9 -> x3, starting transfers between devices: 8.27 us -> 1.91 us  [exchange(): lax.ppermute(array, 'kvp', [(i, i ^ partner) for i in range(devices)])]
    ppermute x9 -> x3, waiting for transfers between devices: 5.19 us -> 0.98 us  [exchange(): lax.ppermute(array, 'kvp', [(i, i ^ partner) for i in range(devices)])]
  transfers between devices with their start and end apart: 9 -> 3, of which waited for: 6 -> 2; matrix products, arithmetic and copies ran while one was open for 0% -> 0% of each run, Pallas kernels for 4% -> 3%
where the time goes in v21:
time: 45.9 us; the launch traced here: 45.6 us
  blocking collectives  34.8 us (76%)
  Pallas kernels  7.94 us (17%)
  starting transfers between devices  1.91 us (4%)
  waiting for transfers between devices  0.98 us (2%)
    all_to_all x4, blocking collectives, exchange_all(): lax.all_to_all(array, 'kvp', split_axis=0, concat_axis=0, axis_index_grou...  34.8 us
    pallas_call x1, Pallas kernels, body(): pl.pallas_call(functools.partial(attend_kernel, heads_dev, devices), out_...  4.3 us
    pallas_call x4, Pallas kernels, body(): pl.pallas_call(functools.partial(project_kernel, x), out_shape=jax.ShapeD...  2.63 us
    ppermute x3, starting transfers between devices, exchange(): lax.ppermute(array, 'kvp', [(i, i ^ partner) for i in range(devices)])  1.91 us
    ppermute x3, waiting for transfers between devices, exchange(): lax.ppermute(array, 'kvp', [(i, i ^ partner) for i in range(devices)])  0.98 us
  transfers between devices with their start and end apart: 3, of which 2 were waited for; matrix products, arithmetic and copies ran while one was open for 0% of the time, Pallas kernels for 3%

profile of v21, /device:TPU:0, one launch (start us, length us, event | category | flops | bytes accessed | tf_op | source)
XLA Modules:
  0.0 45.6 jit_solution(11264331709610856815)
XLA Ops:
  0.0 4.3 %attend.1.staged = f32[16,5,4,128]{3,2,1,0:T(4,128)S(1)} custom-call(s32[4,12]{1,0:T(4,128)} %refs_0_.1, s32[4]{0:T(128)} %refs_1_.1, f32[4,48]{1,0:T(4,128)} %bitcast.2, f32[4,48]{1,0:T(4,128)} %bitcast.3, bf16[4,8192]{1,0:T(4,128)(2,1)} %refs_4_.1, bf16[48,64,512]{2,1,0:T(8,128)(2,1)} %refs_5_.1, bf16[48,64,512]{2,1,0:T(8,128)(2,1)} %refs_6_.1), custom_call_target="tpu_custom_call" | custom-call | flops 100663296 | bytes 6291456 | tf_op jit(solution)/shard_map/attend/pallas_call | solution.py:216
  4.3 0.0 copy-start
  4.4 12.2 %all_to_all.20.arrived = bf16[16,5,4,128]{3,2,1,0:T(4,128)(2,1)S(1)} all-to-all(bf16[16,5,4,128]{3,2,1,0:T(4,128)(2,1)S(1)} %pack.1), channel_id=1, replica_groups={{0,4,8,12},{1,5,9,13},{2,6,10,14},{3,7,11,15},{16,20,24,28},{17,21,25,2..., dimensions={0} | all-to-all | bytes 163840 | tf_op jit(solution)/shard_map/all_to_all | solution.py:275
  16.5 6.8 %all_to_all.21.packed = bf16[16,5,4,128]{3,2,1,0:T(4,128)(2,1)S(1)} all-to-all(bf16[16,5,4,128]{3,2,1,0:T(4,128)(2,1)S(1)} %regroup.1), channel_id=1, replica_groups={{0,1,2,3},{4,5,6,7},{8,9,10,11},{12,13,14,15},{16,17,18,19},{20,21,22,2..., dimensions={0} | all-to-all | bytes 163840 | tf_op jit(solution)/shard_map/all_to_all | solution.py:275
  23.3 0.3 combine.1.left
  23.6 0.0 copy-done
  23.6 0.7 %project_2.1 = bf16[4,4096]{1,0:T(4,128)(2,1)S(1)} custom-call(bf16[4,512]{1,0:T(4,128)(2,1)S(1)} %combine.1.left, bf16[512,16384]{1,0:T(8,128)(2,1)S(1)} %copy-done), custom_call_target="tpu_custom_call" | custom-call | flops 1024 | bytes 1024 | tf_op jit(solution)/shard_map/project_2/pallas_call | solution.py:299
  24.3 0.7 %project_3.1 = bf16[4,4096]{1,0:T(4,128)(2,1)S(1)} custom-call(bf16[4,512]{1,0:T(4,128)(2,1)S(1)} %combine.1.left, bf16[512,16384]{1,0:T(8,128)(2,1)S(1)} %copy-done), custom_call_target="tpu_custom_call" | custom-call | flops 1024 | bytes 1024 | tf_op jit(solution)/shard_map/project_3/pallas_call | solution.py:299
  24.9 0.0 collective-permute-start
  24.9 1.2 %collective-permute-start.1 = (bf16[4,4096]{1,0:T(4,128)(2,1)S(1)}, bf16[4,4096]{1,0:T(4,128)(2,1)S(1)}, u32[]{:S(2)}, u32[]{:S(2)}) collective-permute-start(bf16[4,4096]{1,0:T(4,128)(2,1)S(1)} %project_2.1), channel_id=1, source_target_pairs={{0,2},{1,3},{2,0},{3,1},{4,6},{5,7},{6,4},{7,5},{8,10},{9,11},{10,... | collective-permute-start | bytes 98312 | tf_op jit(solution)/shard_map/ppermute | solution.py:202
  26.2 0.7 %project_1.1 = bf16[4,4096]{1,0:T(4,128)(2,1)S(1)} custom-call(bf16[4,512]{1,0:T(4,128)(2,1)S(1)} %combine.1.left, bf16[512,16384]{1,0:T(8,128)(2,1)S(1)} %copy-done), custom_call_target="tpu_custom_call" | custom-call | flops 1024 | bytes 1024 | tf_op jit(solution)/shard_map/project_1/pallas_call | solution.py:299
  26.8 0.7 %collective-permute-start.2 = (bf16[4,4096]{1,0:T(4,128)(2,1)S(1)}, bf16[4,4096]{1,0:T(4,128)(2,1)S(1)}, u32[]{:S(2)}, u32[]{:S(2)}) collective-permute-start(bf16[4,4096]{1,0:T(4,128)(2,1)S(1)} %project_1.1), channel_id=1, source_target_pairs={{0,1},{1,0},{2,3},{3,2},{4,5},{5,4},{6,7},{7,6},{8,9},{9,8},{10,11... | collective-permute-start | bytes 98312 | tf_op jit(solution)/shard_map/ppermute | solution.py:202
  27.5 0.7 %project_0.1.refs_3_ = f32[4,4096]{1,0:T(4,128)S(1)} custom-call(bf16[4,512]{1,0:T(4,128)(2,1)S(1)} %combine.1.left, bf16[512,16384]{1,0:T(8,128)(2,1)S(1)} %copy-done), custom_call_target="tpu_custom_call" | custom-call | flops 1024 | bytes 1024 | tf_op jit(solution)/shard_map/project_0/pallas_call | solution.py:299
  28.1 0.3 collective-permute-done.refs_0_
  28.4 0.7 %collective-permute-done.1.refs_1_ = bf16[4,4096]{1,0:T(4,128)(2,1)S(1)} collective-permute-done((bf16[4,4096]{1,0:T(4,128)(2,1)S(1)}, bf16[4,4096]{1,0:T(4,128)(2,1)S(1)}, u32[]{:S(2)}, u32[]{:S(2)}) %collective-permute-start.1) | collective-permute-done | bytes 32800 | tf_op jit(solution)/shard_map/ppermute | solution.py:202
  29.1 0.0 collective-permute-done.2.refs_2_
  29.2 8.8 %all_to_all.22.terms = bf16[4,4,4096]{2,1,0:T(4,128)(2,1)S(1)} all-to-all(bf16[4,4,4096]{2,1,0:T(4,128)(2,1)S(1)} %add_near.1), channel_id=1, replica_groups={{0,4,8,12},{1,5,9,13},{2,6,10,14},{3,7,11,15},{16,20,24,28},{17,21,25,2..., dimensions={0} | all-to-all | bytes 262144 | tf_op jit(solution)/shard_map/all_to_all | solution.py:275
  38.0 7.0 %all_to_all.23.parts = bf16[4,4,4096]{2,1,0:T(4,128)(2,1)S(1)} all-to-all(bf16[4,4,4096]{2,1,0:T(4,128)(2,1)S(1)} %add_far.1), channel_id=1, replica_groups={{0,1,2,3},{4,5,6,7},{8,9,10,11},{12,13,14,15},{16,17,18,19},{20,21,22,2..., dimensions={0} | all-to-all | bytes 262144 | tf_op jit(solution)/shard_map/all_to_all | solution.py:275
  45.0 0.7 %lay.1 = bf16[4,16384]{1,0:T(4,128)(2,1)} custom-call(bf16[4,4,4096]{2,1,0:T(4,128)(2,1)S(1)} %all_to_all.23.parts), custom_call_target="tpu_custom_call" | custom-call | flops 1024 | bytes 1024 | tf_op jit(solution)/shard_map/lay/pallas_call | solution.py:251
  (4 shorter events, 0.1 us)
Async XLA Ops:
  4.3 19.3 %copy-start = (bf16[512,16384]{1,0:T(8,128)(2,1)S(1)}, bf16[512,16384]{1,0:T(8,128)(2,1)}, u32[]{:S(2)}) copy-start(bf16[512,16384]{1,0:T(8,128)(2,1)} %weight.7) | copy-start | bytes 50331652
  24.9 3.5 %collective-permute-start = (bf16[4,4096]{1,0:T(4,128)(2,1)S(1)}, bf16[4,4096]{1,0:T(4,128)(2,1)S(1)}, u32[]{:S(2)}, u32[]{:S(2)}) collective-permute-start(bf16[4,4096]{1,0:T(4,128)(2,1)S(1)} %project_3.1), channel_id=1, source_target_pairs={{0,3},{1,2},{2,1},{3,0},{4,7},{5,6},{6,5},{7,4},{8,11},{9,10},{10,... | collective-permute-start | bytes 98312 | tf_op jit(solution)/shard_map/ppermute | solution.py:202
  24.9 4.2 %collective-permute-start.1 = (bf16[4,4096]{1,0:T(4,128)(2,1)S(1)}, bf16[4,4096]{1,0:T(4,128)(2,1)S(1)}, u32[]{:S(2)}, u32[]{:S(2)}) collective-permute-start(bf16[4,4096]{1,0:T(4,128)(2,1)S(1)} %project_2.1), channel_id=1, source_target_pairs={{0,2},{1,3},{2,0},{3,1},{4,6},{5,7},{6,4},{7,5},{8,10},{9,11},{10,... | collective-permute-start | bytes 98312 | tf_op jit(solution)/shard_map/ppermute | solution.py:202
  26.8 2.3 %collective-permute-start.2 = (bf16[4,4096]{1,0:T(4,128)(2,1)S(1)}, bf16[4,4096]{1,0:T(4,128)(2,1)S(1)}, u32[]{:S(2)}, u32[]{:S(2)}) collective-permute-start(bf16[4,4096]{1,0:T(4,128)(2,1)S(1)} %project_1.1), channel_id=1, source_target_pairs={{0,1},{1,0},{2,3},{3,2},{4,5},{5,4},{6,7},{7,6},{8,9},{9,8},{10,11... | collective-permute-start | bytes 98312 | tf_op jit(solution)/shard_map/ppermute | solution.py:202

commit v22 on v19

--- a/solution.py
+++ b/solution.py
@@ -182,7 +182,7 @@
     parts, out = refs[:-1], refs[-1]
     quarter = lax.rem(lax.axis_index("kvp"), len(parts))
     width = parts[0].shape[1]
-    for x, part in enumerate(parts):
+    for x, part in zip((0, 1, 3, 2), parts):
         start = pl.multiple_of(jnp.bitwise_xor(quarter, x) * width, width)
         out[:, pl.ds(start, width)] = part[...]
 
@@ -224,7 +224,7 @@
             pltpu.VMEM((rows, pages * PAGE), jnp.float32),
             pltpu.VMEM((rows, heads, pages * PAGE), jnp.bfloat16),
             pltpu.SemaphoreType.DMA((6,)),
-            pltpu.SemaphoreType.DMA((2, 4)),
+            pltpu.SemaphoreType.DMA((2, 2)),
         ],
         compiler_params=pltpu.CompilerParams(vmem_limit_bytes=ATTEND_VMEM),
         cost_estimate=pl.CostEstimate(
@@ -261,7 +261,7 @@
         name="combine",
     )(received)
     arrived = []
-    for x in reversed(range(inner)):
+    for x in (2, 3, 1, 0):
         terms = pl.pallas_call(
             functools.partial(project_kernel, x),
             out_shape=jax.ShapeDtypeStruct((rows, part), jnp.bfloat16 if x else jnp.float32),
@@ -285,7 +285,7 @@
 
     mine = add(arrived, "add_near")
     mine = add([mine] + [exchange(mine, x * inner, devices) for x in range(1, outer)], "add_far")
-    parts = [mine] + [exchange(mine, x, devices) for x in range(1, inner)]
+    parts = [mine] + [exchange(mine, x, devices) for x in (1, 3, 2)]
     return pl.pallas_call(
         lay_kernel,
         out_shape=jax.ShapeDtypeStruct((rows, features), jnp.bfloat16),

time: 36.3 us -> 36.6 us (level)
  starting transfers between devices: 8.27 us -> 8.83 us
    ppermute x9, starting transfers between devices: 8.27 us -> 8.83 us  [exchange(): lax.ppermute(array, 'kvp', [(i, i ^ partner) for i in range(devices)])]
  transfers between devices with their start and end apart: 9 -> 9, of which waited for: 6 -> 5; matrix products, arithmetic and copies ran while one was open for 0% -> 0% of each run, Pallas kernels for 4% -> 4%
where the time goes in v22:
time: 36.6 us; the launch traced here: 36.4 us
  blocking collectives  14.6 us (40%)
  starting transfers between devices  8.83 us (24%)
  Pallas kernels  7.77 us (21%)
  waiting for transfers between devices  5.13 us (14%)
    all_to_all x1, blocking collectives, body(): lax.all_to_all(packed, 'kvp', split_axis=0, concat_axis=0, tiled=True)  14.6 us
    ppermute x9, starting transfers between devices, exchange(): lax.ppermute(array, 'kvp', [(i, i ^ partner) for i in range(devices)])  8.83 us
    ppermute x9, waiting for transfers between devices, exchange(): lax.ppermute(array, 'kvp', [(i, i ^ partner) for i in range(devices)])  5.13 us
    pallas_call x1, Pallas kernels, body(): pl.pallas_call(functools.partial(attend_kernel, heads_dev, devices), out_...  4.13 us
    pallas_call x4, Pallas kernels, body(): pl.pallas_call(functools.partial(project_kernel, x), out_shape=jax.ShapeD...  2.63 us
  transfers between devices with their start and end apart: 9, of which 5 were waited for; matrix products, arithmetic and copies ran while one was open for 0% of the time, Pallas kernels for 4%

profile of v22, /device:TPU:0, one launch (start us, length us, event | category | flops | bytes accessed | tf_op | source)
XLA Modules:
  0.0 36.4 jit_solution(18184876677464328910)
XLA Ops:
  0.0 4.1 %attend.1.staged = f32[16,5,4,128]{3,2,1,0:T(4,128)S(1)} custom-call(s32[4,12]{1,0:T(4,128)} %refs_0_.1, s32[4]{0:T(128)} %refs_1_.1, f32[4,48]{1,0:T(4,128)} %bitcast.2, f32[4,48]{1,0:T(4,128)} %bitcast.3, bf16[4,8192]{1,0:T(4,128)(2,1)} %refs_4_.1, bf16[48,64,512]{2,1,0:T(8,128)(2,1)} %refs_5_.1, bf16[48,64,512]{2,1,0:T(8,128)(2,1)} %refs_6_.1), custom_call_target="tpu_custom_call" | custom-call | flops 100663296 | bytes 6291456 | tf_op jit(solution)/shard_map/attend/pallas_call | solution.py:208
  4.1 0.0 copy-start
  4.2 14.6 %all_to_all.5.packed = bf16[16,5,4,128]{3,2,1,0:T(4,128)(2,1)S(1)} all-to-all(bf16[16,5,4,128]{3,2,1,0:T(4,128)(2,1)S(1)} %pack.1), channel_id=1, replica_groups=mesh['group'=2,'kvp'=16] {'kvp'}, dimensions={0} | all-to-all | bytes 163840 | tf_op jit(solution)/shard_map/all_to_all | solution.py:248
  18.8 0.3 combine.1.left
  19.0 0.0 copy-done
  19.1 0.7 %project_3.1 = bf16[4,4096]{1,0:T(4,128)(2,1)S(1)} custom-call(bf16[4,512]{1,0:T(4,128)(2,1)S(1)} %combine.1.left, bf16[512,16384]{1,0:T(8,128)(2,1)S(1)} %copy-done), custom_call_target="tpu_custom_call" | custom-call | flops 1024 | bytes 1024 | tf_op jit(solution)/shard_map/project_3/pallas_call | solution.py:265
  19.7 0.7 %project_2.1 = bf16[4,4096]{1,0:T(4,128)(2,1)S(1)} custom-call(bf16[4,512]{1,0:T(4,128)(2,1)S(1)} %combine.1.left, bf16[512,16384]{1,0:T(8,128)(2,1)S(1)} %copy-done), custom_call_target="tpu_custom_call" | custom-call | flops 1024 | bytes 1024 | tf_op jit(solution)/shard_map/project_2/pallas_call | solution.py:265
  20.4 0.0 collective-permute-start
  20.4 0.9 %collective-permute-start.1 = (bf16[4,4096]{1,0:T(4,128)(2,1)S(1)}, bf16[4,4096]{1,0:T(4,128)(2,1)S(1)}, u32[]{:S(2)}, u32[]{:S(2)}) collective-permute-start(bf16[4,4096]{1,0:T(4,128)(2,1)S(1)} %project_3.1), channel_id=1, source_target_pairs={{0,3},{1,2},{2,1},{3,0},{4,7},{5,6},{6,5},{7,4},{8,11},{9,10},{10,... | collective-permute-start | bytes 98312 | tf_op jit(solution)/shard_map/ppermute | solution.py:191
  21.2 0.7 %project_1.1 = bf16[4,4096]{1,0:T(4,128)(2,1)S(1)} custom-call(bf16[4,512]{1,0:T(4,128)(2,1)S(1)} %combine.1.left, bf16[512,16384]{1,0:T(8,128)(2,1)S(1)} %copy-done), custom_call_target="tpu_custom_call" | custom-call | flops 1024 | bytes 1024 | tf_op jit(solution)/shard_map/project_1/pallas_call | solution.py:265
  21.9 1.3 %collective-permute-start.2 = (bf16[4,4096]{1,0:T(4,128)(2,1)S(1)}, bf16[4,4096]{1,0:T(4,128)(2,1)S(1)}, u32[]{:S(2)}, u32[]{:S(2)}) collective-permute-start(bf16[4,4096]{1,0:T(4,128)(2,1)S(1)} %project_1.1), channel_id=1, source_target_pairs={{0,1},{1,0},{2,3},{3,2},{4,5},{5,4},{6,7},{7,6},{8,9},{9,8},{10,11... | collective-permute-start | bytes 98312 | tf_op jit(solution)/shard_map/ppermute | solution.py:191
  23.2 0.7 %project_0.1.refs_3_ = f32[4,4096]{1,0:T(4,128)S(1)} custom-call(bf16[4,512]{1,0:T(4,128)(2,1)S(1)} %combine.1.left, bf16[512,16384]{1,0:T(8,128)(2,1)S(1)} %copy-done), custom_call_target="tpu_custom_call" | custom-call | flops 1024 | bytes 1024 | tf_op jit(solution)/shard_map/project_0/pallas_call | solution.py:265
  23.9 0.5 %collective-permute-done.refs_0_ = bf16[4,4096]{1,0:T(4,128)(2,1)S(1)} collective-permute-done((bf16[4,4096]{1,0:T(4,128)(2,1)S(1)}, bf16[4,4096]{1,0:T(4,128)(2,1)S(1)}, u32[]{:S(2)}, u32[]{:S(2)}) %collective-permute-start) | collective-permute-done | bytes 32800 | tf_op jit(solution)/shard_map/ppermute | solution.py:191
  24.3 0.0 collective-permute-done.1.refs_1_
  24.3 0.0 collective-permute-done.2.refs_2_
  24.4 1.1 %collective-permute-start.5 = (bf16[4,4096]{1,0:T(4,128)(2,1)S(1)}, bf16[4,4096]{1,0:T(4,128)(2,1)S(1)}, u32[]{:S(2)}, u32[]{:S(2)}) collective-permute-start(bf16[4,4096]{1,0:T(4,128)(2,1)S(1)} %add_near.1.refs_0_), channel_id=1, source_target_pairs={{0,12},{1,13},{2,14},{3,15},{4,8},{5,9},{6,10},{7,11},{8,4},{9,5},... | collective-permute-start | bytes 98312 | tf_op jit(solution)/shard_map/ppermute | solution.py:191
  25.5 0.9 %collective-permute-start.4 = (bf16[4,4096]{1,0:T(4,128)(2,1)S(1)}, bf16[4,4096]{1,0:T(4,128)(2,1)S(1)}, u32[]{:S(2)}, u32[]{:S(2)}) collective-permute-start(bf16[4,4096]{1,0:T(4,128)(2,1)S(1)} %add_near.1.refs_0_), channel_id=1, source_target_pairs={{0,8},{1,9},{2,10},{3,11},{4,12},{5,13},{6,14},{7,15},{8,0},{9,1},... | collective-permute-start | bytes 98312 | tf_op jit(solution)/shard_map/ppermute | solution.py:191
  26.3 2.5 %collective-permute-start.3 = (bf16[4,4096]{1,0:T(4,128)(2,1)S(1)}, bf16[4,4096]{1,0:T(4,128)(2,1)S(1)}, u32[]{:S(2)}, u32[]{:S(2)}) collective-permute-start(bf16[4,4096]{1,0:T(4,128)(2,1)S(1)} %add_near.1.refs_0_), channel_id=1, source_target_pairs={{0,4},{1,5},{2,6},{3,7},{4,0},{5,1},{6,2},{7,3},{8,12},{9,13},{10,... | collective-permute-start | bytes 98312 | tf_op jit(solution)/shard_map/ppermute | solution.py:191
  28.8 1.5 %collective-permute-done.5.refs_3_ = bf16[4,4096]{1,0:T(4,128)(2,1)S(1)} collective-permute-done((bf16[4,4096]{1,0:T(4,128)(2,1)S(1)}, bf16[4,4096]{1,0:T(4,128)(2,1)S(1)}, u32[]{:S(2)}, u32[]{:S(2)}) %collective-permute-start.5) | collective-permute-done | bytes 32800 | tf_op jit(solution)/shard_map/ppermute | solution.py:191
  30.3 0.6 %collective-permute-done.4.refs_2_ = bf16[4,4096]{1,0:T(4,128)(2,1)S(1)} collective-permute-done((bf16[4,4096]{1,0:T(4,128)(2,1)S(1)}, bf16[4,4096]{1,0:T(4,128)(2,1)S(1)}, u32[]{:S(2)}, u32[]{:S(2)}) %collective-permute-start.4) | collective-permute-done | bytes 32800 | tf_op jit(solution)/shard_map/ppermute | solution.py:191
  30.9 0.0 collective-permute-done.3.refs_1_
  31.0 1.4 %collective-permute-start.8 = (bf16[4,4096]{1,0:T(4,128)(2,1)S(1)}, bf16[4,4096]{1,0:T(4,128)(2,1)S(1)}, u32[]{:S(2)}, u32[]{:S(2)}) collective-permute-start(bf16[4,4096]{1,0:T(4,128)(2,1)S(1)} %add_far.1.refs_0_), channel_id=1, source_target_pairs={{0,2},{1,3},{2,0},{3,1},{4,6},{5,7},{6,4},{7,5},{8,10},{9,11},{10,... | collective-permute-start | bytes 98312 | tf_op jit(solution)/shard_map/ppermute | solution.py:191
  32.4 0.0 collective-permute-start.7
  32.4 0.8 %collective-permute-start.6 = (bf16[4,4096]{1,0:T(4,128)(2,1)S(1)}, bf16[4,4096]{1,0:T(4,128)(2,1)S(1)}, u32[]{:S(2)}, u32[]{:S(2)}) collective-permute-start(bf16[4,4096]{1,0:T(4,128)(2,1)S(1)} %add_far.1.refs_0_), channel_id=1, source_target_pairs={{0,1},{1,0},{2,3},{3,2},{4,5},{5,4},{6,7},{7,6},{8,9},{9,8},{10,11... | collective-permute-start | bytes 98312 | tf_op jit(solution)/shard_map/ppermute | solution.py:191
  33.2 1.8 %collective-permute-done.8.refs_3_ = bf16[4,4096]{1,0:T(4,128)(2,1)S(1)} collective-permute-done((bf16[4,4096]{1,0:T(4,128)(2,1)S(1)}, bf16[4,4096]{1,0:T(4,128)(2,1)S(1)}, u32[]{:S(2)}, u32[]{:S(2)}) %collective-permute-start.8) | collective-permute-done | bytes 32800 | tf_op jit(solution)/shard_map/ppermute | solution.py:191
  35.0 0.8 %collective-permute-done.7.refs_2_ = bf16[4,4096]{1,0:T(4,128)(2,1)S(1)} collective-permute-done((bf16[4,4096]{1,0:T(4,128)(2,1)S(1)}, bf16[4,4096]{1,0:T(4,128)(2,1)S(1)}, u32[]{:S(2)}, u32[]{:S(2)}) %collective-permute-start.7) | collective-permute-done | bytes 32800 | tf_op jit(solution)/shard_map/ppermute | solution.py:191
  35.7 0.0 collective-permute-done.6.refs_1_
  35.7 0.7 %lay.1 = bf16[4,16384]{1,0:T(4,128)(2,1)} custom-call(bf16[4,4096]{1,0:T(4,128)(2,1)S(1)} %add_far.1.refs_0_, bf16[4,4096]{1,0:T(4,128)(2,1)S(1)} %collective-permute-done.6.refs_1_, bf16[4,4096]{1,0:T(4,128)(2,1)S(1)} %collective-permute-done.7.refs_2_, bf16[4,4096]{1,0:T(4,128)(2,1)S(1)} %collective-permute-done.8.refs_3_), custom_call_target="tpu_custom_call" | custom-call | tf_op jit(solution)/shard_map/lay/pallas_call | solution.py:289
  (3 shorter events, 0.1 us)
Async XLA Ops:
  4.1 14.9 %copy-start = (bf16[512,16384]{1,0:T(8,128)(2,1)S(1)}, bf16[512,16384]{1,0:T(8,128)(2,1)}, u32[]{:S(2)}) copy-start(bf16[512,16384]{1,0:T(8,128)(2,1)} %weight.7) | copy-start | bytes 50331652
  20.4 3.9 %collective-permute-start = (bf16[4,4096]{1,0:T(4,128)(2,1)S(1)}, bf16[4,4096]{1,0:T(4,128)(2,1)S(1)}, u32[]{:S(2)}, u32[]{:S(2)}) collective-permute-start(bf16[4,4096]{1,0:T(4,128)(2,1)S(1)} %project_2.1), channel_id=1, source_target_pairs={{0,2},{1,3},{2,0},{3,1},{4,6},{5,7},{6,4},{7,5},{8,10},{9,11},{10,... | collective-permute-start | bytes 98312 | tf_op jit(solution)/shard_map/ppermute | solution.py:191
  20.4 3.9 %collective-permute-start.1 = (bf16[4,4096]{1,0:T(4,128)(2,1)S(1)}, bf16[4,4096]{1,0:T(4,128)(2,1)S(1)}, u32[]{:S(2)}, u32[]{:S(2)}) collective-permute-start(bf16[4,4096]{1,0:T(4,128)(2,1)S(1)} %project_3.1), channel_id=1, source_target_pairs={{0,3},{1,2},{2,1},{3,0},{4,7},{5,6},{6,5},{7,4},{8,11},{9,10},{10,... | collective-permute-start | bytes 98312 | tf_op jit(solution)/shard_map/ppermute | solution.py:191
  21.9 2.4 %collective-permute-start.2 = (bf16[4,4096]{1,0:T(4,128)(2,1)S(1)}, bf16[4,4096]{1,0:T(4,128)(2,1)S(1)}, u32[]{:S(2)}, u32[]{:S(2)}) collective-permute-start(bf16[4,4096]{1,0:T(4,128)(2,1)S(1)} %project_1.1), channel_id=1, source_target_pairs={{0,1},{1,0},{2,3},{3,2},{4,5},{5,4},{6,7},{7,6},{8,9},{9,8},{10,11... | collective-permute-start | bytes 98312 | tf_op jit(solution)/shard_map/ppermute | solution.py:191
  24.4 5.9 %collective-permute-start.5 = (bf16[4,4096]{1,0:T(4,128)(2,1)S(1)}, bf16[4,4096]{1,0:T(4,128)(2,1)S(1)}, u32[]{:S(2)}, u32[]{:S(2)}) collective-permute-start(bf16[4,4096]{1,0:T(4,128)(2,1)S(1)} %add_near.1.refs_0_), channel_id=1, source_target_pairs={{0,12},{1,13},{2,14},{3,15},{4,8},{5,9},{6,10},{7,11},{8,4},{9,5},... | collective-permute-start | bytes 98312 | tf_op jit(solution)/shard_map/ppermute | solution.py:191
  25.5 5.4 %collective-permute-start.4 = (bf16[4,4096]{1,0:T(4,128)(2,1)S(1)}, bf16[4,4096]{1,0:T(4,128)(2,1)S(1)}, u32[]{:S(2)}, u32[]{:S(2)}) collective-permute-start(bf16[4,4096]{1,0:T(4,128)(2,1)S(1)} %add_near.1.refs_0_), channel_id=1, source_target_pairs={{0,8},{1,9},{2,10},{3,11},{4,12},{5,13},{6,14},{7,15},{8,0},{9,1},... | collective-permute-start | bytes 98312 | tf_op jit(solution)/shard_map/ppermute | solution.py:191
  26.3 4.6 %collective-permute-start.3 = (bf16[4,4096]{1,0:T(4,128)(2,1)S(1)}, bf16[4,4096]{1,0:T(4,128)(2,1)S(1)}, u32[]{:S(2)}, u32[]{:S(2)}) collective-permute-start(bf16[4,4096]{1,0:T(4,128)(2,1)S(1)} %add_near.1.refs_0_), channel_id=1, source_target_pairs={{0,4},{1,5},{2,6},{3,7},{4,0},{5,1},{6,2},{7,3},{8,12},{9,13},{10,... | collective-permute-start | bytes 98312 | tf_op jit(solution)/shard_map/ppermute | solution.py:191
  31.0 4.0 %collective-permute-start.8 = (bf16[4,4096]{1,0:T(4,128)(2,1)S(1)}, bf16[4,4096]{1,0:T(4,128)(2,1)S(1)}, u32[]{:S(2)}, u32[]{:S(2)}) collective-permute-start(bf16[4,4096]{1,0:T(4,128)(2,1)S(1)} %add_far.1.refs_0_), channel_id=1, source_target_pairs={{0,2},{1,3},{2,0},{3,1},{4,6},{5,7},{6,4},{7,5},{8,10},{9,11},{10,... | collective-permute-start | bytes 98312 | tf_op jit(solution)/shard_map/ppermute | solution.py:191
  32.4 3.3 %collective-permute-start.7 = (bf16[4,4096]{1,0:T(4,128)(2,1)S(1)}, bf16[4,4096]{1,0:T(4,128)(2,1)S(1)}, u32[]{:S(2)}, u32[]{:S(2)}) collective-permute-start(bf16[4,4096]{1,0:T(4,128)(2,1)S(1)} %add_far.1.refs_0_), channel_id=1, source_target_pairs={{0,3},{1,2},{2,1},{3,0},{4,7},{5,6},{6,5},{7,4},{8,11},{9,10},{10,... | collective-permute-start | bytes 98312 | tf_op jit(solution)/shard_map/ppermute | solution.py:191
  32.4 3.3 %collective-permute-start.6 = (bf16[4,4096]{1,0:T(4,128)(2,1)S(1)}, bf16[4,4096]{1,0:T(4,128)(2,1)S(1)}, u32[]{:S(2)}, u32[]{:S(2)}) collective-permute-start(bf16[4,4096]{1,0:T(4,128)(2,1)S(1)} %add_far.1.refs_0_), channel_id=1, source_target_pairs={{0,1},{1,0},{2,3},{3,2},{4,5},{5,4},{6,7},{7,6},{8,9},{9,8},{10,11... | collective-permute-start | bytes 98312 | tf_op jit(solution)/shard_map/ppermute | solution.py:191

commit v23 on v19

--- a/solution.py
+++ b/solution.py
@@ -37,6 +37,14 @@
     pieces = sems.shape[1]
     piece = keys.shape[0] // pieces
 
+    large = []
+    for which, source, target in ((0, keys, key_buf), (1, values, value_buf)):
+        large.append([])
+        for i in range(pieces):
+            here = pl.ds(i * piece, piece)
+            large[-1].append(pltpu.make_async_copy(source.at[here], target.at[here], sems.at[which, i]))
+    for copy in large[0]:
+        copy.start()
     small = []
     for i, (source, target) in enumerate(
         (
@@ -50,14 +58,6 @@
     ):
         small.append(pltpu.make_async_copy(source, target, small_sems.at[i]))
         small[-1].start()
-    large = []
-    for which, source, target in ((0, keys, key_buf), (1, values, value_buf)):
-        large.append([])
-        for i in range(pieces):
-            here = pl.ds(i * piece, piece)
-            large[-1].append(pltpu.make_async_copy(source.at[here], target.at[here], sems.at[which, i]))
-    for copy in large[0]:
-        copy.start()
 
     me = lax.axis_index("kvp")
     lane = lax.broadcasted_iota(jnp.int32, (group, HD), 1)
@@ -224,7 +224,7 @@
             pltpu.VMEM((rows, pages * PAGE), jnp.float32),
             pltpu.VMEM((rows, heads, pages * PAGE), jnp.bfloat16),
             pltpu.SemaphoreType.DMA((6,)),
-            pltpu.SemaphoreType.DMA((2, 4)),
+            pltpu.SemaphoreType.DMA((2, 2)),
         ],
         compiler_params=pltpu.CompilerParams(vmem_limit_bytes=ATTEND_VMEM),
         cost_estimate=pl.CostEstimate(

time: 36.3 us -> 36.5 us (level)
  no operation moved by 1% of the time
where the time goes in v23:
time: 36.5 us; the launch traced here: 36.3 us
  blocking collectives  14.6 us (40%)
  starting transfers between devices  8.27 us (23%)
  Pallas kernels  8.13 us (22%)
  waiting for transfers between devices  5.19 us (14%)
    all_to_all x1, blocking collectives, body(): lax.all_to_all(packed, 'kvp', split_axis=0, concat_axis=0, tiled=True)  14.6 us
    ppermute x9, starting transfers between devices, exchange(): lax.ppermute(array, 'kvp', [(i, i ^ partner) for i in range(devices)])  8.27 us
    ppermute x9, waiting for transfers between devices, exchange(): lax.ppermute(array, 'kvp', [(i, i ^ partner) for i in range(devices)])  5.19 us
    pallas_call x1, Pallas kernels, body(): pl.pallas_call(functools.partial(attend_kernel, heads_dev, devices), out_...  4.49 us
    pallas_call x4, Pallas kernels, body(): pl.pallas_call(functools.partial(project_kernel, x), out_shape=jax.ShapeD...  2.63 us
  transfers between devices with their start and end apart: 9, of which 6 were waited for; matrix products, arithmetic and copies ran while one was open for 0% of the time, Pallas kernels for 4%

profile of v23, /device:TPU:0, one launch (start us, length us, event | category | flops | bytes accessed | tf_op | source)
XLA Modules:
  0.0 36.3 jit_solution(7808643618193206756)
XLA Ops:
  0.0 4.5 %attend.1.staged = f32[16,5,4,128]{3,2,1,0:T(4,128)S(1)} custom-call(s32[4,12]{1,0:T(4,128)} %refs_0_.1, s32[4]{0:T(128)} %refs_1_.1, f32[4,48]{1,0:T(4,128)} %bitcast.2, f32[4,48]{1,0:T(4,128)} %bitcast.3, bf16[4,8192]{1,0:T(4,128)(2,1)} %refs_4_.1, bf16[48,64,512]{2,1,0:T(8,128)(2,1)} %refs_5_.1, bf16[48,64,512]{2,1,0:T(8,128)(2,1)} %refs_6_.1), custom_call_target="tpu_custom_call" | custom-call | flops 100663296 | bytes 6291456 | tf_op jit(solution)/shard_map/attend/pallas_call | solution.py:208
  4.5 0.0 copy-start
  4.5 14.6 %all_to_all.5.packed = bf16[16,5,4,128]{3,2,1,0:T(4,128)(2,1)S(1)} all-to-all(bf16[16,5,4,128]{3,2,1,0:T(4,128)(2,1)S(1)} %pack.1), channel_id=1, replica_groups=mesh['group'=2,'kvp'=16] {'kvp'}, dimensions={0} | all-to-all | bytes 163840 | tf_op jit(solution)/shard_map/all_to_all | solution.py:248
  19.1 0.3 combine.1.left
  19.4 0.0 copy-done
  19.4 0.7 %project_2.1 = bf16[4,4096]{1,0:T(4,128)(2,1)S(1)} custom-call(bf16[4,512]{1,0:T(4,128)(2,1)S(1)} %combine.1.left, bf16[512,16384]{1,0:T(8,128)(2,1)S(1)} %copy-done), custom_call_target="tpu_custom_call" | custom-call | flops 1024 | bytes 1024 | tf_op jit(solution)/shard_map/project_2/pallas_call | solution.py:265
  20.1 0.7 %project_3.1 = bf16[4,4096]{1,0:T(4,128)(2,1)S(1)} custom-call(bf16[4,512]{1,0:T(4,128)(2,1)S(1)} %combine.1.left, bf16[512,16384]{1,0:T(8,128)(2,1)S(1)} %copy-done), custom_call_target="tpu_custom_call" | custom-call | flops 1024 | bytes 1024 | tf_op jit(solution)/shard_map/project_3/pallas_call | solution.py:265
  20.7 0.0 collective-permute-start
  20.7 1.1 %collective-permute-start.1 = (bf16[4,4096]{1,0:T(4,128)(2,1)S(1)}, bf16[4,4096]{1,0:T(4,128)(2,1)S(1)}, u32[]{:S(2)}, u32[]{:S(2)}) collective-permute-start(bf16[4,4096]{1,0:T(4,128)(2,1)S(1)} %project_2.1), channel_id=1, source_target_pairs={{0,2},{1,3},{2,0},{3,1},{4,6},{5,7},{6,4},{7,5},{8,10},{9,11},{10,... | collective-permute-start | bytes 98312 | tf_op jit(solution)/shard_map/ppermute | solution.py:191
  21.9 0.7 %project_1.1 = bf16[4,4096]{1,0:T(4,128)(2,1)S(1)} custom-call(bf16[4,512]{1,0:T(4,128)(2,1)S(1)} %combine.1.left, bf16[512,16384]{1,0:T(8,128)(2,1)S(1)} %copy-done), custom_call_target="tpu_custom_call" | custom-call | flops 1024 | bytes 1024 | tf_op jit(solution)/shard_map/project_1/pallas_call | solution.py:265
  22.5 0.8 %collective-permute-start.2 = (bf16[4,4096]{1,0:T(4,128)(2,1)S(1)}, bf16[4,4096]{1,0:T(4,128)(2,1)S(1)}, u32[]{:S(2)}, u32[]{:S(2)}) collective-permute-start(bf16[4,4096]{1,0:T(4,128)(2,1)S(1)} %project_1.1), channel_id=1, source_target_pairs={{0,1},{1,0},{2,3},{3,2},{4,5},{5,4},{6,7},{7,6},{8,9},{9,8},{10,11... | collective-permute-start | bytes 98312 | tf_op jit(solution)/shard_map/ppermute | solution.py:191
  23.3 0.7 %project_0.1.refs_3_ = f32[4,4096]{1,0:T(4,128)S(1)} custom-call(bf16[4,512]{1,0:T(4,128)(2,1)S(1)} %combine.1.left, bf16[512,16384]{1,0:T(8,128)(2,1)S(1)} %copy-done), custom_call_target="tpu_custom_call" | custom-call | flops 1024 | bytes 1024 | tf_op jit(solution)/shard_map/project_0/pallas_call | solution.py:265
  23.9 0.2 collective-permute-done.refs_0_
  24.1 0.7 %collective-permute-done.1.refs_1_ = bf16[4,4096]{1,0:T(4,128)(2,1)S(1)} collective-permute-done((bf16[4,4096]{1,0:T(4,128)(2,1)S(1)}, bf16[4,4096]{1,0:T(4,128)(2,1)S(1)}, u32[]{:S(2)}, u32[]{:S(2)}) %collective-permute-start.1) | collective-permute-done | bytes 32800 | tf_op jit(solution)/shard_map/ppermute | solution.py:191
  24.8 0.0 collective-permute-done.2.refs_2_
  24.9 1.0 %collective-permute-start.5 = (bf16[4,4096]{1,0:T(4,128)(2,1)S(1)}, bf16[4,4096]{1,0:T(4,128)(2,1)S(1)}, u32[]{:S(2)}, u32[]{:S(2)}) collective-permute-start(bf16[4,4096]{1,0:T(4,128)(2,1)S(1)} %add_near.1.refs_0_), channel_id=1, source_target_pairs={{0,12},{1,13},{2,14},{3,15},{4,8},{5,9},{6,10},{7,11},{8,4},{9,5},... | collective-permute-start | bytes 98312 | tf_op jit(solution)/shard_map/ppermute | solution.py:191
  25.9 0.8 %collective-permute-start.4 = (bf16[4,4096]{1,0:T(4,128)(2,1)S(1)}, bf16[4,4096]{1,0:T(4,128)(2,1)S(1)}, u32[]{:S(2)}, u32[]{:S(2)}) collective-permute-start(bf16[4,4096]{1,0:T(4,128)(2,1)S(1)} %add_near.1.refs_0_), channel_id=1, source_target_pairs={{0,8},{1,9},{2,10},{3,11},{4,12},{5,13},{6,14},{7,15},{8,0},{9,1},... | collective-permute-start | bytes 98312 | tf_op jit(solution)/shard_map/ppermute | solution.py:191
  26.7 2.6 %collective-permute-start.3 = (bf16[4,4096]{1,0:T(4,128)(2,1)S(1)}, bf16[4,4096]{1,0:T(4,128)(2,1)S(1)}, u32[]{:S(2)}, u32[]{:S(2)}) collective-permute-start(bf16[4,4096]{1,0:T(4,128)(2,1)S(1)} %add_near.1.refs_0_), channel_id=1, source_target_pairs={{0,4},{1,5},{2,6},{3,7},{4,0},{5,1},{6,2},{7,3},{8,12},{9,13},{10,... | collective-permute-start | bytes 98312 | tf_op jit(solution)/shard_map/ppermute | solution.py:191
  29.3 1.5 %collective-permute-done.5.refs_3_ = bf16[4,4096]{1,0:T(4,128)(2,1)S(1)} collective-permute-done((bf16[4,4096]{1,0:T(4,128)(2,1)S(1)}, bf16[4,4096]{1,0:T(4,128)(2,1)S(1)}, u32[]{:S(2)}, u32[]{:S(2)}) %collective-permute-start.5) | collective-permute-done | bytes 32800 | tf_op jit(solution)/shard_map/ppermute | solution.py:191
  30.8 0.6 %collective-permute-done.4.refs_2_ = bf16[4,4096]{1,0:T(4,128)(2,1)S(1)} collective-permute-done((bf16[4,4096]{1,0:T(4,128)(2,1)S(1)}, bf16[4,4096]{1,0:T(4,128)(2,1)S(1)}, u32[]{:S(2)}, u32[]{:S(2)}) %collective-permute-start.4) | collective-permute-done | bytes 32800 | tf_op jit(solution)/shard_map/ppermute | solution.py:191
  31.4 0.0 collective-permute-done.3.refs_1_
  31.4 0.1 collective-permute-start.8
  31.5 1.3 %collective-permute-start.7 = (bf16[4,4096]{1,0:T(4,128)(2,1)S(1)}, bf16[4,4096]{1,0:T(4,128)(2,1)S(1)}, u32[]{:S(2)}, u32[]{:S(2)}) collective-permute-start(bf16[4,4096]{1,0:T(4,128)(2,1)S(1)} %add_far.1.refs_0_), channel_id=1, source_target_pairs={{0,2},{1,3},{2,0},{3,1},{4,6},{5,7},{6,4},{7,5},{8,10},{9,11},{10,... | collective-permute-start | bytes 98312 | tf_op jit(solution)/shard_map/ppermute | solution.py:191
  32.8 0.6 %collective-permute-start.6 = (bf16[4,4096]{1,0:T(4,128)(2,1)S(1)}, bf16[4,4096]{1,0:T(4,128)(2,1)S(1)}, u32[]{:S(2)}, u32[]{:S(2)}) collective-permute-start(bf16[4,4096]{1,0:T(4,128)(2,1)S(1)} %add_far.1.refs_0_), channel_id=1, source_target_pairs={{0,1},{1,0},{2,3},{3,2},{4,5},{5,4},{6,7},{7,6},{8,9},{9,8},{10,11... | collective-permute-start | bytes 98312 | tf_op jit(solution)/shard_map/ppermute | solution.py:191
  33.4 1.6 %collective-permute-done.8.refs_3_ = bf16[4,4096]{1,0:T(4,128)(2,1)S(1)} collective-permute-done((bf16[4,4096]{1,0:T(4,128)(2,1)S(1)}, bf16[4,4096]{1,0:T(4,128)(2,1)S(1)}, u32[]{:S(2)}, u32[]{:S(2)}) %collective-permute-start.8) | collective-permute-done | bytes 32800 | tf_op jit(solution)/shard_map/ppermute | solution.py:191
  35.0 0.6 %collective-permute-done.7.refs_2_ = bf16[4,4096]{1,0:T(4,128)(2,1)S(1)} collective-permute-done((bf16[4,4096]{1,0:T(4,128)(2,1)S(1)}, bf16[4,4096]{1,0:T(4,128)(2,1)S(1)}, u32[]{:S(2)}, u32[]{:S(2)}) %collective-permute-start.7) | collective-permute-done | bytes 32800 | tf_op jit(solution)/shard_map/ppermute | solution.py:191
  35.6 0.0 collective-permute-done.6.refs_1_
  35.6 0.7 %lay.1 = bf16[4,16384]{1,0:T(4,128)(2,1)} custom-call(bf16[4,4096]{1,0:T(4,128)(2,1)S(1)} %add_far.1.refs_0_, bf16[4,4096]{1,0:T(4,128)(2,1)S(1)} %collective-permute-done.6.refs_1_, bf16[4,4096]{1,0:T(4,128)(2,1)S(1)} %collective-permute-done.7.refs_2_, bf16[4,4096]{1,0:T(4,128)(2,1)S(1)} %collective-permute-done.8.refs_3_), custom_call_target="tpu_custom_call" | custom-call | tf_op jit(solution)/shard_map/lay/pallas_call | solution.py:289
  (3 shorter events, 0.1 us)
Async XLA Ops:
  4.5 14.9 %copy-start = (bf16[512,16384]{1,0:T(8,128)(2,1)S(1)}, bf16[512,16384]{1,0:T(8,128)(2,1)}, u32[]{:S(2)}) copy-start(bf16[512,16384]{1,0:T(8,128)(2,1)} %weight.7) | copy-start | bytes 50331652
  20.7 3.4 %collective-permute-start = (bf16[4,4096]{1,0:T(4,128)(2,1)S(1)}, bf16[4,4096]{1,0:T(4,128)(2,1)S(1)}, u32[]{:S(2)}, u32[]{:S(2)}) collective-permute-start(bf16[4,4096]{1,0:T(4,128)(2,1)S(1)} %project_3.1), channel_id=1, source_target_pairs={{0,3},{1,2},{2,1},{3,0},{4,7},{5,6},{6,5},{7,4},{8,11},{9,10},{10,... | collective-permute-start | bytes 98312 | tf_op jit(solution)/shard_map/ppermute | solution.py:191
  20.7 4.1 %collective-permute-start.1 = (bf16[4,4096]{1,0:T(4,128)(2,1)S(1)}, bf16[4,4096]{1,0:T(4,128)(2,1)S(1)}, u32[]{:S(2)}, u32[]{:S(2)}) collective-permute-start(bf16[4,4096]{1,0:T(4,128)(2,1)S(1)} %project_2.1), channel_id=1, source_target_pairs={{0,2},{1,3},{2,0},{3,1},{4,6},{5,7},{6,4},{7,5},{8,10},{9,11},{10,... | collective-permute-start | bytes 98312 | tf_op jit(solution)/shard_map/ppermute | solution.py:191
  22.5 2.3 %collective-permute-start.2 = (bf16[4,4096]{1,0:T(4,128)(2,1)S(1)}, bf16[4,4096]{1,0:T(4,128)(2,1)S(1)}, u32[]{:S(2)}, u32[]{:S(2)}) collective-permute-start(bf16[4,4096]{1,0:T(4,128)(2,1)S(1)} %project_1.1), channel_id=1, source_target_pairs={{0,1},{1,0},{2,3},{3,2},{4,5},{5,4},{6,7},{7,6},{8,9},{9,8},{10,11... | collective-permute-start | bytes 98312 | tf_op jit(solution)/shard_map/ppermute | solution.py:191
  24.9 5.9 %collective-permute-start.5 = (bf16[4,4096]{1,0:T(4,128)(2,1)S(1)}, bf16[4,4096]{1,0:T(4,128)(2,1)S(1)}, u32[]{:S(2)}, u32[]{:S(2)}) collective-permute-start(bf16[4,4096]{1,0:T(4,128)(2,1)S(1)} %add_near.1.refs_0_), channel_id=1, source_target_pairs={{0,12},{1,13},{2,14},{3,15},{4,8},{5,9},{6,10},{7,11},{8,4},{9,5},... | collective-permute-start | bytes 98312 | tf_op jit(solution)/shard_map/ppermute | solution.py:191
  25.9 5.5 %collective-permute-start.4 = (bf16[4,4096]{1,0:T(4,128)(2,1)S(1)}, bf16[4,4096]{1,0:T(4,128)(2,1)S(1)}, u32[]{:S(2)}, u32[]{:S(2)}) collective-permute-start(bf16[4,4096]{1,0:T(4,128)(2,1)S(1)} %add_near.1.refs_0_), channel_id=1, source_target_pairs={{0,8},{1,9},{2,10},{3,11},{4,12},{5,13},{6,14},{7,15},{8,0},{9,1},... | collective-permute-start | bytes 98312 | tf_op jit(solution)/shard_map/ppermute | solution.py:191
  26.7 4.7 %collective-permute-start.3 = (bf16[4,4096]{1,0:T(4,128)(2,1)S(1)}, bf16[4,4096]{1,0:T(4,128)(2,1)S(1)}, u32[]{:S(2)}, u32[]{:S(2)}) collective-permute-start(bf16[4,4096]{1,0:T(4,128)(2,1)S(1)} %add_near.1.refs_0_), channel_id=1, source_target_pairs={{0,4},{1,5},{2,6},{3,7},{4,0},{5,1},{6,2},{7,3},{8,12},{9,13},{10,... | collective-permute-start | bytes 98312 | tf_op jit(solution)/shard_map/ppermute | solution.py:191
  31.4 3.5 %collective-permute-start.8 = (bf16[4,4096]{1,0:T(4,128)(2,1)S(1)}, bf16[4,4096]{1,0:T(4,128)(2,1)S(1)}, u32[]{:S(2)}, u32[]{:S(2)}) collective-permute-start(bf16[4,4096]{1,0:T(4,128)(2,1)S(1)} %add_far.1.refs_0_), channel_id=1, source_target_pairs={{0,3},{1,2},{2,1},{3,0},{4,7},{5,6},{6,5},{7,4},{8,11},{9,10},{10,... | collective-permute-start | bytes 98312 | tf_op jit(solution)/shard_map/ppermute | solution.py:191
  31.5 4.1 %collective-permute-start.7 = (bf16[4,4096]{1,0:T(4,128)(2,1)S(1)}, bf16[4,4096]{1,0:T(4,128)(2,1)S(1)}, u32[]{:S(2)}, u32[]{:S(2)}) collective-permute-start(bf16[4,4096]{1,0:T(4,128)(2,1)S(1)} %add_far.1.refs_0_), channel_id=1, source_target_pairs={{0,2},{1,3},{2,0},{3,1},{4,6},{5,7},{6,4},{7,5},{8,10},{9,11},{10,... | collective-permute-start | bytes 98312 | tf_op jit(solution)/shard_map/ppermute | solution.py:191
  32.8 2.8 %collective-permute-start.6 = (bf16[4,4096]{1,0:T(4,128)(2,1)S(1)}, bf16[4,4096]{1,0:T(4,128)(2,1)S(1)}, u32[]{:S(2)}, u32[]{:S(2)}) collective-permute-start(bf16[4,4096]{1,0:T(4,128)(2,1)S(1)} %add_far.1.refs_0_), channel_id=1, source_target_pairs={{0,1},{1,0},{2,3},{3,2},{4,5},{5,4},{6,7},{7,6},{8,9},{9,8},{10,11... | collective-permute-start | bytes 98312 | tf_op jit(solution)/shard_map/ppermute | solution.py:191

commit v24 on v19

--- a/solution.py
+++ b/solution.py
@@ -66,10 +66,11 @@
     spread = (page_of == lax.broadcasted_iota(jnp.int32, (pages, context), 0)).astype(jnp.float32).astype(jnp.bfloat16)
     slot = lax.broadcasted_iota(jnp.int32, (keys.shape[0], context), 0).astype(jnp.float32)
     zeros = jnp.zeros((group, HD), jnp.bfloat16)
-    for copy in small:
-        copy.wait()
+    small[0].wait()
     for copy in large[1]:
         copy.start()
+    for copy in small[1:]:
+        copy.wait()
 
     scales = jnp.concatenate([key_scale[...] * (math.log2(math.e) / math.sqrt(HD)), value_scale[...]], axis=0)
     high, low = split_two(scales)
@@ -224,7 +225,7 @@
             pltpu.VMEM((rows, pages * PAGE), jnp.float32),
             pltpu.VMEM((rows, heads, pages * PAGE), jnp.bfloat16),
             pltpu.SemaphoreType.DMA((6,)),
-            pltpu.SemaphoreType.DMA((2, 4)),
+            pltpu.SemaphoreType.DMA((2, 2)),
         ],
         compiler_params=pltpu.CompilerParams(vmem_limit_bytes=ATTEND_VMEM),
         cost_estimate=pl.CostEstimate(

time: 36.3 us -> 35.9 us (0.989)
  no operation moved by 1% of the time
where the time goes in v24:
time: 35.9 us; the launch traced here: 35.7 us
  blocking collectives  14.6 us (41%)
  starting transfers between devices  8.27 us (23%)
  Pallas kernels  7.59 us (21%)
  waiting for transfers between devices  5.19 us (14%)
    all_to_all x1, blocking collectives, body(): lax.all_to_all(packed, 'kvp', split_axis=0, concat_axis=0, tiled=True)  14.6 us
    ppermute x9, starting transfers between devices, exchange(): lax.ppermute(array, 'kvp', [(i, i ^ partner) for i in range(devices)])  8.27 us
    ppermute x9, waiting for transfers between devices, exchange(): lax.ppermute(array, 'kvp', [(i, i ^ partner) for i in range(devices)])  5.19 us
    pallas_call x1, Pallas kernels, body(): pl.pallas_call(functools.partial(attend_kernel, heads_dev, devices), out_...  3.95 us
    pallas_call x4, Pallas kernels, body(): pl.pallas_call(functools.partial(project_kernel, x), out_shape=jax.ShapeD...  2.63 us
  transfers between devices with their start and end apart: 9, of which 6 were waited for; matrix products, arithmetic and copies ran while one was open for 0% of the time, Pallas kernels for 4%

profile of v24, /device:TPU:0, one launch (start us, length us, event | category | flops | bytes accessed | tf_op | source)
XLA Modules:
  0.0 35.7 jit_solution(1164869317268531643)
XLA Ops:
  0.0 3.9 %attend.1.staged = f32[16,5,4,128]{3,2,1,0:T(4,128)S(1)} custom-call(s32[4,12]{1,0:T(4,128)} %refs_0_.1, s32[4]{0:T(128)} %refs_1_.1, f32[4,48]{1,0:T(4,128)} %bitcast.2, f32[4,48]{1,0:T(4,128)} %bitcast.3, bf16[4,8192]{1,0:T(4,128)(2,1)} %refs_4_.1, bf16[48,64,512]{2,1,0:T(8,128)(2,1)} %refs_5_.1, bf16[48,64,512]{2,1,0:T(8,128)(2,1)} %refs_6_.1), custom_call_target="tpu_custom_call" | custom-call | flops 100663296 | bytes 6291456 | tf_op jit(solution)/shard_map/attend/pallas_call | solution.py:209
  4.0 0.0 copy-start
  4.0 14.6 %all_to_all.5.packed = bf16[16,5,4,128]{3,2,1,0:T(4,128)(2,1)S(1)} all-to-all(bf16[16,5,4,128]{3,2,1,0:T(4,128)(2,1)S(1)} %pack.1), channel_id=1, replica_groups=mesh['group'=2,'kvp'=16] {'kvp'}, dimensions={0} | all-to-all | bytes 163840 | tf_op jit(solution)/shard_map/all_to_all | solution.py:249
  18.6 0.3 combine.1.left
  18.9 0.0 copy-done
  18.9 0.7 %project_2.1 = bf16[4,4096]{1,0:T(4,128)(2,1)S(1)} custom-call(bf16[4,512]{1,0:T(4,128)(2,1)S(1)} %combine.1.left, bf16[512,16384]{1,0:T(8,128)(2,1)S(1)} %copy-done), custom_call_target="tpu_custom_call" | custom-call | flops 1024 | bytes 1024 | tf_op jit(solution)/shard_map/project_2/pallas_call | solution.py:266
  19.5 0.7 %project_3.1 = bf16[4,4096]{1,0:T(4,128)(2,1)S(1)} custom-call(bf16[4,512]{1,0:T(4,128)(2,1)S(1)} %combine.1.left, bf16[512,16384]{1,0:T(8,128)(2,1)S(1)} %copy-done), custom_call_target="tpu_custom_call" | custom-call | flops 1024 | bytes 1024 | tf_op jit(solution)/shard_map/project_3/pallas_call | solution.py:266
  20.2 0.0 collective-permute-start
  20.2 1.1 %collective-permute-start.1 = (bf16[4,4096]{1,0:T(4,128)(2,1)S(1)}, bf16[4,4096]{1,0:T(4,128)(2,1)S(1)}, u32[]{:S(2)}, u32[]{:S(2)}) collective-permute-start(bf16[4,4096]{1,0:T(4,128)(2,1)S(1)} %project_2.1), channel_id=1, source_target_pairs={{0,2},{1,3},{2,0},{3,1},{4,6},{5,7},{6,4},{7,5},{8,10},{9,11},{10,... | collective-permute-start | bytes 98312 | tf_op jit(solution)/shard_map/ppermute | solution.py:192
  21.3 0.7 %project_1.1 = bf16[4,4096]{1,0:T(4,128)(2,1)S(1)} custom-call(bf16[4,512]{1,0:T(4,128)(2,1)S(1)} %combine.1.left, bf16[512,16384]{1,0:T(8,128)(2,1)S(1)} %copy-done), custom_call_target="tpu_custom_call" | custom-call | flops 1024 | bytes 1024 | tf_op jit(solution)/shard_map/project_1/pallas_call | solution.py:266
  22.0 0.8 %collective-permute-start.2 = (bf16[4,4096]{1,0:T(4,128)(2,1)S(1)}, bf16[4,4096]{1,0:T(4,128)(2,1)S(1)}, u32[]{:S(2)}, u32[]{:S(2)}) collective-permute-start(bf16[4,4096]{1,0:T(4,128)(2,1)S(1)} %project_1.1), channel_id=1, source_target_pairs={{0,1},{1,0},{2,3},{3,2},{4,5},{5,4},{6,7},{7,6},{8,9},{9,8},{10,11... | collective-permute-start | bytes 98312 | tf_op jit(solution)/shard_map/ppermute | solution.py:192
  22.7 0.7 %project_0.1.refs_3_ = f32[4,4096]{1,0:T(4,128)S(1)} custom-call(bf16[4,512]{1,0:T(4,128)(2,1)S(1)} %combine.1.left, bf16[512,16384]{1,0:T(8,128)(2,1)S(1)} %copy-done), custom_call_target="tpu_custom_call" | custom-call | flops 1024 | bytes 1024 | tf_op jit(solution)/shard_map/project_0/pallas_call | solution.py:266
  23.4 0.2 collective-permute-done.refs_0_
  23.6 0.7 %collective-permute-done.1.refs_1_ = bf16[4,4096]{1,0:T(4,128)(2,1)S(1)} collective-permute-done((bf16[4,4096]{1,0:T(4,128)(2,1)S(1)}, bf16[4,4096]{1,0:T(4,128)(2,1)S(1)}, u32[]{:S(2)}, u32[]{:S(2)}) %collective-permute-start.1) | collective-permute-done | bytes 32800 | tf_op jit(solution)/shard_map/ppermute | solution.py:192
  24.3 0.0 collective-permute-done.2.refs_2_
  24.3 1.0 %collective-permute-start.5 = (bf16[4,4096]{1,0:T(4,128)(2,1)S(1)}, bf16[4,4096]{1,0:T(4,128)(2,1)S(1)}, u32[]{:S(2)}, u32[]{:S(2)}) collective-permute-start(bf16[4,4096]{1,0:T(4,128)(2,1)S(1)} %add_near.1.refs_0_), channel_id=1, source_target_pairs={{0,12},{1,13},{2,14},{3,15},{4,8},{5,9},{6,10},{7,11},{8,4},{9,5},... | collective-permute-start | bytes 98312 | tf_op jit(solution)/shard_map/ppermute | solution.py:192
  25.3 0.8 %collective-permute-start.4 = (bf16[4,4096]{1,0:T(4,128)(2,1)S(1)}, bf16[4,4096]{1,0:T(4,128)(2,1)S(1)}, u32[]{:S(2)}, u32[]{:S(2)}) collective-permute-start(bf16[4,4096]{1,0:T(4,128)(2,1)S(1)} %add_near.1.refs_0_), channel_id=1, source_target_pairs={{0,8},{1,9},{2,10},{3,11},{4,12},{5,13},{6,14},{7,15},{8,0},{9,1},... | collective-permute-start | bytes 98312 | tf_op jit(solution)/shard_map/ppermute | solution.py:192
  26.2 2.6 %collective-permute-start.3 = (bf16[4,4096]{1,0:T(4,128)(2,1)S(1)}, bf16[4,4096]{1,0:T(4,128)(2,1)S(1)}, u32[]{:S(2)}, u32[]{:S(2)}) collective-permute-start(bf16[4,4096]{1,0:T(4,128)(2,1)S(1)} %add_near.1.refs_0_), channel_id=1, source_target_pairs={{0,4},{1,5},{2,6},{3,7},{4,0},{5,1},{6,2},{7,3},{8,12},{9,13},{10,... | collective-permute-start | bytes 98312 | tf_op jit(solution)/shard_map/ppermute | solution.py:192
  28.8 1.5 %collective-permute-done.5.refs_3_ = bf16[4,4096]{1,0:T(4,128)(2,1)S(1)} collective-permute-done((bf16[4,4096]{1,0:T(4,128)(2,1)S(1)}, bf16[4,4096]{1,0:T(4,128)(2,1)S(1)}, u32[]{:S(2)}, u32[]{:S(2)}) %collective-permute-start.5) | collective-permute-done | bytes 32800 | tf_op jit(solution)/shard_map/ppermute | solution.py:192
  30.3 0.6 %collective-permute-done.4.refs_2_ = bf16[4,4096]{1,0:T(4,128)(2,1)S(1)} collective-permute-done((bf16[4,4096]{1,0:T(4,128)(2,1)S(1)}, bf16[4,4096]{1,0:T(4,128)(2,1)S(1)}, u32[]{:S(2)}, u32[]{:S(2)}) %collective-permute-start.4) | collective-permute-done | bytes 32800 | tf_op jit(solution)/shard_map/ppermute | solution.py:192
  30.9 0.0 collective-permute-done.3.refs_1_
  30.9 0.1 collective-permute-start.8
  31.0 1.3 %collective-permute-start.7 = (bf16[4,4096]{1,0:T(4,128)(2,1)S(1)}, bf16[4,4096]{1,0:T(4,128)(2,1)S(1)}, u32[]{:S(2)}, u32[]{:S(2)}) collective-permute-start(bf16[4,4096]{1,0:T(4,128)(2,1)S(1)} %add_far.1.refs_0_), channel_id=1, source_target_pairs={{0,2},{1,3},{2,0},{3,1},{4,6},{5,7},{6,4},{7,5},{8,10},{9,11},{10,... | collective-permute-start | bytes 98312 | tf_op jit(solution)/shard_map/ppermute | solution.py:192
  32.3 0.6 %collective-permute-start.6 = (bf16[4,4096]{1,0:T(4,128)(2,1)S(1)}, bf16[4,4096]{1,0:T(4,128)(2,1)S(1)}, u32[]{:S(2)}, u32[]{:S(2)}) collective-permute-start(bf16[4,4096]{1,0:T(4,128)(2,1)S(1)} %add_far.1.refs_0_), channel_id=1, source_target_pairs={{0,1},{1,0},{2,3},{3,2},{4,5},{5,4},{6,7},{7,6},{8,9},{9,8},{10,11... | collective-permute-start | bytes 98312 | tf_op jit(solution)/shard_map/ppermute | solution.py:192
  32.8 1.6 %collective-permute-done.8.refs_3_ = bf16[4,4096]{1,0:T(4,128)(2,1)S(1)} collective-permute-done((bf16[4,4096]{1,0:T(4,128)(2,1)S(1)}, bf16[4,4096]{1,0:T(4,128)(2,1)S(1)}, u32[]{:S(2)}, u32[]{:S(2)}) %collective-permute-start.8) | collective-permute-done | bytes 32800 | tf_op jit(solution)/shard_map/ppermute | solution.py:192
  34.4 0.6 %collective-permute-done.7.refs_2_ = bf16[4,4096]{1,0:T(4,128)(2,1)S(1)} collective-permute-done((bf16[4,4096]{1,0:T(4,128)(2,1)S(1)}, bf16[4,4096]{1,0:T(4,128)(2,1)S(1)}, u32[]{:S(2)}, u32[]{:S(2)}) %collective-permute-start.7) | collective-permute-done | bytes 32800 | tf_op jit(solution)/shard_map/ppermute | solution.py:192
  35.0 0.0 collective-permute-done.6.refs_1_
  35.0 0.7 %lay.1 = bf16[4,16384]{1,0:T(4,128)(2,1)} custom-call(bf16[4,4096]{1,0:T(4,128)(2,1)S(1)} %add_far.1.refs_0_, bf16[4,4096]{1,0:T(4,128)(2,1)S(1)} %collective-permute-done.6.refs_1_, bf16[4,4096]{1,0:T(4,128)(2,1)S(1)} %collective-permute-done.7.refs_2_, bf16[4,4096]{1,0:T(4,128)(2,1)S(1)} %collective-permute-done.8.refs_3_), custom_call_target="tpu_custom_call" | custom-call | tf_op jit(solution)/shard_map/lay/pallas_call | solution.py:290
  (3 shorter events, 0.1 us)
Async XLA Ops:
  4.0 14.9 %copy-start = (bf16[512,16384]{1,0:T(8,128)(2,1)S(1)}, bf16[512,16384]{1,0:T(8,128)(2,1)}, u32[]{:S(2)}) copy-start(bf16[512,16384]{1,0:T(8,128)(2,1)} %weight.7) | copy-start | bytes 50331652
  20.2 3.4 %collective-permute-start = (bf16[4,4096]{1,0:T(4,128)(2,1)S(1)}, bf16[4,4096]{1,0:T(4,128)(2,1)S(1)}, u32[]{:S(2)}, u32[]{:S(2)}) collective-permute-start(bf16[4,4096]{1,0:T(4,128)(2,1)S(1)} %project_3.1), channel_id=1, source_target_pairs={{0,3},{1,2},{2,1},{3,0},{4,7},{5,6},{6,5},{7,4},{8,11},{9,10},{10,... | collective-permute-start | bytes 98312 | tf_op jit(solution)/shard_map/ppermute | solution.py:192
  20.2 4.1 %collective-permute-start.1 = (bf16[4,4096]{1,0:T(4,128)(2,1)S(1)}, bf16[4,4096]{1,0:T(4,128)(2,1)S(1)}, u32[]{:S(2)}, u32[]{:S(2)}) collective-permute-start(bf16[4,4096]{1,0:T(4,128)(2,1)S(1)} %project_2.1), channel_id=1, source_target_pairs={{0,2},{1,3},{2,0},{3,1},{4,6},{5,7},{6,4},{7,5},{8,10},{9,11},{10,... | collective-permute-start | bytes 98312 | tf_op jit(solution)/shard_map/ppermute | solution.py:192
  22.0 2.3 %collective-permute-start.2 = (bf16[4,4096]{1,0:T(4,128)(2,1)S(1)}, bf16[4,4096]{1,0:T(4,128)(2,1)S(1)}, u32[]{:S(2)}, u32[]{:S(2)}) collective-permute-start(bf16[4,4096]{1,0:T(4,128)(2,1)S(1)} %project_1.1), channel_id=1, source_target_pairs={{0,1},{1,0},{2,3},{3,2},{4,5},{5,4},{6,7},{7,6},{8,9},{9,8},{10,11... | collective-permute-start | bytes 98312 | tf_op jit(solution)/shard_map/ppermute | solution.py:192
  24.3 5.9 %collective-permute-start.5 = (bf16[4,4096]{1,0:T(4,128)(2,1)S(1)}, bf16[4,4096]{1,0:T(4,128)(2,1)S(1)}, u32[]{:S(2)}, u32[]{:S(2)}) collective-permute-start(bf16[4,4096]{1,0:T(4,128)(2,1)S(1)} %add_near.1.refs_0_), channel_id=1, source_target_pairs={{0,12},{1,13},{2,14},{3,15},{4,8},{5,9},{6,10},{7,11},{8,4},{9,5},... | collective-permute-start | bytes 98312 | tf_op jit(solution)/shard_map/ppermute | solution.py:192
  25.3 5.5 %collective-permute-start.4 = (bf16[4,4096]{1,0:T(4,128)(2,1)S(1)}, bf16[4,4096]{1,0:T(4,128)(2,1)S(1)}, u32[]{:S(2)}, u32[]{:S(2)}) collective-permute-start(bf16[4,4096]{1,0:T(4,128)(2,1)S(1)} %add_near.1.refs_0_), channel_id=1, source_target_pairs={{0,8},{1,9},{2,10},{3,11},{4,12},{5,13},{6,14},{7,15},{8,0},{9,1},... | collective-permute-start | bytes 98312 | tf_op jit(solution)/shard_map/ppermute | solution.py:192
  26.2 4.7 %collective-permute-start.3 = (bf16[4,4096]{1,0:T(4,128)(2,1)S(1)}, bf16[4,4096]{1,0:T(4,128)(2,1)S(1)}, u32[]{:S(2)}, u32[]{:S(2)}) collective-permute-start(bf16[4,4096]{1,0:T(4,128)(2,1)S(1)} %add_near.1.refs_0_), channel_id=1, source_target_pairs={{0,4},{1,5},{2,6},{3,7},{4,0},{5,1},{6,2},{7,3},{8,12},{9,13},{10,... | collective-permute-start | bytes 98312 | tf_op jit(solution)/shard_map/ppermute | solution.py:192
  30.9 3.5 %collective-permute-start.8 = (bf16[4,4096]{1,0:T(4,128)(2,1)S(1)}, bf16[4,4096]{1,0:T(4,128)(2,1)S(1)}, u32[]{:S(2)}, u32[]{:S(2)}) collective-permute-start(bf16[4,4096]{1,0:T(4,128)(2,1)S(1)} %add_far.1.refs_0_), channel_id=1, source_target_pairs={{0,3},{1,2},{2,1},{3,0},{4,7},{5,6},{6,5},{7,4},{8,11},{9,10},{10,... | collective-permute-start | bytes 98312 | tf_op jit(solution)/shard_map/ppermute | solution.py:192
  31.0 4.1 %collective-permute-start.7 = (bf16[4,4096]{1,0:T(4,128)(2,1)S(1)}, bf16[4,4096]{1,0:T(4,128)(2,1)S(1)}, u32[]{:S(2)}, u32[]{:S(2)}) collective-permute-start(bf16[4,4096]{1,0:T(4,128)(2,1)S(1)} %add_far.1.refs_0_), channel_id=1, source_target_pairs={{0,2},{1,3},{2,0},{3,1},{4,6},{5,7},{6,4},{7,5},{8,10},{9,11},{10,... | collective-permute-start | bytes 98312 | tf_op jit(solution)/shard_map/ppermute | solution.py:192
  32.3 2.8 %collective-permute-start.6 = (bf16[4,4096]{1,0:T(4,128)(2,1)S(1)}, bf16[4,4096]{1,0:T(4,128)(2,1)S(1)}, u32[]{:S(2)}, u32[]{:S(2)}) collective-permute-start(bf16[4,4096]{1,0:T(4,128)(2,1)S(1)} %add_far.1.refs_0_), channel_id=1, source_target_pairs={{0,1},{1,0},{2,3},{3,2},{4,5},{5,4},{6,7},{7,6},{8,9},{9,8},{10,11... | collective-permute-start | bytes 98312 | tf_op jit(solution)/shard_map/ppermute | solution.py:192

commit v25 on v24

--- a/solution.py
+++ b/solution.py
@@ -13,6 +13,7 @@
 ATTEND_VMEM = 60 * 1024 * 1024
 HIDDEN = -1e30
 LOWEST = -1e20
+ORDER_FLOPS = 5_000_000_000
 EXCHANGE_FLOPS = 40_000_000_000
 SMALL_VMEM = 8 * 1024 * 1024
 VMEM = pl.BlockSpec(memory_space=pltpu.VMEM)
@@ -225,7 +226,7 @@
             pltpu.VMEM((rows, pages * PAGE), jnp.float32),
             pltpu.VMEM((rows, heads, pages * PAGE), jnp.bfloat16),
             pltpu.SemaphoreType.DMA((6,)),
-            pltpu.SemaphoreType.DMA((2, 2)),
+            pltpu.SemaphoreType.DMA((2, 1)),
         ],
         compiler_params=pltpu.CompilerParams(vmem_limit_bytes=ATTEND_VMEM),
         cost_estimate=pl.CostEstimate(
@@ -262,7 +263,7 @@
         name="combine",
     )(received)
     arrived = []
-    for x in reversed(range(inner)):
+    for x in (2, 3, 1, 0):
         terms = pl.pallas_call(
             functools.partial(project_kernel, x),
             out_shape=jax.ShapeDtypeStruct((rows, part), jnp.bfloat16 if x else jnp.float32),
@@ -274,17 +275,20 @@
         )(left, resident)
         arrived.append(exchange(terms, x, devices) if x else terms)
 
-    def add(terms, name):
+    def add(terms, name, kind=jnp.bfloat16, flops=1024):
         return pl.pallas_call(
             add_kernel,
-            out_shape=jax.ShapeDtypeStruct((rows, part), jnp.bfloat16),
+            out_shape=jax.ShapeDtypeStruct((rows, part), kind),
             in_specs=[VMEM] * len(terms),
             out_specs=VMEM,
             compiler_params=pltpu.CompilerParams(vmem_limit_bytes=SMALL_VMEM),
+            cost_estimate=pl.CostEstimate(flops=flops, bytes_accessed=1024, transcendentals=0),
             name=name,
         )(*terms)
 
-    mine = add(arrived, "add_near")
+    mine = add([arrived[3], arrived[0]], "add_across", jnp.float32, ORDER_FLOPS)
+    mine = add([mine, arrived[1]], "add_other", jnp.float32, ORDER_FLOPS)
+    mine = add([mine, arrived[2]], "add_near")
     mine = add([mine] + [exchange(mine, x * inner, devices) for x in range(1, outer)], "add_far")
     parts = [mine] + [exchange(mine, x, devices) for x in range(1, inner)]
     return pl.pallas_call(

time: 35.9 us -> 37 us (1.031)
  waiting for transfers between devices: 5.19 us -> 5.91 us
    ppermute x9, waiting for transfers between devices: 5.19 us -> 5.91 us  [exchange(): lax.ppermute(array, 'kvp', [(i, i ^ partner) for i in range(devices)])]
  transfers between devices with their start and end apart: 9 -> 9, of which waited for: 6 -> 5; matrix products, arithmetic and copies ran while one was open for 0% -> 0% of each run, Pallas kernels for 4% -> 6%
where the time goes in v25:
time: 37 us; the launch traced here: 36.8 us
  blocking collectives  14.6 us (39%)
  starting transfers between devices  8.56 us (23%)
  Pallas kernels  7.64 us (21%)
  waiting for transfers between devices  5.91 us (16%)
    all_to_all x1, blocking collectives, body(): lax.all_to_all(packed, 'kvp', split_axis=0, concat_axis=0, tiled=True)  14.6 us
    ppermute x9, starting transfers between devices, exchange(): lax.ppermute(array, 'kvp', [(i, i ^ partner) for i in range(devices)])  8.56 us
    ppermute x9, waiting for transfers between devices, exchange(): lax.ppermute(array, 'kvp', [(i, i ^ partner) for i in range(devices)])  5.91 us
    pallas_call x1, Pallas kernels, body(): pl.pallas_call(functools.partial(attend_kernel, heads_dev, devices), out_...  3.96 us
    pallas_call x4, Pallas kernels, body(): pl.pallas_call(functools.partial(project_kernel, x), out_shape=jax.ShapeD...  2.67 us
  transfers between devices with their start and end apart: 9, of which 5 were waited for; matrix products, arithmetic and copies ran while one was open for 0% of the time, Pallas kernels for 6%

profile of v25, /device:TPU:0, one launch (start us, length us, event | category | flops | bytes accessed | tf_op | source)
XLA Modules:
  0.0 36.8 jit_solution(17521422835244833692)
XLA Ops:
  0.0 4.0 %attend.1.staged = f32[16,5,4,128]{3,2,1,0:T(4,128)S(1)} custom-call(s32[4,12]{1,0:T(4,128)} %refs_0_.1, s32[4]{0:T(128)} %refs_1_.1, f32[4,48]{1,0:T(4,128)} %bitcast.2, f32[4,48]{1,0:T(4,128)} %bitcast.3, bf16[4,8192]{1,0:T(4,128)(2,1)} %refs_4_.1, bf16[48,64,512]{2,1,0:T(8,128)(2,1)} %refs_5_.1, bf16[48,64,512]{2,1,0:T(8,128)(2,1)} %refs_6_.1), custom_call_target="tpu_custom_call" | custom-call | flops 100663296 | bytes 6291456 | tf_op jit(solution)/shard_map/attend/pallas_call | solution.py:210
  4.0 0.0 copy-start
  4.0 14.6 %all_to_all.5.packed = bf16[16,5,4,128]{3,2,1,0:T(4,128)(2,1)S(1)} all-to-all(bf16[16,5,4,128]{3,2,1,0:T(4,128)(2,1)S(1)} %pack.1), channel_id=1, replica_groups=mesh['group'=2,'kvp'=16] {'kvp'}, dimensions={0} | all-to-all | bytes 163840 | tf_op jit(solution)/shard_map/all_to_all | solution.py:250
  18.6 0.3 combine.1.left
  18.9 0.0 copy-done
  18.9 0.7 %project_2.1 = bf16[4,4096]{1,0:T(4,128)(2,1)S(1)} custom-call(bf16[4,512]{1,0:T(4,128)(2,1)S(1)} %combine.1.left, bf16[512,16384]{1,0:T(8,128)(2,1)S(1)} %copy-done), custom_call_target="tpu_custom_call" | custom-call | flops 1024 | bytes 1024 | tf_op jit(solution)/shard_map/project_2/pallas_call | solution.py:267
  19.5 0.0 collective-permute-start
  19.5 0.7 %project_1.1 = bf16[4,4096]{1,0:T(4,128)(2,1)S(1)} custom-call(bf16[4,512]{1,0:T(4,128)(2,1)S(1)} %combine.1.left, bf16[512,16384]{1,0:T(8,128)(2,1)S(1)} %copy-done), custom_call_target="tpu_custom_call" | custom-call | flops 1024 | bytes 1024 | tf_op jit(solution)/shard_map/project_1/pallas_call | solution.py:267
  20.2 0.7 %project_3.1 = bf16[4,4096]{1,0:T(4,128)(2,1)S(1)} custom-call(bf16[4,512]{1,0:T(4,128)(2,1)S(1)} %combine.1.left, bf16[512,16384]{1,0:T(8,128)(2,1)S(1)} %copy-done), custom_call_target="tpu_custom_call" | custom-call | flops 1024 | bytes 1024 | tf_op jit(solution)/shard_map/project_3/pallas_call | solution.py:267
  20.9 0.7 %project_0.1.refs_0_ = f32[4,4096]{1,0:T(4,128)S(1)} custom-call(bf16[4,512]{1,0:T(4,128)(2,1)S(1)} %combine.1.left, bf16[512,16384]{1,0:T(8,128)(2,1)S(1)} %copy-done), custom_call_target="tpu_custom_call" | custom-call | flops 1024 | bytes 1024 | tf_op jit(solution)/shard_map/project_0/pallas_call | solution.py:267
  21.5 0.9 %collective-permute-start.1 = (bf16[4,4096]{1,0:T(4,128)(2,1)S(1)}, bf16[4,4096]{1,0:T(4,128)(2,1)S(1)}, u32[]{:S(2)}, u32[]{:S(2)}) collective-permute-start(bf16[4,4096]{1,0:T(4,128)(2,1)S(1)} %project_3.1), channel_id=1, source_target_pairs={{0,3},{1,2},{2,1},{3,0},{4,7},{5,6},{6,5},{7,4},{8,11},{9,10},{10,... | collective-permute-start | bytes 98312 | tf_op jit(solution)/shard_map/ppermute | solution.py:193
  22.4 1.3 %collective-permute-start.2 = (bf16[4,4096]{1,0:T(4,128)(2,1)S(1)}, bf16[4,4096]{1,0:T(4,128)(2,1)S(1)}, u32[]{:S(2)}, u32[]{:S(2)}) collective-permute-start(bf16[4,4096]{1,0:T(4,128)(2,1)S(1)} %project_1.1), channel_id=1, source_target_pairs={{0,1},{1,0},{2,3},{3,2},{4,5},{5,4},{6,7},{7,6},{8,9},{9,8},{10,11... | collective-permute-start | bytes 98312 | tf_op jit(solution)/shard_map/ppermute | solution.py:193
  23.7 0.0 collective-permute-done.refs_1_
  23.7 1.2 %collective-permute-done.1.refs_1_ = bf16[4,4096]{1,0:T(4,128)(2,1)S(1)} collective-permute-done((bf16[4,4096]{1,0:T(4,128)(2,1)S(1)}, bf16[4,4096]{1,0:T(4,128)(2,1)S(1)}, u32[]{:S(2)}, u32[]{:S(2)}) %collective-permute-start.1) | collective-permute-done | bytes 32800 | tf_op jit(solution)/shard_map/ppermute | solution.py:193
  24.9 0.0 collective-permute-done.2.refs_1_
  25.0 1.7 %collective-permute-start.5 = (bf16[4,4096]{1,0:T(4,128)(2,1)S(1)}, bf16[4,4096]{1,0:T(4,128)(2,1)S(1)}, u32[]{:S(2)}, u32[]{:S(2)}) collective-permute-start(bf16[4,4096]{1,0:T(4,128)(2,1)S(1)} %add_near.1.refs_0_), channel_id=1, source_target_pairs={{0,12},{1,13},{2,14},{3,15},{4,8},{5,9},{6,10},{7,11},{8,4},{9,5},... | collective-permute-start | bytes 98312 | tf_op jit(solution)/shard_map/ppermute | solution.py:193
  26.6 0.8 %collective-permute-start.4 = (bf16[4,4096]{1,0:T(4,128)(2,1)S(1)}, bf16[4,4096]{1,0:T(4,128)(2,1)S(1)}, u32[]{:S(2)}, u32[]{:S(2)}) collective-permute-start(bf16[4,4096]{1,0:T(4,128)(2,1)S(1)} %add_near.1.refs_0_), channel_id=1, source_target_pairs={{0,8},{1,9},{2,10},{3,11},{4,12},{5,13},{6,14},{7,15},{8,0},{9,1},... | collective-permute-start | bytes 98312 | tf_op jit(solution)/shard_map/ppermute | solution.py:193
  27.5 2.0 %collective-permute-start.3 = (bf16[4,4096]{1,0:T(4,128)(2,1)S(1)}, bf16[4,4096]{1,0:T(4,128)(2,1)S(1)}, u32[]{:S(2)}, u32[]{:S(2)}) collective-permute-start(bf16[4,4096]{1,0:T(4,128)(2,1)S(1)} %add_near.1.refs_0_), channel_id=1, source_target_pairs={{0,4},{1,5},{2,6},{3,7},{4,0},{5,1},{6,2},{7,3},{8,12},{9,13},{10,... | collective-permute-start | bytes 98312 | tf_op jit(solution)/shard_map/ppermute | solution.py:193
  29.4 1.5 %collective-permute-done.5.refs_3_ = bf16[4,4096]{1,0:T(4,128)(2,1)S(1)} collective-permute-done((bf16[4,4096]{1,0:T(4,128)(2,1)S(1)}, bf16[4,4096]{1,0:T(4,128)(2,1)S(1)}, u32[]{:S(2)}, u32[]{:S(2)}) %collective-permute-start.5) | collective-permute-done | bytes 32800 | tf_op jit(solution)/shard_map/ppermute | solution.py:193
  30.9 1.0 %collective-permute-done.4.refs_2_ = bf16[4,4096]{1,0:T(4,128)(2,1)S(1)} collective-permute-done((bf16[4,4096]{1,0:T(4,128)(2,1)S(1)}, bf16[4,4096]{1,0:T(4,128)(2,1)S(1)}, u32[]{:S(2)}, u32[]{:S(2)}) %collective-permute-start.4) | collective-permute-done | bytes 32800 | tf_op jit(solution)/shard_map/ppermute | solution.py:193
  32.0 0.0 collective-permute-done.3.refs_1_
  32.0 0.1 collective-permute-start.8
  32.1 1.6 %collective-permute-start.7 = (bf16[4,4096]{1,0:T(4,128)(2,1)S(1)}, bf16[4,4096]{1,0:T(4,128)(2,1)S(1)}, u32[]{:S(2)}, u32[]{:S(2)}) collective-permute-start(bf16[4,4096]{1,0:T(4,128)(2,1)S(1)} %add_far.1.refs_0_), channel_id=1, source_target_pairs={{0,2},{1,3},{2,0},{3,1},{4,6},{5,7},{6,4},{7,5},{8,10},{9,11},{10,... | collective-permute-start | bytes 98312 | tf_op jit(solution)/shard_map/ppermute | solution.py:193
  33.7 0.3 collective-permute-start.6
  33.9 1.7 %collective-permute-done.8.refs_3_ = bf16[4,4096]{1,0:T(4,128)(2,1)S(1)} collective-permute-done((bf16[4,4096]{1,0:T(4,128)(2,1)S(1)}, bf16[4,4096]{1,0:T(4,128)(2,1)S(1)}, u32[]{:S(2)}, u32[]{:S(2)}) %collective-permute-start.8) | collective-permute-done | bytes 32800 | tf_op jit(solution)/shard_map/ppermute | solution.py:193
  35.6 0.5 %collective-permute-done.7.refs_2_ = bf16[4,4096]{1,0:T(4,128)(2,1)S(1)} collective-permute-done((bf16[4,4096]{1,0:T(4,128)(2,1)S(1)}, bf16[4,4096]{1,0:T(4,128)(2,1)S(1)}, u32[]{:S(2)}, u32[]{:S(2)}) %collective-permute-start.7) | collective-permute-done | bytes 32800 | tf_op jit(solution)/shard_map/ppermute | solution.py:193
  36.1 0.0 collective-permute-done.6.refs_1_
  36.1 0.7 %lay.1 = bf16[4,16384]{1,0:T(4,128)(2,1)} custom-call(bf16[4,4096]{1,0:T(4,128)(2,1)S(1)} %add_far.1.refs_0_, bf16[4,4096]{1,0:T(4,128)(2,1)S(1)} %collective-permute-done.6.refs_1_, bf16[4,4096]{1,0:T(4,128)(2,1)S(1)} %collective-permute-done.7.refs_2_, bf16[4,4096]{1,0:T(4,128)(2,1)S(1)} %collective-permute-done.8.refs_3_), custom_call_target="tpu_custom_call" | custom-call | tf_op jit(solution)/shard_map/lay/pallas_call | solution.py:294
  (5 shorter events, 0.1 us)
Async XLA Ops:
  4.0 14.9 %copy-start = (bf16[512,16384]{1,0:T(8,128)(2,1)S(1)}, bf16[512,16384]{1,0:T(8,128)(2,1)}, u32[]{:S(2)}) copy-start(bf16[512,16384]{1,0:T(8,128)(2,1)} %weight.7) | copy-start | bytes 50331652
  19.5 4.2 %collective-permute-start = (bf16[4,4096]{1,0:T(4,128)(2,1)S(1)}, bf16[4,4096]{1,0:T(4,128)(2,1)S(1)}, u32[]{:S(2)}, u32[]{:S(2)}) collective-permute-start(bf16[4,4096]{1,0:T(4,128)(2,1)S(1)} %project_2.1), channel_id=1, source_target_pairs={{0,2},{1,3},{2,0},{3,1},{4,6},{5,7},{6,4},{7,5},{8,10},{9,11},{10,... | collective-permute-start | bytes 98312 | tf_op jit(solution)/shard_map/ppermute | solution.py:193
  21.5 3.4 %collective-permute-start.1 = (bf16[4,4096]{1,0:T(4,128)(2,1)S(1)}, bf16[4,4096]{1,0:T(4,128)(2,1)S(1)}, u32[]{:S(2)}, u32[]{:S(2)}) collective-permute-start(bf16[4,4096]{1,0:T(4,128)(2,1)S(1)} %project_3.1), channel_id=1, source_target_pairs={{0,3},{1,2},{2,1},{3,0},{4,7},{5,6},{6,5},{7,4},{8,11},{9,10},{10,... | collective-permute-start | bytes 98312 | tf_op jit(solution)/shard_map/ppermute | solution.py:193
  22.4 2.5 %collective-permute-start.2 = (bf16[4,4096]{1,0:T(4,128)(2,1)S(1)}, bf16[4,4096]{1,0:T(4,128)(2,1)S(1)}, u32[]{:S(2)}, u32[]{:S(2)}) collective-permute-start(bf16[4,4096]{1,0:T(4,128)(2,1)S(1)} %project_1.1), channel_id=1, source_target_pairs={{0,1},{1,0},{2,3},{3,2},{4,5},{5,4},{6,7},{7,6},{8,9},{9,8},{10,11... | collective-permute-start | bytes 98312 | tf_op jit(solution)/shard_map/ppermute | solution.py:193
  25.0 6.0 %collective-permute-start.5 = (bf16[4,4096]{1,0:T(4,128)(2,1)S(1)}, bf16[4,4096]{1,0:T(4,128)(2,1)S(1)}, u32[]{:S(2)}, u32[]{:S(2)}) collective-permute-start(bf16[4,4096]{1,0:T(4,128)(2,1)S(1)} %add_near.1.refs_0_), channel_id=1, source_target_pairs={{0,12},{1,13},{2,14},{3,15},{4,8},{5,9},{6,10},{7,11},{8,4},{9,5},... | collective-permute-start | bytes 98312 | tf_op jit(solution)/shard_map/ppermute | solution.py:193
  26.6 5.3 %collective-permute-start.4 = (bf16[4,4096]{1,0:T(4,128)(2,1)S(1)}, bf16[4,4096]{1,0:T(4,128)(2,1)S(1)}, u32[]{:S(2)}, u32[]{:S(2)}) collective-permute-start(bf16[4,4096]{1,0:T(4,128)(2,1)S(1)} %add_near.1.refs_0_), channel_id=1, source_target_pairs={{0,8},{1,9},{2,10},{3,11},{4,12},{5,13},{6,14},{7,15},{8,0},{9,1},... | collective-permute-start | bytes 98312 | tf_op jit(solution)/shard_map/ppermute | solution.py:193
  27.5 4.5 %collective-permute-start.3 = (bf16[4,4096]{1,0:T(4,128)(2,1)S(1)}, bf16[4,4096]{1,0:T(4,128)(2,1)S(1)}, u32[]{:S(2)}, u32[]{:S(2)}) collective-permute-start(bf16[4,4096]{1,0:T(4,128)(2,1)S(1)} %add_near.1.refs_0_), channel_id=1, source_target_pairs={{0,4},{1,5},{2,6},{3,7},{4,0},{5,1},{6,2},{7,3},{8,12},{9,13},{10,... | collective-permute-start | bytes 98312 | tf_op jit(solution)/shard_map/ppermute | solution.py:193
  32.0 3.6 %collective-permute-start.8 = (bf16[4,4096]{1,0:T(4,128)(2,1)S(1)}, bf16[4,4096]{1,0:T(4,128)(2,1)S(1)}, u32[]{:S(2)}, u32[]{:S(2)}) collective-permute-start(bf16[4,4096]{1,0:T(4,128)(2,1)S(1)} %add_far.1.refs_0_), channel_id=1, source_target_pairs={{0,3},{1,2},{2,1},{3,0},{4,7},{5,6},{6,5},{7,4},{8,11},{9,10},{10,... | collective-permute-start | bytes 98312 | tf_op jit(solution)/shard_map/ppermute | solution.py:193
  32.1 4.0 %collective-permute-start.7 = (bf16[4,4096]{1,0:T(4,128)(2,1)S(1)}, bf16[4,4096]{1,0:T(4,128)(2,1)S(1)}, u32[]{:S(2)}, u32[]{:S(2)}) collective-permute-start(bf16[4,4096]{1,0:T(4,128)(2,1)S(1)} %add_far.1.refs_0_), channel_id=1, source_target_pairs={{0,2},{1,3},{2,0},{3,1},{4,6},{5,7},{6,4},{7,5},{8,10},{9,11},{10,... | collective-permute-start | bytes 98312 | tf_op jit(solution)/shard_map/ppermute | solution.py:193
  33.7 2.5 %collective-permute-start.6 = (bf16[4,4096]{1,0:T(4,128)(2,1)S(1)}, bf16[4,4096]{1,0:T(4,128)(2,1)S(1)}, u32[]{:S(2)}, u32[]{:S(2)}) collective-permute-start(bf16[4,4096]{1,0:T(4,128)(2,1)S(1)} %add_far.1.refs_0_), channel_id=1, source_target_pairs={{0,1},{1,0},{2,3},{3,2},{4,5},{5,4},{6,7},{7,6},{8,9},{9,8},{10,11... | collective-permute-start | bytes 98312 | tf_op jit(solution)/shard_map/ppermute | solution.py:193

commit v26 on v25

--- a/solution.py
+++ b/solution.py
@@ -13,7 +13,7 @@
 ATTEND_VMEM = 60 * 1024 * 1024
 HIDDEN = -1e30
 LOWEST = -1e20
-ORDER_FLOPS = 5_000_000_000
+ORDER_FLOPS = 200_000_000
 EXCHANGE_FLOPS = 40_000_000_000
 SMALL_VMEM = 8 * 1024 * 1024
 VMEM = pl.BlockSpec(memory_space=pltpu.VMEM)

time: 37 us -> 36.4 us (0.984)
  waiting for transfers between devices: 5.91 us -> 5.38 us
    ppermute x9, waiting for transfers between devices: 5.91 us -> 5.38 us  [exchange(): lax.ppermute(array, 'kvp', [(i, i ^ partner) for i in range(devices)])]
  transfers between devices with their start and end apart: 9 -> 9, of which waited for: 5 -> 7; matrix products, arithmetic and copies ran while one was open for 0% -> 0% of each run, Pallas kernels for 6% -> 6%
where the time goes in v26:
time: 36.4 us; the launch traced here: 36.2 us
  blocking collectives  14.6 us (40%)
  starting transfers between devices  8.55 us (23%)
  Pallas kernels  7.62 us (21%)
  waiting for transfers between devices  5.38 us (15%)
    all_to_all x1, blocking collectives, body(): lax.all_to_all(packed, 'kvp', split_axis=0, concat_axis=0, tiled=True)  14.6 us
    ppermute x9, starting transfers between devices, exchange(): lax.ppermute(array, 'kvp', [(i, i ^ partner) for i in range(devices)])  8.55 us
    ppermute x9, waiting for transfers between devices, exchange(): lax.ppermute(array, 'kvp', [(i, i ^ partner) for i in range(devices)])  5.38 us
    pallas_call x1, Pallas kernels, body(): pl.pallas_call(functools.partial(attend_kernel, heads_dev, devices), out_...  3.96 us
    pallas_call x4, Pallas kernels, body(): pl.pallas_call(functools.partial(project_kernel, x), out_shape=jax.ShapeD...  2.65 us
  transfers between devices with their start and end apart: 9, of which 7 were waited for; matrix products, arithmetic and copies ran while one was open for 0% of the time, Pallas kernels for 6%

profile of v26, /device:TPU:0, one launch (start us, length us, event | category | flops | bytes accessed | tf_op | source)
XLA Modules:
  0.0 36.2 jit_solution(11328788284586618458)
XLA Ops:
  0.0 4.0 %attend.1.staged = f32[16,5,4,128]{3,2,1,0:T(4,128)S(1)} custom-call(s32[4,12]{1,0:T(4,128)} %refs_0_.1, s32[4]{0:T(128)} %refs_1_.1, f32[4,48]{1,0:T(4,128)} %bitcast.2, f32[4,48]{1,0:T(4,128)} %bitcast.3, bf16[4,8192]{1,0:T(4,128)(2,1)} %refs_4_.1, bf16[48,64,512]{2,1,0:T(8,128)(2,1)} %refs_5_.1, bf16[48,64,512]{2,1,0:T(8,128)(2,1)} %refs_6_.1), custom_call_target="tpu_custom_call" | custom-call | flops 100663296 | bytes 6291456 | tf_op jit(solution)/shard_map/attend/pallas_call | solution.py:210
  4.0 0.0 copy-start
  4.0 14.6 %all_to_all.5.packed = bf16[16,5,4,128]{3,2,1,0:T(4,128)(2,1)S(1)} all-to-all(bf16[16,5,4,128]{3,2,1,0:T(4,128)(2,1)S(1)} %pack.1), channel_id=1, replica_groups=mesh['group'=2,'kvp'=16] {'kvp'}, dimensions={0} | all-to-all | bytes 163840 | tf_op jit(solution)/shard_map/all_to_all | solution.py:250
  18.6 0.3 combine.1.left
  18.9 0.0 copy-done
  18.9 0.7 %project_2.1 = bf16[4,4096]{1,0:T(4,128)(2,1)S(1)} custom-call(bf16[4,512]{1,0:T(4,128)(2,1)S(1)} %combine.1.left, bf16[512,16384]{1,0:T(8,128)(2,1)S(1)} %copy-done), custom_call_target="tpu_custom_call" | custom-call | flops 1024 | bytes 1024 | tf_op jit(solution)/shard_map/project_2/pallas_call | solution.py:267
  19.5 0.0 collective-permute-start
  19.5 0.7 %project_3.1 = bf16[4,4096]{1,0:T(4,128)(2,1)S(1)} custom-call(bf16[4,512]{1,0:T(4,128)(2,1)S(1)} %combine.1.left, bf16[512,16384]{1,0:T(8,128)(2,1)S(1)} %copy-done), custom_call_target="tpu_custom_call" | custom-call | flops 1024 | bytes 1024 | tf_op jit(solution)/shard_map/project_3/pallas_call | solution.py:267
  20.2 0.9 %collective-permute-start.1 = (bf16[4,4096]{1,0:T(4,128)(2,1)S(1)}, bf16[4,4096]{1,0:T(4,128)(2,1)S(1)}, u32[]{:S(2)}, u32[]{:S(2)}) collective-permute-start(bf16[4,4096]{1,0:T(4,128)(2,1)S(1)} %project_3.1), channel_id=1, source_target_pairs={{0,3},{1,2},{2,1},{3,0},{4,7},{5,6},{6,5},{7,4},{8,11},{9,10},{10,... | collective-permute-start | bytes 98312 | tf_op jit(solution)/shard_map/ppermute | solution.py:193
  21.1 0.7 %project_1.1 = bf16[4,4096]{1,0:T(4,128)(2,1)S(1)} custom-call(bf16[4,512]{1,0:T(4,128)(2,1)S(1)} %combine.1.left, bf16[512,16384]{1,0:T(8,128)(2,1)S(1)} %copy-done), custom_call_target="tpu_custom_call" | custom-call | flops 1024 | bytes 1024 | tf_op jit(solution)/shard_map/project_1/pallas_call | solution.py:267
  21.7 0.7 %project_0.1.refs_0_ = f32[4,4096]{1,0:T(4,128)S(1)} custom-call(bf16[4,512]{1,0:T(4,128)(2,1)S(1)} %combine.1.left, bf16[512,16384]{1,0:T(8,128)(2,1)S(1)} %copy-done), custom_call_target="tpu_custom_call" | custom-call | flops 1024 | bytes 1024 | tf_op jit(solution)/shard_map/project_0/pallas_call | solution.py:267
  22.4 1.3 %collective-permute-start.2 = (bf16[4,4096]{1,0:T(4,128)(2,1)S(1)}, bf16[4,4096]{1,0:T(4,128)(2,1)S(1)}, u32[]{:S(2)}, u32[]{:S(2)}) collective-permute-start(bf16[4,4096]{1,0:T(4,128)(2,1)S(1)} %project_1.1), channel_id=1, source_target_pairs={{0,1},{1,0},{2,3},{3,2},{4,5},{5,4},{6,7},{7,6},{8,9},{9,8},{10,11... | collective-permute-start | bytes 98312 | tf_op jit(solution)/shard_map/ppermute | solution.py:193
  23.7 0.0 collective-permute-done.refs_1_
  23.7 0.1 collective-permute-done.1.refs_1_
  23.9 0.7 %collective-permute-done.2.refs_1_ = bf16[4,4096]{1,0:T(4,128)(2,1)S(1)} collective-permute-done((bf16[4,4096]{1,0:T(4,128)(2,1)S(1)}, bf16[4,4096]{1,0:T(4,128)(2,1)S(1)}, u32[]{:S(2)}, u32[]{:S(2)}) %collective-permute-start.2) | collective-permute-done | bytes 32800 | tf_op jit(solution)/shard_map/ppermute | solution.py:193
  24.6 0.7 %collective-permute-start.5 = (bf16[4,4096]{1,0:T(4,128)(2,1)S(1)}, bf16[4,4096]{1,0:T(4,128)(2,1)S(1)}, u32[]{:S(2)}, u32[]{:S(2)}) collective-permute-start(bf16[4,4096]{1,0:T(4,128)(2,1)S(1)} %add_near.1.refs_0_), channel_id=1, source_target_pairs={{0,12},{1,13},{2,14},{3,15},{4,8},{5,9},{6,10},{7,11},{8,4},{9,5},... | collective-permute-start | bytes 98312 | tf_op jit(solution)/shard_map/ppermute | solution.py:193
  25.3 0.8 %collective-permute-start.4 = (bf16[4,4096]{1,0:T(4,128)(2,1)S(1)}, bf16[4,4096]{1,0:T(4,128)(2,1)S(1)}, u32[]{:S(2)}, u32[]{:S(2)}) collective-permute-start(bf16[4,4096]{1,0:T(4,128)(2,1)S(1)} %add_near.1.refs_0_), channel_id=1, source_target_pairs={{0,8},{1,9},{2,10},{3,11},{4,12},{5,13},{6,14},{7,15},{8,0},{9,1},... | collective-permute-start | bytes 98312 | tf_op jit(solution)/shard_map/ppermute | solution.py:193
  26.1 2.9 %collective-permute-start.3 = (bf16[4,4096]{1,0:T(4,128)(2,1)S(1)}, bf16[4,4096]{1,0:T(4,128)(2,1)S(1)}, u32[]{:S(2)}, u32[]{:S(2)}) collective-permute-start(bf16[4,4096]{1,0:T(4,128)(2,1)S(1)} %add_near.1.refs_0_), channel_id=1, source_target_pairs={{0,4},{1,5},{2,6},{3,7},{4,0},{5,1},{6,2},{7,3},{8,12},{9,13},{10,... | collective-permute-start | bytes 98312 | tf_op jit(solution)/shard_map/ppermute | solution.py:193
  29.0 1.6 %collective-permute-done.5.refs_3_ = bf16[4,4096]{1,0:T(4,128)(2,1)S(1)} collective-permute-done((bf16[4,4096]{1,0:T(4,128)(2,1)S(1)}, bf16[4,4096]{1,0:T(4,128)(2,1)S(1)}, u32[]{:S(2)}, u32[]{:S(2)}) %collective-permute-start.5) | collective-permute-done | bytes 32800 | tf_op jit(solution)/shard_map/ppermute | solution.py:193
  30.7 0.3 collective-permute-done.4.refs_2_
  30.9 0.2 collective-permute-done.3.refs_1_
  31.2 0.1 collective-permute-start.8
  31.3 1.0 %collective-permute-start.7 = (bf16[4,4096]{1,0:T(4,128)(2,1)S(1)}, bf16[4,4096]{1,0:T(4,128)(2,1)S(1)}, u32[]{:S(2)}, u32[]{:S(2)}) collective-permute-start(bf16[4,4096]{1,0:T(4,128)(2,1)S(1)} %add_far.1.refs_0_), channel_id=1, source_target_pairs={{0,2},{1,3},{2,0},{3,1},{4,6},{5,7},{6,4},{7,5},{8,10},{9,11},{10,... | collective-permute-start | bytes 98312 | tf_op jit(solution)/shard_map/ppermute | solution.py:193
  32.3 0.8 %collective-permute-start.6 = (bf16[4,4096]{1,0:T(4,128)(2,1)S(1)}, bf16[4,4096]{1,0:T(4,128)(2,1)S(1)}, u32[]{:S(2)}, u32[]{:S(2)}) collective-permute-start(bf16[4,4096]{1,0:T(4,128)(2,1)S(1)} %add_far.1.refs_0_), channel_id=1, source_target_pairs={{0,1},{1,0},{2,3},{3,2},{4,5},{5,4},{6,7},{7,6},{8,9},{9,8},{10,11... | collective-permute-start | bytes 98312 | tf_op jit(solution)/shard_map/ppermute | solution.py:193
  33.1 1.5 %collective-permute-done.8.refs_3_ = bf16[4,4096]{1,0:T(4,128)(2,1)S(1)} collective-permute-done((bf16[4,4096]{1,0:T(4,128)(2,1)S(1)}, bf16[4,4096]{1,0:T(4,128)(2,1)S(1)}, u32[]{:S(2)}, u32[]{:S(2)}) %collective-permute-start.8) | collective-permute-done | bytes 32800 | tf_op jit(solution)/shard_map/ppermute | solution.py:193
  34.6 1.0 %collective-permute-done.7.refs_2_ = bf16[4,4096]{1,0:T(4,128)(2,1)S(1)} collective-permute-done((bf16[4,4096]{1,0:T(4,128)(2,1)S(1)}, bf16[4,4096]{1,0:T(4,128)(2,1)S(1)}, u32[]{:S(2)}, u32[]{:S(2)}) %collective-permute-start.7) | collective-permute-done | bytes 32800 | tf_op jit(solution)/shard_map/ppermute | solution.py:193
  35.5 0.0 collective-permute-done.6.refs_1_
  35.5 0.7 %lay.1 = bf16[4,16384]{1,0:T(4,128)(2,1)} custom-call(bf16[4,4096]{1,0:T(4,128)(2,1)S(1)} %add_far.1.refs_0_, bf16[4,4096]{1,0:T(4,128)(2,1)S(1)} %collective-permute-done.6.refs_1_, bf16[4,4096]{1,0:T(4,128)(2,1)S(1)} %collective-permute-done.7.refs_2_, bf16[4,4096]{1,0:T(4,128)(2,1)S(1)} %collective-permute-done.8.refs_3_), custom_call_target="tpu_custom_call" | custom-call | tf_op jit(solution)/shard_map/lay/pallas_call | solution.py:294
  (5 shorter events, 0.1 us)
Async XLA Ops:
  4.0 14.9 %copy-start = (bf16[512,16384]{1,0:T(8,128)(2,1)S(1)}, bf16[512,16384]{1,0:T(8,128)(2,1)}, u32[]{:S(2)}) copy-start(bf16[512,16384]{1,0:T(8,128)(2,1)} %weight.7) | copy-start | bytes 50331652
  19.5 4.2 %collective-permute-start = (bf16[4,4096]{1,0:T(4,128)(2,1)S(1)}, bf16[4,4096]{1,0:T(4,128)(2,1)S(1)}, u32[]{:S(2)}, u32[]{:S(2)}) collective-permute-start(bf16[4,4096]{1,0:T(4,128)(2,1)S(1)} %project_2.1), channel_id=1, source_target_pairs={{0,2},{1,3},{2,0},{3,1},{4,6},{5,7},{6,4},{7,5},{8,10},{9,11},{10,... | collective-permute-start | bytes 98312 | tf_op jit(solution)/shard_map/ppermute | solution.py:193
  20.2 3.6 %collective-permute-start.1 = (bf16[4,4096]{1,0:T(4,128)(2,1)S(1)}, bf16[4,4096]{1,0:T(4,128)(2,1)S(1)}, u32[]{:S(2)}, u32[]{:S(2)}) collective-permute-start(bf16[4,4096]{1,0:T(4,128)(2,1)S(1)} %project_3.1), channel_id=1, source_target_pairs={{0,3},{1,2},{2,1},{3,0},{4,7},{5,6},{6,5},{7,4},{8,11},{9,10},{10,... | collective-permute-start | bytes 98312 | tf_op jit(solution)/shard_map/ppermute | solution.py:193
  22.4 2.2 %collective-permute-start.2 = (bf16[4,4096]{1,0:T(4,128)(2,1)S(1)}, bf16[4,4096]{1,0:T(4,128)(2,1)S(1)}, u32[]{:S(2)}, u32[]{:S(2)}) collective-permute-start(bf16[4,4096]{1,0:T(4,128)(2,1)S(1)} %project_1.1), channel_id=1, source_target_pairs={{0,1},{1,0},{2,3},{3,2},{4,5},{5,4},{6,7},{7,6},{8,9},{9,8},{10,11... | collective-permute-start | bytes 98312 | tf_op jit(solution)/shard_map/ppermute | solution.py:193
  24.6 6.1 %collective-permute-start.5 = (bf16[4,4096]{1,0:T(4,128)(2,1)S(1)}, bf16[4,4096]{1,0:T(4,128)(2,1)S(1)}, u32[]{:S(2)}, u32[]{:S(2)}) collective-permute-start(bf16[4,4096]{1,0:T(4,128)(2,1)S(1)} %add_near.1.refs_0_), channel_id=1, source_target_pairs={{0,12},{1,13},{2,14},{3,15},{4,8},{5,9},{6,10},{7,11},{8,4},{9,5},... | collective-permute-start | bytes 98312 | tf_op jit(solution)/shard_map/ppermute | solution.py:193
  25.3 5.6 %collective-permute-start.4 = (bf16[4,4096]{1,0:T(4,128)(2,1)S(1)}, bf16[4,4096]{1,0:T(4,128)(2,1)S(1)}, u32[]{:S(2)}, u32[]{:S(2)}) collective-permute-start(bf16[4,4096]{1,0:T(4,128)(2,1)S(1)} %add_near.1.refs_0_), channel_id=1, source_target_pairs={{0,8},{1,9},{2,10},{3,11},{4,12},{5,13},{6,14},{7,15},{8,0},{9,1},... | collective-permute-start | bytes 98312 | tf_op jit(solution)/shard_map/ppermute | solution.py:193
  26.1 5.0 %collective-permute-start.3 = (bf16[4,4096]{1,0:T(4,128)(2,1)S(1)}, bf16[4,4096]{1,0:T(4,128)(2,1)S(1)}, u32[]{:S(2)}, u32[]{:S(2)}) collective-permute-start(bf16[4,4096]{1,0:T(4,128)(2,1)S(1)} %add_near.1.refs_0_), channel_id=1, source_target_pairs={{0,4},{1,5},{2,6},{3,7},{4,0},{5,1},{6,2},{7,3},{8,12},{9,13},{10,... | collective-permute-start | bytes 98312 | tf_op jit(solution)/shard_map/ppermute | solution.py:193
  31.2 3.4 %collective-permute-start.8 = (bf16[4,4096]{1,0:T(4,128)(2,1)S(1)}, bf16[4,4096]{1,0:T(4,128)(2,1)S(1)}, u32[]{:S(2)}, u32[]{:S(2)}) collective-permute-start(bf16[4,4096]{1,0:T(4,128)(2,1)S(1)} %add_far.1.refs_0_), channel_id=1, source_target_pairs={{0,3},{1,2},{2,1},{3,0},{4,7},{5,6},{6,5},{7,4},{8,11},{9,10},{10,... | collective-permute-start | bytes 98312 | tf_op jit(solution)/shard_map/ppermute | solution.py:193
  31.3 4.3 %collective-permute-start.7 = (bf16[4,4096]{1,0:T(4,128)(2,1)S(1)}, bf16[4,4096]{1,0:T(4,128)(2,1)S(1)}, u32[]{:S(2)}, u32[]{:S(2)}) collective-permute-start(bf16[4,4096]{1,0:T(4,128)(2,1)S(1)} %add_far.1.refs_0_), channel_id=1, source_target_pairs={{0,2},{1,3},{2,0},{3,1},{4,6},{5,7},{6,4},{7,5},{8,10},{9,11},{10,... | collective-permute-start | bytes 98312 | tf_op jit(solution)/shard_map/ppermute | solution.py:193
  32.3 3.3 %collective-permute-start.6 = (bf16[4,4096]{1,0:T(4,128)(2,1)S(1)}, bf16[4,4096]{1,0:T(4,128)(2,1)S(1)}, u32[]{:S(2)}, u32[]{:S(2)}) collective-permute-start(bf16[4,4096]{1,0:T(4,128)(2,1)S(1)} %add_far.1.refs_0_), channel_id=1, source_target_pairs={{0,1},{1,0},{2,3},{3,2},{4,5},{5,4},{6,7},{7,6},{8,9},{9,8},{10,11... | collective-permute-start | bytes 98312 | tf_op jit(solution)/shard_map/ppermute | solution.py:193

commit v27 on v24

--- a/solution.py
+++ b/solution.py
@@ -13,7 +13,7 @@
 ATTEND_VMEM = 60 * 1024 * 1024
 HIDDEN = -1e30
 LOWEST = -1e20
-EXCHANGE_FLOPS = 40_000_000_000
+EXCHANGE_FLOPS = 5_000_000_000
 SMALL_VMEM = 8 * 1024 * 1024
 VMEM = pl.BlockSpec(memory_space=pltpu.VMEM)
 HBM = pl.BlockSpec(memory_space=pltpu.HBM)
@@ -138,18 +138,41 @@
             staged[d, rows] = stats[k][start : start + heads_dev]
 
 
-def pack_kernel(staged, packed):
-    packed[...] = staged[...].astype(jnp.bfloat16)
+def pack_kernel(staged, keep, send):
+    core = lax.rem(lax.axis_index("kvp"), 2)
+    for i in range(keep.shape[0]):
+        keep[i] = staged[2 * i + core]
+        send[i] = staged[2 * i + 1 - core].astype(send.dtype)
+
+
+def lanes_ahead(value, by):
+    lanes = value.shape[-1]
+    return pltpu.roll(value, (lanes - by) % lanes, axis=2)
+
+
+def merge_kernel(keep, arrived, packed):
+    rows = keep.shape[1] - 1
+    own, other = keep[:, rows], arrived[:, rows].astype(jnp.float32)
+    own_max, other_max = (stats + lanes_ahead(stats, 1) for stats in (own, other))
+    own_total, other_total = (lanes_ahead(stats, 2) + lanes_ahead(stats, 3) for stats in (own, other))
+    high, low = split_two(jnp.maximum(own_max, other_max))
+    own_scale = jnp.exp2(own_max - (high + low))
+    other_scale = jnp.exp2(other_max - (high + low))
+    total_high, total_low = split_two(own_total * own_scale + other_total * other_scale)
+    at = lax.rem(lax.broadcasted_iota(jnp.int32, own.shape, 2), 4)
+    merged = high
+    for i, value in ((1, low), (2, total_high), (3, total_low)):
+        merged = jnp.where(at == i, lanes_ahead(value, -i), merged)
+    packed[:, rows] = merged.astype(packed.dtype)
+    for r in range(rows):
+        lane = slice(4 * r, 4 * r + 1)
+        partial = keep[:, r] * own_scale[:, :, lane] + arrived[:, r].astype(jnp.float32) * other_scale[:, :, lane]
+        packed[:, r] = partial.astype(packed.dtype)
 
 
 def combine_kernel(heads_dev, packed, left, attended):
     rows = left.shape[0]
     stats = packed[:, rows].astype(jnp.float32)
-    lanes = stats.shape[-1]
-
-    def lanes_ahead(value, by):
-        return pltpu.roll(value, lanes - by, axis=2)
-
     maxima = stats + lanes_ahead(stats, 1)
     rescale = jnp.exp2(maxima - jnp.max(maxima, axis=0, keepdims=True))
     totals = lanes_ahead(stats, 2) + lanes_ahead(stats, 3)
@@ -236,17 +259,31 @@
         name="attend",
     )(*[in_hbm(a) for a in (page_table, lengths, key_scale.T, value_scale.T, queries, key_cache, value_cache)])
 
-    packed = pl.pallas_call(
+    chips = devices // 2
+    block = (chips,) + staged.shape[1:]
+    keep, send = pl.pallas_call(
         pack_kernel,
-        out_shape=jax.ShapeDtypeStruct(staged.shape, jnp.bfloat16),
+        out_shape=[jax.ShapeDtypeStruct(block, jnp.float32), jax.ShapeDtypeStruct(block, jnp.bfloat16)],
         in_specs=[VMEM],
-        out_specs=VMEM,
+        out_specs=[VMEM] * 2,
         compiler_params=pltpu.CompilerParams(vmem_limit_bytes=SMALL_VMEM),
         cost_estimate=pl.CostEstimate(flops=EXCHANGE_FLOPS, bytes_accessed=6 * staged.size, transcendentals=0),
         name="pack",
     )(staged)
-
-    received = lax.all_to_all(packed, "kvp", split_axis=0, concat_axis=0, tiled=True)
+    packed = pl.pallas_call(
+        merge_kernel,
+        out_shape=jax.ShapeDtypeStruct(block, jnp.bfloat16),
+        in_specs=[VMEM] * 2,
+        out_specs=VMEM,
+        compiler_params=pltpu.CompilerParams(vmem_limit_bytes=SMALL_VMEM),
+        cost_estimate=pl.CostEstimate(flops=1024, bytes_accessed=1024, transcendentals=0),
+        name="merge",
+    )(keep, exchange(send, 1, devices))
+
+    parity = [[2 * i + core for i in range(chips)] for core in (0, 1)]
+    received = lax.all_to_all(
+        packed, "kvp", split_axis=0, concat_axis=0, axis_index_groups=parity, tiled=True
+    )
 
     resident = pltpu.with_memory_space_constraint(out_weight, pltpu.VMEM)
     depth = heads_dev * HD

time: 35.9 us -> 36.8 us (1.025)
  waiting for transfers between devices: 5.19 us -> 5.92 us
  blocking collectives: 14.6 us -> 14 us
  starting transfers between devices: 8.27 us -> 8.78 us
    ppermute x9 -> x10, waiting for transfers between devices: 5.19 us -> 5.92 us  [exchange(): lax.ppermute(array, 'kvp', [(i, i ^ partner) for i in range(devices)])]
    all_to_all x1, blocking collectives: 14.6 us -> 14 us  [body(): lax.all_to_all(packed, 'kvp', split_axis=0, concat_axis=0, axis_index_gro...]
    ppermute x9 -> x10, starting transfers between devices: 8.27 us -> 8.78 us  [exchange(): lax.ppermute(array, 'kvp', [(i, i ^ partner) for i in range(devices)])]
  transfers between devices with their start and end apart: 9 -> 10, of which waited for: 6 -> 8; matrix products, arithmetic and copies ran while one was open for 0% -> 0% of each run, Pallas kernels for 4% -> 4%
where the time goes in v27:
time: 36.8 us; the launch traced here: 36.6 us
  blocking collectives  14 us (38%)
  starting transfers between devices  8.78 us (24%)
  Pallas kernels  7.79 us (21%)
  waiting for transfers between devices  5.92 us (16%)
    all_to_all x1, blocking collectives, body(): lax.all_to_all(packed, 'kvp', split_axis=0, concat_axis=0, axis_index_gro...  14 us
    ppermute x10, starting transfers between devices, exchange(): lax.ppermute(array, 'kvp', [(i, i ^ partner) for i in range(devices)])  8.78 us
    ppermute x10, waiting for transfers between devices, exchange(): lax.ppermute(array, 'kvp', [(i, i ^ partner) for i in range(devices)])  5.92 us
    pallas_call x1, Pallas kernels, body(): pl.pallas_call(functools.partial(attend_kernel, heads_dev, devices), out_...  3.95 us
    pallas_call x4, Pallas kernels, body(): pl.pallas_call(functools.partial(project_kernel, x), out_shape=jax.ShapeD...  2.63 us
  transfers between devices with their start and end apart: 10, of which 8 were waited for; matrix products, arithmetic and copies ran while one was open for 0% of the time, Pallas kernels for 4%

profile of v27, /device:TPU:0, one launch (start us, length us, event | category | flops | bytes accessed | tf_op | source)
XLA Modules:
  0.0 36.6 jit_solution(10229600395851883367)
XLA Ops:
  0.0 3.9 %attend.1.staged = f32[16,5,4,128]{3,2,1,0:T(4,128)S(1)} custom-call(s32[4,12]{1,0:T(4,128)} %refs_0_.1, s32[4]{0:T(128)} %refs_1_.1, f32[4,48]{1,0:T(4,128)} %bitcast.2, f32[4,48]{1,0:T(4,128)} %bitcast.3, bf16[4,8192]{1,0:T(4,128)(2,1)} %refs_4_.1, bf16[48,64,512]{2,1,0:T(8,128)(2,1)} %refs_5_.1, bf16[48,64,512]{2,1,0:T(8,128)(2,1)} %refs_6_.1), custom_call_target="tpu_custom_call" | custom-call | flops 100663296 | bytes 6291456 | tf_op jit(solution)/shard_map/attend/pallas_call | solution.py:232
  4.0 0.0 copy-start
  4.0 0.5 %collective-permute-start = (bf16[8,5,4,128]{3,2,1,0:T(4,128)(2,1)S(1)}, bf16[8,5,4,128]{3,2,1,0:T(4,128)(2,1)S(1)}, u32[]{:S(2)}, u32[]{:S(2)}) collective-permute-start(bf16[8,5,4,128]{3,2,1,0:T(4,128)(2,1)S(1)} %get-tuple-element.8), channel_id=1, source_target_pairs={{0,1},{1,0},{2,3},{3,2},{4,5},{5,4},{6,7},{7,6},{8,9},{9,8},{10,11... | collective-permute-start | bytes 122888 | tf_op jit(solution)/shard_map/ppermute | solution.py:215
  4.5 0.9 %collective-permute-done.arrived = bf16[8,5,4,128]{3,2,1,0:T(4,128)(2,1)S(1)} collective-permute-done((bf16[8,5,4,128]{3,2,1,0:T(4,128)(2,1)S(1)}, bf16[8,5,4,128]{3,2,1,0:T(4,128)(2,1)S(1)}, u32[]{:S(2)}, u32[]{:S(2)}) %collective-permute-start) | collective-permute-done | bytes 40992 | tf_op jit(solution)/shard_map/ppermute | solution.py:215
  5.4 0.2 merge.1
  5.6 14.0 %all_to_all.5.packed = bf16[8,5,4,128]{3,2,1,0:T(4,128)(2,1)S(1)} all-to-all(bf16[8,5,4,128]{3,2,1,0:T(4,128)(2,1)S(1)} %merge.1), channel_id=1, replica_groups={{0,2,4,6,8,10,12,14},{1,3,5,7,9,11,13,15},{16,18,20,22,24,26,28,30},{17..., dimensions={0} | all-to-all | bytes 81920 | tf_op jit(solution)/shard_map/all_to_all | solution.py:284
  19.6 0.2 combine.1.left
  19.8 0.0 copy-done
  19.9 0.7 %project_2.1 = bf16[4,4096]{1,0:T(4,128)(2,1)S(1)} custom-call(bf16[4,512]{1,0:T(4,128)(2,1)S(1)} %combine.1.left, bf16[512,16384]{1,0:T(8,128)(2,1)S(1)} %copy-done), custom_call_target="tpu_custom_call" | custom-call | flops 1024 | bytes 1024 | tf_op jit(solution)/shard_map/project_2/pallas_call | solution.py:303
  20.5 0.7 %project_3.1 = bf16[4,4096]{1,0:T(4,128)(2,1)S(1)} custom-call(bf16[4,512]{1,0:T(4,128)(2,1)S(1)} %combine.1.left, bf16[512,16384]{1,0:T(8,128)(2,1)S(1)} %copy-done), custom_call_target="tpu_custom_call" | custom-call | flops 1024 | bytes 1024 | tf_op jit(solution)/shard_map/project_3/pallas_call | solution.py:303
  21.2 0.0 collective-permute-start.1
  21.2 0.5 %collective-permute-start.2 = (bf16[4,4096]{1,0:T(4,128)(2,1)S(1)}, bf16[4,4096]{1,0:T(4,128)(2,1)S(1)}, u32[]{:S(2)}, u32[]{:S(2)}) collective-permute-start(bf16[4,4096]{1,0:T(4,128)(2,1)S(1)} %project_2.1), channel_id=1, source_target_pairs={{0,2},{1,3},{2,0},{3,1},{4,6},{5,7},{6,4},{7,5},{8,10},{9,11},{10,... | collective-permute-start | bytes 98312 | tf_op jit(solution)/shard_map/ppermute | solution.py:215
  21.7 0.7 %project_1.1 = bf16[4,4096]{1,0:T(4,128)(2,1)S(1)} custom-call(bf16[4,512]{1,0:T(4,128)(2,1)S(1)} %combine.1.left, bf16[512,16384]{1,0:T(8,128)(2,1)S(1)} %copy-done), custom_call_target="tpu_custom_call" | custom-call | flops 1024 | bytes 1024 | tf_op jit(solution)/shard_map/project_1/pallas_call | solution.py:303
  22.4 1.4 %collective-permute-start.3 = (bf16[4,4096]{1,0:T(4,128)(2,1)S(1)}, bf16[4,4096]{1,0:T(4,128)(2,1)S(1)}, u32[]{:S(2)}, u32[]{:S(2)}) collective-permute-start(bf16[4,4096]{1,0:T(4,128)(2,1)S(1)} %project_1.1), channel_id=1, source_target_pairs={{0,1},{1,0},{2,3},{3,2},{4,5},{5,4},{6,7},{7,6},{8,9},{9,8},{10,11... | collective-permute-start | bytes 98312 | tf_op jit(solution)/shard_map/ppermute | solution.py:215
  23.7 0.7 %project_0.1.refs_3_ = f32[4,4096]{1,0:T(4,128)S(1)} custom-call(bf16[4,512]{1,0:T(4,128)(2,1)S(1)} %combine.1.left, bf16[512,16384]{1,0:T(8,128)(2,1)S(1)} %copy-done), custom_call_target="tpu_custom_call" | custom-call | flops 1024 | bytes 1024 | tf_op jit(solution)/shard_map/project_0/pallas_call | solution.py:303
  24.4 0.2 collective-permute-done.1.refs_0_
  24.5 0.7 %collective-permute-done.2.refs_1_ = bf16[4,4096]{1,0:T(4,128)(2,1)S(1)} collective-permute-done((bf16[4,4096]{1,0:T(4,128)(2,1)S(1)}, bf16[4,4096]{1,0:T(4,128)(2,1)S(1)}, u32[]{:S(2)}, u32[]{:S(2)}) %collective-permute-start.2) | collective-permute-done | bytes 32800 | tf_op jit(solution)/shard_map/ppermute | solution.py:215
  25.2 0.0 collective-permute-done.3.refs_2_
  25.3 0.7 %collective-permute-start.6 = (bf16[4,4096]{1,0:T(4,128)(2,1)S(1)}, bf16[4,4096]{1,0:T(4,128)(2,1)S(1)}, u32[]{:S(2)}, u32[]{:S(2)}) collective-permute-start(bf16[4,4096]{1,0:T(4,128)(2,1)S(1)} %add_near.1.refs_0_), channel_id=1, source_target_pairs={{0,12},{1,13},{2,14},{3,15},{4,8},{5,9},{6,10},{7,11},{8,4},{9,5},... | collective-permute-start | bytes 98312 | tf_op jit(solution)/shard_map/ppermute | solution.py:215
  26.0 1.4 %collective-permute-start.5 = (bf16[4,4096]{1,0:T(4,128)(2,1)S(1)}, bf16[4,4096]{1,0:T(4,128)(2,1)S(1)}, u32[]{:S(2)}, u32[]{:S(2)}) collective-permute-start(bf16[4,4096]{1,0:T(4,128)(2,1)S(1)} %add_near.1.refs_0_), channel_id=1, source_target_pairs={{0,8},{1,9},{2,10},{3,11},{4,12},{5,13},{6,14},{7,15},{8,0},{9,1},... | collective-permute-start | bytes 98312 | tf_op jit(solution)/shard_map/ppermute | solution.py:215
  27.4 2.4 %collective-permute-start.4 = (bf16[4,4096]{1,0:T(4,128)(2,1)S(1)}, bf16[4,4096]{1,0:T(4,128)(2,1)S(1)}, u32[]{:S(2)}, u32[]{:S(2)}) collective-permute-start(bf16[4,4096]{1,0:T(4,128)(2,1)S(1)} %add_near.1.refs_0_), channel_id=1, source_target_pairs={{0,4},{1,5},{2,6},{3,7},{4,0},{5,1},{6,2},{7,3},{8,12},{9,13},{10,... | collective-permute-start | bytes 98312 | tf_op jit(solution)/shard_map/ppermute | solution.py:215
  29.7 1.4 %collective-permute-done.6.refs_3_ = bf16[4,4096]{1,0:T(4,128)(2,1)S(1)} collective-permute-done((bf16[4,4096]{1,0:T(4,128)(2,1)S(1)}, bf16[4,4096]{1,0:T(4,128)(2,1)S(1)}, u32[]{:S(2)}, u32[]{:S(2)}) %collective-permute-start.6) | collective-permute-done | bytes 32800 | tf_op jit(solution)/shard_map/ppermute | solution.py:215
  31.2 0.4 collective-permute-done.5.refs_2_
  31.5 0.1 collective-permute-done.4.refs_1_
  31.7 0.1 collective-permute-start.9
  31.7 0.8 %collective-permute-start.8 = (bf16[4,4096]{1,0:T(4,128)(2,1)S(1)}, bf16[4,4096]{1,0:T(4,128)(2,1)S(1)}, u32[]{:S(2)}, u32[]{:S(2)}) collective-permute-start(bf16[4,4096]{1,0:T(4,128)(2,1)S(1)} %add_far.1.refs_0_), channel_id=1, source_target_pairs={{0,2},{1,3},{2,0},{3,1},{4,6},{5,7},{6,4},{7,5},{8,10},{9,11},{10,... | collective-permute-start | bytes 98312 | tf_op jit(solution)/shard_map/ppermute | solution.py:215
  32.5 1.0 %collective-permute-start.7 = (bf16[4,4096]{1,0:T(4,128)(2,1)S(1)}, bf16[4,4096]{1,0:T(4,128)(2,1)S(1)}, u32[]{:S(2)}, u32[]{:S(2)}) collective-permute-start(bf16[4,4096]{1,0:T(4,128)(2,1)S(1)} %add_far.1.refs_0_), channel_id=1, source_target_pairs={{0,1},{1,0},{2,3},{3,2},{4,5},{5,4},{6,7},{7,6},{8,9},{9,8},{10,11... | collective-permute-start | bytes 98312 | tf_op jit(solution)/shard_map/ppermute | solution.py:215
  33.6 1.5 %collective-permute-done.9.refs_3_ = bf16[4,4096]{1,0:T(4,128)(2,1)S(1)} collective-permute-done((bf16[4,4096]{1,0:T(4,128)(2,1)S(1)}, bf16[4,4096]{1,0:T(4,128)(2,1)S(1)}, u32[]{:S(2)}, u32[]{:S(2)}) %collective-permute-start.9) | collective-permute-done | bytes 32800 | tf_op jit(solution)/shard_map/ppermute | solution.py:215
  35.1 0.8 %collective-permute-done.8.refs_2_ = bf16[4,4096]{1,0:T(4,128)(2,1)S(1)} collective-permute-done((bf16[4,4096]{1,0:T(4,128)(2,1)S(1)}, bf16[4,4096]{1,0:T(4,128)(2,1)S(1)}, u32[]{:S(2)}, u32[]{:S(2)}) %collective-permute-start.8) | collective-permute-done | bytes 32800 | tf_op jit(solution)/shard_map/ppermute | solution.py:215
  35.9 0.0 collective-permute-done.7.refs_1_
  35.9 0.7 %lay.1 = bf16[4,16384]{1,0:T(4,128)(2,1)} custom-call(bf16[4,4096]{1,0:T(4,128)(2,1)S(1)} %add_far.1.refs_0_, bf16[4,4096]{1,0:T(4,128)(2,1)S(1)} %collective-permute-done.7.refs_1_, bf16[4,4096]{1,0:T(4,128)(2,1)S(1)} %collective-permute-done.8.refs_2_, bf16[4,4096]{1,0:T(4,128)(2,1)S(1)} %collective-permute-done.9.refs_3_), custom_call_target="tpu_custom_call" | custom-call | tf_op jit(solution)/shard_map/lay/pallas_call | solution.py:327
  (3 shorter events, 0.1 us)
Async XLA Ops:
  4.0 15.9 %copy-start = (bf16[512,16384]{1,0:T(8,128)(2,1)S(1)}, bf16[512,16384]{1,0:T(8,128)(2,1)}, u32[]{:S(2)}) copy-start(bf16[512,16384]{1,0:T(8,128)(2,1)} %weight.7) | copy-start | bytes 50331652
  4.0 1.4 %collective-permute-start = (bf16[8,5,4,128]{3,2,1,0:T(4,128)(2,1)S(1)}, bf16[8,5,4,128]{3,2,1,0:T(4,128)(2,1)S(1)}, u32[]{:S(2)}, u32[]{:S(2)}) collective-permute-start(bf16[8,5,4,128]{3,2,1,0:T(4,128)(2,1)S(1)} %get-tuple-element.8), channel_id=1, source_target_pairs={{0,1},{1,0},{2,3},{3,2},{4,5},{5,4},{6,7},{7,6},{8,9},{9,8},{10,11... | collective-permute-start | bytes 122888 | tf_op jit(solution)/shard_map/ppermute | solution.py:215
  21.2 3.4 %collective-permute-start.1 = (bf16[4,4096]{1,0:T(4,128)(2,1)S(1)}, bf16[4,4096]{1,0:T(4,128)(2,1)S(1)}, u32[]{:S(2)}, u32[]{:S(2)}) collective-permute-start(bf16[4,4096]{1,0:T(4,128)(2,1)S(1)} %project_3.1), channel_id=1, source_target_pairs={{0,3},{1,2},{2,1},{3,0},{4,7},{5,6},{6,5},{7,4},{8,11},{9,10},{10,... | collective-permute-start | bytes 98312 | tf_op jit(solution)/shard_map/ppermute | solution.py:215
  21.2 4.1 %collective-permute-start.2 = (bf16[4,4096]{1,0:T(4,128)(2,1)S(1)}, bf16[4,4096]{1,0:T(4,128)(2,1)S(1)}, u32[]{:S(2)}, u32[]{:S(2)}) collective-permute-start(bf16[4,4096]{1,0:T(4,128)(2,1)S(1)} %project_2.1), channel_id=1, source_target_pairs={{0,2},{1,3},{2,0},{3,1},{4,6},{5,7},{6,4},{7,5},{8,10},{9,11},{10,... | collective-permute-start | bytes 98312 | tf_op jit(solution)/shard_map/ppermute | solution.py:215
  22.4 2.9 %collective-permute-start.3 = (bf16[4,4096]{1,0:T(4,128)(2,1)S(1)}, bf16[4,4096]{1,0:T(4,128)(2,1)S(1)}, u32[]{:S(2)}, u32[]{:S(2)}) collective-permute-start(bf16[4,4096]{1,0:T(4,128)(2,1)S(1)} %project_1.1), channel_id=1, source_target_pairs={{0,1},{1,0},{2,3},{3,2},{4,5},{5,4},{6,7},{7,6},{8,9},{9,8},{10,11... | collective-permute-start | bytes 98312 | tf_op jit(solution)/shard_map/ppermute | solution.py:215
  25.3 5.9 %collective-permute-start.6 = (bf16[4,4096]{1,0:T(4,128)(2,1)S(1)}, bf16[4,4096]{1,0:T(4,128)(2,1)S(1)}, u32[]{:S(2)}, u32[]{:S(2)}) collective-permute-start(bf16[4,4096]{1,0:T(4,128)(2,1)S(1)} %add_near.1.refs_0_), channel_id=1, source_target_pairs={{0,12},{1,13},{2,14},{3,15},{4,8},{5,9},{6,10},{7,11},{8,4},{9,5},... | collective-permute-start | bytes 98312 | tf_op jit(solution)/shard_map/ppermute | solution.py:215
  26.0 5.5 %collective-permute-start.5 = (bf16[4,4096]{1,0:T(4,128)(2,1)S(1)}, bf16[4,4096]{1,0:T(4,128)(2,1)S(1)}, u32[]{:S(2)}, u32[]{:S(2)}) collective-permute-start(bf16[4,4096]{1,0:T(4,128)(2,1)S(1)} %add_near.1.refs_0_), channel_id=1, source_target_pairs={{0,8},{1,9},{2,10},{3,11},{4,12},{5,13},{6,14},{7,15},{8,0},{9,1},... | collective-permute-start | bytes 98312 | tf_op jit(solution)/shard_map/ppermute | solution.py:215
  27.4 4.3 %collective-permute-start.4 = (bf16[4,4096]{1,0:T(4,128)(2,1)S(1)}, bf16[4,4096]{1,0:T(4,128)(2,1)S(1)}, u32[]{:S(2)}, u32[]{:S(2)}) collective-permute-start(bf16[4,4096]{1,0:T(4,128)(2,1)S(1)} %add_near.1.refs_0_), channel_id=1, source_target_pairs={{0,4},{1,5},{2,6},{3,7},{4,0},{5,1},{6,2},{7,3},{8,12},{9,13},{10,... | collective-permute-start | bytes 98312 | tf_op jit(solution)/shard_map/ppermute | solution.py:215
  31.7 3.4 %collective-permute-start.9 = (bf16[4,4096]{1,0:T(4,128)(2,1)S(1)}, bf16[4,4096]{1,0:T(4,128)(2,1)S(1)}, u32[]{:S(2)}, u32[]{:S(2)}) collective-permute-start(bf16[4,4096]{1,0:T(4,128)(2,1)S(1)} %add_far.1.refs_0_), channel_id=1, source_target_pairs={{0,3},{1,2},{2,1},{3,0},{4,7},{5,6},{6,5},{7,4},{8,11},{9,10},{10,... | collective-permute-start | bytes 98312 | tf_op jit(solution)/shard_map/ppermute | solution.py:215
  31.7 4.1 %collective-permute-start.8 = (bf16[4,4096]{1,0:T(4,128)(2,1)S(1)}, bf16[4,4096]{1,0:T(4,128)(2,1)S(1)}, u32[]{:S(2)}, u32[]{:S(2)}) collective-permute-start(bf16[4,4096]{1,0:T(4,128)(2,1)S(1)} %add_far.1.refs_0_), channel_id=1, source_target_pairs={{0,2},{1,3},{2,0},{3,1},{4,6},{5,7},{6,4},{7,5},{8,10},{9,11},{10,... | collective-permute-start | bytes 98312 | tf_op jit(solution)/shard_map/ppermute | solution.py:215
  32.5 3.3 %collective-permute-start.7 = (bf16[4,4096]{1,0:T(4,128)(2,1)S(1)}, bf16[4,4096]{1,0:T(4,128)(2,1)S(1)}, u32[]{:S(2)}, u32[]{:S(2)}) collective-permute-start(bf16[4,4096]{1,0:T(4,128)(2,1)S(1)} %add_far.1.refs_0_), channel_id=1, source_target_pairs={{0,1},{1,0},{2,3},{3,2},{4,5},{5,4},{6,7},{7,6},{8,9},{9,8},{10,11... | collective-permute-start | bytes 98312 | tf_op jit(solution)/shard_map/ppermute | solution.py:215

commit v28 on v24

--- a/solution.py
+++ b/solution.py
@@ -87,30 +87,30 @@
     for h in range(heads):
         query_rows[h * rows : (h + 1) * rows, :] = queries[:, h * HD : (h + 1) * HD].astype(jnp.float32)
 
-    def pages_of(buf, r, k):
-        return jnp.concatenate(
-            [buf[table[r, p], :, k * HD : (k + 2) * HD] for p in range(pages)], axis=0
-        )
+    def pages_of(buf, r):
+        return jnp.concatenate([buf[table[r, p]] for p in range(pages)], axis=0)
 
     for copy in large[0]:
         copy.wait()
     stats = [jnp.zeros((group, HD), jnp.float32)] * kv_heads
     for r in range(rows):
         query = query_rows[pl.ds(r, heads, stride=rows), :].astype(jnp.bfloat16)
+        left = jnp.concatenate(
+            [
+                jnp.concatenate(
+                    [query[k * group : (k + 1) * group] if i == k else zeros for i in range(kv_heads)], axis=1
+                )
+                for k in range(kv_heads)
+            ],
+            axis=0,
+        )
+        both = lax.dot_general(
+            left, pages_of(key_buf, r), (((1,), (1,)), ((), ())), preferred_element_type=jnp.float32
+        )
         for k in range(0, kv_heads, 2):
-            left = jnp.concatenate(
-                [
-                    jnp.concatenate([query[k * group : (k + 1) * group], zeros], axis=1),
-                    jnp.concatenate([zeros, query[(k + 1) * group : (k + 2) * group]], axis=1),
-                ],
-                axis=0,
-            )
-            both = lax.dot_general(
-                left, pages_of(key_buf, r, k), (((1,), (1,)), ((), ())), preferred_element_type=jnp.float32
-            )
             for i in (0, 1):
                 at_key, at_value = k + i, kv_heads + k + i
-                scores = both[i * group : (i + 1) * group] * factors[r, at_key : at_key + 1] + bias[r : r + 1]
+                scores = both[(k + i) * group : (k + i + 1) * group] * factors[r, at_key : at_key + 1] + bias[r : r + 1]
                 highest = jnp.maximum(jnp.max(scores, axis=1, keepdims=True), LOWEST)
                 high, low = split_two(highest)
                 prob = jnp.exp2(scores - (high + low))
@@ -123,12 +123,10 @@
     for copy in large[1]:
         copy.wait()
     for r in range(rows):
+        both = jnp.dot(weights[r], pages_of(value_buf, r), preferred_element_type=jnp.float32)
         for k in range(0, kv_heads, 2):
-            both = jnp.dot(
-                weights[r, k * group : (k + 2) * group], pages_of(value_buf, r, k), preferred_element_type=jnp.float32
-            )
             for i in (0, 1):
-                partial = both[i * group : (i + 1) * group, i * HD : (i + 1) * HD]
+                partial = both[(k + i) * group : (k + i + 1) * group, (k + i) * HD : (k + i + 1) * HD]
                 for start in range(0, group, heads_dev):
                     d = ((k + i) * group + start) // heads_dev
                     staged[d, r] = partial[start : start + heads_dev]

time: 35.9 us -> 36 us (level)
  no operation moved by 1% of the time
where the time goes in v28:
time: 36 us; the launch traced here: 35.8 us
  blocking collectives  14.6 us (41%)
  starting transfers between devices  8.27 us (23%)
  Pallas kernels  7.64 us (21%)
  waiting for transfers between devices  5.19 us (14%)
    all_to_all x1, blocking collectives, body(): lax.all_to_all(packed, 'kvp', split_axis=0, concat_axis=0, tiled=True)  14.6 us
    ppermute x9, starting transfers between devices, exchange(): lax.ppermute(array, 'kvp', [(i, i ^ partner) for i in range(devices)])  8.27 us
    ppermute x9, waiting for transfers between devices, exchange(): lax.ppermute(array, 'kvp', [(i, i ^ partner) for i in range(devices)])  5.19 us
    pallas_call x1, Pallas kernels, body(): pl.pallas_call(functools.partial(attend_kernel, heads_dev, devices), out_...  4 us
    pallas_call x4, Pallas kernels, body(): pl.pallas_call(functools.partial(project_kernel, x), out_shape=jax.ShapeD...  2.63 us
  transfers between devices with their start and end apart: 9, of which 6 were waited for; matrix products, arithmetic and copies ran while one was open for 0% of the time, Pallas kernels for 4%

profile of v28, /device:TPU:0, one launch (start us, length us, event | category | flops | bytes accessed | tf_op | source)
XLA Modules:
  0.0 35.8 jit_solution(1388137989004191983)
XLA Ops:
  0.0 4.0 %attend.1.staged = f32[16,5,4,128]{3,2,1,0:T(4,128)S(1)} custom-call(s32[4,12]{1,0:T(4,128)} %refs_0_.1, s32[4]{0:T(128)} %refs_1_.1, f32[4,48]{1,0:T(4,128)} %bitcast.2, f32[4,48]{1,0:T(4,128)} %bitcast.3, bf16[4,8192]{1,0:T(4,128)(2,1)} %refs_4_.1, bf16[48,64,512]{2,1,0:T(8,128)(2,1)} %refs_5_.1, bf16[48,64,512]{2,1,0:T(8,128)(2,1)} %refs_6_.1), custom_call_target="tpu_custom_call" | custom-call | flops 100663296 | bytes 6291456 | tf_op jit(solution)/shard_map/attend/pallas_call | solution.py:207
  4.0 0.0 copy-start
  4.1 14.6 %all_to_all.5.packed = bf16[16,5,4,128]{3,2,1,0:T(4,128)(2,1)S(1)} all-to-all(bf16[16,5,4,128]{3,2,1,0:T(4,128)(2,1)S(1)} %pack.1), channel_id=1, replica_groups=mesh['group'=2,'kvp'=16] {'kvp'}, dimensions={0} | all-to-all | bytes 163840 | tf_op jit(solution)/shard_map/all_to_all | solution.py:247
  18.7 0.3 combine.1.left
  18.9 0.0 copy-done
  18.9 0.7 %project_2.1 = bf16[4,4096]{1,0:T(4,128)(2,1)S(1)} custom-call(bf16[4,512]{1,0:T(4,128)(2,1)S(1)} %combine.1.left, bf16[512,16384]{1,0:T(8,128)(2,1)S(1)} %copy-done), custom_call_target="tpu_custom_call" | custom-call | flops 1024 | bytes 1024 | tf_op jit(solution)/shard_map/project_2/pallas_call | solution.py:264
  19.6 0.7 %project_3.1 = bf16[4,4096]{1,0:T(4,128)(2,1)S(1)} custom-call(bf16[4,512]{1,0:T(4,128)(2,1)S(1)} %combine.1.left, bf16[512,16384]{1,0:T(8,128)(2,1)S(1)} %copy-done), custom_call_target="tpu_custom_call" | custom-call | flops 1024 | bytes 1024 | tf_op jit(solution)/shard_map/project_3/pallas_call | solution.py:264
  20.3 0.0 collective-permute-start
  20.3 1.1 %collective-permute-start.1 = (bf16[4,4096]{1,0:T(4,128)(2,1)S(1)}, bf16[4,4096]{1,0:T(4,128)(2,1)S(1)}, u32[]{:S(2)}, u32[]{:S(2)}) collective-permute-start(bf16[4,4096]{1,0:T(4,128)(2,1)S(1)} %project_2.1), channel_id=1, source_target_pairs={{0,2},{1,3},{2,0},{3,1},{4,6},{5,7},{6,4},{7,5},{8,10},{9,11},{10,... | collective-permute-start | bytes 98312 | tf_op jit(solution)/shard_map/ppermute | solution.py:190
  21.4 0.7 %project_1.1 = bf16[4,4096]{1,0:T(4,128)(2,1)S(1)} custom-call(bf16[4,512]{1,0:T(4,128)(2,1)S(1)} %combine.1.left, bf16[512,16384]{1,0:T(8,128)(2,1)S(1)} %copy-done), custom_call_target="tpu_custom_call" | custom-call | flops 1024 | bytes 1024 | tf_op jit(solution)/shard_map/project_1/pallas_call | solution.py:264
  22.0 0.8 %collective-permute-start.2 = (bf16[4,4096]{1,0:T(4,128)(2,1)S(1)}, bf16[4,4096]{1,0:T(4,128)(2,1)S(1)}, u32[]{:S(2)}, u32[]{:S(2)}) collective-permute-start(bf16[4,4096]{1,0:T(4,128)(2,1)S(1)} %project_1.1), channel_id=1, source_target_pairs={{0,1},{1,0},{2,3},{3,2},{4,5},{5,4},{6,7},{7,6},{8,9},{9,8},{10,11... | collective-permute-start | bytes 98312 | tf_op jit(solution)/shard_map/ppermute | solution.py:190
  22.8 0.7 %project_0.1.refs_3_ = f32[4,4096]{1,0:T(4,128)S(1)} custom-call(bf16[4,512]{1,0:T(4,128)(2,1)S(1)} %combine.1.left, bf16[512,16384]{1,0:T(8,128)(2,1)S(1)} %copy-done), custom_call_target="tpu_custom_call" | custom-call | flops 1024 | bytes 1024 | tf_op jit(solution)/shard_map/project_0/pallas_call | solution.py:264
  23.5 0.2 collective-permute-done.refs_0_
  23.6 0.7 %collective-permute-done.1.refs_1_ = bf16[4,4096]{1,0:T(4,128)(2,1)S(1)} collective-permute-done((bf16[4,4096]{1,0:T(4,128)(2,1)S(1)}, bf16[4,4096]{1,0:T(4,128)(2,1)S(1)}, u32[]{:S(2)}, u32[]{:S(2)}) %collective-permute-start.1) | collective-permute-done | bytes 32800 | tf_op jit(solution)/shard_map/ppermute | solution.py:190
  24.3 0.0 collective-permute-done.2.refs_2_
  24.4 1.0 %collective-permute-start.5 = (bf16[4,4096]{1,0:T(4,128)(2,1)S(1)}, bf16[4,4096]{1,0:T(4,128)(2,1)S(1)}, u32[]{:S(2)}, u32[]{:S(2)}) collective-permute-start(bf16[4,4096]{1,0:T(4,128)(2,1)S(1)} %add_near.1.refs_0_), channel_id=1, source_target_pairs={{0,12},{1,13},{2,14},{3,15},{4,8},{5,9},{6,10},{7,11},{8,4},{9,5},... | collective-permute-start | bytes 98312 | tf_op jit(solution)/shard_map/ppermute | solution.py:190
  25.4 0.8 %collective-permute-start.4 = (bf16[4,4096]{1,0:T(4,128)(2,1)S(1)}, bf16[4,4096]{1,0:T(4,128)(2,1)S(1)}, u32[]{:S(2)}, u32[]{:S(2)}) collective-permute-start(bf16[4,4096]{1,0:T(4,128)(2,1)S(1)} %add_near.1.refs_0_), channel_id=1, source_target_pairs={{0,8},{1,9},{2,10},{3,11},{4,12},{5,13},{6,14},{7,15},{8,0},{9,1},... | collective-permute-start | bytes 98312 | tf_op jit(solution)/shard_map/ppermute | solution.py:190
  26.2 2.6 %collective-permute-start.3 = (bf16[4,4096]{1,0:T(4,128)(2,1)S(1)}, bf16[4,4096]{1,0:T(4,128)(2,1)S(1)}, u32[]{:S(2)}, u32[]{:S(2)}) collective-permute-start(bf16[4,4096]{1,0:T(4,128)(2,1)S(1)} %add_near.1.refs_0_), channel_id=1, source_target_pairs={{0,4},{1,5},{2,6},{3,7},{4,0},{5,1},{6,2},{7,3},{8,12},{9,13},{10,... | collective-permute-start | bytes 98312 | tf_op jit(solution)/shard_map/ppermute | solution.py:190
  28.8 1.5 %collective-permute-done.5.refs_3_ = bf16[4,4096]{1,0:T(4,128)(2,1)S(1)} collective-permute-done((bf16[4,4096]{1,0:T(4,128)(2,1)S(1)}, bf16[4,4096]{1,0:T(4,128)(2,1)S(1)}, u32[]{:S(2)}, u32[]{:S(2)}) %collective-permute-start.5) | collective-permute-done | bytes 32800 | tf_op jit(solution)/shard_map/ppermute | solution.py:190
  30.3 0.6 %collective-permute-done.4.refs_2_ = bf16[4,4096]{1,0:T(4,128)(2,1)S(1)} collective-permute-done((bf16[4,4096]{1,0:T(4,128)(2,1)S(1)}, bf16[4,4096]{1,0:T(4,128)(2,1)S(1)}, u32[]{:S(2)}, u32[]{:S(2)}) %collective-permute-start.4) | collective-permute-done | bytes 32800 | tf_op jit(solution)/shard_map/ppermute | solution.py:190
  30.9 0.0 collective-permute-done.3.refs_1_
  31.0 0.1 collective-permute-start.8
  31.0 1.3 %collective-permute-start.7 = (bf16[4,4096]{1,0:T(4,128)(2,1)S(1)}, bf16[4,4096]{1,0:T(4,128)(2,1)S(1)}, u32[]{:S(2)}, u32[]{:S(2)}) collective-permute-start(bf16[4,4096]{1,0:T(4,128)(2,1)S(1)} %add_far.1.refs_0_), channel_id=1, source_target_pairs={{0,2},{1,3},{2,0},{3,1},{4,6},{5,7},{6,4},{7,5},{8,10},{9,11},{10,... | collective-permute-start | bytes 98312 | tf_op jit(solution)/shard_map/ppermute | solution.py:190
  32.3 0.6 %collective-permute-start.6 = (bf16[4,4096]{1,0:T(4,128)(2,1)S(1)}, bf16[4,4096]{1,0:T(4,128)(2,1)S(1)}, u32[]{:S(2)}, u32[]{:S(2)}) collective-permute-start(bf16[4,4096]{1,0:T(4,128)(2,1)S(1)} %add_far.1.refs_0_), channel_id=1, source_target_pairs={{0,1},{1,0},{2,3},{3,2},{4,5},{5,4},{6,7},{7,6},{8,9},{9,8},{10,11... | collective-permute-start | bytes 98312 | tf_op jit(solution)/shard_map/ppermute | solution.py:190
  32.9 1.6 %collective-permute-done.8.refs_3_ = bf16[4,4096]{1,0:T(4,128)(2,1)S(1)} collective-permute-done((bf16[4,4096]{1,0:T(4,128)(2,1)S(1)}, bf16[4,4096]{1,0:T(4,128)(2,1)S(1)}, u32[]{:S(2)}, u32[]{:S(2)}) %collective-permute-start.8) | collective-permute-done | bytes 32800 | tf_op jit(solution)/shard_map/ppermute | solution.py:190
  34.5 0.6 %collective-permute-done.7.refs_2_ = bf16[4,4096]{1,0:T(4,128)(2,1)S(1)} collective-permute-done((bf16[4,4096]{1,0:T(4,128)(2,1)S(1)}, bf16[4,4096]{1,0:T(4,128)(2,1)S(1)}, u32[]{:S(2)}, u32[]{:S(2)}) %collective-permute-start.7) | collective-permute-done | bytes 32800 | tf_op jit(solution)/shard_map/ppermute | solution.py:190
  35.1 0.0 collective-permute-done.6.refs_1_
  35.1 0.7 %lay.1 = bf16[4,16384]{1,0:T(4,128)(2,1)} custom-call(bf16[4,4096]{1,0:T(4,128)(2,1)S(1)} %add_far.1.refs_0_, bf16[4,4096]{1,0:T(4,128)(2,1)S(1)} %collective-permute-done.6.refs_1_, bf16[4,4096]{1,0:T(4,128)(2,1)S(1)} %collective-permute-done.7.refs_2_, bf16[4,4096]{1,0:T(4,128)(2,1)S(1)} %collective-permute-done.8.refs_3_), custom_call_target="tpu_custom_call" | custom-call | tf_op jit(solution)/shard_map/lay/pallas_call | solution.py:288
  (3 shorter events, 0.1 us)
Async XLA Ops:
  4.0 14.9 %copy-start = (bf16[512,16384]{1,0:T(8,128)(2,1)S(1)}, bf16[512,16384]{1,0:T(8,128)(2,1)}, u32[]{:S(2)}) copy-start(bf16[512,16384]{1,0:T(8,128)(2,1)} %weight.7) | copy-start | bytes 50331652
  20.3 3.4 %collective-permute-start = (bf16[4,4096]{1,0:T(4,128)(2,1)S(1)}, bf16[4,4096]{1,0:T(4,128)(2,1)S(1)}, u32[]{:S(2)}, u32[]{:S(2)}) collective-permute-start(bf16[4,4096]{1,0:T(4,128)(2,1)S(1)} %project_3.1), channel_id=1, source_target_pairs={{0,3},{1,2},{2,1},{3,0},{4,7},{5,6},{6,5},{7,4},{8,11},{9,10},{10,... | collective-permute-start | bytes 98312 | tf_op jit(solution)/shard_map/ppermute | solution.py:190
  20.3 4.1 %collective-permute-start.1 = (bf16[4,4096]{1,0:T(4,128)(2,1)S(1)}, bf16[4,4096]{1,0:T(4,128)(2,1)S(1)}, u32[]{:S(2)}, u32[]{:S(2)}) collective-permute-start(bf16[4,4096]{1,0:T(4,128)(2,1)S(1)} %project_2.1), channel_id=1, source_target_pairs={{0,2},{1,3},{2,0},{3,1},{4,6},{5,7},{6,4},{7,5},{8,10},{9,11},{10,... | collective-permute-start | bytes 98312 | tf_op jit(solution)/shard_map/ppermute | solution.py:190
  22.0 2.3 %collective-permute-start.2 = (bf16[4,4096]{1,0:T(4,128)(2,1)S(1)}, bf16[4,4096]{1,0:T(4,128)(2,1)S(1)}, u32[]{:S(2)}, u32[]{:S(2)}) collective-permute-start(bf16[4,4096]{1,0:T(4,128)(2,1)S(1)} %project_1.1), channel_id=1, source_target_pairs={{0,1},{1,0},{2,3},{3,2},{4,5},{5,4},{6,7},{7,6},{8,9},{9,8},{10,11... | collective-permute-start | bytes 98312 | tf_op jit(solution)/shard_map/ppermute | solution.py:190
  24.4 5.9 %collective-permute-start.5 = (bf16[4,4096]{1,0:T(4,128)(2,1)S(1)}, bf16[4,4096]{1,0:T(4,128)(2,1)S(1)}, u32[]{:S(2)}, u32[]{:S(2)}) collective-permute-start(bf16[4,4096]{1,0:T(4,128)(2,1)S(1)} %add_near.1.refs_0_), channel_id=1, source_target_pairs={{0,12},{1,13},{2,14},{3,15},{4,8},{5,9},{6,10},{7,11},{8,4},{9,5},... | collective-permute-start | bytes 98312 | tf_op jit(solution)/shard_map/ppermute | solution.py:190
  25.4 5.5 %collective-permute-start.4 = (bf16[4,4096]{1,0:T(4,128)(2,1)S(1)}, bf16[4,4096]{1,0:T(4,128)(2,1)S(1)}, u32[]{:S(2)}, u32[]{:S(2)}) collective-permute-start(bf16[4,4096]{1,0:T(4,128)(2,1)S(1)} %add_near.1.refs_0_), channel_id=1, source_target_pairs={{0,8},{1,9},{2,10},{3,11},{4,12},{5,13},{6,14},{7,15},{8,0},{9,1},... | collective-permute-start | bytes 98312 | tf_op jit(solution)/shard_map/ppermute | solution.py:190
  26.2 4.7 %collective-permute-start.3 = (bf16[4,4096]{1,0:T(4,128)(2,1)S(1)}, bf16[4,4096]{1,0:T(4,128)(2,1)S(1)}, u32[]{:S(2)}, u32[]{:S(2)}) collective-permute-start(bf16[4,4096]{1,0:T(4,128)(2,1)S(1)} %add_near.1.refs_0_), channel_id=1, source_target_pairs={{0,4},{1,5},{2,6},{3,7},{4,0},{5,1},{6,2},{7,3},{8,12},{9,13},{10,... | collective-permute-start | bytes 98312 | tf_op jit(solution)/shard_map/ppermute | solution.py:190
  31.0 3.5 %collective-permute-start.8 = (bf16[4,4096]{1,0:T(4,128)(2,1)S(1)}, bf16[4,4096]{1,0:T(4,128)(2,1)S(1)}, u32[]{:S(2)}, u32[]{:S(2)}) collective-permute-start(bf16[4,4096]{1,0:T(4,128)(2,1)S(1)} %add_far.1.refs_0_), channel_id=1, source_target_pairs={{0,3},{1,2},{2,1},{3,0},{4,7},{5,6},{6,5},{7,4},{8,11},{9,10},{10,... | collective-permute-start | bytes 98312 | tf_op jit(solution)/shard_map/ppermute | solution.py:190
  31.0 4.1 %collective-permute-start.7 = (bf16[4,4096]{1,0:T(4,128)(2,1)S(1)}, bf16[4,4096]{1,0:T(4,128)(2,1)S(1)}, u32[]{:S(2)}, u32[]{:S(2)}) collective-permute-start(bf16[4,4096]{1,0:T(4,128)(2,1)S(1)} %add_far.1.refs_0_), channel_id=1, source_target_pairs={{0,2},{1,3},{2,0},{3,1},{4,6},{5,7},{6,4},{7,5},{8,10},{9,11},{10,... | collective-permute-start | bytes 98312 | tf_op jit(solution)/shard_map/ppermute | solution.py:190
  32.3 2.8 %collective-permute-start.6 = (bf16[4,4096]{1,0:T(4,128)(2,1)S(1)}, bf16[4,4096]{1,0:T(4,128)(2,1)S(1)}, u32[]{:S(2)}, u32[]{:S(2)}) collective-permute-start(bf16[4,4096]{1,0:T(4,128)(2,1)S(1)} %add_far.1.refs_0_), channel_id=1, source_target_pairs={{0,1},{1,0},{2,3},{3,2},{4,5},{5,4},{6,7},{7,6},{8,9},{9,8},{10,11... | collective-permute-start | bytes 98312 | tf_op jit(solution)/shard_map/ppermute | solution.py:190

commit v29 on v24

--- a/solution.py
+++ b/solution.py
@@ -142,7 +142,7 @@
     packed[...] = staged[...].astype(jnp.bfloat16)
 
 
-def combine_kernel(heads_dev, packed, left, attended):
+def project_first_kernel(heads_dev, partner, packed, weight, left, out, attended):
     rows = left.shape[0]
     stats = packed[:, rows].astype(jnp.float32)
     lanes = stats.shape[-1]
@@ -162,6 +162,7 @@
         [attended[pl.ds(j, rows, stride=heads_dev), :].astype(jnp.bfloat16) for j in range(heads_dev)], axis=1
     )
     left[...] = rounded
+    project_kernel(partner, left, weight, out)
 
 
 def project_kernel(partner, left, weight, out):
@@ -252,18 +253,20 @@
     depth = heads_dev * HD
     cost = pl.CostEstimate(flops=1024, bytes_accessed=1024, transcendentals=0)
     small = pltpu.CompilerParams(vmem_limit_bytes=SMALL_VMEM)
-    left = pl.pallas_call(
-        functools.partial(combine_kernel, heads_dev),
-        out_shape=jax.ShapeDtypeStruct((rows, depth), jnp.bfloat16),
-        in_specs=[VMEM],
-        out_specs=VMEM,
+    rounded = jax.ShapeDtypeStruct((rows, part), jnp.bfloat16)
+    left, across = pl.pallas_call(
+        functools.partial(project_first_kernel, heads_dev, 2),
+        out_shape=[jax.ShapeDtypeStruct((rows, depth), jnp.bfloat16), rounded],
+        in_specs=[VMEM] * 2,
+        out_specs=[VMEM] * 2,
         scratch_shapes=[pltpu.VMEM((rows * heads_dev, HD), jnp.float32)],
         compiler_params=small,
-        name="combine",
-    )(received)
+        cost_estimate=cost,
+        name="project_first",
+    )(received, resident)
     arrived = []
     for x in reversed(range(inner)):
-        terms = pl.pallas_call(
+        terms = across if x == 2 else pl.pallas_call(
             functools.partial(project_kernel, x),
             out_shape=jax.ShapeDtypeStruct((rows, part), jnp.bfloat16 if x else jnp.float32),
             in_specs=[VMEM] * 2,

time: 35.9 us -> 36.7 us (1.022)
  waiting for transfers between devices: 5.19 us -> 5.68 us
    pallas_call x1, Pallas kernels: 0.25 us -> 0.91 us  [body(): pl.pallas_call(functools.partial(project_first_kernel, heads_dev, 2), out...]
    pallas_call x4 -> x3, Pallas kernels: 2.63 us -> 1.98 us  [body(): pl.pallas_call(functools.partial(project_kernel, x), out_shape=jax.ShapeD...]
    ppermute x9, waiting for transfers between devices: 5.19 us -> 5.68 us  [exchange(): lax.ppermute(array, 'kvp', [(i, i ^ partner) for i in range(devices)])]
  transfers between devices with their start and end apart: 9 -> 9, of which waited for: 6 -> 7; matrix products, arithmetic and copies ran while one was open for 0% -> 0% of each run, Pallas kernels for 4% -> 2%
where the time goes in v29:
time: 36.7 us; the launch traced here: 36.5 us
  blocking collectives  14.6 us (40%)
  starting transfers between devices  8.54 us (23%)
  Pallas kernels  7.59 us (21%)
  waiting for transfers between devices  5.68 us (15%)
    all_to_all x1, blocking collectives, body(): lax.all_to_all(packed, 'kvp', split_axis=0, concat_axis=0, tiled=True)  14.6 us
    ppermute x9, starting transfers between devices, exchange(): lax.ppermute(array, 'kvp', [(i, i ^ partner) for i in range(devices)])  8.54 us
    ppermute x9, waiting for transfers between devices, exchange(): lax.ppermute(array, 'kvp', [(i, i ^ partner) for i in range(devices)])  5.68 us
    pallas_call x1, Pallas kernels, body(): pl.pallas_call(functools.partial(attend_kernel, heads_dev, devices), out_...  3.95 us
    pallas_call x3, Pallas kernels, body(): pl.pallas_call(functools.partial(project_kernel, x), out_shape=jax.ShapeD...  1.98 us
    pallas_call x1, Pallas kernels, body(): pl.pallas_call(functools.partial(project_first_kernel, heads_dev, 2), out...  0.91 us
  transfers between devices with their start and end apart: 9, of which 7 were waited for; matrix products, arithmetic and copies ran while one was open for 0% of the time, Pallas kernels for 2%

profile of v29, /device:TPU:0, one launch (start us, length us, event | category | flops | bytes accessed | tf_op | source)
XLA Modules:
  0.0 36.5 jit_solution(15242373582200833029)
XLA Ops:
  0.0 3.9 %attend.1.staged = f32[16,5,4,128]{3,2,1,0:T(4,128)S(1)} custom-call(s32[4,12]{1,0:T(4,128)} %refs_0_.1, s32[4]{0:T(128)} %refs_1_.1, f32[4,48]{1,0:T(4,128)} %bitcast.2, f32[4,48]{1,0:T(4,128)} %bitcast.3, bf16[4,8192]{1,0:T(4,128)(2,1)} %refs_4_.1, bf16[48,64,512]{2,1,0:T(8,128)(2,1)} %refs_5_.1, bf16[48,64,512]{2,1,0:T(8,128)(2,1)} %refs_6_.1), custom_call_target="tpu_custom_call" | custom-call | flops 100663296 | bytes 6291456 | tf_op jit(solution)/shard_map/attend/pallas_call | solution.py:210
  4.0 0.0 copy-start
  4.0 14.6 %all_to_all.5.packed = bf16[16,5,4,128]{3,2,1,0:T(4,128)(2,1)S(1)} all-to-all(bf16[16,5,4,128]{3,2,1,0:T(4,128)(2,1)S(1)} %pack.1), channel_id=1, replica_groups=mesh['group'=2,'kvp'=16] {'kvp'}, dimensions={0} | all-to-all | bytes 163840 | tf_op jit(solution)/shard_map/all_to_all | solution.py:250
  18.6 0.0 copy-done
  18.6 0.9 %project_first.1 = (bf16[4,512]{1,0:T(4,128)(2,1)S(1)}, bf16[4,4096]{1,0:T(4,128)(2,1)S(1)}) custom-call(bf16[16,5,4,128]{3,2,1,0:T(4,128)(2,1)S(1)} %all_to_all.5.packed, bf16[512,16384]{1,0:T(8,128)(2,1)S(1)} %copy-done), custom_call_target="tpu_custom_call" | custom-call | flops 1024 | bytes 1024 | tf_op jit(solution)/shard_map/project_first/pallas_call | solution.py:257
  19.5 0.7 %project_1.1 = bf16[4,4096]{1,0:T(4,128)(2,1)S(1)} custom-call(bf16[4,512]{1,0:T(4,128)(2,1)S(1)} %get-tuple-element.7.left, bf16[512,16384]{1,0:T(8,128)(2,1)S(1)} %copy-done), custom_call_target="tpu_custom_call" | custom-call | flops 1024 | bytes 1024 | tf_op jit(solution)/shard_map/project_1/pallas_call | solution.py:269
  20.2 0.7 %project_3.1 = bf16[4,4096]{1,0:T(4,128)(2,1)S(1)} custom-call(bf16[4,512]{1,0:T(4,128)(2,1)S(1)} %get-tuple-element.7.left, bf16[512,16384]{1,0:T(8,128)(2,1)S(1)} %copy-done), custom_call_target="tpu_custom_call" | custom-call | flops 1024 | bytes 1024 | tf_op jit(solution)/shard_map/project_3/pallas_call | solution.py:269
  20.8 0.0 collective-permute-start
  20.9 0.1 collective-permute-start.2
  20.9 2.1 %collective-permute-start.1 = (bf16[4,4096]{1,0:T(4,128)(2,1)S(1)}, bf16[4,4096]{1,0:T(4,128)(2,1)S(1)}, u32[]{:S(2)}, u32[]{:S(2)}) collective-permute-start(bf16[4,4096]{1,0:T(4,128)(2,1)S(1)} %get-tuple-element.8), channel_id=1, source_target_pairs={{0,2},{1,3},{2,0},{3,1},{4,6},{5,7},{6,4},{7,5},{8,10},{9,11},{10,... | collective-permute-start | bytes 98312 | tf_op jit(solution)/shard_map/ppermute | solution.py:193
  23.0 0.7 %project_0.1.refs_3_ = f32[4,4096]{1,0:T(4,128)S(1)} custom-call(bf16[4,512]{1,0:T(4,128)(2,1)S(1)} %get-tuple-element.7.left, bf16[512,16384]{1,0:T(8,128)(2,1)S(1)} %copy-done), custom_call_target="tpu_custom_call" | custom-call | flops 1024 | bytes 1024 | tf_op jit(solution)/shard_map/project_0/pallas_call | solution.py:269
  23.7 0.6 %collective-permute-done.refs_0_ = bf16[4,4096]{1,0:T(4,128)(2,1)S(1)} collective-permute-done((bf16[4,4096]{1,0:T(4,128)(2,1)S(1)}, bf16[4,4096]{1,0:T(4,128)(2,1)S(1)}, u32[]{:S(2)}, u32[]{:S(2)}) %collective-permute-start) | collective-permute-done | bytes 32800 | tf_op jit(solution)/shard_map/ppermute | solution.py:193
  24.2 0.0 collective-permute-done.2.refs_2_
  24.2 0.7 %collective-permute-done.1.refs_1_ = bf16[4,4096]{1,0:T(4,128)(2,1)S(1)} collective-permute-done((bf16[4,4096]{1,0:T(4,128)(2,1)S(1)}, bf16[4,4096]{1,0:T(4,128)(2,1)S(1)}, u32[]{:S(2)}, u32[]{:S(2)}) %collective-permute-start.1) | collective-permute-done | bytes 32800 | tf_op jit(solution)/shard_map/ppermute | solution.py:193
  25.0 1.3 %collective-permute-start.5 = (bf16[4,4096]{1,0:T(4,128)(2,1)S(1)}, bf16[4,4096]{1,0:T(4,128)(2,1)S(1)}, u32[]{:S(2)}, u32[]{:S(2)}) collective-permute-start(bf16[4,4096]{1,0:T(4,128)(2,1)S(1)} %add_near.1.refs_0_), channel_id=1, source_target_pairs={{0,12},{1,13},{2,14},{3,15},{4,8},{5,9},{6,10},{7,11},{8,4},{9,5},... | collective-permute-start | bytes 98312 | tf_op jit(solution)/shard_map/ppermute | solution.py:193
  26.3 0.9 %collective-permute-start.4 = (bf16[4,4096]{1,0:T(4,128)(2,1)S(1)}, bf16[4,4096]{1,0:T(4,128)(2,1)S(1)}, u32[]{:S(2)}, u32[]{:S(2)}) collective-permute-start(bf16[4,4096]{1,0:T(4,128)(2,1)S(1)} %add_near.1.refs_0_), channel_id=1, source_target_pairs={{0,8},{1,9},{2,10},{3,11},{4,12},{5,13},{6,14},{7,15},{8,0},{9,1},... | collective-permute-start | bytes 98312 | tf_op jit(solution)/shard_map/ppermute | solution.py:193
  27.1 2.3 %collective-permute-start.3 = (bf16[4,4096]{1,0:T(4,128)(2,1)S(1)}, bf16[4,4096]{1,0:T(4,128)(2,1)S(1)}, u32[]{:S(2)}, u32[]{:S(2)}) collective-permute-start(bf16[4,4096]{1,0:T(4,128)(2,1)S(1)} %add_near.1.refs_0_), channel_id=1, source_target_pairs={{0,4},{1,5},{2,6},{3,7},{4,0},{5,1},{6,2},{7,3},{8,12},{9,13},{10,... | collective-permute-start | bytes 98312 | tf_op jit(solution)/shard_map/ppermute | solution.py:193
  29.4 1.3 %collective-permute-done.5.refs_3_ = bf16[4,4096]{1,0:T(4,128)(2,1)S(1)} collective-permute-done((bf16[4,4096]{1,0:T(4,128)(2,1)S(1)}, bf16[4,4096]{1,0:T(4,128)(2,1)S(1)}, u32[]{:S(2)}, u32[]{:S(2)}) %collective-permute-start.5) | collective-permute-done | bytes 32800 | tf_op jit(solution)/shard_map/ppermute | solution.py:193
  30.7 0.8 %collective-permute-done.4.refs_2_ = bf16[4,4096]{1,0:T(4,128)(2,1)S(1)} collective-permute-done((bf16[4,4096]{1,0:T(4,128)(2,1)S(1)}, bf16[4,4096]{1,0:T(4,128)(2,1)S(1)}, u32[]{:S(2)}, u32[]{:S(2)}) %collective-permute-start.4) | collective-permute-done | bytes 32800 | tf_op jit(solution)/shard_map/ppermute | solution.py:193
  31.5 0.1 collective-permute-done.3.refs_1_
  31.7 0.1 collective-permute-start.8
  31.8 1.7 %collective-permute-start.7 = (bf16[4,4096]{1,0:T(4,128)(2,1)S(1)}, bf16[4,4096]{1,0:T(4,128)(2,1)S(1)}, u32[]{:S(2)}, u32[]{:S(2)}) collective-permute-start(bf16[4,4096]{1,0:T(4,128)(2,1)S(1)} %add_far.1.refs_0_), channel_id=1, source_target_pairs={{0,2},{1,3},{2,0},{3,1},{4,6},{5,7},{6,4},{7,5},{8,10},{9,11},{10,... | collective-permute-start | bytes 98312 | tf_op jit(solution)/shard_map/ppermute | solution.py:193
  33.5 0.2 collective-permute-start.6
  33.6 1.6 %collective-permute-done.8.refs_3_ = bf16[4,4096]{1,0:T(4,128)(2,1)S(1)} collective-permute-done((bf16[4,4096]{1,0:T(4,128)(2,1)S(1)}, bf16[4,4096]{1,0:T(4,128)(2,1)S(1)}, u32[]{:S(2)}, u32[]{:S(2)}) %collective-permute-start.8) | collective-permute-done | bytes 32800 | tf_op jit(solution)/shard_map/ppermute | solution.py:193
  35.2 0.5 %collective-permute-done.7.refs_2_ = bf16[4,4096]{1,0:T(4,128)(2,1)S(1)} collective-permute-done((bf16[4,4096]{1,0:T(4,128)(2,1)S(1)}, bf16[4,4096]{1,0:T(4,128)(2,1)S(1)}, u32[]{:S(2)}, u32[]{:S(2)}) %collective-permute-start.7) | collective-permute-done | bytes 32800 | tf_op jit(solution)/shard_map/ppermute | solution.py:193
  35.8 0.0 collective-permute-done.6.refs_1_
  35.8 0.7 %lay.1 = bf16[4,16384]{1,0:T(4,128)(2,1)} custom-call(bf16[4,4096]{1,0:T(4,128)(2,1)S(1)} %add_far.1.refs_0_, bf16[4,4096]{1,0:T(4,128)(2,1)S(1)} %collective-permute-done.6.refs_1_, bf16[4,4096]{1,0:T(4,128)(2,1)S(1)} %collective-permute-done.7.refs_2_, bf16[4,4096]{1,0:T(4,128)(2,1)S(1)} %collective-permute-done.8.refs_3_), custom_call_target="tpu_custom_call" | custom-call | tf_op jit(solution)/shard_map/lay/pallas_call | solution.py:293
  (3 shorter events, 0.1 us)
Async XLA Ops:
  4.0 14.7 %copy-start = (bf16[512,16384]{1,0:T(8,128)(2,1)S(1)}, bf16[512,16384]{1,0:T(8,128)(2,1)}, u32[]{:S(2)}) copy-start(bf16[512,16384]{1,0:T(8,128)(2,1)} %weight.7) | copy-start | bytes 50331652
  20.8 3.4 %collective-permute-start = (bf16[4,4096]{1,0:T(4,128)(2,1)S(1)}, bf16[4,4096]{1,0:T(4,128)(2,1)S(1)}, u32[]{:S(2)}, u32[]{:S(2)}) collective-permute-start(bf16[4,4096]{1,0:T(4,128)(2,1)S(1)} %project_3.1), channel_id=1, source_target_pairs={{0,3},{1,2},{2,1},{3,0},{4,7},{5,6},{6,5},{7,4},{8,11},{9,10},{10,... | collective-permute-start | bytes 98312 | tf_op jit(solution)/shard_map/ppermute | solution.py:193
  20.9 3.4 %collective-permute-start.2 = (bf16[4,4096]{1,0:T(4,128)(2,1)S(1)}, bf16[4,4096]{1,0:T(4,128)(2,1)S(1)}, u32[]{:S(2)}, u32[]{:S(2)}) collective-permute-start(bf16[4,4096]{1,0:T(4,128)(2,1)S(1)} %project_1.1), channel_id=1, source_target_pairs={{0,1},{1,0},{2,3},{3,2},{4,5},{5,4},{6,7},{7,6},{8,9},{9,8},{10,11... | collective-permute-start | bytes 98312 | tf_op jit(solution)/shard_map/ppermute | solution.py:193
  20.9 4.0 %collective-permute-start.1 = (bf16[4,4096]{1,0:T(4,128)(2,1)S(1)}, bf16[4,4096]{1,0:T(4,128)(2,1)S(1)}, u32[]{:S(2)}, u32[]{:S(2)}) collective-permute-start(bf16[4,4096]{1,0:T(4,128)(2,1)S(1)} %get-tuple-element.8), channel_id=1, source_target_pairs={{0,2},{1,3},{2,0},{3,1},{4,6},{5,7},{6,4},{7,5},{8,10},{9,11},{10,... | collective-permute-start | bytes 98312 | tf_op jit(solution)/shard_map/ppermute | solution.py:193
  25.0 5.8 %collective-permute-start.5 = (bf16[4,4096]{1,0:T(4,128)(2,1)S(1)}, bf16[4,4096]{1,0:T(4,128)(2,1)S(1)}, u32[]{:S(2)}, u32[]{:S(2)}) collective-permute-start(bf16[4,4096]{1,0:T(4,128)(2,1)S(1)} %add_near.1.refs_0_), channel_id=1, source_target_pairs={{0,12},{1,13},{2,14},{3,15},{4,8},{5,9},{6,10},{7,11},{8,4},{9,5},... | collective-permute-start | bytes 98312 | tf_op jit(solution)/shard_map/ppermute | solution.py:193
  26.3 5.3 %collective-permute-start.4 = (bf16[4,4096]{1,0:T(4,128)(2,1)S(1)}, bf16[4,4096]{1,0:T(4,128)(2,1)S(1)}, u32[]{:S(2)}, u32[]{:S(2)}) collective-permute-start(bf16[4,4096]{1,0:T(4,128)(2,1)S(1)} %add_near.1.refs_0_), channel_id=1, source_target_pairs={{0,8},{1,9},{2,10},{3,11},{4,12},{5,13},{6,14},{7,15},{8,0},{9,1},... | collective-permute-start | bytes 98312 | tf_op jit(solution)/shard_map/ppermute | solution.py:193
  27.1 4.5 %collective-permute-start.3 = (bf16[4,4096]{1,0:T(4,128)(2,1)S(1)}, bf16[4,4096]{1,0:T(4,128)(2,1)S(1)}, u32[]{:S(2)}, u32[]{:S(2)}) collective-permute-start(bf16[4,4096]{1,0:T(4,128)(2,1)S(1)} %add_near.1.refs_0_), channel_id=1, source_target_pairs={{0,4},{1,5},{2,6},{3,7},{4,0},{5,1},{6,2},{7,3},{8,12},{9,13},{10,... | collective-permute-start | bytes 98312 | tf_op jit(solution)/shard_map/ppermute | solution.py:193
  31.7 3.6 %collective-permute-start.8 = (bf16[4,4096]{1,0:T(4,128)(2,1)S(1)}, bf16[4,4096]{1,0:T(4,128)(2,1)S(1)}, u32[]{:S(2)}, u32[]{:S(2)}) collective-permute-start(bf16[4,4096]{1,0:T(4,128)(2,1)S(1)} %add_far.1.refs_0_), channel_id=1, source_target_pairs={{0,3},{1,2},{2,1},{3,0},{4,7},{5,6},{6,5},{7,4},{8,11},{9,10},{10,... | collective-permute-start | bytes 98312 | tf_op jit(solution)/shard_map/ppermute | solution.py:193
  31.8 4.0 %collective-permute-start.7 = (bf16[4,4096]{1,0:T(4,128)(2,1)S(1)}, bf16[4,4096]{1,0:T(4,128)(2,1)S(1)}, u32[]{:S(2)}, u32[]{:S(2)}) collective-permute-start(bf16[4,4096]{1,0:T(4,128)(2,1)S(1)} %add_far.1.refs_0_), channel_id=1, source_target_pairs={{0,2},{1,3},{2,0},{3,1},{4,6},{5,7},{6,4},{7,5},{8,10},{9,11},{10,... | collective-permute-start | bytes 98312 | tf_op jit(solution)/shard_map/ppermute | solution.py:193
  33.5 2.3 %collective-permute-start.6 = (bf16[4,4096]{1,0:T(4,128)(2,1)S(1)}, bf16[4,4096]{1,0:T(4,128)(2,1)S(1)}, u32[]{:S(2)}, u32[]{:S(2)}) collective-permute-start(bf16[4,4096]{1,0:T(4,128)(2,1)S(1)} %add_far.1.refs_0_), channel_id=1, source_target_pairs={{0,1},{1,0},{2,3},{3,2},{4,5},{5,4},{6,7},{7,6},{8,9},{9,8},{10,11... | collective-permute-start | bytes 98312 | tf_op jit(solution)/shard_map/ppermute | solution.py:193

commit v30 on v24

--- a/solution.py
+++ b/solution.py
@@ -225,7 +225,7 @@
             pltpu.VMEM((rows, pages * PAGE), jnp.float32),
             pltpu.VMEM((rows, heads, pages * PAGE), jnp.bfloat16),
             pltpu.SemaphoreType.DMA((6,)),
-            pltpu.SemaphoreType.DMA((2, 2)),
+            pltpu.SemaphoreType.DMA((2, 1)),
         ],
         compiler_params=pltpu.CompilerParams(vmem_limit_bytes=ATTEND_VMEM),
         cost_estimate=pl.CostEstimate(

time: 35.9 us -> 35.9 us (level)
  no operation moved by 1% of the time
where the time goes in v30:
time: 35.9 us; the launch traced here: 35.7 us
  blocking collectives  14.6 us (41%)
  starting transfers between devices  8.27 us (23%)
  Pallas kernels  7.6 us (21%)
  waiting for transfers between devices  5.19 us (14%)
    all_to_all x1, blocking collectives, body(): lax.all_to_all(packed, 'kvp', split_axis=0, concat_axis=0, tiled=True)  14.6 us
    ppermute x9, starting transfers between devices, exchange(): lax.ppermute(array, 'kvp', [(i, i ^ partner) for i in range(devices)])  8.27 us
    ppermute x9, waiting for transfers between devices, exchange(): lax.ppermute(array, 'kvp', [(i, i ^ partner) for i in range(devices)])  5.19 us
    pallas_call x1, Pallas kernels, body(): pl.pallas_call(functools.partial(attend_kernel, heads_dev, devices), out_...  3.96 us
    pallas_call x4, Pallas kernels, body(): pl.pallas_call(functools.partial(project_kernel, x), out_shape=jax.ShapeD...  2.63 us
  transfers between devices with their start and end apart: 9, of which 6 were waited for; matrix products, arithmetic and copies ran while one was open for 0% of the time, Pallas kernels for 4%

profile of v30, /device:TPU:0, one launch (start us, length us, event | category | flops | bytes accessed | tf_op | source)
XLA Modules:
  0.0 35.7 jit_solution(8425449097386982256)
XLA Ops:
  0.0 4.0 %attend.1.staged = f32[16,5,4,128]{3,2,1,0:T(4,128)S(1)} custom-call(s32[4,12]{1,0:T(4,128)} %refs_0_.1, s32[4]{0:T(128)} %refs_1_.1, f32[4,48]{1,0:T(4,128)} %bitcast.2, f32[4,48]{1,0:T(4,128)} %bitcast.3, bf16[4,8192]{1,0:T(4,128)(2,1)} %refs_4_.1, bf16[48,64,512]{2,1,0:T(8,128)(2,1)} %refs_5_.1, bf16[48,64,512]{2,1,0:T(8,128)(2,1)} %refs_6_.1), custom_call_target="tpu_custom_call" | custom-call | flops 100663296 | bytes 6291456 | tf_op jit(solution)/shard_map/attend/pallas_call | solution.py:209
  4.0 0.0 copy-start
  4.0 14.6 %all_to_all.5.packed = bf16[16,5,4,128]{3,2,1,0:T(4,128)(2,1)S(1)} all-to-all(bf16[16,5,4,128]{3,2,1,0:T(4,128)(2,1)S(1)} %pack.1), channel_id=1, replica_groups=mesh['group'=2,'kvp'=16] {'kvp'}, dimensions={0} | all-to-all | bytes 163840 | tf_op jit(solution)/shard_map/all_to_all | solution.py:249
  18.6 0.3 combine.1.left
  18.9 0.0 copy-done
  18.9 0.7 %project_2.1 = bf16[4,4096]{1,0:T(4,128)(2,1)S(1)} custom-call(bf16[4,512]{1,0:T(4,128)(2,1)S(1)} %combine.1.left, bf16[512,16384]{1,0:T(8,128)(2,1)S(1)} %copy-done), custom_call_target="tpu_custom_call" | custom-call | flops 1024 | bytes 1024 | tf_op jit(solution)/shard_map/project_2/pallas_call | solution.py:266
  19.5 0.7 %project_3.1 = bf16[4,4096]{1,0:T(4,128)(2,1)S(1)} custom-call(bf16[4,512]{1,0:T(4,128)(2,1)S(1)} %combine.1.left, bf16[512,16384]{1,0:T(8,128)(2,1)S(1)} %copy-done), custom_call_target="tpu_custom_call" | custom-call | flops 1024 | bytes 1024 | tf_op jit(solution)/shard_map/project_3/pallas_call | solution.py:266
  20.2 0.0 collective-permute-start
  20.2 1.1 %collective-permute-start.1 = (bf16[4,4096]{1,0:T(4,128)(2,1)S(1)}, bf16[4,4096]{1,0:T(4,128)(2,1)S(1)}, u32[]{:S(2)}, u32[]{:S(2)}) collective-permute-start(bf16[4,4096]{1,0:T(4,128)(2,1)S(1)} %project_2.1), channel_id=1, source_target_pairs={{0,2},{1,3},{2,0},{3,1},{4,6},{5,7},{6,4},{7,5},{8,10},{9,11},{10,... | collective-permute-start | bytes 98312 | tf_op jit(solution)/shard_map/ppermute | solution.py:192
  21.3 0.7 %project_1.1 = bf16[4,4096]{1,0:T(4,128)(2,1)S(1)} custom-call(bf16[4,512]{1,0:T(4,128)(2,1)S(1)} %combine.1.left, bf16[512,16384]{1,0:T(8,128)(2,1)S(1)} %copy-done), custom_call_target="tpu_custom_call" | custom-call | flops 1024 | bytes 1024 | tf_op jit(solution)/shard_map/project_1/pallas_call | solution.py:266
  22.0 0.8 %collective-permute-start.2 = (bf16[4,4096]{1,0:T(4,128)(2,1)S(1)}, bf16[4,4096]{1,0:T(4,128)(2,1)S(1)}, u32[]{:S(2)}, u32[]{:S(2)}) collective-permute-start(bf16[4,4096]{1,0:T(4,128)(2,1)S(1)} %project_1.1), channel_id=1, source_target_pairs={{0,1},{1,0},{2,3},{3,2},{4,5},{5,4},{6,7},{7,6},{8,9},{9,8},{10,11... | collective-permute-start | bytes 98312 | tf_op jit(solution)/shard_map/ppermute | solution.py:192
  22.8 0.7 %project_0.1.refs_3_ = f32[4,4096]{1,0:T(4,128)S(1)} custom-call(bf16[4,512]{1,0:T(4,128)(2,1)S(1)} %combine.1.left, bf16[512,16384]{1,0:T(8,128)(2,1)S(1)} %copy-done), custom_call_target="tpu_custom_call" | custom-call | flops 1024 | bytes 1024 | tf_op jit(solution)/shard_map/project_0/pallas_call | solution.py:266
  23.4 0.2 collective-permute-done.refs_0_
  23.6 0.7 %collective-permute-done.1.refs_1_ = bf16[4,4096]{1,0:T(4,128)(2,1)S(1)} collective-permute-done((bf16[4,4096]{1,0:T(4,128)(2,1)S(1)}, bf16[4,4096]{1,0:T(4,128)(2,1)S(1)}, u32[]{:S(2)}, u32[]{:S(2)}) %collective-permute-start.1) | collective-permute-done | bytes 32800 | tf_op jit(solution)/shard_map/ppermute | solution.py:192
  24.3 0.0 collective-permute-done.2.refs_2_
  24.3 1.0 %collective-permute-start.5 = (bf16[4,4096]{1,0:T(4,128)(2,1)S(1)}, bf16[4,4096]{1,0:T(4,128)(2,1)S(1)}, u32[]{:S(2)}, u32[]{:S(2)}) collective-permute-start(bf16[4,4096]{1,0:T(4,128)(2,1)S(1)} %add_near.1.refs_0_), channel_id=1, source_target_pairs={{0,12},{1,13},{2,14},{3,15},{4,8},{5,9},{6,10},{7,11},{8,4},{9,5},... | collective-permute-start | bytes 98312 | tf_op jit(solution)/shard_map/ppermute | solution.py:192
  25.3 0.8 %collective-permute-start.4 = (bf16[4,4096]{1,0:T(4,128)(2,1)S(1)}, bf16[4,4096]{1,0:T(4,128)(2,1)S(1)}, u32[]{:S(2)}, u32[]{:S(2)}) collective-permute-start(bf16[4,4096]{1,0:T(4,128)(2,1)S(1)} %add_near.1.refs_0_), channel_id=1, source_target_pairs={{0,8},{1,9},{2,10},{3,11},{4,12},{5,13},{6,14},{7,15},{8,0},{9,1},... | collective-permute-start | bytes 98312 | tf_op jit(solution)/shard_map/ppermute | solution.py:192
  26.2 2.6 %collective-permute-start.3 = (bf16[4,4096]{1,0:T(4,128)(2,1)S(1)}, bf16[4,4096]{1,0:T(4,128)(2,1)S(1)}, u32[]{:S(2)}, u32[]{:S(2)}) collective-permute-start(bf16[4,4096]{1,0:T(4,128)(2,1)S(1)} %add_near.1.refs_0_), channel_id=1, source_target_pairs={{0,4},{1,5},{2,6},{3,7},{4,0},{5,1},{6,2},{7,3},{8,12},{9,13},{10,... | collective-permute-start | bytes 98312 | tf_op jit(solution)/shard_map/ppermute | solution.py:192
  28.8 1.5 %collective-permute-done.5.refs_3_ = bf16[4,4096]{1,0:T(4,128)(2,1)S(1)} collective-permute-done((bf16[4,4096]{1,0:T(4,128)(2,1)S(1)}, bf16[4,4096]{1,0:T(4,128)(2,1)S(1)}, u32[]{:S(2)}, u32[]{:S(2)}) %collective-permute-start.5) | collective-permute-done | bytes 32800 | tf_op jit(solution)/shard_map/ppermute | solution.py:192
  30.3 0.6 %collective-permute-done.4.refs_2_ = bf16[4,4096]{1,0:T(4,128)(2,1)S(1)} collective-permute-done((bf16[4,4096]{1,0:T(4,128)(2,1)S(1)}, bf16[4,4096]{1,0:T(4,128)(2,1)S(1)}, u32[]{:S(2)}, u32[]{:S(2)}) %collective-permute-start.4) | collective-permute-done | bytes 32800 | tf_op jit(solution)/shard_map/ppermute | solution.py:192
  30.9 0.0 collective-permute-done.3.refs_1_
  30.9 0.1 collective-permute-start.8
  31.0 1.3 %collective-permute-start.7 = (bf16[4,4096]{1,0:T(4,128)(2,1)S(1)}, bf16[4,4096]{1,0:T(4,128)(2,1)S(1)}, u32[]{:S(2)}, u32[]{:S(2)}) collective-permute-start(bf16[4,4096]{1,0:T(4,128)(2,1)S(1)} %add_far.1.refs_0_), channel_id=1, source_target_pairs={{0,2},{1,3},{2,0},{3,1},{4,6},{5,7},{6,4},{7,5},{8,10},{9,11},{10,... | collective-permute-start | bytes 98312 | tf_op jit(solution)/shard_map/ppermute | solution.py:192
  32.3 0.6 %collective-permute-start.6 = (bf16[4,4096]{1,0:T(4,128)(2,1)S(1)}, bf16[4,4096]{1,0:T(4,128)(2,1)S(1)}, u32[]{:S(2)}, u32[]{:S(2)}) collective-permute-start(bf16[4,4096]{1,0:T(4,128)(2,1)S(1)} %add_far.1.refs_0_), channel_id=1, source_target_pairs={{0,1},{1,0},{2,3},{3,2},{4,5},{5,4},{6,7},{7,6},{8,9},{9,8},{10,11... | collective-permute-start | bytes 98312 | tf_op jit(solution)/shard_map/ppermute | solution.py:192
  32.8 1.6 %collective-permute-done.8.refs_3_ = bf16[4,4096]{1,0:T(4,128)(2,1)S(1)} collective-permute-done((bf16[4,4096]{1,0:T(4,128)(2,1)S(1)}, bf16[4,4096]{1,0:T(4,128)(2,1)S(1)}, u32[]{:S(2)}, u32[]{:S(2)}) %collective-permute-start.8) | collective-permute-done | bytes 32800 | tf_op jit(solution)/shard_map/ppermute | solution.py:192
  34.4 0.6 %collective-permute-done.7.refs_2_ = bf16[4,4096]{1,0:T(4,128)(2,1)S(1)} collective-permute-done((bf16[4,4096]{1,0:T(4,128)(2,1)S(1)}, bf16[4,4096]{1,0:T(4,128)(2,1)S(1)}, u32[]{:S(2)}, u32[]{:S(2)}) %collective-permute-start.7) | collective-permute-done | bytes 32800 | tf_op jit(solution)/shard_map/ppermute | solution.py:192
  35.0 0.0 collective-permute-done.6.refs_1_
  35.0 0.7 %lay.1 = bf16[4,16384]{1,0:T(4,128)(2,1)} custom-call(bf16[4,4096]{1,0:T(4,128)(2,1)S(1)} %add_far.1.refs_0_, bf16[4,4096]{1,0:T(4,128)(2,1)S(1)} %collective-permute-done.6.refs_1_, bf16[4,4096]{1,0:T(4,128)(2,1)S(1)} %collective-permute-done.7.refs_2_, bf16[4,4096]{1,0:T(4,128)(2,1)S(1)} %collective-permute-done.8.refs_3_), custom_call_target="tpu_custom_call" | custom-call | tf_op jit(solution)/shard_map/lay/pallas_call | solution.py:290
  (3 shorter events, 0.1 us)
Async XLA Ops:
  4.0 14.9 %copy-start = (bf16[512,16384]{1,0:T(8,128)(2,1)S(1)}, bf16[512,16384]{1,0:T(8,128)(2,1)}, u32[]{:S(2)}) copy-start(bf16[512,16384]{1,0:T(8,128)(2,1)} %weight.7) | copy-start | bytes 50331652
  20.2 3.4 %collective-permute-start = (bf16[4,4096]{1,0:T(4,128)(2,1)S(1)}, bf16[4,4096]{1,0:T(4,128)(2,1)S(1)}, u32[]{:S(2)}, u32[]{:S(2)}) collective-permute-start(bf16[4,4096]{1,0:T(4,128)(2,1)S(1)} %project_3.1), channel_id=1, source_target_pairs={{0,3},{1,2},{2,1},{3,0},{4,7},{5,6},{6,5},{7,4},{8,11},{9,10},{10,... | collective-permute-start | bytes 98312 | tf_op jit(solution)/shard_map/ppermute | solution.py:192
  20.2 4.1 %collective-permute-start.1 = (bf16[4,4096]{1,0:T(4,128)(2,1)S(1)}, bf16[4,4096]{1,0:T(4,128)(2,1)S(1)}, u32[]{:S(2)}, u32[]{:S(2)}) collective-permute-start(bf16[4,4096]{1,0:T(4,128)(2,1)S(1)} %project_2.1), channel_id=1, source_target_pairs={{0,2},{1,3},{2,0},{3,1},{4,6},{5,7},{6,4},{7,5},{8,10},{9,11},{10,... | collective-permute-start | bytes 98312 | tf_op jit(solution)/shard_map/ppermute | solution.py:192
  22.0 2.3 %collective-permute-start.2 = (bf16[4,4096]{1,0:T(4,128)(2,1)S(1)}, bf16[4,4096]{1,0:T(4,128)(2,1)S(1)}, u32[]{:S(2)}, u32[]{:S(2)}) collective-permute-start(bf16[4,4096]{1,0:T(4,128)(2,1)S(1)} %project_1.1), channel_id=1, source_target_pairs={{0,1},{1,0},{2,3},{3,2},{4,5},{5,4},{6,7},{7,6},{8,9},{9,8},{10,11... | collective-permute-start | bytes 98312 | tf_op jit(solution)/shard_map/ppermute | solution.py:192
  24.3 5.9 %collective-permute-start.5 = (bf16[4,4096]{1,0:T(4,128)(2,1)S(1)}, bf16[4,4096]{1,0:T(4,128)(2,1)S(1)}, u32[]{:S(2)}, u32[]{:S(2)}) collective-permute-start(bf16[4,4096]{1,0:T(4,128)(2,1)S(1)} %add_near.1.refs_0_), channel_id=1, source_target_pairs={{0,12},{1,13},{2,14},{3,15},{4,8},{5,9},{6,10},{7,11},{8,4},{9,5},... | collective-permute-start | bytes 98312 | tf_op jit(solution)/shard_map/ppermute | solution.py:192
  25.3 5.5 %collective-permute-start.4 = (bf16[4,4096]{1,0:T(4,128)(2,1)S(1)}, bf16[4,4096]{1,0:T(4,128)(2,1)S(1)}, u32[]{:S(2)}, u32[]{:S(2)}) collective-permute-start(bf16[4,4096]{1,0:T(4,128)(2,1)S(1)} %add_near.1.refs_0_), channel_id=1, source_target_pairs={{0,8},{1,9},{2,10},{3,11},{4,12},{5,13},{6,14},{7,15},{8,0},{9,1},... | collective-permute-start | bytes 98312 | tf_op jit(solution)/shard_map/ppermute | solution.py:192
  26.2 4.7 %collective-permute-start.3 = (bf16[4,4096]{1,0:T(4,128)(2,1)S(1)}, bf16[4,4096]{1,0:T(4,128)(2,1)S(1)}, u32[]{:S(2)}, u32[]{:S(2)}) collective-permute-start(bf16[4,4096]{1,0:T(4,128)(2,1)S(1)} %add_near.1.refs_0_), channel_id=1, source_target_pairs={{0,4},{1,5},{2,6},{3,7},{4,0},{5,1},{6,2},{7,3},{8,12},{9,13},{10,... | collective-permute-start | bytes 98312 | tf_op jit(solution)/shard_map/ppermute | solution.py:192
  30.9 3.5 %collective-permute-start.8 = (bf16[4,4096]{1,0:T(4,128)(2,1)S(1)}, bf16[4,4096]{1,0:T(4,128)(2,1)S(1)}, u32[]{:S(2)}, u32[]{:S(2)}) collective-permute-start(bf16[4,4096]{1,0:T(4,128)(2,1)S(1)} %add_far.1.refs_0_), channel_id=1, source_target_pairs={{0,3},{1,2},{2,1},{3,0},{4,7},{5,6},{6,5},{7,4},{8,11},{9,10},{10,... | collective-permute-start | bytes 98312 | tf_op jit(solution)/shard_map/ppermute | solution.py:192
  31.0 4.1 %collective-permute-start.7 = (bf16[4,4096]{1,0:T(4,128)(2,1)S(1)}, bf16[4,4096]{1,0:T(4,128)(2,1)S(1)}, u32[]{:S(2)}, u32[]{:S(2)}) collective-permute-start(bf16[4,4096]{1,0:T(4,128)(2,1)S(1)} %add_far.1.refs_0_), channel_id=1, source_target_pairs={{0,2},{1,3},{2,0},{3,1},{4,6},{5,7},{6,4},{7,5},{8,10},{9,11},{10,... | collective-permute-start | bytes 98312 | tf_op jit(solution)/shard_map/ppermute | solution.py:192
  32.3 2.8 %collective-permute-start.6 = (bf16[4,4096]{1,0:T(4,128)(2,1)S(1)}, bf16[4,4096]{1,0:T(4,128)(2,1)S(1)}, u32[]{:S(2)}, u32[]{:S(2)}) collective-permute-start(bf16[4,4096]{1,0:T(4,128)(2,1)S(1)} %add_far.1.refs_0_), channel_id=1, source_target_pairs={{0,1},{1,0},{2,3},{3,2},{4,5},{5,4},{6,7},{7,6},{8,9},{9,8},{10,11... | collective-permute-start | bytes 98312 | tf_op jit(solution)/shard_map/ppermute | solution.py:192
